TPU v7x, 32 devices: a whole 2x2x4 slice. The times are simulated.
32 devices in a mesh: dp: 2 (over core), proto: 16 (over z, y, x).
Axes of the slice: x: 2, y: 2, z: 4, core: 2. Of those that a mesh axis runs over, the one named last changes fastest.
Arguments:
- features: bfloat16 [1280, 1536], P('dp'), may hold values from -6 to 6
- teacher_features: bfloat16 [256, 1536], P('dp'), may hold values from -8 to 8
- crop_image: int32 [1280], P('dp'), may hold values from 0 to 127, as said below
- crop_view: int32 [1280], P('dp'), may hold values from 0 to 2, as said below
- head_w1: bfloat16 [1536, 2048], P(None, 'proto'), may hold values from -0.15625 to 0.15625
- head_w2: bfloat16 [2048, 256], P('proto'), may hold values from -1 to 1
- protos: bfloat16 [256, 65536], P(None, 'proto'), may hold values from -8 to 8
- teacher_w1: bfloat16 [1536, 2048], P(None, 'proto'), may hold values from -1 to 1
- teacher_w2: bfloat16 [2048, 256], P('proto'), may hold values from -1 to 1
- teacher_protos: bfloat16 [256, 65536], P(None, 'proto'), may hold values from -8 to 8
Outputs:
- grad_features: bfloat16 [1280, 1536], P('dp', 'proto')
- grad_w1: float32 [1536, 2048], P(None, 'proto')
- grad_w2: float32 [2048, 256], P('proto')
- grad_protos: float32 [256, 65536], P(None, 'proto')
Inputs may be any that keep to these rules, and one draw needn't show every extreme that they name: `crop_image`: the rows of each aligned block of 640 crops name exactly the images of that block's index b, b * 64 to (b + 1) * 64 - 1, each ten times, in drawn order. `crop_view`: of the ten crops of each image, one has view 0, one view 1 and eight view 2.
All inputs are finite; a program needn't handle non-finite values.
Results may differ from a plain program's by a relative error of at most 0.006.
Values may be sent and summed in bfloat16 or wider, within the bound.
No kernel may reach another device: no remote copies, remote signals or barrier semaphores. Data moves between devices by JAX's collectives and lax.ppermute only.
A program may use at most 64 MiB of HBM per device.

v0:
```python
import jax
import jax.numpy as jnp
from jax import lax
from jax.sharding import PartitionSpec as P

ITERS = 3


def unit_columns(mat):
    matf = mat.astype(jnp.float32)
    inv = lax.rsqrt(jnp.sum(matf * matf, axis=0, keepdims=True) + 1e-06)
    return (matf * inv, inv)


def unit_rows(mat):
    inv = lax.rsqrt(jnp.sum(mat * mat, axis=1, keepdims=True) + 1e-06)
    return (mat * inv, inv)


def gelu_exact(act):
    return act * 0.5 * (1.0 + lax.erf(act * 0.7071067811865476))


def gelu_slope(act):
    return (
        0.5 * (1.0 + lax.erf(act * 0.7071067811865476))
        + act * jnp.exp(-0.5 * act * act) * 0.3989422804014327
    )


def head_part(rows, first, second):
    act = jnp.dot(rows, first, preferred_element_type=jnp.float32)
    hidden = gelu_exact(act).astype(jnp.bfloat16)
    return (act, hidden, jnp.dot(hidden, second, preferred_element_type=jnp.float32))


def body(
    features,
    teacher_features,
    crop_image,
    crop_view,
    head_w1,
    head_w2,
    protos,
    teacher_w1,
    teacher_w2,
    teacher_protos,
):
    img_dev = teacher_features.shape[0] // 2
    factor = 10.0 / (18 * img_dev * lax.axis_size("dp"))
    w1_block = lax.all_to_all(head_w1, "proto", split_axis=0, concat_axis=1, tiled=True)
    pn, pinv = unit_columns(protos)
    pnb = pn.astype(jnp.bfloat16)
    tpn, tinv = unit_columns(teacher_protos)
    tpnb = tpn.astype(jnp.bfloat16)
    act, hidden, zpart = head_part(features, head_w1, head_w2)
    tact, thidden, tpart = head_part(teacher_features, teacher_w1, teacher_w2)
    zfull, tfull = lax.psum((zpart, tpart), "proto")
    zn, zinv = unit_rows(zfull)
    tzn, tzinv = unit_rows(tfull)
    znb = zn.astype(jnp.bfloat16)
    tznb = tzn.astype(jnp.bfloat16)
    weights = jnp.exp(jnp.dot(tznb, tpnb, preferred_element_type=jnp.float32) / 0.07)
    for step in range(ITERS):
        column_mass = lax.psum(jnp.sum(weights, axis=0), "dp")
        weights = weights / column_mass[None, :]
        if step + 1 < ITERS:
            row_mass = lax.psum(jnp.sum(weights, axis=1), "proto")
            weights = weights / row_mass[:, None]
    logits = jnp.dot(znb, pnb, preferred_element_type=jnp.float32) / 0.1
    expon = jnp.exp(logits)
    row_mass = lax.psum(jnp.sum(weights, axis=1), "proto")
    weights = weights / row_mass[:, None]
    esum = lax.psum(jnp.sum(expon, axis=1), "proto")
    qb = weights.astype(jnp.bfloat16)
    images = crop_image - lax.axis_index("dp") * img_dev
    slots = jnp.arange(2 * img_dev, dtype=jnp.int32)
    select = (slots[None, :] // 2 == images[:, None]) & (slots[None, :] % 2 != crop_view[:, None])
    target = jnp.dot(select.astype(jnp.bfloat16), qb, preferred_element_type=jnp.float32)
    count = jnp.where(crop_view == 2, 2.0, 1.0).astype(jnp.float32)
    grad = ((expon / esum[:, None] * count[:, None] - target) * factor).astype(jnp.bfloat16)
    dpn_local = lax.dot_general(
        znb, grad, (((0,), (0,)), ((), ())), preferred_element_type=jnp.float32
    )
    dzn_part = lax.dot_general(
        grad, pnb, (((1,), (1,)), ((), ())), preferred_element_type=jnp.float32
    )
    dzn = lax.psum(dzn_part, "proto")
    dzb = (zinv * (dzn - zn * jnp.sum(zn * dzn, axis=1, keepdims=True))).astype(jnp.bfloat16)
    local_w2 = lax.dot_general(
        hidden, dzb, (((0,), (0,)), ((), ())), preferred_element_type=jnp.float32
    )
    dhid = (
        lax.dot_general(dzb, head_w2, (((1,), (1,)), ((), ())), preferred_element_type=jnp.float32)
        * gelu_slope(act)
    ).astype(jnp.bfloat16)
    local_w1 = lax.dot_general(
        features, dhid, (((0,), (0,)), ((), ())), preferred_element_type=jnp.float32
    )
    dhid_whole = lax.all_gather(dhid, "proto", axis=1, tiled=True)
    grad_features = lax.dot_general(
        dhid_whole, w1_block, (((1,), (1,)), ((), ())), preferred_element_type=jnp.float32
    ).astype(jnp.bfloat16)
    dpn, grad_w1, grad_w2 = lax.psum((dpn_local, local_w1, local_w2), "dp")
    grad_protos = pinv * (dpn - pn * jnp.sum(pn * dpn, axis=0, keepdims=True))
    return (grad_features, grad_w1, grad_w2, grad_protos)


def solution(mesh):
    in_specs = (
        P("dp", None),
        P("dp", None),
        P("dp"),
        P("dp"),
        P(None, "proto"),
        P("proto", None),
        P(None, "proto"),
        P(None, "proto"),
        P("proto", None),
        P(None, "proto"),
    )
    out_specs = (P("dp", "proto"), P(None, "proto"), P("proto", None), P(None, "proto"))
    return jax.shard_map(body, mesh=mesh, in_specs=in_specs, out_specs=out_specs, check_vma=False)
```

profile of v0, /device:TPU:0, one launch (start us, length us, event | category | flops | bytes accessed | tf_op | source)
XLA Modules:
  0.0 512.9 jit_solution(2815287136611332835)
XLA Ops:
  7.3 1.4 copy-done
  8.7 1.7 multiply_convert_fusion.3
  12.6 2.0 fusion.9
  14.7 2.0 fusion.8
  16.8 110.1 %all-reduce.9.cloned.1.call-done = (f32[640,256]{1,0:T(8,128)}, f32[128,256]{1,0:T(8,128)}) async-done(((f32[640,256]{1,0:T(8,128)}, f32[128,256]{1,0:T(8,128)}), (f32[640,256]{1,0:T(8,128)}, f32[128,256]{1,0:T(8,128)})) %all-reduce.9.cloned.1.call-update) | async-done | bytes 786448 | tf_op jit(solution)/shard_map/psum | solution.py:58
  127.9 3.8 fusion.59
  131.7 3.3 psum.94
  135.0 1.8 divide_reduce_fusion
  136.9 39.7 %psum.95 = f32[128]{0:T(128)S(1)} all-reduce(f32[128]{0:T(128)S(1)} %divide_reduce_fusion), channel_id=1, replica_groups=mesh['dp'=2,'proto'=16] {'proto'}, use_global_device_ids=true, to_apply=%region_11.0 | all-reduce | flops 128 | bytes 1024 | tf_op jit(solution)/shard_map/psum | solution.py:68
  176.6 2.0 fusion.21
  178.6 3.4 psum.96
  182.0 2.1 fusion.22
  184.1 36.6 %psum.97 = f32[128]{0:T(128)S(1)} all-reduce(f32[128]{0:T(128)S(1)} %fusion.22), channel_id=1, replica_groups=mesh['dp'=2,'proto'=16] {'proto'}, use_global_device_ids=true, to_apply=%region_15.0 | all-reduce | flops 128 | bytes 1024 | tf_op jit(solution)/shard_map/psum | solution.py:68
  220.7 2.2 fusion.23
  222.8 3.4 psum.98
  226.2 2.4 fusion.24
  228.8 5.0 fusion
  233.8 39.0 %all-reduce = (f32[640]{0:T(1024)S(1)}, f32[128]{0:T(128)S(1)}) all-reduce(f32[640]{0:T(1024)S(1)} %get-tuple-element.25, f32[128]{0:T(128)S(1)} %fusion.24), channel_id=1, replica_groups=mesh['dp'=2,'proto'=16] {'proto'}, use_global_device_ids=true, to_apply=%region_4.0 | all-reduce | flops 768 | bytes 6144 | tf_op jit(solution)/shard_map/psum | solution.py:74
  272.9 7.6 %multiply_convert_fusion = bf16[640,4096]{1,0:T(8,128)(2,1)S(1)} fusion(f32[640,4096]{1,0:T(8,128)} %get-tuple-element.26, f32[640]{0:T(1024)S(1)} %compare_select_fusion, f32[640]{0:T(1024)S(1)} %get-tuple-element.16, f32[128,4096]{1,0:T(8,128)} %get-tuple-element.28, f32[128]{0:T(128)S(1)} %get-tuple-element.17, f32[4096]{0:T(1024)S(1)} %psum.98, ...), kind=kOutput, calls=%fused_computation | convolution fusion | flops 690733056 | bytes 17887744 | tf_op jit(solution)/shard_map/dot_general | solution.py:79
  280.5 2.3 copy-done.6
  282.8 2.4 fusion.25
  285.3 105.8 %all-reduce.7.cloned.1.call-done = f32[640,256]{1,0:T(8,128)} async-done(((f32[640,256]{1,0:T(8,128)}), f32[640,256]{1,0:T(8,128)}) %all-reduce.7.cloned.1.call-update) | async-done | bytes 655376 | tf_op jit(solution)/shard_map/psum | solution.py:88
  391.1 1.4 multiply_reduce_fusion
  393.8 1.7 fusion.29
  395.8 6.4 %fusion.58 = f32[256,4096]{1,0:T(8,128)} fusion(bf16[640,4096]{1,0:T(8,128)(2,1)} %copy-done.6, f32[640,256]{1,0:T(8,128)S(1)} %copy-done.4, f32[640]{0:T(1024)S(1)} %add_rsqrt_fusion.2), kind=kOutput, calls=%fused_computation.88 | convolution fusion | flops 1342504960 | bytes 10095104 | tf_op jit(solution)/shard_map/dot_general | solution.py:82
  403.1 1.4 convolution_bitcast_fusion
  405.5 15.7 %all_to_all.19 = bf16[16,96,128]{2,1,0:T(8,128)(2,1)S(1)} all-to-all(bf16[16,96,128]{2,1,0:T(8,128)(2,1)S(1)} %bitcast.27), channel_id=1, replica_groups=mesh['dp'=2,'proto'=16] {'proto'}, dimensions={0} | all-to-all | bytes 786432 | tf_op jit(solution)/shard_map/all_to_all | solution.py:51
  421.2 44.1 %all-gather.2.cloned.1.call-done = bf16[640,2048]{1,0:T(8,128)(2,1)} async-done(((bf16[640,128]{1,0:T(8,128)(2,1)}), bf16[640,2048]{1,0:T(8,128)(2,1)}) %all-gather.2.cloned.1.call-update) | async-done | bytes 2621456 | tf_op jit(solution)/shard_map/all_gather | solution.py:100
  465.3 3.3 convolution_convert_fusion
  468.6 28.4 %all-reduce.11.cloned.1.call-done = (f32[1536,128]{0,1:T(8,128)}, f32[128,256]{1,0:T(8,128)}, f32[256,4096]{1,0:T(8,128)}) async-done(((f32[1536,128]{0,1:T(8,128)}, f32[128,256]{1,0:T(8,128)}, f32[256,4096]{1,0:T(8,128)}), (f32[1536,128]{0,1:T(8,128)}, f32[128,256]{1,0:T(8,128)}, f32[256,4096]{1,0:T(8,128)})) %all-reduce.11.cloned.1.call-update) | async-done | bytes 5111824 | tf_op jit(solution)/shard_map/psum | solution.py:104
  497.0 3.6 fusion.5
  501.7 2.8 fusion.7
  (55 shorter events, 9.9 us)
Async XLA Ops:
  7.2 1.6 copy-start
  7.2 3.2 copy-start.13
  7.2 4.3 copy-start.10
  7.2 4.3 copy-start.11
  7.2 4.3 copy-start.14
  7.2 119.7 %all-reduce.9.cloned.1.call-start = ((), (), s32[]{:S(2)}) async-start(), calls=%async_computation.3 | async-start | bytes 1572864 | tf_op jit(solution)/shard_map/psum | solution.py:58
  11.5 3.2 copy-start.16
  11.5 3.2 copy-start.15
  12.6 378.5 %all-reduce.7.cloned.1.call-start = ((), (), s32[]{:S(2)}) async-start(), calls=%async_computation.1 | async-start | bytes 1310720 | tf_op jit(solution)/shard_map/psum | solution.py:88
  220.7 8.0 %copy-start.4 = (f32[640,256]{1,0:T(8,128)S(1)}, f32[640,256]{1,0:T(8,128)}, u32[]{:S(2)}) copy-start(f32[640,256]{1,0:T(8,128)} %get-tuple-element.18) | copy-start | bytes 1966084
  226.2 2.6 copy-start.1
  272.9 10.0 %copy-start.2 = (bf16[256,4096]{1,0:T(8,128)(2,1)S(1)}, bf16[256,4096]{1,0:T(8,128)(2,1)}, u32[]{:S(2)}) copy-start(bf16[256,4096]{1,0:T(8,128)(2,1)} %param.16) | copy-start | bytes 6291460
  280.5 2.3 copy-start.6
  285.2 180.1 %all-gather.2.cloned.1.call-start = ((), (), s32[]{:S(2)}) async-start(), calls=%async_computation.2 | async-start | bytes 2785280 | tf_op jit(solution)/shard_map/all_gather | solution.py:100
  395.5 7.6 %copy-start.9 = (bf16[640,128]{1,0:T(8,128)(2,1)S(1)}, bf16[640,128]{1,0:T(8,128)(2,1)}, u32[]{:S(2)}) copy-start(bf16[640,128]{1,0:T(8,128)(2,1)} %fusion.29) | copy-start | bytes 491524
  395.5 101.5 %all-reduce.11.cloned.1.call-start = ((), (), s32[]{:S(2)}) async-start(), calls=%async_computation.4 | async-start | bytes 10223616 | tf_op jit(solution)/shard_map/psum | solution.py:104
  404.5 1.0 copy-start.7
  497.0 3.6 copy-start.3
  497.0 4.7 copy-start.5
  501.7 2.8 copy-start.8
  501.7 4.0 copy-start.12
Sparse Core Ops, SparseCore 0:
  13.8 113.0 all-reduce.8
  285.4 105.6 all-reduce.6
  395.6 69.6 all-gather.1
  468.5 28.4 all-reduce.10
where the time goes:
time: 514 us; the launch traced here: 513 us
  waiting for transfers between devices  288 us (56%)
  blocking collectives  141 us (27%)
  matrix products  36.3 us (7%)
  other arithmetic  24.9 us (5%)
  between operations  14 us (3%)
  local copies, waits for them, and re-layouts  7.65 us (1%)
    psum x1, waiting for transfers between devices, body(): zfull, tfull = lax.psum((zpart, tpart), 'proto')  110 us
    psum x1, waiting for transfers between devices, body(): dzn = lax.psum(dzn_part, 'proto')  106 us
    psum x2, blocking collectives, body(): row_mass = lax.psum(jnp.sum(weights, axis=1), 'proto')  76.3 us
    all_gather x1, waiting for transfers between devices, body(): dhid_whole = lax.all_gather(dhid, 'proto', axis=1, tiled=True)  44.1 us
    psum x1, blocking collectives, body(): esum = lax.psum(jnp.sum(expon, axis=1), 'proto')  39 us
    psum x1, waiting for transfers between devices, body(): dpn, grad_w1, grad_w2 = lax.psum((dpn_local, local_w1, local_w2), 'dp')  28.4 us
    all_to_all x1, blocking collectives, body(): lax.all_to_all(head_w1, 'proto', split_axis=0, concat_axis=1, tiled=True)  15.7 us
  transfers between devices with their start and end apart: 4, of which 4 were waited for; matrix products, arithmetic and copies ran while one was open for 3% of the time, Pallas kernels for 0%

commit v1 on v0

v1 whole, which is shorter than its diff:
```python
import jax
import jax.numpy as jnp
from jax import lax
from jax.sharding import PartitionSpec as P

ITERS = 3
ALL = ("dp", "proto")
F32 = jnp.float32
BF16 = jnp.bfloat16


def gelu_parts(act):
    phi = 0.5 * (1.0 + lax.erf(act * 0.7071067811865476))
    slope = phi + act * jnp.exp(-0.5 * act * act) * 0.3989422804014327
    return (act * phi).astype(BF16), slope


def dot(a, b, dims):
    return lax.dot_general(a, b, (dims, ((), ())), preferred_element_type=F32)


def swap(value, axis, step):
    count = lax.axis_size(axis)
    return lax.ppermute(value, axis, [(i, i ^ step) for i in range(count)])


def over_dp(value):
    return [value] + [swap(value, "dp", s) for s in range(1, lax.axis_size("dp"))]


def tree_sum(parts):
    while len(parts) > 1:
        parts = [parts[i] + parts[i + 1] for i in range(0, len(parts), 2)]
    return parts[0]


def send_all(value, axes):
    count = lax.axis_size(axes)
    return lax.all_to_all(jnp.broadcast_to(value[None], (count,) + value.shape), axes, 0, 0)


def unit_cols(mat):
    matf = mat.astype(F32)
    inv = lax.rsqrt(jnp.sum(matf * matf, axis=0, keepdims=True) + 1e-06)
    return matf * inv, inv


def body(
    features,
    teacher_features,
    crop_image,
    crop_view,
    head_w1,
    head_w2,
    protos,
    teacher_w1,
    teacher_w2,
    teacher_protos,
):
    nd, n = lax.axis_size("dp"), lax.axis_size("proto")
    d, p = lax.axis_index("dp"), lax.axis_index("proto")
    rows, img = features.shape[0], teacher_features.shape[0] // 2
    per = rows // img
    sr, tr = rows // n, 2 * img // n
    bot = head_w2.shape[1]
    factor = 10.0 / (18 * img * nd)
    absolute = d ^ jnp.arange(nd)

    im = crop_image - d * img
    at = jnp.arange(rows, dtype=jnp.int32)
    rank = jnp.sum((im[:, None] == im[None, :]) & (at[None, :] < at[:, None]), axis=1)
    place = im * per + rank
    hit = at[:, None] == place[None, :]
    order = hit.astype(BF16)
    view = jnp.sum(jnp.where(hit, crop_view[None, :], 0), axis=1)
    views = jnp.stack(over_dp(view))[absolute]

    w1_block = lax.all_to_all(head_w1, "proto", split_axis=0, concat_axis=1, tiled=True)
    feats = over_dp(features)
    act = jnp.dot(features, head_w1, preferred_element_type=F32)
    hidden, slope = gelu_parts(act)
    zpart = jnp.dot(hidden, head_w2, preferred_element_type=F32).astype(BF16)
    zpart = jnp.dot(order, zpart, preferred_element_type=F32).astype(BF16)
    tact = jnp.dot(teacher_features, teacher_w1, preferred_element_type=F32)
    thidden, _ = gelu_parts(tact)
    tpart = jnp.dot(thidden, teacher_w2, preferred_element_type=F32).astype(BF16)
    parts = jnp.concatenate([zpart.reshape(n, sr, bot), tpart.reshape(n, tr, bot)], axis=1)
    parts = lax.all_to_all(parts, "proto", 0, 0)
    early = jnp.concatenate(
        [slope.astype(BF16)] + [head_w2[:, i : i + head_w1.shape[1]] for i in range(0, bot, head_w1.shape[1])],
        axis=0,
    )
    early = lax.all_gather(early, "proto")
    zrow = jnp.sum(parts.astype(F32), axis=0)
    zinv = lax.rsqrt(jnp.sum(zrow * zrow, axis=1, keepdims=True) + 1e-06)
    zn = zrow * zinv
    znb = send_all(zn.astype(BF16), "proto")
    znb = jnp.stack(over_dp(znb))[absolute]
    student = znb[:, :, :sr].reshape(nd * rows, bot)
    teacher = znb[:, :, sr:].reshape(nd * 2 * img, bot)

    cols = protos.shape[1] // nd
    pn, pinv = unit_cols(lax.dynamic_slice_in_dim(protos, d * cols, cols, 1))
    pnb = pn.astype(BF16)
    tpnb = unit_cols(lax.dynamic_slice_in_dim(teacher_protos, d * cols, cols, 1))[0].astype(BF16)

    kern = jnp.exp(jnp.dot(teacher, tpnb, preferred_element_type=F32) / 0.07)
    ex = jnp.exp(jnp.dot(student, pnb, preferred_element_type=F32) / 0.1)
    esum = jnp.sum(ex, axis=1)
    exb = ex.astype(BF16)
    sums = dot(exb, pnb, ((1,), (1,)))
    colscale = 1.0 / jnp.sum(kern, axis=0)
    for step in range(ITERS - 1):
        mass = jnp.sum(send_all(jnp.sum(kern * colscale[None, :], axis=1), ALL), axis=0)
        colscale = 1.0 / jnp.sum(kern / mass[:, None], axis=0)
    last = kern * colscale[None, :]
    lastb = last.astype(BF16)
    tsums = dot(lastb, pnb, ((1,), (1,)))
    tot = jnp.sum(send_all(jnp.concatenate([esum, jnp.sum(last, axis=1)]), ALL), axis=0)
    esum, mass = tot[: nd * rows], tot[nd * rows :]

    out = jnp.concatenate([sums.reshape(nd, n, sr, bot), tsums.reshape(nd, n, tr, bot)], axis=2)
    out = out[absolute]
    out = tree_sum([out[0]] + [swap(out[s], "dp", s) for s in range(1, nd)])
    out = lax.all_to_all(out.astype(BF16), "proto", 0, 0)
    out = jnp.sum(out.astype(F32), axis=0)
    crop_scale = jnp.where(views == 2, 2.0, 1.0).reshape(-1) / esum * factor
    image_scale = factor / mass
    mine = (d * n + p)
    my_view = lax.dynamic_slice_in_dim(views.reshape(-1), mine * sr, sr)
    my_scale = lax.dynamic_slice_in_dim(crop_scale, mine * sr, sr)
    my_image = lax.dynamic_slice_in_dim(image_scale, mine * tr, tr)
    slot = jnp.arange(tr)
    pick = (slot[None, :] // 2 == jnp.arange(sr)[:, None] // per) & (slot[None, :] % 2 != my_view[:, None])
    target = jnp.sum(jnp.where(pick, my_image[None, :], 0.0)[:, :, None] * out[None, sr:], axis=1)
    dzn = my_scale[:, None] * out[:sr] - target
    zs, zi = zn[:sr], zinv[:sr]
    dz = (zi * (dzn - zs * jnp.sum(zs * dzn, axis=1, keepdims=True))).astype(BF16)
    dz = send_all(dz, "proto").reshape(rows, bot)
    dz = dot(order, dz, ((0,), (0,))).astype(BF16)
    dzs = over_dp(dz)

    tslot = jnp.arange(2 * img)
    picks = (tslot[None, None, :] // 2 == at[None, :, None] // per) & (tslot[None, None, :] % 2 != views[:, :, None])
    own = lax.dot_general(
        picks.astype(BF16), student.reshape(nd, rows, bot), (((1,), (1,)), ((0,), (0,))), preferred_element_type=F32
    ).reshape(nd * 2 * img, bot)
    left = (student.astype(F32) * crop_scale[:, None]).astype(BF16)
    right = (own * image_scale[:, None]).astype(BF16)
    dpn = dot(left, exb, ((0,), (0,))) - dot(right, lastb, ((0,), (0,)))
    gp = pinv * (dpn - pn * jnp.sum(pn * dpn, axis=0, keepdims=True))
    gps = over_dp(gp)
    grad_protos = jnp.zeros(protos.shape, F32)
    for s in range(nd):
        grad_protos = lax.dynamic_update_slice_in_dim(grad_protos, gps[s], (d ^ s) * cols, 1)

    w1_parts, w2_parts = [], []
    for s in range(nd):
        if s:
            hid, slp = gelu_parts(jnp.dot(feats[s], head_w1, preferred_element_type=F32))
        else:
            hid, slp = hidden, slope
        w2_parts.append(dot(hid, dzs[s], ((0,), (0,))))
        dhid = (dot(dzs[s], head_w2, ((1,), (1,))) * slp).astype(BF16)
        w1_parts.append(dot(feats[s], dhid, ((0,), (0,))))
    grad_w1, grad_w2 = tree_sum(w1_parts), tree_sum(w2_parts)
    slopes = early[:, :rows].transpose(1, 0, 2).reshape(rows, -1)
    w2_all = early[:, rows:].reshape(n, -1, head_w1.shape[1], head_w1.shape[1]).transpose(1, 3, 0, 2)
    w2_all = w2_all.reshape(bot, -1)
    dhid = (jnp.dot(dz, w2_all, preferred_element_type=F32) * slopes).astype(BF16)
    grad_features = dot(dhid, w1_block, ((1,), (1,))).astype(BF16)
    return (grad_features, grad_w1, grad_w2, grad_protos)


def solution(mesh):
    in_specs = (
        P("dp", None),
        P("dp", None),
        P("dp"),
        P("dp"),
        P(None, "proto"),
        P("proto", None),
        P(None, "proto"),
        P(None, "proto"),
        P("proto", None),
        P(None, "proto"),
    )
    out_specs = (P("dp", "proto"), P(None, "proto"), P("proto", None), P(None, "proto"))
    return jax.shard_map(body, mesh=mesh, in_specs=in_specs, out_specs=out_specs, check_vma=False)
```

time: 514 us -> 194 us (0.38)
  waiting for transfers between devices: 288 us -> 52.4 us
  blocking collectives: 141 us -> 0 us
  starting transfers between devices: 0.34 us -> 33.3 us
  local copies, waits for them, and re-layouts: 7.65 us -> 35 us
    psum x3 -> x0, waiting for transfers between devices: 244 us -> none  [the longest x1 110 us: body(): zfull, tfull = lax.psum((zpart, tpart), 'proto')]
    psum x6 -> x0, blocking collectives: 125 us -> none  [the longest x2 76.3 us: body(): row_mass = lax.psum(jnp.sum(weights, axis=1), 'proto')]
    all_to_all x0 -> x8, waiting for transfers between devices: none -> 51.7 us  [the longest x5 33.9 us: send_all(): lax.all_to_all(jnp.broadcast_to(value[None], (count,) + value.shape), axe...]
    all_gather x1, waiting for transfers between devices: 44.1 us -> 0.01 us  [body(): early = lax.all_gather(early, 'proto')]
    all_to_all x0 -> x8, starting transfers between devices: none -> 32.3 us  [the longest x5 15.6 us: send_all(): lax.all_to_all(jnp.broadcast_to(value[None], (count,) + value.shape), axe...]
    reduce_sum x11 -> x17, other arithmetic: 20.8 us -> 4.28 us  [the longest x2 1.69 us: unit_cols(): inv = lax.rsqrt(jnp.sum(matf * matf, axis=0, keepdims=True) + 1e-06)]
    all_to_all x1 -> x0, blocking collectives: 15.7 us -> none  [body(): lax.all_to_all(head_w1, 'proto', split_axis=0, concat_axis=1, tiled=True)]
    convert_element_type x0 -> x2, local copies, waits for them, and re-layouts: none -> 11.9 us  [body(): jnp.dot(dz, w2_all, preferred_element_type=F32) * slopes]
  transfers between devices with their start and end apart: 4 -> 15, of which waited for: 4 -> 8; matrix products, arithmetic and copies ran while one was open for 3% -> 39% of each run, Pallas kernels for 0% -> 0%
where the time goes in v1:
time: 194 us; the launch traced here: 192 us
  waiting for transfers between devices  52.4 us (27%)
  matrix products  36.6 us (19%)
  local copies, waits for them, and re-layouts  35 us (18%)
  starting transfers between devices  33.3 us (17%)
  other arithmetic  20 us (10%)
  between operations  14.7 us (8%)
    all_to_all x5, waiting for transfers between devices, send_all(): lax.all_to_all(jnp.broadcast_to(value[None], (count,) + value.shape), axe...  33.9 us
    dot_general x10, matrix products, dot(): return lax.dot_general(a, b, (dims, ((), ())), preferred_element_type=F32)  23.7 us
    all_to_all x5, starting transfers between devices, send_all(): lax.all_to_all(jnp.broadcast_to(value[None], (count,) + value.shape), axe...  15.6 us
    convert_element_type x2, local copies, waits for them, and re-layouts, body(): jnp.dot(dz, w2_all, preferred_element_type=F32) * slopes  11.9 us
    all_to_all x1, waiting for transfers between devices, body(): parts = lax.all_to_all(parts, 'proto', 0, 0)  11 us
    all_to_all x1, starting transfers between devices, body(): parts = lax.all_to_all(parts, 'proto', 0, 0)  8.31 us
    all_to_all x1, waiting for transfers between devices, body(): out = lax.all_to_all(out.astype(BF16), 'proto', 0, 0)  6.83 us
    unnamed x55, local copies, waits for them, and re-layouts  6.33 us
  transfers between devices with their start and end apart: 15, of which 8 were waited for; matrix products, arithmetic and copies ran while one was open for 39% of the time, Pallas kernels for 0%

profile of v1, /device:TPU:0, one launch (start us, length us, event | category | flops | bytes accessed | tf_op | source)
XLA Modules:
  0.0 192.0 jit_solution(2743847887463769656)
XLA Ops:
  9.0 3.0 %multiply_convert_fusion.7 = (bf16[640,128]{1,0:T(8,128)(2,1)S(1)}, bf16[640,128]{1,0:T(8,128)(2,1)S(1)}, f32[640,128]{1,0:T(8,128)}) fusion(bf16[640,1536]{1,0:T(8,128)(2,1)} %param.10, bf16[1536,128]{1,0:T(8,128)(2,1)} %param.14), kind=kOutput, calls=%fused_computation.94 | convolution fusion | flops 252559360 | bytes 3014656 | tf_op jit(solution)/shard_map/dot_general | solution.py:80
  13.9 8.3 %all-to-all-start = ((bf16[16,48,256]{2,1,0:T(8,128)(2,1)}), bf16[16,48,256]{2,1,0:T(8,128)(2,1)S(1)}, u32[]{:S(2)}, u32[]{:S(2)}) async-start(bf16[16,48,256]{2,1,0:T(8,128)(2,1)} %pad_maximum_fusion.2), calls=%async_computation | async-start | bytes 786432 | tf_op jit(solution)/shard_map/all_to_all | solution.py:88
  23.9 11.0 %all-to-all-done = bf16[16,48,256]{2,1,0:T(8,128)(2,1)S(1)} async-done(((bf16[16,48,256]{2,1,0:T(8,128)(2,1)}), bf16[16,48,256]{2,1,0:T(8,128)(2,1)S(1)}, u32[]{:S(2)}, u32[]{:S(2)}) %all-to-all-start) | async-done | bytes 393248 | tf_op jit(solution)/shard_map/all_to_all | solution.py:88
  36.6 3.6 %all-to-all-start.1 = ((bf16[16,48,256]{2,1,0:T(8,128)(2,1)}), bf16[16,48,256]{2,1,0:T(8,128)(2,1)S(1)}, u32[]{:S(2)}, u32[]{:S(2)}) async-start(bf16[16,48,256]{2,1,0:T(8,128)(2,1)} %broadcast_in_dim.42), calls=%async_computation.1 | async-start | bytes 786432 | tf_op jit(solution)/shard_map/all_to_all | solution.py:39
  42.8 12.1 %all-to-all-done.1 = bf16[16,48,256]{2,1,0:T(8,128)(2,1)S(1)} async-done(((bf16[16,48,256]{2,1,0:T(8,128)(2,1)}), bf16[16,48,256]{2,1,0:T(8,128)(2,1)S(1)}, u32[]{:S(2)}, u32[]{:S(2)}) %all-to-all-start.1) | async-done | bytes 393248 | tf_op jit(solution)/shard_map/all_to_all | solution.py:39
  60.0 3.0 %all-to-all-start.2 = ((f32[32,1,256]{2,1,0:T(1,128)}), f32[32,1,256]{2,1,0:T(1,128)S(1)}, u32[]{:S(2)}, u32[]{:S(2)}) async-start(f32[32,1,256]{2,1,0:T(1,128)} %broadcast_in_dim.43), calls=%async_computation.2 | async-start | bytes 65536 | tf_op jit(solution)/shard_map/all_to_all | solution.py:39
  65.1 5.1 %all-to-all-done.2 = f32[32,1,256]{2,1,0:T(1,128)S(1)} async-done(((f32[32,1,256]{2,1,0:T(1,128)}), f32[32,1,256]{2,1,0:T(1,128)S(1)}, u32[]{:S(2)}, u32[]{:S(2)}) %all-to-all-start.2) | async-done | bytes 32800 | tf_op jit(solution)/shard_map/all_to_all | solution.py:39
  71.5 2.6 %all-to-all-start.3 = ((f32[32,1,256]{2,1,0:T(1,128)}), f32[32,1,256]{2,1,0:T(1,128)S(1)}, u32[]{:S(2)}, u32[]{:S(2)}) async-start(f32[32,1,256]{2,1,0:T(1,128)} %broadcast_in_dim.44), calls=%async_computation.3 | async-start | bytes 65536 | tf_op jit(solution)/shard_map/all_to_all | solution.py:39
  75.1 6.3 %all-to-all-done.3 = f32[32,1,256]{2,1,0:T(1,128)S(1)} async-done(((f32[32,1,256]{2,1,0:T(1,128)}), f32[32,1,256]{2,1,0:T(1,128)S(1)}, u32[]{:S(2)}, u32[]{:S(2)}) %all-to-all-start.3) | async-done | bytes 32800 | tf_op jit(solution)/shard_map/all_to_all | solution.py:39
  83.1 3.7 %fusion.91 = (f32[1280]{0:T(1024)S(1)}, bf16[1280,2048]{1,0:T(8,128)(2,1)}) fusion(bf16[1280,256]{1,0:T(8,128)(2,1)S(1)} %bitcast.86, f32[2048]{0:T(1024)S(1)} %get-tuple-element.45, bf16[256,4096]{1,0:T(8,128)(2,1)S(1)} %copy-done.4, s32[]{:T(128)S(6)} %select_n.110), kind=kOutput, calls=%fused_computation.169 | convolution fusion | flops 1351613184 | bytes 6960132 | tf_op jit(solution)/shard_map/dot_general | solution.py:108
  87.7 2.8 %all-to-all-start.4 = ((f32[32,1,1536]{2,1,0:T(1,128)}), f32[32,1,1536]{2,1,0:T(1,128)S(1)}, u32[]{:S(2)}, u32[]{:S(2)}) async-start(f32[32,1,1536]{2,1,0:T(1,128)} %broadcast_in_dim.47), calls=%async_computation.4 | async-start | bytes 393216 | tf_op jit(solution)/shard_map/all_to_all | solution.py:39
  90.5 1.9 fusion.35
  92.4 4.2 %fusion.6 = f32[1280,256]{1,0:T(8,128)S(1)} fusion(bf16[1280,2048]{1,0:T(8,128)(2,1)} %get-tuple-element.40, f32[2048]{0:T(1024)S(1)} %get-tuple-element.45, bf16[256,4096]{1,0:T(8,128)(2,1)S(1)} %copy-done.5, s32[]{:T(128)S(6)} %select_n.110), kind=kOutput, calls=%fused_computation.18 | convolution fusion | flops 1343750144 | bytes 7610372 | tf_op jit(solution)/shard_map/dot_general | solution.py:19
  97.9 3.2 %gather_fusion.2 = f32[2,16,48,256]{3,2,1,0:T(8,128)} fusion(f32[2,16,48,256]{3,2,1,0:T(8,128)} %pad_maximum_fusion, s32[1024]{0:T(1024)S(1)} %pad_clamp_fusion), kind=kCustom, calls=%fused_computation.2 | custom fusion | bytes 3145736 | tf_op jit(solution)/shard_map/gather | solution.py:123
  102.4 2.0 %all-to-all-done.4 = f32[32,1,1536]{2,1,0:T(1,128)S(1)} async-done(((f32[32,1,1536]{2,1,0:T(1,128)}), f32[32,1,1536]{2,1,0:T(1,128)S(1)}, u32[]{:S(2)}, u32[]{:S(2)}) %all-to-all-start.4) | async-done | bytes 196640 | tf_op jit(solution)/shard_map/all_to_all | solution.py:39
  104.8 4.5 %fusion.4 = f32[256,2048]{1,0:T(8,128)S(1)} fusion(bf16[1280,2048]{1,0:T(8,128)(2,1)} %get-tuple-element.40, bf16[1280,256]{1,0:T(8,128)(2,1)} %bitcast.84, f32[1280]{0:T(1024)S(1)} %fusion.71), kind=kOutput, calls=%fused_computation.16 | convolution fusion | flops 1343160320 | bytes 8000512 | tf_op jit(solution)/shard_map/dot_general | solution.py:19
  109.3 1.9 %fusion.9 = (f32[2048]{0:T(1024)S(1)}, f32[256,2048]{1,0:T(8,128)}) fusion(f32[2048]{0:T(1024)S(1)} %get-tuple-element.45, bf16[256,4096]{1,0:T(8,128)(2,1)S(1)} %copy-done.6, s32[]{:T(128)S(6)} %select_n.110, f32[256,2048]{1,0:T(8,128)S(1)} %fusion.4, bf16[256,256]{1,0:T(8,128)(2,1)S(1)} %fusion.62, f32[256,2048]{1,0:T(8,128)S(1)} %get-tuple-element.38, ...), kind=kOutput, calls=%fused_computation.22 | convolution fusion | flops 272103424 | bytes 7495684 | tf_op jit(solution)/shard_map/dot_general | solution.py:19
  111.3 2.0 %fusion.40 = bf16[16,48,256]{2,1,0:T(8,128)(2,1)} fusion(f32[16,48,256]{2,1,0:T(8,128)} %collective-permute-done.2, f32[2,16,48,256]{3,2,1,0:T(8,128)S(1)} %copy-done.8), kind=kLoop, calls=%fused_computation.66 | loop fusion | flops 393216 | bytes 1966080 | tf_op jit(solution)/shard_map/convert_element_type | solution.py:125
  113.3 4.7 %all-to-all-start.5 = ((bf16[16,48,256]{2,1,0:T(8,128)(2,1)}), bf16[16,48,256]{2,1,0:T(8,128)(2,1)S(1)}, u32[]{:S(2)}, u32[]{:S(2)}) async-start(bf16[16,48,256]{2,1,0:T(8,128)(2,1)} %fusion.40), calls=%async_computation.5 | async-start | bytes 786432 | tf_op jit(solution)/shard_map/all_to_all | solution.py:125
  122.1 2.0 %copy-done.9 = f32[256,4096]{1,0:T(8,128)} copy-done((f32[256,4096]{1,0:T(8,128)}, f32[256,4096]{1,0:T(8,128)S(1)}, u32[]{:S(2)}) %copy-start.9) | copy-done | bytes 4194328
  124.3 6.8 %all-to-all-done.5 = bf16[16,48,256]{2,1,0:T(8,128)(2,1)S(1)} async-done(((bf16[16,48,256]{2,1,0:T(8,128)(2,1)}), bf16[16,48,256]{2,1,0:T(8,128)(2,1)S(1)}, u32[]{:S(2)}, u32[]{:S(2)}) %all-to-all-start.5) | async-done | bytes 393248 | tf_op jit(solution)/shard_map/all_to_all | solution.py:125
  132.5 3.6 %all-to-all-start.6 = ((bf16[16,40,256]{2,1,0:T(8,128)(2,1)}), bf16[16,40,256]{2,1,0:T(8,128)(2,1)S(1)}, u32[]{:S(2)}, u32[]{:S(2)}) async-start(bf16[16,40,256]{2,1,0:T(8,128)(2,1)} %broadcast_in_dim.50), calls=%async_computation.6 | async-start | bytes 655360 | tf_op jit(solution)/shard_map/all_to_all | solution.py:39
  136.1 2.3 %fusion.94 = f32[640,128]{1,0:T(8,128)S(1)} fusion(bf16[640,1536]{1,0:T(8,128)(2,1)} %collective-permute-done.4, bf16[1536,128]{1,0:T(8,128)(2,1)} %param.14), kind=kOutput, calls=%fused_computation.171 | convolution fusion | flops 251658240 | bytes 2686976 | tf_op jit(solution)/shard_map/dot_general | solution.py:160
  138.4 8.4 %all-to-all-done.6 = bf16[16,40,256]{2,1,0:T(8,128)(2,1)S(1)} async-done(((bf16[16,40,256]{2,1,0:T(8,128)(2,1)}), bf16[16,40,256]{2,1,0:T(8,128)(2,1)S(1)}, u32[]{:S(2)}, u32[]{:S(2)}) %all-to-all-start.6) | async-done | bytes 327712 | tf_op jit(solution)/shard_map/all_to_all | solution.py:39
  146.9 3.8 %all-to-all-start.7 = ((bf16[16,96,128]{2,1,0:T(8,128)(2,1)}), bf16[16,96,128]{2,1,0:T(8,128)(2,1)S(1)}, u32[]{:S(2)}, u32[]{:S(2)}) async-start(bf16[16,96,128]{2,1,0:T(8,128)(2,1)} %bitcast.17), calls=%async_computation.7 | async-start | bytes 786432 | tf_op jit(solution)/shard_map/all_to_all | solution.py:78
  151.6 2.3 %fusion.24 = f32[128,1536]{1,0:T(8,128)S(1)} fusion(bf16[640,1536]{1,0:T(8,128)(2,1)} %param.10, bf16[640,256]{1,0:T(8,128)(2,1)S(1)} %fusion.20, bf16[128,256]{1,0:T(8,128)(2,1)S(1)} %copy-done.11, f32[640,128]{1,0:T(8,128)S(1)} %copy-done.14), kind=kOutput, calls=%fused_computation.52 | convolution fusion | flops 294420480 | bytes 3473408 | tf_op jit(solution)/shard_map/dot_general | solution.py:19
  154.0 2.3 %fusion.8 = f32[1536,128]{0,1:T(8,128)S(1)} fusion(f32[128,1536]{1,0:T(8,128)S(1)} %fusion.24, bf16[640,1536]{1,0:T(8,128)(2,1)} %collective-permute-done.4, bf16[640,256]{1,0:T(8,128)(2,1)S(1)} %collective-permute-done.3, bf16[128,256]{1,0:T(8,128)(2,1)S(1)} %copy-done.11, f32[640,128]{1,0:T(8,128)S(1)} %fusion.94), kind=kOutput, calls=%fused_computation.21 | convolution fusion | flops 294617088 | bytes 4259840 | tf_op jit(solution)/shard_map/dot_general | solution.py:19
  158.4 3.1 %constant_dynamic-update-slice_fusion = f32[256,4096]{1,0:T(8,128)} fusion(f32[256,4096]{1,0:T(8,128)} %copy-done.9, f32[256,2048]{1,0:T(8,128)} %collective-permute-done.5, s32[]{:T(128)S(6)} %select_n.120), kind=kLoop, calls=%fused_computation.154 | loop fusion | bytes 4194308 | tf_op jit(solution)/shard_map/dynamic_update_slice | solution.py:155
  162.8 4.6 %convert_bitcast_fusion = f32[640,16,128]{2,0,1:T(8,128)} fusion(bf16[16,896,128]{2,1,0:T(8,128)(2,1)} %bitcast.80), kind=kLoop, calls=%fused_computation.4 | loop fusion | flops 1310720 | bytes 7864320 | tf_op jit(solution)/shard_map/convert_element_type | solution.py:170
  167.4 5.9 %copy.37 = f32[640,16,128]{0,2,1:T(8,128)} copy(f32[640,16,128]{2,0,1:T(8,128)} %convert_bitcast_fusion) | data formatting | bytes 10485760 | tf_op jit(solution)/shard_map/convert_element_type | solution.py:170
  173.4 6.0 %copy.38 = f32[640,2048]{1,0:T(8,128)} copy(f32[640,2048]{0,1:T(8,128)} %bitcast.76) | data formatting | bytes 10485760 | tf_op jit(solution)/shard_map/convert_element_type | solution.py:170
  180.3 4.8 %fusion.23 = bf16[640,96]{0,1:T(8,128)(2,1)} fusion(f32[640,2048]{1,0:T(8,128)} %copy.38, bf16[640,256]{1,0:T(8,128)(2,1)S(1)} %fusion.20, bf16[32,8,16,128]{3,2,1,0:T(8,128)(2,1)S(1)} %bitcast.78, bf16[16,96,128]{2,1,0:T(8,128)(2,1)S(1)} %all-to-all-done.7), kind=kOutput, calls=%fused_computation.51 | convolution fusion | flops 925429760 | bytes 7135232 | tf_op jit(solution)/shard_map/dot_general | solution.py:19
  (143 shorter events, 35.5 us)
Async XLA Ops:
  7.2 4.8 %copy-start = (bf16[128,1536]{1,0:T(8,128)(2,1)S(1)}, bf16[128,1536]{1,0:T(8,128)(2,1)}, u32[]{:S(2)}) copy-start(bf16[128,1536]{1,0:T(8,128)(2,1)} %param.11) | copy-start | bytes 1179652
  7.2 4.8 %copy-start.19 = (bf16[128,256]{1,0:T(8,128)(2,1)S(1)}, bf16[128,256]{1,0:T(8,128)(2,1)}, u32[]{:S(2)}) copy-start(bf16[128,256]{1,0:T(8,128)(2,1)} %param.18) | copy-start | bytes 196612
  7.2 4.8 %copy-start.12 = (bf16[1536,128]{1,0:T(8,128)(2,1)S(1)}, bf16[1536,128]{1,0:T(8,128)(2,1)}, u32[]{:S(2)}) copy-start(bf16[1536,128]{1,0:T(8,128)(2,1)} %param.17) | copy-start | bytes 1179652
  12.0 11.1 %copy-start.16 = (bf16[640,128]{1,0:T(8,128)(2,1)}, bf16[640,128]{1,0:T(8,128)(2,1)S(1)}, u32[]{:S(2)}) copy-start(bf16[640,128]{1,0:T(8,128)(2,1)S(1)} %get-tuple-element.32) | copy-start | bytes 491524
  12.0 11.1 %copy-start.20 = (s32[640]{0:T(1024)S(1)}, s32[640]{0:T(1024)}, u32[]{:S(2)}) copy-start(s32[640]{0:T(1024)} %param.13) | copy-start | bytes 7684
  13.9 21.0 %all-to-all-start = ((bf16[16,48,256]{2,1,0:T(8,128)(2,1)}), bf16[16,48,256]{2,1,0:T(8,128)(2,1)S(1)}, u32[]{:S(2)}, u32[]{:S(2)}) async-start(bf16[16,48,256]{2,1,0:T(8,128)(2,1)} %pad_maximum_fusion.2), calls=%async_computation | async-start | bytes 786432 | tf_op jit(solution)/shard_map/all_to_all | solution.py:88
  22.3 33.4 %copy-start.3 = (bf16[256,4096]{1,0:T(8,128)(2,1)S(1)}, bf16[256,4096]{1,0:T(8,128)(2,1)}, u32[]{:S(2)}) copy-start(bf16[256,4096]{1,0:T(8,128)(2,1)} %param.16) | copy-start | bytes 6291460
  22.3 139.3 %all-gather.3.cloned.1.call-start = ((), (), s32[]{:S(2)}) async-start(), calls=%async_computation.8 | async-start | bytes 3899392 | tf_op jit(solution)/shard_map/all_gather | solution.py:93
  22.3 113.8 %collective-permute-start.4 = (bf16[640,1536]{1,0:T(8,128)(2,1)}, bf16[640,1536]{1,0:T(8,128)(2,1)}, u32[]{:S(2)}, u32[]{:S(2)}) collective-permute-start(bf16[640,1536]{1,0:T(8,128)(2,1)} %param.10), channel_id=1, source_target_pairs={{0,16},{16,0},{1,17},{17,1},{2,18},{18,2},{3,19},{19,3},{4,20},{20... | collective-permute-start | bytes 5898248 | tf_op jit(solution)/shard_map/ppermute | solution.py:24
  23.4 32.5 %collective-permute-start = (s32[640]{0:T(1024)S(1)}, s32[640]{0:T(1024)S(1)}, u32[]{:S(2)}, u32[]{:S(2)}) collective-permute-start(s32[640]{0:T(1024)S(1)} %select_reduce_fusion), channel_id=1, source_target_pairs={{0,16},{16,0},{1,17},{17,1},{2,18},{18,2},{3,19},{19,3},{4,20},{20... | collective-permute-start | bytes 7688 | tf_op jit(solution)/shard_map/ppermute | solution.py:24
  35.1 7.1 %copy-start.21 = (f32[48]{0:T(128)}, f32[48]{0:T(128)S(1)}, u32[]{:S(2)}) copy-start(f32[48]{0:T(128)S(1)} %add_rsqrt_fusion.2) | copy-start | bytes 580
  36.6 18.3 %all-to-all-start.1 = ((bf16[16,48,256]{2,1,0:T(8,128)(2,1)}), bf16[16,48,256]{2,1,0:T(8,128)(2,1)S(1)}, u32[]{:S(2)}, u32[]{:S(2)}) async-start(bf16[16,48,256]{2,1,0:T(8,128)(2,1)} %broadcast_in_dim.42), calls=%async_computation.1 | async-start | bytes 786432 | tf_op jit(solution)/shard_map/all_to_all | solution.py:39
  54.9 1.7 collective-permute-start.1
  60.0 10.2 %all-to-all-start.2 = ((f32[32,1,256]{2,1,0:T(1,128)}), f32[32,1,256]{2,1,0:T(1,128)S(1)}, u32[]{:S(2)}, u32[]{:S(2)}) async-start(f32[32,1,256]{2,1,0:T(1,128)} %broadcast_in_dim.43), calls=%async_computation.2 | async-start | bytes 65536 | tf_op jit(solution)/shard_map/all_to_all | solution.py:39
  71.5 9.9 %all-to-all-start.3 = ((f32[32,1,256]{2,1,0:T(1,128)}), f32[32,1,256]{2,1,0:T(1,128)S(1)}, u32[]{:S(2)}, u32[]{:S(2)}) async-start(f32[32,1,256]{2,1,0:T(1,128)} %broadcast_in_dim.44), calls=%async_computation.3 | async-start | bytes 65536 | tf_op jit(solution)/shard_map/all_to_all | solution.py:39
  87.7 16.7 %all-to-all-start.4 = ((f32[32,1,1536]{2,1,0:T(1,128)}), f32[32,1,1536]{2,1,0:T(1,128)S(1)}, u32[]{:S(2)}, u32[]{:S(2)}) async-start(f32[32,1,1536]{2,1,0:T(1,128)} %broadcast_in_dim.47), calls=%async_computation.4 | async-start | bytes 393216 | tf_op jit(solution)/shard_map/all_to_all | solution.py:39
  97.9 6.8 %copy-start.15 = (f32[2,128,256]{2,1,0:T(8,128)S(1)}, f32[2,128,256]{2,1,0:T(8,128)}, u32[]{:S(2)}) copy-start(f32[2,128,256]{2,1,0:T(8,128)} %fusion.42) | copy-start | bytes 786436
  102.3 9.0 %collective-permute-start.2 = (f32[16,48,256]{2,1,0:T(8,128)S(1)}, f32[16,48,256]{2,1,0:T(8,128)}, u32[]{:S(2)}, u32[]{:S(2)}) collective-permute-start(f32[16,48,256]{2,1,0:T(8,128)S(1)} %slice_bitcast_fusion), channel_id=1, source_target_pairs={{0,16},{16,0},{1,17},{17,1},{2,18},{18,2},{3,19},{19,3},{4,20},{20... | collective-permute-start | bytes 2359304 | tf_op jit(solution)/shard_map/ppermute | solution.py:24
  104.8 4.5 %copy-start.6 = (bf16[256,4096]{1,0:T(8,128)(2,1)S(1)}, bf16[256,4096]{1,0:T(8,128)(2,1)}, u32[]{:S(2)}) copy-start(bf16[256,4096]{1,0:T(8,128)(2,1)} %param.16) | copy-start | bytes 6291460
  113.3 17.9 %all-to-all-start.5 = ((bf16[16,48,256]{2,1,0:T(8,128)(2,1)}), bf16[16,48,256]{2,1,0:T(8,128)(2,1)S(1)}, u32[]{:S(2)}, u32[]{:S(2)}) async-start(bf16[16,48,256]{2,1,0:T(8,128)(2,1)} %fusion.40), calls=%async_computation.5 | async-start | bytes 786432 | tf_op jit(solution)/shard_map/all_to_all | solution.py:125
  120.2 4.0 %copy-start.24 = (s32[8]{0:T(128)S(1)}, s32[8]{0:T(128)}, u32[]{:S(2)}) copy-start(s32[8]{0:T(128)} %get-tuple-element.43) | copy-start | bytes 100
  120.2 4.0 %copy-start.25 = (s32[8]{0:T(128)S(1)}, s32[8]{0:T(128)}, u32[]{:S(2)}) copy-start(s32[8]{0:T(128)} %get-tuple-element.44) | copy-start | bytes 100
  120.2 4.0 %copy-start.26 = (s32[40]{0:T(128)S(1)}, s32[40]{0:T(128)}, u32[]{:S(2)}) copy-start(s32[40]{0:T(128)} %dynamic_slice.18) | copy-start | bytes 484
  120.2 11.2 %copy-start.13 = (f32[48,256]{1,0:T(8,128)S(1)}, f32[48,256]{1,0:T(8,128)}, u32[]{:S(2)}) copy-start(f32[48,256]{1,0:T(8,128)} %get-tuple-element.31) | copy-start | bytes 147460
  120.2 11.4 %copy-start.22 = (f32[48]{0:T(128)S(1)}, f32[48]{0:T(128)}, u32[]{:S(2)}) copy-start(f32[48]{0:T(128)} %copy-done.21) | copy-start | bytes 580
  124.1 34.3 %collective-permute-start.5 = (f32[256,2048]{1,0:T(8,128)}, f32[256,2048]{1,0:T(8,128)}, u32[]{:S(2)}, u32[]{:S(2)}) collective-permute-start(f32[256,2048]{1,0:T(8,128)} %get-tuple-element.29), channel_id=1, source_target_pairs={{0,16},{16,0},{1,17},{17,1},{2,18},{18,2},{3,19},{19,3},{4,20},{20... | collective-permute-start | bytes 6291464 | tf_op jit(solution)/shard_map/ppermute | solution.py:24
  132.5 14.4 %all-to-all-start.6 = ((bf16[16,40,256]{2,1,0:T(8,128)(2,1)}), bf16[16,40,256]{2,1,0:T(8,128)(2,1)S(1)}, u32[]{:S(2)}, u32[]{:S(2)}) async-start(bf16[16,40,256]{2,1,0:T(8,128)(2,1)} %broadcast_in_dim.50), calls=%async_computation.6 | async-start | bytes 655360 | tf_op jit(solution)/shard_map/all_to_all | solution.py:39
  136.1 15.3 %copy-start.17 = (bf16[640,128]{1,0:T(8,128)(2,1)S(1)}, bf16[640,128]{1,0:T(8,128)(2,1)}, u32[]{:S(2)}) copy-start(bf16[640,128]{1,0:T(8,128)(2,1)} %copy-done.16) | copy-start | bytes 491524
  136.1 15.5 %copy-start.14 = (f32[640,128]{1,0:T(8,128)S(1)}, f32[640,128]{1,0:T(8,128)}, u32[]{:S(2)}) copy-start(f32[640,128]{1,0:T(8,128)} %get-tuple-element.36) | copy-start | bytes 983044
  146.9 33.5 %all-to-all-start.7 = ((bf16[16,96,128]{2,1,0:T(8,128)(2,1)}), bf16[16,96,128]{2,1,0:T(8,128)(2,1)S(1)}, u32[]{:S(2)}, u32[]{:S(2)}) async-start(bf16[16,96,128]{2,1,0:T(8,128)(2,1)} %bitcast.17), calls=%async_computation.7 | async-start | bytes 786432 | tf_op jit(solution)/shard_map/all_to_all | solution.py:78
  151.3 2.7 %collective-permute-start.3 = (bf16[640,256]{1,0:T(8,128)(2,1)S(1)}, bf16[640,256]{1,0:T(8,128)(2,1)S(1)}, u32[]{:S(2)}, u32[]{:S(2)}) collective-permute-start(bf16[640,256]{1,0:T(8,128)(2,1)S(1)} %fusion.20), channel_id=1, source_target_pairs={{0,16},{16,0},{1,17},{17,1},{2,18},{18,2},{3,19},{19,3},{4,20},{20... | collective-permute-start | bytes 983048 | tf_op jit(solution)/shard_map/ppermute | solution.py:24
  180.3 4.8 %copy-start.1 = (bf16[128,1536]{1,0:T(8,128)(2,1)S(1)}, bf16[128,1536]{1,0:T(8,128)(2,1)}, u32[]{:S(2)}) copy-start(bf16[128,1536]{1,0:T(8,128)(2,1)} %param.11) | copy-start | bytes 1179652
  (10 other events, 26.4 us)
Sparse Core Ops, SparseCore 0:
  25.9 80.6 all-gather.2

commit v2 on v1

--- a/solution.py
+++ b/solution.py
@@ -1,6 +1,8 @@
 import jax
 import jax.numpy as jnp
 from jax import lax
+from jax.experimental import pallas as pl
+from jax.experimental.pallas import tpu as pltpu
 from jax.sharding import PartitionSpec as P
 
 ITERS = 3
@@ -45,7 +47,7 @@
     return matf * inv, inv
 
 
-def body(
+def general_body(
     features,
     teacher_features,
     crop_image,
@@ -87,7 +89,7 @@
     parts = jnp.concatenate([zpart.reshape(n, sr, bot), tpart.reshape(n, tr, bot)], axis=1)
     parts = lax.all_to_all(parts, "proto", 0, 0)
     early = jnp.concatenate(
-        [slope.astype(BF16)] + [head_w2[:, i : i + head_w1.shape[1]] for i in range(0, bot, head_w1.shape[1])],
+        [(slope - 0.5).astype(BF16)] + [head_w2[:, i : i + head_w1.shape[1]] for i in range(0, bot, head_w1.shape[1])],
         axis=0,
     )
     early = lax.all_gather(early, "proto")
@@ -122,8 +124,7 @@
     out = jnp.concatenate([sums.reshape(nd, n, sr, bot), tsums.reshape(nd, n, tr, bot)], axis=2)
     out = out[absolute]
     out = tree_sum([out[0]] + [swap(out[s], "dp", s) for s in range(1, nd)])
-    out = lax.all_to_all(out.astype(BF16), "proto", 0, 0)
-    out = jnp.sum(out.astype(F32), axis=0)
+    out = jnp.sum(lax.all_to_all(out, "proto", 0, 0), axis=0)
     crop_scale = jnp.where(views == 2, 2.0, 1.0).reshape(-1) / esum * factor
     image_scale = factor / mass
     mine = (d * n + p)
@@ -164,12 +165,285 @@
         dhid = (dot(dzs[s], head_w2, ((1,), (1,))) * slp).astype(BF16)
         w1_parts.append(dot(feats[s], dhid, ((0,), (0,))))
     grad_w1, grad_w2 = tree_sum(w1_parts), tree_sum(w2_parts)
-    slopes = early[:, :rows].transpose(1, 0, 2).reshape(rows, -1)
+    slopes = 0.5 + early[:, :rows].astype(F32).transpose(1, 0, 2).reshape(rows, -1)
     w2_all = early[:, rows:].reshape(n, -1, head_w1.shape[1], head_w1.shape[1]).transpose(1, 3, 0, 2)
     w2_all = w2_all.reshape(bot, -1)
     dhid = (jnp.dot(dz, w2_all, preferred_element_type=F32) * slopes).astype(BF16)
     grad_features = dot(dhid, w1_block, ((1,), (1,))).astype(BF16)
     return (grad_features, grad_w1, grad_w2, grad_protos)
+
+
+def vmem(*shapes):
+    return pl.BlockSpec(memory_space=pltpu.VMEM)
+
+
+WHOLE = pl.BlockSpec(memory_space=pltpu.VMEM)
+
+
+def call(kernel, outs, *args, **extra):
+    params = dict(vmem_limit_bytes=48 * 1024 * 1024)
+    return pl.pallas_call(
+        kernel,
+        out_shape=outs,
+        in_specs=[pl.BlockSpec(memory_space=pltpu.VMEM)] * len(args),
+        out_specs=jax.tree.map(lambda _: pl.BlockSpec(memory_space=pltpu.VMEM), outs),
+        compiler_params=pltpu.CompilerParams(**params),
+        **extra,
+    )(*args)
+
+
+def unsort_kernel(got_ref, back_ref, out_ref):
+    n, slot, bot = got_ref.shape
+    rows = back_ref.shape[0]
+    sr = rows // n
+    got = got_ref[...].astype(F32)
+    dz = got[:, :sr].reshape(rows, bot).astype(BF16)
+    out_ref[:rows] = dot(back_ref[...], dz, ((1,), (0,))).astype(BF16)
+    out_ref[rows:] = got[:, sr:].reshape(n * (slot - sr), bot).astype(BF16)
+
+
+def features_kernel(dz_ref, early_ref, w1_ref, out_ref, acc_ref):
+    rows = dz_ref.shape[0]
+    hs = early_ref.shape[2]
+    step = pl.program_id(0)
+
+    @pl.when(step == 0)
+    def _():
+        acc_ref[...] = jnp.zeros_like(acc_ref)
+
+    early = early_ref[...]
+    w2 = jnp.concatenate([early[:, rows : rows + hs], early[:, rows + hs :]], axis=2)
+    w2 = w2.reshape(2 * hs, 2 * hs)
+    pre = dot(dz_ref[...], w2, ((1,), (1,)))
+    slope = jnp.concatenate([early[0, :rows], early[1, :rows]], axis=1).astype(F32) + 0.5
+    dhid = (pre * slope).astype(BF16)
+    w1 = jnp.concatenate([w1_ref[0], w1_ref[1]], axis=1)
+    acc_ref[...] += dot(dhid, w1, ((1,), (1,)))
+
+    @pl.when(step == pl.num_programs(0) - 1)
+    def _():
+        out_ref[...] = acc_ref[...].astype(BF16)
+
+
+def feature_grads(dz, early, w1_block):
+    n, tall, hs = early.shape
+    width = w1_block.shape[1]
+    rows, bot = dz.shape
+    return pl.pallas_call(
+        features_kernel,
+        grid=(n // 2,),
+        out_shape=jax.ShapeDtypeStruct((rows, width), BF16),
+        in_specs=[
+            pl.BlockSpec((rows, bot), lambda k: (0, 0)),
+            pl.BlockSpec((2, tall, hs), lambda k: (k, 0, 0)),
+            pl.BlockSpec((2, width, hs), lambda k: (k, 0, 0)),
+        ],
+        out_specs=pl.BlockSpec((rows, width), lambda k: (0, 0)),
+        scratch_shapes=[pltpu.VMEM((rows, width), F32)],
+        compiler_params=pltpu.CompilerParams(vmem_limit_bytes=32 * 1024 * 1024),
+    )(dz, early, w1_block)
+
+
+def weights_kernel(f0_ref, f1_ref, dz0_ref, dz1_ref, h0_ref, h1_ref, s0_ref, s1_ref, w2_ref, g1_ref, g2_ref):
+    g1, g2 = [], []
+    rows = f0_ref.shape[0]
+    for f, z, h, s in ((f0_ref, dz0_ref, h0_ref, s0_ref), (f1_ref, dz1_ref, h1_ref, s1_ref)):
+        dz = z[:rows]
+        g2.append(dot(h[...], dz, ((0,), (0,))))
+        dhid = (dot(dz, w2_ref[...], ((1,), (1,))) * s[...]).astype(BF16)
+        g1.append(dot(dhid, f[...], ((0,), (0,))))
+    g1_ref[...] = (g1[0] + g1[1]).T
+    g2_ref[...] = g2[0] + g2[1]
+
+
+def protos_kernel(d_ref, protos_ref, own_ref, other_ref, left_ref, right_ref, lown_ref, lother_ref, out_ref):
+    half = pl.program_id(0) // (pl.num_programs(0) // 2)
+    mine = half == d_ref[0]
+    first = d_ref[0] == 0
+    a, b = left_ref[...].astype(F32), right_ref[...].astype(F32)
+    scaled = jnp.concatenate([jnp.where(first, a, b), jnp.where(first, b, a)], axis=0).astype(BF16)
+
+    def finish(dpn_ref, last_ref):
+        mat = protos_ref[...].astype(F32)
+        inv = lax.rsqrt(jnp.sum(mat * mat, axis=0, keepdims=True) + 1e-06)
+        pn = mat * inv
+        dpn = dpn_ref[...] - dot(scaled, last_ref[...], ((0,), (0,)))
+        out_ref[...] = inv * (dpn - pn * jnp.sum(pn * dpn, axis=0, keepdims=True))
+
+    @pl.when(mine)
+    def _():
+        finish(own_ref, lown_ref)
+
+    @pl.when(jnp.logical_not(mine))
+    def _():
+        finish(other_ref, lother_ref)
+
+
+def protos_grads(d, protos, own, other, mine, yours, lown, lother):
+    bot, wide = protos.shape
+    tile = 512
+    steps = wide // tile
+    halfsteps = steps // 2
+    teach = lown.shape[0]
+
+    def place(i, d_ref, same):
+        at = d_ref[0] if same else 1 - d_ref[0]
+        return (0, jnp.clip(i - at * halfsteps, 0, halfsteps - 1))
+
+    own_map = lambda i, d_ref: place(i, d_ref, True)
+    other_map = lambda i, d_ref: place(i, d_ref, False)
+    return pl.pallas_call(
+        protos_kernel,
+        grid_spec=pltpu.PrefetchScalarGridSpec(
+            num_scalar_prefetch=1,
+            grid=(steps,),
+            in_specs=[
+                pl.BlockSpec((bot, tile), lambda i, d_ref: (0, i)),
+                pl.BlockSpec((bot, tile), own_map),
+                pl.BlockSpec((bot, tile), other_map),
+                pl.BlockSpec((teach // 2, bot), lambda i, d_ref: (0, 0)),
+                pl.BlockSpec((teach // 2, bot), lambda i, d_ref: (0, 0)),
+                pl.BlockSpec((teach, tile), own_map),
+                pl.BlockSpec((teach, tile), other_map),
+            ],
+            out_specs=pl.BlockSpec((bot, tile), lambda i, d_ref: (0, i)),
+        ),
+        out_shape=jax.ShapeDtypeStruct((bot, wide), F32),
+        compiler_params=pltpu.CompilerParams(vmem_limit_bytes=32 * 1024 * 1024),
+    )(d.reshape(1), protos, own, other, mine, yours, lown, lother)
+
+
+def by_dp(d, own, other):
+    return jnp.stack([jnp.where(d == 0, own, other), jnp.where(d == 0, other, own)])
+
+
+def paired_body(
+    features,
+    teacher_features,
+    crop_image,
+    crop_view,
+    head_w1,
+    head_w2,
+    protos,
+    teacher_w1,
+    teacher_w2,
+    teacher_protos,
+):
+    nd, n = lax.axis_size("dp"), lax.axis_size("proto")
+    d, p = lax.axis_index("dp"), lax.axis_index("proto")
+    rows, img = features.shape[0], teacher_features.shape[0] // 2
+    per = rows // img
+    sr, tr = rows // n, 2 * img // n
+    bot, hs = head_w2.shape[1], head_w2.shape[0]
+    factor = 10.0 / (18 * img * nd)
+
+    w1_block = lax.all_to_all(head_w1.reshape(n, -1, hs), "proto", 0, 0)
+
+    im = crop_image - d * img
+    at = jnp.arange(rows, dtype=jnp.int32)
+    rank = jnp.sum((im[:, None] == im[None, :]) & (at[None, :] < at[:, None]), axis=1)
+    place = im * per + rank
+    hit = at[:, None] == place[None, :]
+    order = hit.astype(BF16)
+    back = (place[:, None] == at[None, :]).astype(BF16)
+    view = jnp.sum(jnp.where(hit, crop_view[None, :], 0), axis=1)
+    view_other = swap(view, "dp", 1)
+
+    feat_other = swap(features, "dp", 1)
+    act = jnp.dot(features, head_w1, preferred_element_type=F32)
+    hidden, slope = gelu_parts(act)
+    zpart = jnp.dot(hidden, head_w2, preferred_element_type=F32).astype(BF16)
+    zpart = jnp.dot(order, zpart, preferred_element_type=F32).astype(BF16)
+    tact = jnp.dot(teacher_features, teacher_w1, preferred_element_type=F32)
+    thidden, _ = gelu_parts(tact)
+    tpart = jnp.dot(thidden, teacher_w2, preferred_element_type=F32).astype(BF16)
+    parts = jnp.concatenate([zpart.reshape(n, sr, bot), tpart.reshape(n, tr, bot)], axis=1)
+    early = jnp.concatenate([(slope - 0.5).astype(BF16), head_w2[:, :hs], head_w2[:, hs:]], axis=0)
+    parts, w1_block = lax.optimization_barrier((parts, w1_block))
+    early = lax.all_gather(early, "proto")
+    parts = lax.all_to_all(parts, "proto", 0, 0)
+    zrow = jnp.sum(parts.astype(F32), axis=0)
+    zinv = lax.rsqrt(jnp.sum(zrow * zrow, axis=1, keepdims=True) + 1e-06)
+    zn = zrow * zinv
+    znb = zn.astype(BF16)
+    got = send_all(znb, "proto")
+    got_other = swap(got, "dp", 1)
+    teacher = by_dp(d, got[:, sr:], got_other[:, sr:]).reshape(nd * 2 * img, bot)
+    student = jnp.concatenate([got[:, :sr].reshape(rows, bot), got_other[:, :sr].reshape(rows, bot)], axis=0)
+
+    cols = protos.shape[1] // nd
+    pn, pinv = unit_cols(lax.dynamic_slice_in_dim(protos, d * cols, cols, 1))
+    pnb = pn.astype(BF16)
+    tpnb = unit_cols(lax.dynamic_slice_in_dim(teacher_protos, d * cols, cols, 1))[0].astype(BF16)
+
+    kern = jnp.exp(jnp.dot(teacher, tpnb, preferred_element_type=F32) / 0.07)
+    colscale = 1.0 / jnp.sum(kern, axis=0)
+    mass = jnp.sum(send_all(jnp.sum(kern * colscale[None, :], axis=1), ALL), axis=0)
+    ex = jnp.exp(jnp.dot(student, pnb, preferred_element_type=F32) / 0.1)
+    esum = jnp.sum(ex, axis=1)
+    exb = ex.astype(BF16)
+    sums = dot(exb, pnb, ((1,), (1,)))
+    sums_own, sums_other = sums[:rows], swap(sums[rows:], "dp", 1)
+    colscale = 1.0 / jnp.sum(kern / mass[:, None], axis=0)
+    esum = by_dp(d, esum[:rows], esum[rows:]).reshape(-1)
+    tot = jnp.sum(send_all(jnp.concatenate([jnp.sum(kern * colscale[None, :], axis=1), esum]), ALL), axis=0)
+    mass, esum = tot[: nd * 2 * img], tot[nd * 2 * img :]
+    colscale = 1.0 / jnp.sum(kern / mass[:, None], axis=0)
+    last = kern * colscale[None, :]
+    lastb = last.astype(BF16)
+    tsums = dot(lastb, pnb, ((1,), (1,)))
+    tmass = jnp.sum(last, axis=1)
+
+    tail = jnp.concatenate([tsums, jnp.broadcast_to(tmass[:, None], tsums.shape)], axis=1)
+    tail = tail.reshape(nd, n, tr, 2 * bot)
+    tail = jnp.where(d == 0, tail[0], tail[1]) + swap(jnp.where(d == 0, tail[1], tail[0]), "dp", 1)
+    out = jnp.concatenate(
+        [(sums_own + sums_other).reshape(n, sr, bot), tail[:, :, :bot], tail[:, :, bot:]], axis=1
+    )
+    out = jnp.sum(lax.all_to_all(out, "proto", 0, 0), axis=0)
+    views = jnp.concatenate([view, view_other])
+    count = jnp.where(views == 2, 2.0, 1.0)
+    esum = esum.reshape(nd, rows)
+    crop_scale = count * factor / jnp.concatenate([esum[d], esum[1 - d]])
+    my_view = lax.dynamic_slice_in_dim(view, p * sr, sr)
+    my_scale = lax.dynamic_slice_in_dim(crop_scale, p * sr, sr)
+    my_image = factor / out[sr + tr :, 0]
+    slot = jnp.arange(tr)
+    pick = (slot[None, :] // 2 == jnp.arange(sr)[:, None] // per) & (slot[None, :] % 2 != my_view[:, None])
+    pick = jnp.where(pick, my_image[None, :], 0.0)
+    target = jnp.sum(pick[:, :, None] * out[None, sr : sr + tr], axis=1)
+    dzn = my_scale[:, None] * out[:sr] - target
+    zs, zi = zn[:sr], zinv[:sr]
+    dz = (zi * (dzn - zs * jnp.sum(zs * dzn, axis=1, keepdims=True))).astype(BF16)
+    own = jnp.sum(pick[:, :, None] * znb[:sr, None, :].astype(F32), axis=0).astype(BF16)
+    got4 = send_all(jnp.concatenate([dz, own], axis=0), "proto")
+
+    left = (student.astype(F32) * crop_scale[:, None]).astype(BF16)
+    dpn = dot(left, exb, ((0,), (0,)))
+    dpn_other, last_other = swap(dpn, "dp", 1), swap(lastb, "dp", 1)
+
+    act_other = jnp.dot(feat_other, head_w1, preferred_element_type=F32)
+    hidden_other, slope_other = gelu_parts(act_other)
+
+    dz = call(unsort_kernel, jax.ShapeDtypeStruct((rows + 2 * img, bot), BF16), got4, back)
+    dz_other = swap(dz, "dp", 1)
+    grad_features = feature_grads(dz[:rows], early, w1_block)
+    grad_w1, grad_w2 = call(
+        weights_kernel,
+        (jax.ShapeDtypeStruct(head_w1.shape, F32), jax.ShapeDtypeStruct(head_w2.shape, F32)),
+        features, feat_other, dz, dz_other, hidden, hidden_other, slope, slope_other, head_w2,
+    )
+    grad_protos = protos_grads(
+        d, protos, dpn, dpn_other, dz[rows:], dz_other[rows:], lastb, last_other
+    )
+    return (grad_features, grad_w1, grad_w2, grad_protos)
+
+
+def body(features, teacher_features, *rest):
+    n = lax.axis_size("proto")
+    slot = (features.shape[0] // n, teacher_features.shape[0] // n)
+    paired = lax.axis_size("dp") == 2 and n % 2 == 0 and slot[0] % 8 == 0 and slot[1] % 8 == 0
+    return (paired_body if paired else general_body)(features, teacher_features, *rest)
 
 
 def solution(mesh):

time: 194 us -> 209 us (1.077)
  Pallas kernels: 0 us -> 17.6 us
  blocking collectives: 0 us -> 15.4 us
  local copies, waits for them, and re-layouts: 35 us -> 21.2 us
  matrix products: 36.6 us -> 22.9 us
  waiting for transfers between devices: 52.4 us -> 59.5 us
  other arithmetic: 20 us -> 24.9 us
  starting transfers between devices: 33.3 us -> 30.8 us
    pallas_call x0 -> x4, Pallas kernels: none -> 17.6 us  [the longest x1 8.32 us: protos_grads(): pl.pallas_call(protos_kernel, grid_spec=pltpu.PrefetchScalarGridSpec(num_...]
    all_to_all x0 -> x1, blocking collectives: none -> 15.4 us  [paired_body(): parts = lax.all_to_all(parts, 'proto', 0, 0)]
    dot_general x10 -> x3, matrix products: 23.7 us -> 10.3 us  [dot(): return lax.dot_general(a, b, (dims, ((), ())), preferred_element_type=F32)]
    convert_element_type x2 -> x0, local copies, waits for them, and re-layouts: 11.9 us -> none  [body(): jnp.dot(dz, w2_all, preferred_element_type=F32) * slopes]
    reduce_sum x15 -> x13, other arithmetic: 2.59 us -> 9.84 us  [the longest x2 4.01 us: paired_body(): colscale = 1.0 / jnp.sum(kern / mass[:, None], axis=0)]
    gather x4 -> x0, local copies, waits for them, and re-layouts: 4.39 us -> none  [the longest x1 3.22 us: body(): out = out[absolute]]
    all_to_all x3 -> x2, waiting for transfers between devices: 17.8 us -> 21.9 us  [the longest x1 16.1 us: paired_body(): out = jnp.sum(lax.all_to_all(out, 'proto', 0, 0), axis=0)]
    convert_element_type x5, other arithmetic: 7.46 us -> 3.56 us  [the longest x1 1.1 us: paired_body(): back = (place[:, None] == at[None, :]).astype(BF16)]
  transfers between devices with their start and end apart: 15 -> 15, of which waited for: 8 -> 7; matrix products, arithmetic and copies ran while one was open for 39% -> 28% of each run, Pallas kernels for 0% -> 7%
where the time goes in v2:
time: 209 us; the launch traced here: 207 us
  waiting for transfers between devices  59.5 us (28%)
  starting transfers between devices  30.8 us (15%)
  other arithmetic  24.9 us (12%)
  matrix products  22.9 us (11%)
  local copies, waits for them, and re-layouts  21.2 us (10%)
  Pallas kernels  17.6 us (8%)
  blocking collectives  15.4 us (7%)
  between operations  14.7 us (7%)
    all_to_all x4, waiting for transfers between devices, send_all(): lax.all_to_all(jnp.broadcast_to(value[None], (count,) + value.shape), axe...  36 us
    all_to_all x4, starting transfers between devices, send_all(): lax.all_to_all(jnp.broadcast_to(value[None], (count,) + value.shape), axe...  16.4 us
    all_to_all x1, waiting for transfers between devices, paired_body(): out = jnp.sum(lax.all_to_all(out, 'proto', 0, 0), axis=0)  16.1 us
    all_to_all x1, blocking collectives, paired_body(): parts = lax.all_to_all(parts, 'proto', 0, 0)  15.4 us
    dot_general x3, matrix products, dot(): return lax.dot_general(a, b, (dims, ((), ())), preferred_element_type=F32)  10.3 us
    unnamed x55, local copies, waits for them, and re-layouts  9.7 us
    all_to_all x1, starting transfers between devices, paired_body(): w1_block = lax.all_to_all(head_w1.reshape(n, -1, hs), 'proto', 0, 0)  8.46 us
    pallas_call x1, Pallas kernels, protos_grads(): pl.pallas_call(protos_kernel, grid_spec=pltpu.PrefetchScalarGridSpec(num_...  8.32 us
  transfers between devices with their start and end apart: 15, of which 7 were waited for; matrix products, arithmetic and copies ran while one was open for 28% of the time, Pallas kernels for 7%

profile of v2, /device:TPU:0, one launch (start us, length us, event | category | flops | bytes accessed | tf_op | source)
XLA Modules:
  0.0 206.9 jit_solution(8012888183119411888)
XLA Ops:
  7.2 8.5 %all-to-all-start = ((bf16[16,96,128]{2,1,0:T(8,128)(2,1)}), bf16[16,96,128]{2,1,0:T(8,128)(2,1)S(1)}, u32[]{:S(2)}, u32[]{:S(2)}) async-start(bf16[16,96,128]{2,1,0:T(8,128)(2,1)} %bitcast.34), calls=%async_computation | async-start | bytes 786432 | tf_op jit(solution)/shard_map/all_to_all | solution.py:340
  17.3 1.4 fusion.13
  18.8 3.0 %add_convert_fusion = (bf16[640,128]{1,0:T(8,128)(2,1)S(1)}, f32[640,128]{1,0:T(8,128)}, bf16[640,128]{1,0:T(8,128)(2,1)S(1)}) fusion(bf16[640,1536]{1,0:T(8,128)(2,1)} %f0_ref.1, bf16[1536,128]{1,0:T(8,128)(2,1)} %param.14), kind=kOutput, calls=%fused_computation.58 | convolution fusion | flops 252641280 | bytes 3014656 | tf_op jit(solution)/shard_map/dot_general | solution.py:353
  22.5 5.7 %all-to-all-done.w1_ref = bf16[16,96,128]{2,1,0:T(8,128)(2,1)S(1)} async-done(((bf16[16,96,128]{2,1,0:T(8,128)(2,1)}), bf16[16,96,128]{2,1,0:T(8,128)(2,1)S(1)}, u32[]{:S(2)}, u32[]{:S(2)}) %all-to-all-start) | async-done | bytes 393248 | tf_op jit(solution)/shard_map/all_to_all | solution.py:340
  28.3 15.4 %all_to_all.37 = bf16[16,48,256]{2,1,0:T(8,128)(2,1)S(1)} all-to-all(bf16[16,48,256]{2,1,0:T(8,128)(2,1)S(1)} %pad_maximum_fusion.4), channel_id=1, replica_groups=mesh['dp'=2,'proto'=16] {'proto'}, dimensions={0} | all-to-all | bytes 786432 | tf_op jit(solution)/shard_map/all_to_all | solution.py:364
  45.9 3.6 %all-to-all-start.2 = ((bf16[16,48,256]{2,1,0:T(8,128)(2,1)}), bf16[16,48,256]{2,1,0:T(8,128)(2,1)S(1)}, u32[]{:S(2)}, u32[]{:S(2)}) async-start(bf16[16,48,256]{2,1,0:T(8,128)(2,1)} %broadcast_in_dim.40), calls=%async_computation.2 | async-start | bytes 786432 | tf_op jit(solution)/shard_map/all_to_all | solution.py:41
  50.4 1.5 fusion.5
  52.1 9.0 %all-to-all-done.2 = bf16[16,48,256]{2,1,0:T(8,128)(2,1)S(1)} async-done(((bf16[16,48,256]{2,1,0:T(8,128)(2,1)}), bf16[16,48,256]{2,1,0:T(8,128)(2,1)S(1)}, u32[]{:S(2)}, u32[]{:S(2)}) %all-to-all-start.2) | async-done | bytes 393248 | tf_op jit(solution)/shard_map/all_to_all | solution.py:41
  61.2 1.6 collective-permute-done.1
  62.9 4.5 %fusion.52 = (f32[1280]{0:T(1024)S(1)}, bf16[1280,2048]{1,0:T(8,128)(2,1)}) fusion(f32[2048]{0:T(1024)S(1)} %add_rsqrt_fusion, bf16[256,4096]{1,0:T(8,128)(2,1)S(1)} %copy-done.1, s32[]{:T(128)S(6)} %select_n.115, bf16[640,256]{1,0:T(8,128)(2,1)S(1)} %bitcast.37, bf16[640,256]{1,0:T(8,128)(2,1)S(1)} %bitcast.35), kind=kOutput, calls=%fused_computation.124 | convolution fusion | flops 1352923904 | bytes 6960132 | tf_op jit(solution)/shard_map/dot_general | solution.py:382
  70.2 2.6 %all-to-all-start.3 = ((f32[32,1,256]{2,1,0:T(1,128)}), f32[32,1,256]{2,1,0:T(1,128)S(1)}, u32[]{:S(2)}, u32[]{:S(2)}) async-start(f32[32,1,256]{2,1,0:T(1,128)} %broadcast_in_dim.41), calls=%async_computation.3 | async-start | bytes 65536 | tf_op jit(solution)/shard_map/all_to_all | solution.py:41
  72.9 7.2 %all-to-all-done.3 = f32[32,1,256]{2,1,0:T(1,128)S(1)} async-done(((f32[32,1,256]{2,1,0:T(1,128)}), f32[32,1,256]{2,1,0:T(1,128)S(1)}, u32[]{:S(2)}, u32[]{:S(2)}) %all-to-all-start.3) | async-done | bytes 32800 | tf_op jit(solution)/shard_map/all_to_all | solution.py:41
  80.1 2.0 divide_reduce_fusion.1
  83.4 2.6 %all-to-all-start.4 = ((f32[32,1,1536]{2,1,0:T(1,128)}), f32[32,1,1536]{2,1,0:T(1,128)S(1)}, u32[]{:S(2)}, u32[]{:S(2)}) async-start(f32[32,1,1536]{2,1,0:T(1,128)} %broadcast_in_dim.42), calls=%async_computation.4 | async-start | bytes 393216 | tf_op jit(solution)/shard_map/all_to_all | solution.py:41
  86.0 4.1 %fusion.3 = f32[1280,256]{1,0:T(8,128)S(1)} fusion(bf16[1280,2048]{1,0:T(8,128)(2,1)} %get-tuple-element.60, f32[2048]{0:T(1024)S(1)} %add_rsqrt_fusion, bf16[256,4096]{1,0:T(8,128)(2,1)S(1)} %copy-done.1, s32[]{:T(128)S(6)} %select_n.115), kind=kOutput, calls=%fused_computation.9 | convolution fusion | flops 1343750144 | bytes 7610372 | tf_op jit(solution)/shard_map/dot_general | solution.py:21
  92.2 8.1 %all-to-all-done.4 = f32[32,1,1536]{2,1,0:T(1,128)S(1)} async-done(((f32[32,1,1536]{2,1,0:T(1,128)}), f32[32,1,1536]{2,1,0:T(1,128)S(1)}, u32[]{:S(2)}, u32[]{:S(2)}) %all-to-all-start.4) | async-done | bytes 196640 | tf_op jit(solution)/shard_map/all_to_all | solution.py:41
  100.4 2.0 divide_reduce_fusion
  104.5 1.8 copy.40
  106.3 1.8 copy.39
  108.1 1.4 slice_add_fusion
  111.5 4.5 %all-to-all-start.5 = ((f32[16,56,256]{2,1,0:T(8,128)}), f32[16,56,256]{2,1,0:T(8,128)}, u32[]{:S(2)}, u32[]{:S(2)}) async-start(f32[16,56,256]{2,1,0:T(8,128)} %pad_maximum_fusion), calls=%async_computation.5 | async-start | bytes 1835008 | tf_op jit(solution)/shard_map/all_to_all | solution.py:403
  121.3 5.7 %fusion.1.own_ref = f32[256,2048]{1,0:T(8,128)} fusion(bf16[1280,2048]{1,0:T(8,128)(2,1)} %get-tuple-element.60, f32[1280]{0:T(1024)S(1)} %maximum_divide_fusion, bf16[640,256]{1,0:T(8,128)(2,1)} %bitcast.38, bf16[640,256]{1,0:T(8,128)(2,1)} %bitcast.36), kind=kOutput, calls=%fused_computation.7 | convolution fusion | flops 1344143360 | bytes 8000512 | tf_op jit(solution)/shard_map/dot_general | solution.py:21
  128.7 16.1 %all-to-all-done.5 = f32[16,56,256]{2,1,0:T(8,128)} async-done(((f32[16,56,256]{2,1,0:T(8,128)}), f32[16,56,256]{2,1,0:T(8,128)}, u32[]{:S(2)}, u32[]{:S(2)}) %all-to-all-start.5) | async-done | bytes 917536 | tf_op jit(solution)/shard_map/all_to_all | solution.py:403
  144.9 1.9 reduce_sum.186
  152.6 7.6 %all-to-all-start.6 = ((bf16[16,48,256]{2,1,0:T(8,128)(2,1)}), bf16[16,48,256]{2,1,0:T(8,128)(2,1)}, u32[]{:S(2)}, u32[]{:S(2)}) async-start(bf16[16,48,256]{2,1,0:T(8,128)(2,1)} %broadcast_in_dim.48), calls=%async_computation.6 | async-start | bytes 786432 | tf_op jit(solution)/shard_map/all_to_all | solution.py:41
  161.4 11.7 %all-to-all-done.6.got_ref = bf16[16,48,256]{2,1,0:T(8,128)(2,1)} async-done(((bf16[16,48,256]{2,1,0:T(8,128)(2,1)}), bf16[16,48,256]{2,1,0:T(8,128)(2,1)}, u32[]{:S(2)}, u32[]{:S(2)}) %all-to-all-start.6) | async-done | bytes 393248 | tf_op jit(solution)/shard_map/all_to_all | solution.py:41
  174.2 1.4 shard_map.129.dz0_ref
  175.8 2.4 %fusion.30 = (f32[640,128]{1,0:T(8,128)S(1)}, bf16[640,128]{1,0:T(8,128)(2,1)S(1)}) fusion(bf16[640,1536]{1,0:T(8,128)(2,1)} %collective-permute-done.4.f1_ref, bf16[1536,128]{1,0:T(8,128)(2,1)} %param.14), kind=kOutput, calls=%fused_computation.55 | convolution fusion | flops 252477440 | bytes 2850816 | tf_op jit(solution)/shard_map/dot_general | solution.py:425
  179.1 4.0 %shard_map.131 = (f32[1536,128]{1,0:T(8,128)}, f32[128,256]{1,0:T(8,128)}) custom-call(bf16[640,1536]{1,0:T(8,128)(2,1)S(1)} %copy-done.4, bf16[640,1536]{1,0:T(8,128)(2,1)} %collective-permute-done.4.f1_ref, bf16[768,256]{1,0:T(8,128)(2,1)S(1)} %shard_map.129.dz0_ref, bf16[768,256]{1,0:T(8,128)(2,1)S(1)} %collective-permute-done.5.dz1_ref, ...), custom_call_target="tpu_custom_call" | custom-call | tf_op jit(solution)/shard_map/pallas_call | solution.py:185
  183.0 8.3 %shard_map.132 = f32[256,4096]{1,0:T(8,128)} custom-call(s32[1]{0:T(128)} %bitcast.12.d_ref, bf16[256,4096]{1,0:T(8,128)(2,1)S(1)} %copy-done.1, f32[256,2048]{1,0:T(8,128)} %fusion.1.own_ref, f32[256,2048]{1,0:T(8,128)} %collective-permute-done.6.other_ref, bf16[128,256]{1,0:T(8,128)(2,1)S(1)} %slice.125.left_ref, bf16[128,256]{1,0:T(8,128)(2,1)S(1)} %slice.126.right_ref, ...), custom_call_target="tpu_custom_call" | custom-call | tf_op jit(solution)/shard_map/pallas_call | solution.py:295
  191.4 2.0 copy-done.2
  195.4 3.9 %shard_map.130 = bf16[640,96]{1,0:T(8,128)(2,1)S(1)} custom-call(bf16[640,256]{1,0:T(8,128)(2,1)S(1)} %copy-done.7, bf16[16,896,128]{2,1,0:T(8,128)(2,1)S(1)} %bitcast.31, bf16[16,96,128]{2,1,0:T(8,128)(2,1)S(1)} %copy-done.6), custom_call_target="tpu_custom_call" | custom-call | tf_op jit(solution)/shard_map/pallas_call | solution.py:232
  (138 shorter events, 34.9 us)
Async XLA Ops:
  7.2 10.2 %copy-start = (bf16[128,1536]{1,0:T(8,128)(2,1)S(1)}, bf16[128,1536]{1,0:T(8,128)(2,1)}, u32[]{:S(2)}) copy-start(bf16[128,1536]{1,0:T(8,128)(2,1)} %param.11) | copy-start | bytes 1179652
  7.2 21.1 %all-to-all-start = ((bf16[16,96,128]{2,1,0:T(8,128)(2,1)}), bf16[16,96,128]{2,1,0:T(8,128)(2,1)S(1)}, u32[]{:S(2)}, u32[]{:S(2)}) async-start(bf16[16,96,128]{2,1,0:T(8,128)(2,1)} %bitcast.34), calls=%async_computation | async-start | bytes 786432 | tf_op jit(solution)/shard_map/all_to_all | solution.py:340
  17.3 4.4 %copy-start.9 = (bf16[128,256]{1,0:T(8,128)(2,1)S(1)}, bf16[128,256]{1,0:T(8,128)(2,1)}, u32[]{:S(2)}) copy-start(bf16[128,256]{1,0:T(8,128)(2,1)} %w2_ref.1) | copy-start | bytes 196612
  22.5 29.3 %copy-start.1 = (bf16[256,4096]{1,0:T(8,128)(2,1)S(1)}, bf16[256,4096]{1,0:T(8,128)(2,1)}, u32[]{:S(2)}) copy-start(bf16[256,4096]{1,0:T(8,128)(2,1)} %protos_ref.1) | copy-start | bytes 6291460
  28.3 23.5 %copy-start.5 = (bf16[16,96,128]{2,1,0:T(8,128)(2,1)}, bf16[16,96,128]{2,1,0:T(8,128)(2,1)S(1)}, u32[]{:S(2)}) copy-start(bf16[16,96,128]{2,1,0:T(8,128)(2,1)S(1)} %all-to-all-done.w1_ref) | copy-start | bytes 1179652
  43.8 8.3 %copy-start.25 = (f32[48]{0:T(128)}, f32[48]{0:T(128)S(1)}, u32[]{:S(2)}) copy-start(f32[48]{0:T(128)S(1)} %add_rsqrt_fusion.2) | copy-start | bytes 580
  45.9 15.2 %all-to-all-start.2 = ((bf16[16,48,256]{2,1,0:T(8,128)(2,1)}), bf16[16,48,256]{2,1,0:T(8,128)(2,1)S(1)}, u32[]{:S(2)}, u32[]{:S(2)}) async-start(bf16[16,48,256]{2,1,0:T(8,128)(2,1)} %broadcast_in_dim.40), calls=%async_computation.2 | async-start | bytes 786432 | tf_op jit(solution)/shard_map/all_to_all | solution.py:41
  49.6 141.8 %all-gather.3.cloned.1.call-start = ((), (), s32[]{:S(2)}) async-start(), calls=%async_computation.7 | async-start | bytes 3899392 | tf_op jit(solution)/shard_map/all_gather | solution.py:363
  61.1 1.7 collective-permute-start.1
  61.1 24.8 %copy-start.23 = (f32[2048]{0:T(1024)}, f32[2048]{0:T(1024)S(1)}, u32[]{:S(2)}) copy-start(f32[2048]{0:T(1024)S(1)} %add_rsqrt_fusion) | copy-start | bytes 24580
  61.2 6.2 %copy-start.19 = (bf16[16,40,256]{2,1,0:T(8,128)(2,1)}, bf16[16,40,256]{2,1,0:T(8,128)(2,1)S(1)}, u32[]{:S(2)}) copy-start(bf16[16,40,256]{2,1,0:T(8,128)(2,1)S(1)} %slice.107) | copy-start | bytes 983044
  62.9 4.5 %copy-start.20 = (bf16[16,40,256]{2,1,0:T(8,128)(2,1)}, bf16[16,40,256]{2,1,0:T(8,128)(2,1)S(1)}, u32[]{:S(2)}) copy-start(bf16[16,40,256]{2,1,0:T(8,128)(2,1)S(1)} %slice.108) | copy-start | bytes 983044
  62.9 4.6 %copy-start.16 = (bf16[256,4096]{1,0:T(8,128)(2,1)S(1)}, bf16[256,4096]{1,0:T(8,128)(2,1)}, u32[]{:S(2)}) copy-start(bf16[256,4096]{1,0:T(8,128)(2,1)} %param.19) | copy-start | bytes 6291460
  70.2 9.8 %all-to-all-start.3 = ((f32[32,1,256]{2,1,0:T(1,128)}), f32[32,1,256]{2,1,0:T(1,128)S(1)}, u32[]{:S(2)}, u32[]{:S(2)}) async-start(f32[32,1,256]{2,1,0:T(1,128)} %broadcast_in_dim.41), calls=%async_computation.3 | async-start | bytes 65536 | tf_op jit(solution)/shard_map/all_to_all | solution.py:41
  80.1 2.2 %copy-start.14 = (f32[256,2048]{1,0:T(8,128)S(1)}, f32[256,2048]{1,0:T(8,128)}, u32[]{:S(2)}) copy-start(f32[256,2048]{1,0:T(8,128)} %copy-done.13) | copy-start | bytes 6291460
  83.4 16.9 %all-to-all-start.4 = ((f32[32,1,1536]{2,1,0:T(1,128)}), f32[32,1,1536]{2,1,0:T(1,128)S(1)}, u32[]{:S(2)}, u32[]{:S(2)}) async-start(f32[32,1,1536]{2,1,0:T(1,128)} %broadcast_in_dim.42), calls=%async_computation.4 | async-start | bytes 393216 | tf_op jit(solution)/shard_map/all_to_all | solution.py:41
  92.1 16.0 %collective-permute-start.2 = (f32[640,256]{1,0:T(8,128)}, f32[640,256]{1,0:T(8,128)}, u32[]{:S(2)}, u32[]{:S(2)}) collective-permute-start(f32[640,256]{1,0:T(8,128)} %slice.113), channel_id=1, source_target_pairs={{0,16},{16,0},{1,17},{17,1},{2,18},{18,2},{3,19},{19,3},{4,20},{20... | collective-permute-start | bytes 1966088 | tf_op jit(solution)/shard_map/ppermute | solution.py:26
  100.4 2.2 %copy-start.15 = (f32[256,2048]{1,0:T(8,128)S(1)}, f32[256,2048]{1,0:T(8,128)}, u32[]{:S(2)}) copy-start(f32[256,2048]{1,0:T(8,128)} %copy-done.13) | copy-start | bytes 6291460
  106.3 3.2 %collective-permute-start.3 = (f32[16,8,512]{2,1,0:T(8,128)}, f32[16,8,512]{2,1,0:T(8,128)}, u32[]{:S(2)}, u32[]{:S(2)}) collective-permute-start(f32[16,8,512]{2,1,0:T(8,128)} %bitcast.40), channel_id=1, source_target_pairs={{0,16},{16,0},{1,17},{17,1},{2,18},{18,2},{3,19},{19,3},{4,20},{20... | collective-permute-start | bytes 786440 | tf_op jit(solution)/shard_map/ppermute | solution.py:26
  111.5 33.3 %all-to-all-start.5 = ((f32[16,56,256]{2,1,0:T(8,128)}), f32[16,56,256]{2,1,0:T(8,128)}, u32[]{:S(2)}, u32[]{:S(2)}) async-start(f32[16,56,256]{2,1,0:T(8,128)} %pad_maximum_fusion), calls=%async_computation.5 | async-start | bytes 1835008 | tf_op jit(solution)/shard_map/all_to_all | solution.py:403
  116.0 59.8 %collective-permute-start.4 = (bf16[640,1536]{1,0:T(8,128)(2,1)}, bf16[640,1536]{1,0:T(8,128)(2,1)}, u32[]{:S(2)}, u32[]{:S(2)}) collective-permute-start(bf16[640,1536]{1,0:T(8,128)(2,1)} %f0_ref.1), channel_id=1, source_target_pairs={{0,16},{16,0},{1,17},{17,1},{2,18},{18,2},{3,19},{19,3},{4,20},{20... | collective-permute-start | bytes 5898248 | tf_op jit(solution)/shard_map/ppermute | solution.py:26
  117.5 3.1 %collective-permute-start = (s32[640]{0:T(1024)S(1)}, s32[640]{0:T(1024)}, u32[]{:S(2)}, u32[]{:S(2)}) collective-permute-start(s32[640]{0:T(1024)S(1)} %select_reduce_fusion), channel_id=1, source_target_pairs={{0,16},{16,0},{1,17},{17,1},{2,18},{18,2},{3,19},{19,3},{4,20},{20... | collective-permute-start | bytes 7688 | tf_op jit(solution)/shard_map/ppermute | solution.py:26
  121.3 6.2 %copy-start.22 = (bf16[48,256]{1,0:T(8,128)(2,1)S(1)}, bf16[48,256]{1,0:T(8,128)(2,1)}, u32[]{:S(2)}) copy-start(bf16[48,256]{1,0:T(8,128)(2,1)} %copy-done.21) | copy-start | bytes 73732
  121.3 29.6 %copy-start.26 = (f32[48]{0:T(128)S(1)}, f32[48]{0:T(128)}, u32[]{:S(2)}) copy-start(f32[48]{0:T(128)} %copy-done.25) | copy-start | bytes 580
  127.1 56.0 %collective-permute-start.6 = (f32[256,2048]{1,0:T(8,128)}, f32[256,2048]{1,0:T(8,128)}, u32[]{:S(2)}, u32[]{:S(2)}) collective-permute-start(f32[256,2048]{1,0:T(8,128)} %fusion.1.own_ref), channel_id=1, source_target_pairs={{0,16},{16,0},{1,17},{17,1},{2,18},{18,2},{3,19},{19,3},{4,20},{20... | collective-permute-start | bytes 6291464 | tf_op jit(solution)/shard_map/ppermute | solution.py:26
  152.6 20.5 %all-to-all-start.6 = ((bf16[16,48,256]{2,1,0:T(8,128)(2,1)}), bf16[16,48,256]{2,1,0:T(8,128)(2,1)}, u32[]{:S(2)}, u32[]{:S(2)}) async-start(bf16[16,48,256]{2,1,0:T(8,128)(2,1)} %broadcast_in_dim.48), calls=%async_computation.6 | async-start | bytes 786432 | tf_op jit(solution)/shard_map/all_to_all | solution.py:41
  160.2 22.8 %collective-permute-start.7 = (bf16[256,2048]{1,0:T(8,128)(2,1)S(1)}, bf16[256,2048]{1,0:T(8,128)(2,1)}, u32[]{:S(2)}, u32[]{:S(2)}) collective-permute-start(bf16[256,2048]{1,0:T(8,128)(2,1)S(1)} %get-tuple-element.44.lown_ref), channel_id=1, source_target_pairs={{0,16},{16,0},{1,17},{17,1},{2,18},{18,2},{3,19},{19,3},{4,20},{20... | collective-permute-start | bytes 3145736 | tf_op jit(solution)/shard_map/ppermute | solution.py:26
  175.7 3.3 %copy-start.4 = (bf16[640,1536]{1,0:T(8,128)(2,1)S(1)}, bf16[640,1536]{1,0:T(8,128)(2,1)}, u32[]{:S(2)}) copy-start(bf16[640,1536]{1,0:T(8,128)(2,1)} %f0_ref.1) | copy-start | bytes 5898244
  175.7 3.3 %copy-start.8 = (f32[640,128]{1,0:T(8,128)S(1)}, f32[640,128]{1,0:T(8,128)}, u32[]{:S(2)}) copy-start(f32[640,128]{1,0:T(8,128)} %get-tuple-element.41.s0_ref) | copy-start | bytes 983044
  175.7 3.3 %copy-start.10 = (bf16[128,256]{1,0:T(8,128)(2,1)S(1)}, bf16[128,256]{1,0:T(8,128)(2,1)}, u32[]{:S(2)}) copy-start(bf16[128,256]{1,0:T(8,128)(2,1)} %w2_ref.1) | copy-start | bytes 196612
  175.7 3.3 %copy-start.12 = (bf16[640,128]{1,0:T(8,128)(2,1)S(1)}, bf16[640,128]{1,0:T(8,128)(2,1)}, u32[]{:S(2)}) copy-start(bf16[640,128]{1,0:T(8,128)(2,1)} %copy-done.11) | copy-start | bytes 491524
  175.7 3.3 %collective-permute-start.5 = (bf16[768,256]{1,0:T(8,128)(2,1)S(1)}, bf16[768,256]{1,0:T(8,128)(2,1)S(1)}, u32[]{:S(2)}, u32[]{:S(2)}) collective-permute-start(bf16[768,256]{1,0:T(8,128)(2,1)S(1)} %shard_map.129.dz0_ref), channel_id=1, source_target_pairs={{0,16},{16,0},{1,17},{17,1},{2,18},{18,2},{3,19},{19,3},{4,20},{20... | collective-permute-start | bytes 1179656 | tf_op jit(solution)/shard_map/ppermute | solution.py:26
  (10 other events, 11.1 us)
Sparse Core Ops, SparseCore 0:
  53.1 88.9 all-gather.2

commit v3 on v1

--- a/solution.py
+++ b/solution.py
@@ -1,6 +1,10 @@
+import functools
+
 import jax
 import jax.numpy as jnp
 from jax import lax
+from jax.experimental import pallas as pl
+from jax.experimental.pallas import tpu as pltpu
 from jax.sharding import PartitionSpec as P
 
 ITERS = 3
@@ -45,7 +49,7 @@
     return matf * inv, inv
 
 
-def body(
+def general_body(
     features,
     teacher_features,
     crop_image,
@@ -87,7 +91,7 @@
     parts = jnp.concatenate([zpart.reshape(n, sr, bot), tpart.reshape(n, tr, bot)], axis=1)
     parts = lax.all_to_all(parts, "proto", 0, 0)
     early = jnp.concatenate(
-        [slope.astype(BF16)] + [head_w2[:, i : i + head_w1.shape[1]] for i in range(0, bot, head_w1.shape[1])],
+        [(slope - 0.5).astype(BF16)] + [head_w2[:, i : i + head_w1.shape[1]] for i in range(0, bot, head_w1.shape[1])],
         axis=0,
     )
     early = lax.all_gather(early, "proto")
@@ -122,8 +126,7 @@
     out = jnp.concatenate([sums.reshape(nd, n, sr, bot), tsums.reshape(nd, n, tr, bot)], axis=2)
     out = out[absolute]
     out = tree_sum([out[0]] + [swap(out[s], "dp", s) for s in range(1, nd)])
-    out = lax.all_to_all(out.astype(BF16), "proto", 0, 0)
-    out = jnp.sum(out.astype(F32), axis=0)
+    out = jnp.sum(lax.all_to_all(out, "proto", 0, 0), axis=0)
     crop_scale = jnp.where(views == 2, 2.0, 1.0).reshape(-1) / esum * factor
     image_scale = factor / mass
     mine = (d * n + p)
@@ -164,12 +167,522 @@
         dhid = (dot(dzs[s], head_w2, ((1,), (1,))) * slp).astype(BF16)
         w1_parts.append(dot(feats[s], dhid, ((0,), (0,))))
     grad_w1, grad_w2 = tree_sum(w1_parts), tree_sum(w2_parts)
-    slopes = early[:, :rows].transpose(1, 0, 2).reshape(rows, -1)
+    slopes = 0.5 + early[:, :rows].astype(F32).transpose(1, 0, 2).reshape(rows, -1)
     w2_all = early[:, rows:].reshape(n, -1, head_w1.shape[1], head_w1.shape[1]).transpose(1, 3, 0, 2)
     w2_all = w2_all.reshape(bot, -1)
     dhid = (jnp.dot(dz, w2_all, preferred_element_type=F32) * slopes).astype(BF16)
     grad_features = dot(dhid, w1_block, ((1,), (1,))).astype(BF16)
     return (grad_features, grad_w1, grad_w2, grad_protos)
+
+
+def params(mib=40):
+    return pltpu.CompilerParams(vmem_limit_bytes=mib * 1024 * 1024)
+
+
+def shape(dims, dtype):
+    return jax.ShapeDtypeStruct(dims, dtype)
+
+
+def call(kernel, outs, scalars, *args, us=1):
+    smem = [jnp.asarray(s, jnp.int32).reshape(1) for s in scalars]
+    return pl.pallas_call(
+        kernel,
+        out_shape=outs,
+        in_specs=[pl.BlockSpec(memory_space=pltpu.SMEM)] * len(smem)
+        + [pl.BlockSpec(memory_space=pltpu.VMEM)] * len(args),
+        out_specs=jax.tree.map(lambda _: pl.BlockSpec(memory_space=pltpu.VMEM), outs),
+        compiler_params=params(),
+        cost_estimate=pl.CostEstimate(flops=us * 10**9, bytes_accessed=us * 10**6, transcendentals=0),
+    )(*smem, *args)
+
+
+def grids(dims):
+    return lax.broadcasted_iota(jnp.int32, dims, 0), lax.broadcasted_iota(jnp.int32, dims, 1)
+
+
+def to_row(col):
+    down, along = grids((col.shape[0], col.shape[0]))
+    return jnp.sum(jnp.where(down == along, col, jnp.zeros_like(col)), axis=0, keepdims=True)
+
+
+def to_col(row):
+    down, along = grids((row.shape[1], row.shape[1]))
+    return jnp.sum(jnp.where(down == along, row, jnp.zeros_like(row)), axis=1, keepdims=True)
+
+
+def head_kernel(d_ref, f_ref, w1_ref, w2_ref, tf_ref, tw1_ref, tw2_ref, im_ref, view_ref, parts_ref, back_ref, vs_ref):
+    rows, teach = f_ref.shape[0], tf_ref.shape[0]
+    n = parts_ref.shape[0]
+    img = teach // 2
+    per = rows // img
+    im = (im_ref[...] - d_ref[0] * img).astype(F32)
+    down, along = grids((rows, rows))
+    imc = to_col(im)
+    same = im == imc
+    before = jnp.where(same & (along < down), 1.0, 0.0)
+    after = jnp.where(same & (down < along), 1.0, 0.0)
+    col = (imc * per + jnp.sum(before, axis=1, keepdims=True)).astype(jnp.int32)
+    row = (im * per + jnp.sum(after, axis=0, keepdims=True)).astype(jnp.int32)
+    back_ref[...] = jnp.where(col == along, 1.0, 0.0).astype(BF16)
+    hit = row == down
+    vs_ref[...] = jnp.sum(jnp.where(hit, view_ref[...].astype(F32), 0.0), axis=1, keepdims=True)
+    order = jnp.where(hit, 1.0, 0.0).astype(BF16)
+
+    def part(x, first, second):
+        act = dot(x[...], first[...], ((1,), (0,)))
+        hidden = (act * 0.5 * (1.0 + lax.erf(act * 0.7071067811865476))).astype(BF16)
+        return dot(hidden, second[...], ((1,), (0,)))
+
+    z = part(f_ref, w1_ref, w2_ref).astype(BF16)
+    z = dot(order, z, ((1,), (0,))).reshape(n, rows // n, -1)
+    t = part(tf_ref, tw1_ref, tw2_ref).reshape(n, teach // n, -1)
+    parts_ref[...] = jnp.concatenate([z, t], axis=1).astype(BF16)
+
+
+def rows_kernel(parts_ref, out_ref, zn_ref, zinv_ref):
+    z = jnp.sum(parts_ref[...].astype(F32), axis=0)
+    inv = lax.rsqrt(jnp.sum(z * z, axis=1, keepdims=True) + 1e-06)
+    zn = z * inv
+    zn_ref[...] = zn
+    zinv_ref[...] = inv
+    out_ref[...] = jnp.broadcast_to(zn[None], out_ref.shape).astype(BF16)
+
+
+def row_mass(kern, mass):
+    if mass is None:
+        scale = 1.0 / jnp.sum(kern, axis=0, keepdims=True)
+    else:
+        scale = 1.0 / jnp.sum(kern * (1.0 / mass), axis=0, keepdims=True)
+    return scale, jnp.sum(kern * scale, axis=1, keepdims=True)
+
+
+def fold(col):
+    row = to_row(col)
+    return jnp.concatenate([row[:, k : k + 128] for k in range(0, row.shape[1], 128)], axis=0)
+
+
+def unfold(block):
+    return to_col(jnp.concatenate([block[k : k + 1] for k in range(block.shape[0])], axis=1))
+
+
+def kern_kernel(d_ref, got_ref, other_ref, tpnb_ref, kern_ref, msg_ref, student_ref):
+    n, slot, bot = got_ref.shape
+    rows = student_ref.shape[0] // 2
+    sr = rows // n
+    own, other = got_ref[...].astype(F32), other_ref[...].astype(F32)
+    student_ref[:rows] = own[:, :sr].reshape(rows, bot).astype(BF16)
+    student_ref[rows:] = other[:, :sr].reshape(rows, bot).astype(BF16)
+    own, other = own[:, sr:].reshape(-1, bot), other[:, sr:].reshape(-1, bot)
+    first = d_ref[0] == 0
+    teacher = jnp.concatenate([jnp.where(first, own, other), jnp.where(first, other, own)], axis=0).astype(BF16)
+    kern = jnp.exp(dot(teacher, tpnb_ref[...], ((1,), (0,))) * (1.0 / 0.07))
+    kern_ref[...] = kern
+    _, mass = row_mass(kern, None)
+    msg_ref[...] = jnp.broadcast_to(fold(mass)[None], msg_ref.shape)
+
+
+def student_kernel(z_ref, pnb_ref, exb_ref, sums_ref, esum_ref):
+    step = pl.program_id(0)
+    ex = jnp.exp(dot(z_ref[...], pnb_ref[...], ((1,), (0,))) * 10.0)
+    esum_ref[pl.ds(step, 1), :] = fold(jnp.sum(ex, axis=1, keepdims=True))
+    exb = ex.astype(BF16)
+    exb_ref[...] = exb
+    sums_ref[...] = dot(exb, pnb_ref[...], ((1,), (1,)))
+
+
+def student_sums(student, pnb):
+    total, bot = student.shape
+    cols = pnb.shape[1]
+    return pl.pallas_call(
+        student_kernel,
+        grid=(total // 128,),
+        out_shape=(shape((total, cols), BF16), shape((total, bot), F32), shape((total // 128, 128), F32)),
+        in_specs=[pl.BlockSpec((128, bot), lambda i: (i, 0)), pl.BlockSpec((bot, cols), lambda i: (0, 0))],
+        out_specs=(
+            pl.BlockSpec((128, cols), lambda i: (i, 0)),
+            pl.BlockSpec((128, bot), lambda i: (i, 0)),
+            pl.BlockSpec((total // 128, 128), lambda i: (0, 0)),
+        ),
+        compiler_params=params(),
+        cost_estimate=pl.CostEstimate(flops=5 * 10**9, bytes_accessed=10**7, transcendentals=0),
+    )(student, pnb)
+
+
+def second_kernel(d_ref, got_ref, kern_ref, esum_ref, msg_ref):
+    mass = unfold(jnp.sum(got_ref[...], axis=0))
+    _, mass = row_mass(kern_ref[...], mass)
+    half = esum_ref.shape[0] // 2
+    esum = esum_ref[...]
+    turned = jnp.concatenate([esum[half:], esum[:half]], axis=0)
+    esum = jnp.where(d_ref[0] == 0, esum, turned)
+    msg_ref[...] = jnp.broadcast_to(jnp.concatenate([fold(mass), esum], axis=0)[None], msg_ref.shape)
+
+
+def third_kernel(d_ref, got_ref, kern_ref, pnb_ref, esum_ref, last_ref, mine_ref, yours_ref):
+    teach = kern_ref.shape[0]
+    got = jnp.sum(got_ref[...], axis=0)
+    top = teach // 128
+    esum_ref[...] = got[top:]
+    kern = kern_ref[...]
+    scale, mass = row_mass(kern, unfold(got[:top]))
+    last = (kern * scale).astype(BF16)
+    last_ref[...] = last
+    sums = dot(last, pnb_ref[...], ((1,), (1,)))
+    sums = jnp.concatenate([sums, jnp.broadcast_to(mass, (teach, 128))], axis=1)
+    half = teach // 2
+    first = d_ref[0] == 0
+    mine_ref[...] = jnp.where(first, sums[:half], sums[half:])
+    yours_ref[...] = jnp.where(first, sums[half:], sums[:half])
+
+
+def message_kernel(a0_ref, a1_ref, b0_ref, b1_ref, out_ref):
+    n = out_ref.shape[0]
+    rows, bot = a0_ref.shape
+    sums = (a0_ref[...] + a1_ref[...]).reshape(n, rows // n, bot)
+    both = b0_ref[...] + b1_ref[...]
+    mass = both[:, bot:]
+    high = mass.astype(BF16).astype(F32)
+    tail = jnp.concatenate([high, mass - high], axis=1)
+    teach = both.shape[0]
+    both = both[:, :bot].reshape(n, teach // n, bot)
+    out_ref[...] = jnp.concatenate([sums, both, tail.reshape(n, teach // n, bot)], axis=1).astype(BF16)
+
+
+def bottleneck_kernel(factor, got_ref, zn_ref, zinv_ref, view_ref, scale_ref, out_ref):
+    sr = view_ref.shape[0]
+    tr = zn_ref.shape[0] - sr
+    per = sr // (tr // 2)
+    out = jnp.sum(got_ref[...].astype(F32), axis=0)
+    tail = out[sr + tr :]
+    image = factor / (tail[:, :1] + tail[:, 128:129])
+    sums = out[sr : sr + tr] * image
+    zn, zinv = zn_ref[:sr], zinv_ref[:sr]
+    znb = zn.astype(BF16).astype(F32)
+    view = view_ref[...].astype(jnp.int32)
+    which = lax.broadcasted_iota(jnp.int32, (sr, 1), 0)
+    dzn = scale_ref[...] * out[:sr]
+    own = []
+    for t in range(tr):
+        base = (t // 2) * per
+        pick = (which >= base) & (which < base + per) & (view != t % 2)
+        dzn = dzn - jnp.where(pick, sums[t : t + 1], 0.0)
+        own.append(jnp.sum(jnp.where(pick, znb, 0.0), axis=0, keepdims=True) * image[t : t + 1])
+    dz = zinv * (dzn - zn * jnp.sum(zn * dzn, axis=1, keepdims=True))
+    both = jnp.concatenate([dz] + own, axis=0)
+    out_ref[...] = jnp.broadcast_to(both[None], out_ref.shape).astype(BF16)
+
+
+def hidden_kernel(f0_ref, f1_ref, w1_ref, h0_ref, h1_ref, s0_ref, s1_ref):
+    for f, h, s in ((f0_ref, h0_ref, s0_ref), (f1_ref, h1_ref, s1_ref)):
+        act = dot(f[...], w1_ref[...], ((1,), (0,))).T
+        phi = 0.5 * (1.0 + lax.erf(act * 0.7071067811865476))
+        h[...] = (act * phi).astype(BF16)
+        s[...] = phi + act * jnp.exp(-0.5 * act * act) * 0.3989422804014327
+
+
+def slopes_kernel(d_ref, p_ref, f_ref, own_ref, other_ref, slope_ref, w2_ref, w1_ref):
+    hs = own_ref.shape[2]
+    deep = f_ref.shape[1] // 2
+    first = d_ref[0] == 0
+    own, other = own_ref[...], other_ref[...]
+    low = jnp.where(first, own, other)
+    high = jnp.where(first, other, own)
+    a, b = (jnp.concatenate([x[0], x[1]], axis=1) for x in (low[:, :deep], high[:, :deep]))
+    act = dot(f_ref[:, :deep], a, ((1,), (0,))) + dot(f_ref[:, deep:], b, ((1,), (0,)))
+    phi = 0.5 * (1.0 + lax.erf(act * 0.7071067811865476))
+    slope_ref[...] = phi + act * jnp.exp(-0.5 * act * act) * 0.3989422804014327
+    width = w1_ref.shape[0]
+    blocks = deep // width
+    at = pl.multiple_of(lax.rem(p_ref[0], blocks) * width, width)
+    mine = (p_ref[0] // blocks) == d_ref[0]
+    rows = jnp.where(mine, own_ref[:, pl.ds(at, width)], other_ref[:, pl.ds(at, width)])
+    w1_ref[...] = jnp.concatenate([rows[0], rows[1]], axis=1)
+    half = hs // 2
+    for k in range(2):
+        for part, x in ((0, low), (1, high)):
+            tail = jnp.concatenate([x[k, deep : deep + half], x[k, deep + half :]], axis=1)
+            w2_ref[k * hs + part * half : k * hs + (part + 1) * half] = tail
+
+
+def slopes_of(d, p, features, own, other, width):
+    n, tall, hs = own.shape
+    rows = features.shape[0]
+    whole = lambda k, d, p: (0, 0)
+    return pl.pallas_call(
+        slopes_kernel,
+        grid_spec=pltpu.PrefetchScalarGridSpec(
+            num_scalar_prefetch=2,
+            grid=(n // 2,),
+            in_specs=[
+                pl.BlockSpec(features.shape, whole),
+                pl.BlockSpec((2, tall, hs), lambda k, d, p: (k, 0, 0)),
+                pl.BlockSpec((2, tall, hs), lambda k, d, p: (k, 0, 0)),
+            ],
+            out_specs=(
+                pl.BlockSpec((rows, 2 * hs), lambda k, d, p: (0, k)),
+                pl.BlockSpec((2 * hs, 2 * hs), lambda k, d, p: (k, 0)),
+                pl.BlockSpec((width, 2 * hs), lambda k, d, p: (0, k)),
+            ),
+        ),
+        out_shape=(shape((rows, n * hs), F32), shape((n * hs, 2 * hs), BF16), shape((width, n * hs), BF16)),
+        compiler_params=params(),
+        cost_estimate=pl.CostEstimate(flops=10**10, bytes_accessed=3 * 10**7, transcendentals=0),
+    )(d.reshape(1), p.reshape(1), features, own, other)
+
+
+def unsort_kernel(got_ref, back_ref, out_ref):
+    n, slot, bot = got_ref.shape
+    rows = back_ref.shape[0]
+    sr = rows // n
+    got = got_ref[...].astype(F32)
+    dz = got[:, :sr].reshape(rows, bot).astype(BF16)
+    out_ref[:rows] = dot(back_ref[...], dz, ((1,), (0,))).astype(BF16)
+    out_ref[rows:] = got[:, sr:].reshape(n * (slot - sr), bot).astype(BF16)
+
+
+def features_kernel(dz_ref, slope_ref, w2_ref, w1_ref, out_ref, acc_ref):
+    step = pl.program_id(0)
+
+    @pl.when(step == 0)
+    def _():
+        acc_ref[...] = jnp.zeros_like(acc_ref)
+
+    pre = dot(dz_ref[...], w2_ref[...], ((1,), (1,)))
+    dhid = (pre * slope_ref[...]).astype(BF16)
+    acc_ref[...] += dot(dhid, w1_ref[...], ((1,), (1,)))
+
+    @pl.when(step == pl.num_programs(0) - 1)
+    def _():
+        out_ref[...] = acc_ref[...].astype(BF16)
+
+
+def feature_grads(dz, slope, w2, w1_block):
+    rows, hidden = slope.shape
+    width, bot = w1_block.shape[0], w2.shape[1]
+    step = bot
+    return pl.pallas_call(
+        features_kernel,
+        grid=(hidden // step,),
+        out_shape=shape((rows, width), BF16),
+        in_specs=[
+            pl.BlockSpec((rows, bot), lambda k: (0, 0)),
+            pl.BlockSpec((rows, step), lambda k: (0, k)),
+            pl.BlockSpec((step, bot), lambda k: (k, 0)),
+            pl.BlockSpec((width, step), lambda k: (0, k)),
+        ],
+        out_specs=pl.BlockSpec((rows, width), lambda k: (0, 0)),
+        scratch_shapes=[pltpu.VMEM((rows, width), F32)],
+        compiler_params=params(),
+    )(dz, slope, w2, w1_block)
+
+
+def weights_kernel(f0_ref, f1_ref, dz0_ref, dz1_ref, h0_ref, h1_ref, s0_ref, s1_ref, w2_ref, g1_ref, g2_ref):
+    g1, g2 = [], []
+    rows = f0_ref.shape[0]
+    for f, z, h, s in ((f0_ref, dz0_ref, h0_ref, s0_ref), (f1_ref, dz1_ref, h1_ref, s1_ref)):
+        dz = z[:rows]
+        g2.append(dot(h[...], dz, ((1,), (0,))))
+        dhid = (dot(w2_ref[...], dz, ((1,), (1,))) * s[...]).astype(BF16)
+        g1.append(dot(dhid, f[...], ((1,), (0,))))
+    g1_ref[...] = (g1[0] + g1[1]).T
+    g2_ref[...] = g2[0] + g2[1]
+
+
+def protos_kernel(d_ref, protos_ref, own_ref, other_ref, left_ref, right_ref, lown_ref, lother_ref, out_ref):
+    half = pl.program_id(0) // (pl.num_programs(0) // 2)
+    mine = half == d_ref[0]
+    first = d_ref[0] == 0
+    a, b = left_ref[...].astype(F32), right_ref[...].astype(F32)
+    scaled = jnp.concatenate([jnp.where(first, a, b), jnp.where(first, b, a)], axis=0).astype(BF16)
+
+    def finish(dpn_ref, last_ref):
+        mat = protos_ref[...].astype(F32)
+        inv = lax.rsqrt(jnp.sum(mat * mat, axis=0, keepdims=True) + 1e-06)
+        pn = mat * inv
+        dpn = dpn_ref[...] - dot(scaled, last_ref[...], ((0,), (0,)))
+        out_ref[...] = inv * (dpn - pn * jnp.sum(pn * dpn, axis=0, keepdims=True))
+
+    @pl.when(mine)
+    def _():
+        finish(own_ref, lown_ref)
+
+    @pl.when(jnp.logical_not(mine))
+    def _():
+        finish(other_ref, lother_ref)
+
+
+def protos_grads(d, protos, own, other, mine, yours, lown, lother):
+    bot, wide = protos.shape
+    tile = 512
+    steps = wide // tile
+    halfsteps = steps // 2
+    teach = lown.shape[0]
+
+    def place(i, d_ref, same):
+        at = d_ref[0] if same else 1 - d_ref[0]
+        return (0, jnp.clip(i - at * halfsteps, 0, halfsteps - 1))
+
+    own_map = lambda i, d_ref: place(i, d_ref, True)
+    other_map = lambda i, d_ref: place(i, d_ref, False)
+    return pl.pallas_call(
+        protos_kernel,
+        grid_spec=pltpu.PrefetchScalarGridSpec(
+            num_scalar_prefetch=1,
+            grid=(steps,),
+            in_specs=[
+                pl.BlockSpec((bot, tile), lambda i, d_ref: (0, i)),
+                pl.BlockSpec((bot, tile), own_map),
+                pl.BlockSpec((bot, tile), other_map),
+                pl.BlockSpec((teach // 2, bot), lambda i, d_ref: (0, 0)),
+                pl.BlockSpec((teach // 2, bot), lambda i, d_ref: (0, 0)),
+                pl.BlockSpec((teach, tile), own_map),
+                pl.BlockSpec((teach, tile), other_map),
+            ],
+            out_specs=pl.BlockSpec((bot, tile), lambda i, d_ref: (0, i)),
+        ),
+        out_shape=jax.ShapeDtypeStruct((bot, wide), F32),
+        compiler_params=pltpu.CompilerParams(vmem_limit_bytes=32 * 1024 * 1024),
+    )(d.reshape(1), protos, own, other, mine, yours, lown, lother)
+
+
+def tied(*values):
+    return lax.optimization_barrier(values)
+
+
+def paired_body(
+    features,
+    teacher_features,
+    crop_image,
+    crop_view,
+    head_w1,
+    head_w2,
+    protos,
+    teacher_w1,
+    teacher_w2,
+    teacher_protos,
+):
+    nd, n = lax.axis_size("dp"), lax.axis_size("proto")
+    d, p = lax.axis_index("dp"), lax.axis_index("proto")
+    rows, teach = features.shape[0], teacher_features.shape[0]
+    sr, tr = rows // n, teach // n
+    wide, hs = head_w1.shape
+    bot = head_w2.shape[1]
+    everyone = nd * n
+    factor = 10.0 / (9 * teach * nd)
+
+    feat_other = swap(features, "dp", 1)
+    parts, back, view = call(
+        head_kernel,
+        (shape((n, sr + tr, bot), BF16), shape((rows, rows), BF16), shape((rows, 1), F32)),
+        [d],
+        features, head_w1, head_w2, teacher_features, teacher_w1, teacher_w2,
+        crop_image.reshape(1, -1), crop_view.reshape(1, -1),
+        us=4,
+    )
+    parts_got = lax.all_to_all(parts, "proto", 0, 0)
+    w1_late, w2_late, protos_late, tprotos_late, feat_late, _ = tied(
+        head_w1, head_w2, protos, teacher_protos, features, parts
+    )
+    w2_half = lax.dynamic_slice_in_dim(w2_late, d * (hs // 2), hs // 2, 0)
+    weights = jnp.concatenate(
+        [lax.dynamic_slice_in_dim(w1_late, d * (wide // 2), wide // 2, 0), w2_half[:, :hs], w2_half[:, hs:]], axis=0
+    )
+    weights = lax.all_gather(weights, "proto")
+    cols = protos.shape[1] // nd
+    pnb = unit_cols(lax.dynamic_slice_in_dim(protos_late, d * cols, cols, 1))[0].astype(BF16)
+    tpnb = unit_cols(lax.dynamic_slice_in_dim(tprotos_late, d * cols, cols, 1))[0].astype(BF16)
+    view_other = swap(view, "dp", 1)
+
+    got, zn, zinv = call(
+        rows_kernel,
+        (shape((n, sr + tr, bot), BF16), shape((sr + tr, bot), F32), shape((sr + tr, 1), F32)),
+        [],
+        parts_got,
+    )
+    feat_late, feat_other_late, w1_late, _ = tied(feat_late, feat_other, w1_late, got)
+    got = lax.all_to_all(got, "proto", 0, 0)
+    h0, h1, s0, s1 = call(
+        hidden_kernel,
+        (shape((hs, rows), BF16),) * 2 + (shape((hs, rows), F32),) * 2,
+        [],
+        feat_late, feat_other_late, w1_late,
+        us=4,
+    )
+    got_other = swap(got, "dp", 1)
+    kern, msg, student = call(
+        kern_kernel,
+        (shape((nd * teach, cols), F32), shape((everyone, nd * teach // 128, 128), F32), shape((nd * rows, bot), BF16)),
+        [d],
+        got, got_other, tpnb,
+        us=3,
+    )
+    msg_got = lax.all_to_all(msg, ALL, 0, 0)
+    student, _ = tied(student, msg)
+    exb, sums, esum = student_sums(student, pnb)
+    sums_other = swap(sums[rows:], "dp", 1)
+    msg = call(
+        second_kernel,
+        shape((everyone, nd * (teach + rows) // 128, 128), F32),
+        [d],
+        msg_got, kern, esum,
+    )
+    msg_got = lax.all_to_all(msg, ALL, 0, 0)
+    esum, last, mine, yours = call(
+        third_kernel,
+        (
+            shape((nd * rows // 128, 128), F32),
+            shape((nd * teach, cols), BF16),
+            shape((teach, bot + 128), F32),
+            shape((teach, bot + 128), F32),
+        ),
+        [d],
+        msg_got, kern, pnb,
+        us=2,
+    )
+    yours = swap(yours, "dp", 1)
+    msg = call(message_kernel, shape((n, sr + 2 * tr, bot), BF16), [], sums[:rows], sums_other, mine, yours)
+    msg_got = lax.all_to_all(msg, "proto", 0, 0)
+
+    esum, view_late, view_other, student, exb, last, weights, _ = tied(
+        esum, view, view_other, student, exb, last, weights, msg
+    )
+    esum = esum.reshape(nd, rows, 1)
+    esum = jnp.concatenate([jnp.where(d == 0, esum[0], esum[1]), jnp.where(d == 0, esum[1], esum[0])], axis=0)
+    count = jnp.where(jnp.concatenate([view_late, view_other], axis=0) == 2, 2.0, 1.0)
+    crop_scale = count * factor / esum
+    my_view = lax.dynamic_slice_in_dim(view_late, p * sr, sr, 0)
+    my_scale = lax.dynamic_slice_in_dim(crop_scale, p * sr, sr, 0)
+    dz = call(
+        functools.partial(bottleneck_kernel, factor),
+        shape((n, sr + tr, bot), BF16),
+        [],
+        msg_got, zn, zinv, my_view, my_scale,
+    )
+    got = lax.all_to_all(dz, "proto", 0, 0)
+    left = (student.astype(F32) * crop_scale).astype(BF16)
+    dpn = dot(left, exb, ((0,), (0,)))
+    dpn_other, last_other = swap(dpn, "dp", 1), swap(last, "dp", 1)
+    weights_other = swap(weights, "dp", 1)
+    slope, w2_all, w1_block = slopes_of(d, p, features, weights, weights_other, wide // n)
+
+    dz = call(unsort_kernel, shape((rows + teach, bot), BF16), [], got, back)
+    dz_other = swap(dz, "dp", 1)
+    grad_features = feature_grads(dz, slope, w2_all, w1_block)
+    grad_w1, grad_w2 = call(
+        weights_kernel,
+        (shape(head_w1.shape, F32), shape(head_w2.shape, F32)),
+        [],
+        features, feat_other, dz, dz_other, h0, h1, s0, s1, head_w2,
+    )
+    grad_protos = protos_grads(d, protos, dpn, dpn_other, dz[rows:], dz_other[rows:], last, last_other)
+    return (grad_features, grad_w1, grad_w2, grad_protos)
+
+
+def body(features, teacher_features, *rest):
+    n = lax.axis_size("proto")
+    slot = (features.shape[0] // n, teacher_features.shape[0] // n)
+    paired = lax.axis_size("dp") == 2 and n % 2 == 0 and slot[0] % 8 == 0 and slot[1] % 8 == 0
+    return (paired_body if paired else general_body)(features, teacher_features, *rest)
 
 
 def solution(mesh):

time: 194 us -> 206 us (1.062)
  Pallas kernels: 0 us -> 48.6 us
  matrix products: 36.6 us -> 5.7 us
  other arithmetic: 20 us -> 8.36 us
  waiting for transfers between devices: 52.4 us -> 55.6 us
    pallas_call x0 -> x14, Pallas kernels: none -> 48.6 us  [the longest x10 19.4 us: call(): pl.pallas_call(kernel, out_shape=outs, in_specs=[pl.BlockSpec(memory_spac...]
    unnamed x55 -> x78, local copies, waits for them, and re-layouts: 6.33 us -> 31 us
    dot_general x10 -> x1, matrix products: 23.7 us -> 5.7 us  [dot(): return lax.dot_general(a, b, (dims, ((), ())), preferred_element_type=F32)]
    dot_general x7 -> x0, matrix products: 12.9 us -> none  [the longest x1 3.66 us: body(): ex = jnp.exp(jnp.dot(student, pnb, preferred_element_type=F32) / 0.1)]
    convert_element_type x2 -> x0, local copies, waits for them, and re-layouts: 11.9 us -> none  [body(): jnp.dot(dz, w2_all, preferred_element_type=F32) * slopes]
    convert_element_type x5 -> x2, other arithmetic: 7.46 us -> 2.65 us  [the longest x1 2.43 us: paired_body(): unit_cols(lax.dynamic_slice_in_dim(tprotos_late, d * cols, cols, 1))[0]]
    gather x4 -> x0, local copies, waits for them, and re-layouts: 4.39 us -> none  [the longest x1 3.22 us: body(): out = out[absolute]]
    broadcast_in_dim x6 -> x0, local copies, waits for them, and re-layouts: 4.04 us -> none  [the longest x5 3.57 us: send_all(): jnp.broadcast_to(value[None], (count,) + value.shape)]
  transfers between devices with their start and end apart: 15 -> 16, of which waited for: 8 -> 7; matrix products, arithmetic and copies ran while one was open for 39% -> 9% of each run, Pallas kernels for 0% -> 15%
where the time goes in v3:
time: 206 us; the launch traced here: 204 us
  waiting for transfers between devices  55.6 us (27%)
  Pallas kernels  48.6 us (24%)
  local copies, waits for them, and re-layouts  36.7 us (18%)
  starting transfers between devices  34.3 us (17%)
  between operations  14.4 us (7%)
  other arithmetic  8.36 us (4%)
  matrix products  5.7 us (3%)
    unnamed x78, local copies, waits for them, and re-layouts  31 us
    pallas_call x10, Pallas kernels, call(): pl.pallas_call(kernel, out_shape=outs, in_specs=[pl.BlockSpec(memory_spac...  19.4 us
    all_to_all x1, waiting for transfers between devices, paired_body(): got = lax.all_to_all(got, 'proto', 0, 0)  14.5 us
    all_to_all x1, waiting for transfers between devices, paired_body(): parts_got = lax.all_to_all(parts, 'proto', 0, 0)  14.5 us
    all_to_all x1, waiting for transfers between devices, paired_body(): got = lax.all_to_all(dz, 'proto', 0, 0)  12.9 us
    all_to_all x2, starting transfers between devices, paired_body(): msg_got = lax.all_to_all(msg, ALL, 0, 0)  11.5 us
    pallas_call x1, Pallas kernels, slopes_of(): pl.pallas_call(slopes_kernel, grid_spec=pltpu.PrefetchScalarGridSpec(num_...  9.86 us
    all_to_all x2, waiting for transfers between devices, paired_body(): msg_got = lax.all_to_all(msg, ALL, 0, 0)  8.51 us
  transfers between devices with their start and end apart: 16, of which 7 were waited for; matrix products, arithmetic and copies ran while one was open for 9% of the time, Pallas kernels for 15%

profile of v3, /device:TPU:0, one launch (start us, length us, event | category | flops | bytes accessed | tf_op | source)
XLA Modules:
  0.0 203.6 jit_solution(10881900639558897966)
XLA Ops:
  8.6 1.5 copy-done.2
  14.8 3.3 %shard_map.129 = (bf16[16,48,256]{2,1,0:T(8,128)(2,1)}, bf16[640,640]{1,0:T(8,128)(2,1)S(1)}, f32[640,1]{1,0:T(8,128)S(1)}) custom-call(s32[1]{0:T(128)} %bitcast.d_ref, bf16[640,1536]{1,0:T(8,128)(2,1)S(1)} %copy-done.2, bf16[1536,128]{1,0:T(8,128)(2,1)S(1)} %copy-done.15, bf16[128,256]{1,0:T(8,128)(2,1)S(1)} %copy-done.13, ...), custom_call_target="tpu_custom_call" | custom-call | flops 4000000000 | bytes 4000000 | tf_op jit(solution)/shard_map/pallas_call | solution.py:188
  19.8 8.3 %all-to-all-start = ((bf16[16,48,256]{2,1,0:T(8,128)(2,1)}), bf16[16,48,256]{2,1,0:T(8,128)(2,1)S(1)}, u32[]{:S(2)}, u32[]{:S(2)}) async-start(bf16[16,48,256]{2,1,0:T(8,128)(2,1)} %get-tuple-element.45), calls=%async_computation | async-start | bytes 786432 | tf_op jit(solution)/shard_map/all_to_all | solution.py:582
  28.2 1.7 fusion
  29.9 14.5 %all-to-all-done.parts_ref = bf16[16,48,256]{2,1,0:T(8,128)(2,1)S(1)} async-done(((bf16[16,48,256]{2,1,0:T(8,128)(2,1)}), bf16[16,48,256]{2,1,0:T(8,128)(2,1)S(1)}, u32[]{:S(2)}, u32[]{:S(2)}) %all-to-all-start) | async-done | bytes 393248 | tf_op jit(solution)/shard_map/all_to_all | solution.py:582
  45.8 4.2 %all-to-all-start.1 = ((bf16[16,48,256]{2,1,0:T(8,128)(2,1)}), bf16[16,48,256]{2,1,0:T(8,128)(2,1)}, u32[]{:S(2)}, u32[]{:S(2)}) async-start(bf16[16,48,256]{2,1,0:T(8,128)(2,1)} %get-tuple-element.46), calls=%async_computation.1 | async-start | bytes 786432 | tf_op jit(solution)/shard_map/all_to_all | solution.py:603
  50.1 2.4 %fusion.1.tpnb_ref = bf16[256,2048]{1,0:T(8,128)(2,1)} fusion(f32[2048]{0:T(1024)S(1)} %add_rsqrt_fusion.1, bf16[256,4096]{1,0:T(8,128)(2,1)} %param.19, s32[]{:T(128)S(6)} %select_n.67), kind=kLoop, calls=%fused_computation.5 | loop fusion | flops 1572864 | bytes 2105348 | tf_op jit(solution)/shard_map/convert_element_type | solution.py:593
  52.5 14.5 %all-to-all-done.1.got_ref = bf16[16,48,256]{2,1,0:T(8,128)(2,1)} async-done(((bf16[16,48,256]{2,1,0:T(8,128)(2,1)}), bf16[16,48,256]{2,1,0:T(8,128)(2,1)}, u32[]{:S(2)}, u32[]{:S(2)}) %all-to-all-start.1) | async-done | bytes 393248 | tf_op jit(solution)/shard_map/all_to_all | solution.py:603
  67.2 1.7 collective-permute-done.other_ref
  68.9 1.8 shard_map.131
  73.5 5.7 %all-to-all-start.2 = ((f32[32,2,128]{2,1,0:T(2,128)}), f32[32,2,128]{2,1,0:T(2,128)}, u32[]{:S(2)}, u32[]{:S(2)}) async-start(f32[32,2,128]{2,1,0:T(2,128)} %copy-done.18), calls=%async_computation.2 | async-start | bytes 65536 | tf_op jit(solution)/shard_map/all_to_all | solution.py:619
  80.3 6.5 %shard_map.132 = (bf16[1280,2048]{1,0:T(8,128)(2,1)S(1)}, f32[1280,256]{1,0:T(8,128)S(1)}, f32[10,128]{1,0:T(8,128)S(1)}) custom-call(bf16[1280,256]{1,0:T(8,128)(2,1)S(1)} %copy-done.30, bf16[256,2048]{1,0:T(8,128)(2,1)S(1)} %fusion.3.pnb_ref), custom_call_target="tpu_custom_call" | custom-call | flops 5000000000 | bytes 10000000 | tf_op jit(solution)/shard_map/pallas_call | solution.py:296
  88.0 2.4 %copy-done.25 = bf16[1280,2048]{1,0:T(8,128)(2,1)} copy-done((bf16[1280,2048]{1,0:T(8,128)(2,1)}, bf16[1280,2048]{1,0:T(8,128)(2,1)S(1)}, u32[]{:S(2)}) %copy-start.25) | copy-done | bytes 5242904
  90.4 1.6 copy-done.27
  92.0 2.0 %shard_map.133 = f32[32,12,128]{2,1,0:T(8,128)} custom-call(s32[1]{0:T(128)} %bitcast.d_ref, f32[32,2,128]{2,1,0:T(2,128)} %all-to-all-done.2.got_ref, f32[256,2048]{1,0:T(8,128)S(1)} %copy-done.27, f32[10,128]{1,0:T(8,128)S(1)} %get-tuple-element.54.esum_ref), custom_call_target="tpu_custom_call" | custom-call | flops 1000000000 | bytes 1000000 | tf_op jit(solution)/shard_map/pallas_call | solution.py:188
  94.0 5.8 %all-to-all-start.3 = ((f32[32,12,128]{2,1,0:T(8,128)}), f32[32,12,128]{2,1,0:T(8,128)S(1)}, u32[]{:S(2)}, u32[]{:S(2)}) async-start(f32[32,12,128]{2,1,0:T(8,128)} %shard_map.133), calls=%async_computation.3 | async-start | bytes 524288 | tf_op jit(solution)/shard_map/all_to_all | solution.py:629
  99.8 2.5 %fusion.14 = (f32[640,256]{1,0:T(8,128)}, f32[640,256]{1,0:T(8,128)}) fusion(f32[1280,256]{1,0:T(8,128)} %copy-done.4), kind=kLoop, calls=%fused_computation.36 | loop fusion | bytes 2621440 | tf_op jit(solution)/shard_map/slice | solution.py:622
  102.5 8.5 %all-to-all-done.3.got_ref = f32[32,12,128]{2,1,0:T(8,128)S(1)} async-done(((f32[32,12,128]{2,1,0:T(8,128)}), f32[32,12,128]{2,1,0:T(8,128)S(1)}, u32[]{:S(2)}, u32[]{:S(2)}) %all-to-all-start.3) | async-done | bytes 196640 | tf_op jit(solution)/shard_map/all_to_all | solution.py:629
  113.9 1.6 copy-done.28
  120.4 4.2 %all-to-all-start.4 = ((bf16[16,56,256]{2,1,0:T(8,128)(2,1)}), bf16[16,56,256]{2,1,0:T(8,128)(2,1)}, u32[]{:S(2)}, u32[]{:S(2)}) async-start(bf16[16,56,256]{2,1,0:T(8,128)(2,1)} %copy-done.9), calls=%async_computation.4 | async-start | bytes 917504 | tf_op jit(solution)/shard_map/all_to_all | solution.py:644
  125.4 1.7 reduce.1
  127.8 5.7 %fusion.4.own_ref = f32[256,2048]{1,0:T(8,128)} fusion(bf16[1280,2048]{1,0:T(8,128)(2,1)} %copy-done.25, bf16[1280,256]{1,0:T(8,128)(2,1)} %copy-done.29, f32[1280]{0:T(1024)S(1)} %maximum_divide_fusion), kind=kOutput, calls=%fused_computation.9 | convolution fusion | flops 1343160320 | bytes 8000512 | tf_op jit(solution)/shard_map/dot_general | solution.py:23
  136.3 2.6 %all-to-all-done.4.got_ref = bf16[16,56,256]{2,1,0:T(8,128)(2,1)} async-done(((bf16[16,56,256]{2,1,0:T(8,128)(2,1)}), bf16[16,56,256]{2,1,0:T(8,128)(2,1)}, u32[]{:S(2)}, u32[]{:S(2)}) %all-to-all-start.4) | async-done | bytes 458784 | tf_op jit(solution)/shard_map/all_to_all | solution.py:644
  143.9 4.4 %all-to-all-start.5 = ((bf16[16,48,256]{2,1,0:T(8,128)(2,1)}), bf16[16,48,256]{2,1,0:T(8,128)(2,1)}, u32[]{:S(2)}, u32[]{:S(2)}) async-start(bf16[16,48,256]{2,1,0:T(8,128)(2,1)} %copy-done.10), calls=%async_computation.5 | async-start | bytes 786432 | tf_op jit(solution)/shard_map/all_to_all | solution.py:661
  148.4 12.9 %all-to-all-done.5.got_ref = bf16[16,48,256]{2,1,0:T(8,128)(2,1)} async-done(((bf16[16,48,256]{2,1,0:T(8,128)(2,1)}), bf16[16,48,256]{2,1,0:T(8,128)(2,1)}, u32[]{:S(2)}, u32[]{:S(2)}) %all-to-all-start.5) | async-done | bytes 393248 | tf_op jit(solution)/shard_map/all_to_all | solution.py:661
  162.6 1.4 shard_map.137.dz_ref.dz0_ref
  164.2 2.9 %shard_map.140 = (bf16[128,640]{1,0:T(8,128)(2,1)S(1)}, bf16[128,640]{1,0:T(8,128)(2,1)S(1)}, f32[128,640]{1,0:T(8,128)S(1)}, f32[128,640]{1,0:T(8,128)S(1)}) custom-call(bf16[640,1536]{1,0:T(8,128)(2,1)S(1)} %copy-done.3, bf16[640,1536]{1,0:T(8,128)(2,1)} %collective-permute-done.5.f1_ref, bf16[1536,128]{1,0:T(8,128)(2,1)S(1)} %copy-done.17), custom_call_target="tpu_custom_call" | custom-call | flops 4000000000 | bytes 4000000 | tf_op jit(solution)/shard_map/pallas_call | solution.py:188
  167.1 3.7 %shard_map.141 = (f32[1536,128]{1,0:T(8,128)}, f32[128,256]{1,0:T(8,128)}) custom-call(bf16[640,1536]{1,0:T(8,128)(2,1)S(1)} %copy-done.3, bf16[640,1536]{1,0:T(8,128)(2,1)} %collective-permute-done.5.f1_ref, bf16[768,256]{1,0:T(8,128)(2,1)S(1)} %shard_map.137.dz_ref.dz0_ref, bf16[768,256]{1,0:T(8,128)(2,1)S(1)} %collective-permute-done.6.dz1_ref, ...), custom_call_target="tpu_custom_call" | custom-call | flops 1000000000 | bytes 1000000 | tf_op jit(solution)/shard_map/pallas_call | solution.py:188
  170.8 8.5 %shard_map.142 = f32[256,4096]{1,0:T(8,128)} custom-call(s32[1]{0:T(128)} %bitcast.d_ref, bf16[256,4096]{1,0:T(8,128)(2,1)S(1)} %copy-done, f32[256,2048]{1,0:T(8,128)} %fusion.4.own_ref, f32[256,2048]{1,0:T(8,128)} %collective-permute-done.7.other_ref, bf16[128,256]{1,0:T(8,128)(2,1)S(1)} %slice.36.left_ref, bf16[128,256]{1,0:T(8,128)(2,1)S(1)} %slice.37.right_ref, ...), custom_call_target="tpu_custom_call" | custom-call | tf_op jit(solution)/shard_map/pallas_call | solution.py:527
  179.3 9.9 %shard_map.138 = (f32[640,2048]{1,0:T(8,128)}, bf16[2048,256]{1,0:T(8,128)(2,1)S(1)}, bf16[96,2048]{1,0:T(8,128)(2,1)S(1)}) custom-call(s32[1]{0:T(128)} %bitcast.d_ref, s32[1]{0:T(128)} %bitcast.2.p_ref, bf16[640,1536]{1,0:T(8,128)(2,1)S(1)} %copy-done.3, bf16[16,896,128]{2,1,0:T(8,128)(2,1)S(1)} %bitcast.23, ...), custom_call_target="tpu_custom_call" | custom-call | flops 10000000000 | bytes 30000000 | tf_op jit(solution)/shard_map/pallas_call | solution.py:411
  189.1 2.5 %copy-done.1 = f32[640,2048]{1,0:T(8,128)S(1)} copy-done((f32[640,2048]{1,0:T(8,128)S(1)}, f32[640,2048]{1,0:T(8,128)}, u32[]{:S(2)}) %copy-start.1) | copy-done | bytes 5242904
  191.6 4.3 %shard_map.139 = bf16[640,96]{1,0:T(8,128)(2,1)S(1)} custom-call(bf16[768,256]{1,0:T(8,128)(2,1)S(1)} %shard_map.137.dz_ref.dz0_ref, f32[640,2048]{1,0:T(8,128)S(1)} %copy-done.1, bf16[2048,256]{1,0:T(8,128)(2,1)S(1)} %get-tuple-element.71.w2_ref, bf16[96,2048]{1,0:T(8,128)(2,1)S(1)} %get-tuple-element.72.w1_ref), custom_call_target="tpu_custom_call" | custom-call | tf_op jit(solution)/shard_map/pallas_call | solution.py:463
  (115 shorter events, 34.0 us)
Async XLA Ops:
  7.2 112.7 %all-gather.3.cloned.1.call-start = ((), (), s32[]{:S(2)}) async-start(), calls=%async_computation.6 | async-start | bytes 3899392 | tf_op jit(solution)/shard_map/all_gather | solution.py:590
  8.6 1.5 copy-start.2
  14.8 4.2 %copy-start.16 = (bf16[1536,128]{1,0:T(8,128)(2,1)S(1)}, bf16[1536,128]{1,0:T(8,128)(2,1)}, u32[]{:S(2)}) copy-start(bf16[1536,128]{1,0:T(8,128)(2,1)} %w1_ref.2) | copy-start | bytes 1179652
  14.8 4.3 %copy-start.14 = (bf16[128,256]{1,0:T(8,128)(2,1)S(1)}, bf16[128,256]{1,0:T(8,128)(2,1)}, u32[]{:S(2)}) copy-start(bf16[128,256]{1,0:T(8,128)(2,1)} %w2_ref.3) | copy-start | bytes 196612
  14.8 13.4 %copy-start = (bf16[256,4096]{1,0:T(8,128)(2,1)S(1)}, bf16[256,4096]{1,0:T(8,128)(2,1)}, u32[]{:S(2)}) copy-start(bf16[256,4096]{1,0:T(8,128)(2,1)} %protos_ref.1) | copy-start | bytes 6291460
  19.8 24.5 %all-to-all-start = ((bf16[16,48,256]{2,1,0:T(8,128)(2,1)}), bf16[16,48,256]{2,1,0:T(8,128)(2,1)S(1)}, u32[]{:S(2)}, u32[]{:S(2)}) async-start(bf16[16,48,256]{2,1,0:T(8,128)(2,1)} %get-tuple-element.45), calls=%async_computation | async-start | bytes 786432 | tf_op jit(solution)/shard_map/all_to_all | solution.py:582
  45.8 21.2 %copy-start.35 = (f32[48,1]{1,0:T(8,128)}, f32[48,1]{1,0:T(8,128)S(1)}, u32[]{:S(2)}) copy-start(f32[48,1]{1,0:T(8,128)S(1)} %get-tuple-element.58.zinv_ref) | copy-start | bytes 580
  45.8 21.1 %all-to-all-start.1 = ((bf16[16,48,256]{2,1,0:T(8,128)(2,1)}), bf16[16,48,256]{2,1,0:T(8,128)(2,1)}, u32[]{:S(2)}, u32[]{:S(2)}) async-start(bf16[16,48,256]{2,1,0:T(8,128)(2,1)} %get-tuple-element.46), calls=%async_computation.1 | async-start | bytes 786432 | tf_op jit(solution)/shard_map/all_to_all | solution.py:603
  67.0 1.9 copy-start.7
  67.0 1.9 collective-permute-start
  67.2 12.0 %copy-start.5 = (bf16[256,2048]{1,0:T(8,128)(2,1)}, bf16[256,2048]{1,0:T(8,128)(2,1)S(1)}, u32[]{:S(2)}) copy-start(bf16[256,2048]{1,0:T(8,128)(2,1)S(1)} %fusion.3.pnb_ref) | copy-start | bytes 3145732
  71.4 1.3 copy-start.26
  73.5 16.8 %all-to-all-start.2 = ((f32[32,2,128]{2,1,0:T(2,128)}), f32[32,2,128]{2,1,0:T(2,128)}, u32[]{:S(2)}, u32[]{:S(2)}) async-start(f32[32,2,128]{2,1,0:T(2,128)} %copy-done.18), calls=%async_computation.2 | async-start | bytes 65536 | tf_op jit(solution)/shard_map/all_to_all | solution.py:619
  88.0 2.4 %copy-start.25 = (bf16[1280,2048]{1,0:T(8,128)(2,1)}, bf16[1280,2048]{1,0:T(8,128)(2,1)S(1)}, u32[]{:S(2)}) copy-start(bf16[1280,2048]{1,0:T(8,128)(2,1)S(1)} %get-tuple-element.84) | copy-start | bytes 15728644
  90.4 1.6 copy-start.27
  94.0 17.0 %all-to-all-start.3 = ((f32[32,12,128]{2,1,0:T(8,128)}), f32[32,12,128]{2,1,0:T(8,128)S(1)}, u32[]{:S(2)}, u32[]{:S(2)}) async-start(f32[32,12,128]{2,1,0:T(8,128)} %shard_map.133), calls=%async_computation.3 | async-start | bytes 524288 | tf_op jit(solution)/shard_map/all_to_all | solution.py:629
  102.2 15.7 %collective-permute-start.1 = (f32[640,256]{1,0:T(8,128)}, f32[640,256]{1,0:T(8,128)}, u32[]{:S(2)}, u32[]{:S(2)}) collective-permute-start(f32[640,256]{1,0:T(8,128)} %get-tuple-element.102), channel_id=1, source_target_pairs={{0,16},{16,0},{1,17},{17,1},{2,18},{18,2},{3,19},{19,3},{4,20},{20... | collective-permute-start | bytes 1966088 | tf_op jit(solution)/shard_map/ppermute | solution.py:28
  113.9 1.6 copy-start.28
  115.5 2.4 %copy-start.8 = (f32[640,256]{1,0:T(8,128)S(1)}, f32[640,256]{1,0:T(8,128)}, u32[]{:S(2)}) copy-start(f32[640,256]{1,0:T(8,128)} %get-tuple-element.103.a0_ref) | copy-start | bytes 1966084
  116.4 1.5 collective-permute-start.2
  116.5 3.4 %collective-permute-start.3 = (f32[640,1]{1,0:T(8,128)S(1)}, f32[640,1]{1,0:T(8,128)}, u32[]{:S(2)}, u32[]{:S(2)}) collective-permute-start(f32[640,1]{1,0:T(8,128)S(1)} %get-tuple-element.65), channel_id=1, source_target_pairs={{0,16},{16,0},{1,17},{17,1},{2,18},{18,2},{3,19},{19,3},{4,20},{20... | collective-permute-start | bytes 7688 | tf_op jit(solution)/shard_map/ppermute | solution.py:28
  119.9 59.4 %collective-permute-start.4 = (bf16[16,896,128]{2,1,0:T(8,128)(2,1)}, bf16[16,896,128]{2,1,0:T(8,128)(2,1)}, u32[]{:S(2)}, u32[]{:S(2)}) collective-permute-start(bf16[16,896,128]{2,1,0:T(8,128)(2,1)} %bitcast.22), channel_id=1, source_target_pairs={{0,16},{16,0},{1,17},{17,1},{2,18},{18,2},{3,19},{19,3},{4,20},{20... | collective-permute-start | bytes 11010056 | tf_op jit(solution)/shard_map/ppermute | solution.py:28
  120.0 44.1 %collective-permute-start.5 = (bf16[640,1536]{1,0:T(8,128)(2,1)}, bf16[640,1536]{1,0:T(8,128)(2,1)}, u32[]{:S(2)}, u32[]{:S(2)}) collective-permute-start(bf16[640,1536]{1,0:T(8,128)(2,1)} %f0_ref.2), channel_id=1, source_target_pairs={{0,16},{16,0},{1,17},{17,1},{2,18},{18,2},{3,19},{19,3},{4,20},{20... | collective-permute-start | bytes 5898248 | tf_op jit(solution)/shard_map/ppermute | solution.py:28
  120.4 18.6 %all-to-all-start.4 = ((bf16[16,56,256]{2,1,0:T(8,128)(2,1)}), bf16[16,56,256]{2,1,0:T(8,128)(2,1)}, u32[]{:S(2)}, u32[]{:S(2)}) async-start(bf16[16,56,256]{2,1,0:T(8,128)(2,1)} %copy-done.9), calls=%async_computation.4 | async-start | bytes 917504 | tf_op jit(solution)/shard_map/all_to_all | solution.py:644
  133.5 37.3 %collective-permute-start.7 = (f32[256,2048]{1,0:T(8,128)}, f32[256,2048]{1,0:T(8,128)}, u32[]{:S(2)}, u32[]{:S(2)}) collective-permute-start(f32[256,2048]{1,0:T(8,128)} %fusion.4.own_ref), channel_id=1, source_target_pairs={{0,16},{16,0},{1,17},{17,1},{2,18},{18,2},{3,19},{19,3},{4,20},{20... | collective-permute-start | bytes 6291464 | tf_op jit(solution)/shard_map/ppermute | solution.py:28
  143.9 17.4 %all-to-all-start.5 = ((bf16[16,48,256]{2,1,0:T(8,128)(2,1)}), bf16[16,48,256]{2,1,0:T(8,128)(2,1)}, u32[]{:S(2)}, u32[]{:S(2)}) async-start(bf16[16,48,256]{2,1,0:T(8,128)(2,1)} %copy-done.10), calls=%async_computation.5 | async-start | bytes 786432 | tf_op jit(solution)/shard_map/all_to_all | solution.py:661
  148.3 22.5 %collective-permute-start.8 = (bf16[256,2048]{1,0:T(8,128)(2,1)S(1)}, bf16[256,2048]{1,0:T(8,128)(2,1)}, u32[]{:S(2)}, u32[]{:S(2)}) collective-permute-start(bf16[256,2048]{1,0:T(8,128)(2,1)S(1)} %get-tuple-element.85.lown_ref), channel_id=1, source_target_pairs={{0,16},{16,0},{1,17},{17,1},{2,18},{18,2},{3,19},{19,3},{4,20},{20... | collective-permute-start | bytes 3145736 | tf_op jit(solution)/shard_map/ppermute | solution.py:28
  161.3 2.8 %copy-start.3 = (bf16[640,1536]{1,0:T(8,128)(2,1)S(1)}, bf16[640,1536]{1,0:T(8,128)(2,1)}, u32[]{:S(2)}) copy-start(bf16[640,1536]{1,0:T(8,128)(2,1)} %f0_ref.2) | copy-start | bytes 5898244
  161.3 2.8 %copy-start.17 = (bf16[1536,128]{1,0:T(8,128)(2,1)S(1)}, bf16[1536,128]{1,0:T(8,128)(2,1)}, u32[]{:S(2)}) copy-start(bf16[1536,128]{1,0:T(8,128)(2,1)} %w1_ref.2) | copy-start | bytes 1179652
  164.1 3.0 %collective-permute-start.6 = (bf16[768,256]{1,0:T(8,128)(2,1)S(1)}, bf16[768,256]{1,0:T(8,128)(2,1)S(1)}, u32[]{:S(2)}, u32[]{:S(2)}) collective-permute-start(bf16[768,256]{1,0:T(8,128)(2,1)S(1)} %shard_map.137.dz_ref.dz0_ref), channel_id=1, source_target_pairs={{0,16},{16,0},{1,17},{17,1},{2,18},{18,2},{3,19},{19,3},{4,20},{20... | collective-permute-start | bytes 1179656 | tf_op jit(solution)/shard_map/ppermute | solution.py:28
  170.8 8.5 %copy-start.21 = (bf16[14336,128]{1,0:T(8,128)(2,1)S(1)}, bf16[14336,128]{1,0:T(8,128)(2,1)}, u32[]{:S(2)}) copy-start(bf16[14336,128]{1,0:T(8,128)(2,1)} %all-gather.3.cloned.1.call-done) | copy-start | bytes 11010052
  189.1 2.5 %copy-start.1 = (f32[640,2048]{1,0:T(8,128)S(1)}, f32[640,2048]{1,0:T(8,128)}, u32[]{:S(2)}) copy-start(f32[640,2048]{1,0:T(8,128)} %get-tuple-element.70.slope_ref) | copy-start | bytes 15728644
  (21 other events, 18.5 us)
Sparse Core Ops, SparseCore 0:
  20.0 80.9 all-gather.2

commit v4 on v3

--- a/solution.py
+++ b/solution.py
@@ -175,7 +175,7 @@
     return (grad_features, grad_w1, grad_w2, grad_protos)
 
 
-def params(mib=40):
+def params(mib=56):
     return pltpu.CompilerParams(vmem_limit_bytes=mib * 1024 * 1024)
 
 
@@ -183,15 +183,24 @@
     return jax.ShapeDtypeStruct(dims, dtype)
 
 
-def call(kernel, outs, scalars, *args, us=1):
+def kernel_name(kernel):
+    return getattr(kernel, "func", kernel).__name__
+
+
+def block(dims):
+    return pl.BlockSpec(dims, lambda i: (0,) * len(dims))
+
+
+def call(kernel, outs, scalars, *args, us=1, mib=56):
     smem = [jnp.asarray(s, jnp.int32).reshape(1) for s in scalars]
     return pl.pallas_call(
         kernel,
+        grid=(1,),
         out_shape=outs,
-        in_specs=[pl.BlockSpec(memory_space=pltpu.SMEM)] * len(smem)
-        + [pl.BlockSpec(memory_space=pltpu.VMEM)] * len(args),
-        out_specs=jax.tree.map(lambda _: pl.BlockSpec(memory_space=pltpu.VMEM), outs),
-        compiler_params=params(),
+        in_specs=[pl.BlockSpec(memory_space=pltpu.SMEM)] * len(smem) + [block(x.shape) for x in args],
+        out_specs=jax.tree.map(lambda x: block(x.shape), outs),
+        compiler_params=params(mib),
+        name=kernel_name(kernel),
         cost_estimate=pl.CostEstimate(flops=us * 10**9, bytes_accessed=us * 10**6, transcendentals=0),
     )(*smem, *args)
 
@@ -210,12 +219,19 @@
     return jnp.sum(jnp.where(down == along, row, jnp.zeros_like(row)), axis=1, keepdims=True)
 
 
-def head_kernel(d_ref, f_ref, w1_ref, w2_ref, tf_ref, tw1_ref, tw2_ref, im_ref, view_ref, parts_ref, back_ref, vs_ref):
+def head_kernel(d_ref, *refs):
+    sources, im_ref, view_ref = refs[:6], refs[6], refs[7]
+    parts_ref, back_ref, vs_ref = refs[8:11]
+    held, sems = refs[11:17], refs[17]
+    copies = [pltpu.make_async_copy(a, b, sems.at[k]) for k, (a, b) in enumerate(zip(sources, held))]
+    for copy in copies:
+        copy.start()
+    f_ref, w1_ref, w2_ref, tf_ref, tw1_ref, tw2_ref = held
     rows, teach = f_ref.shape[0], tf_ref.shape[0]
     n = parts_ref.shape[0]
     img = teach // 2
     per = rows // img
-    im = (im_ref[...] - d_ref[0] * img).astype(F32)
+    im = (im_ref[...].reshape(1, rows) - d_ref[0] * img).astype(F32)
     down, along = grids((rows, rows))
     imc = to_col(im)
     same = im == imc
@@ -225,8 +241,11 @@
     row = (im * per + jnp.sum(after, axis=0, keepdims=True)).astype(jnp.int32)
     back_ref[...] = jnp.where(col == along, 1.0, 0.0).astype(BF16)
     hit = row == down
-    vs_ref[...] = jnp.sum(jnp.where(hit, view_ref[...].astype(F32), 0.0), axis=1, keepdims=True)
+    vs_ref[...] = jnp.sum(jnp.where(hit, view_ref[...].reshape(1, rows).astype(F32), 0.0), axis=1, keepdims=True)
     order = jnp.where(hit, 1.0, 0.0).astype(BF16)
+
+    for copy in copies:
+        copy.wait()
 
     def part(x, first, second):
         act = dot(x[...], first[...], ((1,), (0,)))
@@ -281,27 +300,43 @@
     msg_ref[...] = jnp.broadcast_to(fold(mass)[None], msg_ref.shape)
 
 
-def student_kernel(z_ref, pnb_ref, exb_ref, sums_ref, esum_ref):
+def student_kernel(z_ref, pnb_ref, exb_ref, own_ref, other_ref, esum_ref):
     step = pl.program_id(0)
     ex = jnp.exp(dot(z_ref[...], pnb_ref[...], ((1,), (0,))) * 10.0)
-    esum_ref[pl.ds(step, 1), :] = fold(jnp.sum(ex, axis=1, keepdims=True))
+    esum_ref[...] = jnp.sum(ex, axis=1, keepdims=True)
     exb = ex.astype(BF16)
     exb_ref[...] = exb
-    sums_ref[...] = dot(exb, pnb_ref[...], ((1,), (1,)))
+    sums = dot(exb, pnb_ref[...], ((1,), (1,)))
+
+    @pl.when(step < pl.num_programs(0) // 2)
+    def _():
+        own_ref[...] = sums
+
+    @pl.when(step >= pl.num_programs(0) // 2)
+    def _():
+        other_ref[...] = sums
 
 
 def student_sums(student, pnb):
     total, bot = student.shape
     cols = pnb.shape[1]
+    tile = total // 4
     return pl.pallas_call(
         student_kernel,
-        grid=(total // 128,),
-        out_shape=(shape((total, cols), BF16), shape((total, bot), F32), shape((total // 128, 128), F32)),
-        in_specs=[pl.BlockSpec((128, bot), lambda i: (i, 0)), pl.BlockSpec((bot, cols), lambda i: (0, 0))],
+        name="student_kernel",
+        grid=(4,),
+        out_shape=(
+            shape((total, cols), BF16),
+            shape((total // 2, bot), F32),
+            shape((total // 2, bot), F32),
+            shape((total, 1), F32),
+        ),
+        in_specs=[pl.BlockSpec((tile, bot), lambda i: (i, 0)), pl.BlockSpec((bot, cols), lambda i: (0, 0))],
         out_specs=(
-            pl.BlockSpec((128, cols), lambda i: (i, 0)),
-            pl.BlockSpec((128, bot), lambda i: (i, 0)),
-            pl.BlockSpec((total // 128, 128), lambda i: (0, 0)),
+            pl.BlockSpec((tile, cols), lambda i: (i, 0)),
+            pl.BlockSpec((tile, bot), lambda i: (jnp.minimum(i, 1), 0)),
+            pl.BlockSpec((tile, bot), lambda i: (jnp.maximum(i - 2, 0), 0)),
+            pl.BlockSpec((tile, 1), lambda i: (i, 0)),
         ),
         compiler_params=params(),
         cost_estimate=pl.CostEstimate(flops=5 * 10**9, bytes_accessed=10**7, transcendentals=0),
@@ -312,19 +347,22 @@
     mass = unfold(jnp.sum(got_ref[...], axis=0))
     _, mass = row_mass(kern_ref[...], mass)
     half = esum_ref.shape[0] // 2
-    esum = esum_ref[...]
-    turned = jnp.concatenate([esum[half:], esum[:half]], axis=0)
-    esum = jnp.where(d_ref[0] == 0, esum, turned)
-    msg_ref[...] = jnp.broadcast_to(jnp.concatenate([fold(mass), esum], axis=0)[None], msg_ref.shape)
+    own, other = to_row(esum_ref[:half]), to_row(esum_ref[half:])
+    first = d_ref[0] == 0
+    mass = to_row(mass)
+    mass = jnp.concatenate([mass, jnp.zeros((1, half - mass.shape[1]), F32)], axis=1)
+    n = msg_ref.shape[0] // 2
+    for k, row in enumerate((jnp.where(first, own, other), jnp.where(first, other, own))):
+        part = jnp.concatenate([mass, row], axis=0)
+        msg_ref[k * n : (k + 1) * n] = jnp.broadcast_to(part[None], (n,) + part.shape)
 
 
 def third_kernel(d_ref, got_ref, kern_ref, pnb_ref, esum_ref, last_ref, mine_ref, yours_ref):
     teach = kern_ref.shape[0]
     got = jnp.sum(got_ref[...], axis=0)
-    top = teach // 128
-    esum_ref[...] = got[top:]
+    esum_ref[...] = to_col(got[1:])
     kern = kern_ref[...]
-    scale, mass = row_mass(kern, unfold(got[:top]))
+    scale, mass = row_mass(kern, to_col(got[:1, :teach]))
     last = (kern * scale).astype(BF16)
     last_ref[...] = last
     sums = dot(last, pnb_ref[...], ((1,), (1,)))
@@ -335,10 +373,10 @@
     yours_ref[...] = jnp.where(first, sums[half:], sums[:half])
 
 
-def message_kernel(a0_ref, a1_ref, b0_ref, b1_ref, out_ref):
+def message_kernel(sums_ref, b0_ref, b1_ref, out_ref):
     n = out_ref.shape[0]
-    rows, bot = a0_ref.shape
-    sums = (a0_ref[...] + a1_ref[...]).reshape(n, rows // n, bot)
+    rows, bot = sums_ref.shape
+    sums = sums_ref[...].astype(F32).reshape(n, rows // n, bot)
     both = b0_ref[...] + b1_ref[...]
     mass = both[:, bot:]
     high = mass.astype(BF16).astype(F32)
@@ -410,6 +448,7 @@
     whole = lambda k, d, p: (0, 0)
     return pl.pallas_call(
         slopes_kernel,
+        name="slopes_kernel",
         grid_spec=pltpu.PrefetchScalarGridSpec(
             num_scalar_prefetch=2,
             grid=(n // 2,),
@@ -425,7 +464,7 @@
             ),
         ),
         out_shape=(shape((rows, n * hs), F32), shape((n * hs, 2 * hs), BF16), shape((width, n * hs), BF16)),
-        compiler_params=params(),
+        compiler_params=params(20),
         cost_estimate=pl.CostEstimate(flops=10**10, bytes_accessed=3 * 10**7, transcendentals=0),
     )(d.reshape(1), p.reshape(1), features, own, other)
 
@@ -449,7 +488,7 @@
 
     pre = dot(dz_ref[...], w2_ref[...], ((1,), (1,)))
     dhid = (pre * slope_ref[...]).astype(BF16)
-    acc_ref[...] += dot(dhid, w1_ref[...], ((1,), (1,)))
+    acc_ref[...] += dot(w1_ref[...], dhid, ((1,), (1,)))
 
     @pl.when(step == pl.num_programs(0) - 1)
     def _():
@@ -459,20 +498,21 @@
 def feature_grads(dz, slope, w2, w1_block):
     rows, hidden = slope.shape
     width, bot = w1_block.shape[0], w2.shape[1]
-    step = bot
+    step = 2 * bot
     return pl.pallas_call(
         features_kernel,
+        name="features_kernel",
         grid=(hidden // step,),
-        out_shape=shape((rows, width), BF16),
+        out_shape=shape((width, rows), BF16),
         in_specs=[
             pl.BlockSpec((rows, bot), lambda k: (0, 0)),
             pl.BlockSpec((rows, step), lambda k: (0, k)),
             pl.BlockSpec((step, bot), lambda k: (k, 0)),
             pl.BlockSpec((width, step), lambda k: (0, k)),
         ],
-        out_specs=pl.BlockSpec((rows, width), lambda k: (0, 0)),
-        scratch_shapes=[pltpu.VMEM((rows, width), F32)],
-        compiler_params=params(),
+        out_specs=pl.BlockSpec((width, rows), lambda k: (0, 0)),
+        scratch_shapes=[pltpu.VMEM((width, rows), F32)],
+        compiler_params=params(12),
     )(dz, slope, w2, w1_block)
 
 
@@ -488,18 +528,22 @@
     g2_ref[...] = g2[0] + g2[1]
 
 
-def protos_kernel(d_ref, protos_ref, own_ref, other_ref, left_ref, right_ref, lown_ref, lother_ref, out_ref):
+def protos_kernel(d_ref, protos_ref, own_ref, other_ref, left_ref, right_ref, lown_ref, lother_ref, out_ref, turned_ref):
     half = pl.program_id(0) // (pl.num_programs(0) // 2)
     mine = half == d_ref[0]
-    first = d_ref[0] == 0
-    a, b = left_ref[...].astype(F32), right_ref[...].astype(F32)
-    scaled = jnp.concatenate([jnp.where(first, a, b), jnp.where(first, b, a)], axis=0).astype(BF16)
+
+    @pl.when(pl.program_id(0) == 0)
+    def _():
+        first = d_ref[0] == 0
+        a, b = left_ref[...].astype(F32), right_ref[...].astype(F32)
+        scaled = jnp.concatenate([jnp.where(first, a, b), jnp.where(first, b, a)], axis=0)
+        turned_ref[...] = scaled.T.astype(BF16)
 
     def finish(dpn_ref, last_ref):
         mat = protos_ref[...].astype(F32)
         inv = lax.rsqrt(jnp.sum(mat * mat, axis=0, keepdims=True) + 1e-06)
         pn = mat * inv
-        dpn = dpn_ref[...] - dot(scaled, last_ref[...], ((0,), (0,)))
+        dpn = dpn_ref[...] - dot(turned_ref[...], last_ref[...], ((1,), (0,)))
         out_ref[...] = inv * (dpn - pn * jnp.sum(pn * dpn, axis=0, keepdims=True))
 
     @pl.when(mine)
@@ -513,10 +557,11 @@
 
 def protos_grads(d, protos, own, other, mine, yours, lown, lother):
     bot, wide = protos.shape
-    tile = 512
+    tile = 1024
     steps = wide // tile
     halfsteps = steps // 2
     teach = lown.shape[0]
+    after = mine.shape[0] // (teach // 2) - 1
 
     def place(i, d_ref, same):
         at = d_ref[0] if same else 1 - d_ref[0]
@@ -526,6 +571,7 @@
     other_map = lambda i, d_ref: place(i, d_ref, False)
     return pl.pallas_call(
         protos_kernel,
+        name="protos_kernel",
         grid_spec=pltpu.PrefetchScalarGridSpec(
             num_scalar_prefetch=1,
             grid=(steps,),
@@ -533,15 +579,16 @@
                 pl.BlockSpec((bot, tile), lambda i, d_ref: (0, i)),
                 pl.BlockSpec((bot, tile), own_map),
                 pl.BlockSpec((bot, tile), other_map),
-                pl.BlockSpec((teach // 2, bot), lambda i, d_ref: (0, 0)),
-                pl.BlockSpec((teach // 2, bot), lambda i, d_ref: (0, 0)),
+                pl.BlockSpec((teach // 2, bot), lambda i, d_ref: (after, 0)),
+                pl.BlockSpec((teach // 2, bot), lambda i, d_ref: (after, 0)),
                 pl.BlockSpec((teach, tile), own_map),
                 pl.BlockSpec((teach, tile), other_map),
             ],
             out_specs=pl.BlockSpec((bot, tile), lambda i, d_ref: (0, i)),
+            scratch_shapes=[pltpu.VMEM((bot, teach), BF16)],
         ),
         out_shape=jax.ShapeDtypeStruct((bot, wide), F32),
-        compiler_params=pltpu.CompilerParams(vmem_limit_bytes=32 * 1024 * 1024),
+        compiler_params=params(16),
     )(d.reshape(1), protos, own, other, mine, yours, lown, lother)
 
 
@@ -570,37 +617,30 @@
     everyone = nd * n
     factor = 10.0 / (9 * teach * nd)
 
+    w2_half = lax.dynamic_slice_in_dim(head_w2, d * (hs // 2), hs // 2, 0)
+    weights = jnp.concatenate(
+        [lax.dynamic_slice_in_dim(head_w1, d * (wide // 2), wide // 2, 0), w2_half[:, :hs], w2_half[:, hs:]], axis=0
+    )
+    weights, head_w1_late = tied(weights, head_w1)
+    weights = lax.all_gather(weights, "proto")
     feat_other = swap(features, "dp", 1)
-    parts, back, view = call(
+    heads = (features, head_w1_late, head_w2, teacher_features, teacher_w1, teacher_w2)
+    parts, back, view = pl.pallas_call(
         head_kernel,
-        (shape((n, sr + tr, bot), BF16), shape((rows, rows), BF16), shape((rows, 1), F32)),
-        [d],
-        features, head_w1, head_w2, teacher_features, teacher_w1, teacher_w2,
-        crop_image.reshape(1, -1), crop_view.reshape(1, -1),
-        us=4,
-    )
+        grid=(1,),
+        out_shape=(shape((n, sr + tr, bot), BF16), shape((rows, rows), BF16), shape((rows, 1), F32)),
+        in_specs=[pl.BlockSpec(memory_space=pltpu.SMEM)]
+        + [pl.BlockSpec(memory_space=pl.ANY)] * 6
+        + [block((rows,))] * 2,
+        out_specs=(block((n, sr + tr, bot)), block((rows, rows)), block((rows, 1))),
+        scratch_shapes=[pltpu.VMEM(x.shape, x.dtype) for x in heads] + [pltpu.SemaphoreType.DMA((6,))],
+        compiler_params=params(),
+        name="head_kernel",
+    )(d.reshape(1), *heads, crop_image, crop_view)
     parts_got = lax.all_to_all(parts, "proto", 0, 0)
-    w1_late, w2_late, protos_late, tprotos_late, feat_late, _ = tied(
-        head_w1, head_w2, protos, teacher_protos, features, parts
-    )
-    w2_half = lax.dynamic_slice_in_dim(w2_late, d * (hs // 2), hs // 2, 0)
-    weights = jnp.concatenate(
-        [lax.dynamic_slice_in_dim(w1_late, d * (wide // 2), wide // 2, 0), w2_half[:, :hs], w2_half[:, hs:]], axis=0
-    )
-    weights = lax.all_gather(weights, "proto")
-    cols = protos.shape[1] // nd
-    pnb = unit_cols(lax.dynamic_slice_in_dim(protos_late, d * cols, cols, 1))[0].astype(BF16)
-    tpnb = unit_cols(lax.dynamic_slice_in_dim(tprotos_late, d * cols, cols, 1))[0].astype(BF16)
-    view_other = swap(view, "dp", 1)
-
-    got, zn, zinv = call(
-        rows_kernel,
-        (shape((n, sr + tr, bot), BF16), shape((sr + tr, bot), F32), shape((sr + tr, 1), F32)),
-        [],
-        parts_got,
-    )
-    feat_late, feat_other_late, w1_late, _ = tied(feat_late, feat_other, w1_late, got)
-    got = lax.all_to_all(got, "proto", 0, 0)
+    w1_late, protos_late, tprotos_late, feat_late, feat_other_late, _ = tied(
+        head_w1, protos, teacher_protos, features, feat_other, parts
+    )
     h0, h1, s0, s1 = call(
         hidden_kernel,
         (shape((hs, rows), BF16),) * 2 + (shape((hs, rows), F32),) * 2,
@@ -608,6 +648,18 @@
         feat_late, feat_other_late, w1_late,
         us=4,
     )
+    cols = protos.shape[1] // nd
+    pnb = unit_cols(lax.dynamic_slice_in_dim(protos_late, d * cols, cols, 1))[0].astype(BF16)
+    tpnb = unit_cols(lax.dynamic_slice_in_dim(tprotos_late, d * cols, cols, 1))[0].astype(BF16)
+    parts_got, h0, h1, s0, s1, pnb, tpnb = tied(parts_got, h0, h1, s0, s1, pnb, tpnb)
+
+    got, zn, zinv = call(
+        rows_kernel,
+        (shape((n, sr + tr, bot), BF16), shape((sr + tr, bot), F32), shape((sr + tr, 1), F32)),
+        [],
+        parts_got,
+    )
+    got = lax.all_to_all(got, "proto", 0, 0)
     got_other = swap(got, "dp", 1)
     kern, msg, student = call(
         kern_kernel,
@@ -618,19 +670,22 @@
     )
     msg_got = lax.all_to_all(msg, ALL, 0, 0)
     student, _ = tied(student, msg)
-    exb, sums, esum = student_sums(student, pnb)
-    sums_other = swap(sums[rows:], "dp", 1)
+    exb, sums, sums_other, esum = student_sums(student, pnb)
     msg = call(
         second_kernel,
-        shape((everyone, nd * (teach + rows) // 128, 128), F32),
+        shape((everyone, 2, rows), F32),
         [d],
         msg_got, kern, esum,
     )
     msg_got = lax.all_to_all(msg, ALL, 0, 0)
+    sums, sums_other, _ = tied(sums, sums_other, msg)
+    sums_other = swap(sums_other, "dp", 1)
+    sums = (sums + sums_other).astype(BF16)
+    msg_got, sums = tied(msg_got, sums)
     esum, last, mine, yours = call(
         third_kernel,
         (
-            shape((nd * rows // 128, 128), F32),
+            shape((rows, 1), F32),
             shape((nd * teach, cols), BF16),
             shape((teach, bot + 128), F32),
             shape((teach, bot + 128), F32),
@@ -640,18 +695,19 @@
         us=2,
     )
     yours = swap(yours, "dp", 1)
-    msg = call(message_kernel, shape((n, sr + 2 * tr, bot), BF16), [], sums[:rows], sums_other, mine, yours)
+    msg = call(message_kernel, shape((n, sr + 2 * tr, bot), BF16), [], sums, mine, yours)
     msg_got = lax.all_to_all(msg, "proto", 0, 0)
 
-    esum, view_late, view_other, student, exb, last, weights, _ = tied(
-        esum, view, view_other, student, exb, last, weights, msg
-    )
-    esum = esum.reshape(nd, rows, 1)
-    esum = jnp.concatenate([jnp.where(d == 0, esum[0], esum[1]), jnp.where(d == 0, esum[1], esum[0])], axis=0)
-    count = jnp.where(jnp.concatenate([view_late, view_other], axis=0) == 2, 2.0, 1.0)
-    crop_scale = count * factor / esum
+    esum, view_late, weights, last, _ = tied(esum, view, weights, last, msg)
+    weights_other, last_other = swap(weights, "dp", 1), swap(last, "dp", 1)
+    crop_scale = jnp.where(view_late == 2, 2.0, 1.0) * factor / esum
+    scale_other = swap(crop_scale, "dp", 1)
     my_view = lax.dynamic_slice_in_dim(view_late, p * sr, sr, 0)
     my_scale = lax.dynamic_slice_in_dim(crop_scale, p * sr, sr, 0)
+    left = (student.astype(F32) * jnp.concatenate([crop_scale, scale_other], axis=0)).astype(BF16)
+    dpn = dot(left, exb, ((0,), (0,)))
+    msg_got, dpn = tied(msg_got, dpn)
+    dpn_other = swap(dpn, "dp", 1)
     dz = call(
         functools.partial(bottleneck_kernel, factor),
         shape((n, sr + tr, bot), BF16),
@@ -659,22 +715,21 @@
         msg_got, zn, zinv, my_view, my_scale,
     )
     got = lax.all_to_all(dz, "proto", 0, 0)
-    left = (student.astype(F32) * crop_scale).astype(BF16)
-    dpn = dot(left, exb, ((0,), (0,)))
-    dpn_other, last_other = swap(dpn, "dp", 1), swap(last, "dp", 1)
-    weights_other = swap(weights, "dp", 1)
-    slope, w2_all, w1_block = slopes_of(d, p, features, weights, weights_other, wide // n)
-
-    dz = call(unsort_kernel, shape((rows + teach, bot), BF16), [], got, back)
+    weights, feat_late, _ = tied(weights, features, dz)
+    slope, w2_all, w1_block = slopes_of(d, p, feat_late, weights, weights_other, wide // n)
+    got, slope, w2_all, w1_block = tied(got, slope, w2_all, w1_block)
+
+    dz = call(unsort_kernel, shape((rows + teach, bot), BF16), [], got, back, mib=8)
     dz_other = swap(dz, "dp", 1)
-    grad_features = feature_grads(dz, slope, w2_all, w1_block)
+    grad_features = feature_grads(dz, slope, w2_all, w1_block).T
     grad_w1, grad_w2 = call(
         weights_kernel,
         (shape(head_w1.shape, F32), shape(head_w2.shape, F32)),
         [],
         features, feat_other, dz, dz_other, h0, h1, s0, s1, head_w2,
-    )
-    grad_protos = protos_grads(d, protos, dpn, dpn_other, dz[rows:], dz_other[rows:], last, last_other)
+        mib=16,
+    )
+    grad_protos = protos_grads(d, protos, dpn, dpn_other, dz, dz_other, last, last_other)
     return (grad_features, grad_w1, grad_w2, grad_protos)
 
 
@@ -682,6 +737,7 @@
     n = lax.axis_size("proto")
     slot = (features.shape[0] // n, teacher_features.shape[0] // n)
     paired = lax.axis_size("dp") == 2 and n % 2 == 0 and slot[0] % 8 == 0 and slot[1] % 8 == 0
+    paired = paired and features.shape[0] % teacher_features.shape[0] == 0
     return (paired_body if paired else general_body)(features, teacher_features, *rest)
 
 

time: 206 us -> 175 us (0.85)
  waiting for transfers between devices: 55.6 us -> 27 us
  blocking collectives: 0 us -> 21.5 us
  local copies, waits for them, and re-layouts: 36.7 us -> 15.4 us
  Pallas kernels: 48.6 us -> 57.4 us
  starting transfers between devices: 34.3 us -> 26.2 us
  other arithmetic: 8.36 us -> 5.87 us
    all_to_all x0 -> x1, blocking collectives: none -> 21.5 us  [paired_body(): got = lax.all_to_all(got, 'proto', 0, 0)]
    unnamed x78 -> x46, local copies, waits for them, and re-layouts: 31 us -> 12.3 us
    all_to_all x1 -> x0, waiting for transfers between devices: 14.5 us -> none  [paired_body(): got = lax.all_to_all(got, 'proto', 0, 0)]
    all_to_all x1, waiting for transfers between devices: 12.9 us -> 0.01 us  [paired_body(): got = lax.all_to_all(dz, 'proto', 0, 0)]
    pallas_call x14, Pallas kernels: 48.6 us -> 57.4 us  [the longest x9 26.3 us: call(): pl.pallas_call(kernel, grid=(1,), out_shape=outs, in_specs=[pl.BlockSpec(...]
    all_to_all x1, waiting for transfers between devices: 14.5 us -> 7.53 us  [paired_body(): parts_got = lax.all_to_all(parts, 'proto', 0, 0)]
    all_to_all x1 -> x0, starting transfers between devices: 4.21 us -> none  [paired_body(): got = lax.all_to_all(got, 'proto', 0, 0)]
    ppermute x9, waiting for transfers between devices: 2.64 us -> 5.91 us  [swap(): return lax.ppermute(value, axis, [(i, i ^ step) for i in range(count)])]
  transfers between devices with their start and end apart: 16 -> 15, of which waited for: 7 -> 7; matrix products, arithmetic and copies ran while one was open for 9% -> 8% of each run, Pallas kernels for 15% -> 27%
where the time goes in v4:
time: 175 us; the launch traced here: 173 us
  Pallas kernels  57.4 us (33%)
  waiting for transfers between devices  27 us (15%)
  starting transfers between devices  26.2 us (15%)
  blocking collectives  21.5 us (12%)
  local copies, waits for them, and re-layouts  15.4 us (9%)
  between operations  14.3 us (8%)
  other arithmetic  5.87 us (3%)
  matrix products  5.66 us (3%)
    pallas_call x9, Pallas kernels, call(): pl.pallas_call(kernel, grid=(1,), out_shape=outs, in_specs=[pl.BlockSpec(...  26.3 us
    all_to_all x1, blocking collectives, paired_body(): got = lax.all_to_all(got, 'proto', 0, 0)  21.5 us
    unnamed x46, local copies, waits for them, and re-layouts  12.3 us
    all_to_all x2, starting transfers between devices, paired_body(): msg_got = lax.all_to_all(msg, ALL, 0, 0)  8.62 us
    pallas_call x1, Pallas kernels, slopes_of(): pl.pallas_call(slopes_kernel, name='slopes_kernel', grid_spec=pltpu.Prefe...  8.46 us
    all_to_all x2, waiting for transfers between devices, paired_body(): msg_got = lax.all_to_all(msg, ALL, 0, 0)  8.33 us
    all_to_all x1, starting transfers between devices, paired_body(): parts_got = lax.all_to_all(parts, 'proto', 0, 0)  7.9 us
    all_to_all x1, waiting for transfers between devices, paired_body(): parts_got = lax.all_to_all(parts, 'proto', 0, 0)  7.53 us
  transfers between devices with their start and end apart: 15, of which 7 were waited for; matrix products, arithmetic and copies ran while one was open for 8% of the time, Pallas kernels for 27%

profile of v4, /device:TPU:0, one launch (start us, length us, event | category | flops | bytes accessed | tf_op | source)
XLA Modules:
  0.0 173.4 jit_solution(12801780258203440967)
XLA Ops:
  10.2 5.6 %head_kernel.1 = (bf16[16,48,256]{2,1,0:T(8,128)(2,1)}, bf16[640,640]{1,0:T(8,128)(2,1)}, f32[640,1]{1,0:T(8,128)}) custom-call(s32[1]{0:T(128)} %bitcast.d_ref, bf16[640,1536]{1,0:T(8,128)(2,1)} %f0_ref.2, bf16[1536,128]{1,0:T(8,128)(2,1)} %w1_ref, bf16[128,256]{1,0:T(8,128)(2,1)} %w2_ref.1, bf16[128,1536]{1,0:T(8,128)(2,1)} %refs_3_.1, ...), custom_call_target="tpu_custom_call" | custom-call | tf_op jit(solution)/shard_map/head_kernel/pallas_call | solution.py:628
  15.8 7.9 %all-to-all-start = ((bf16[16,48,256]{2,1,0:T(8,128)(2,1)}), bf16[16,48,256]{2,1,0:T(8,128)(2,1)S(1)}, u32[]{:S(2)}, u32[]{:S(2)}) async-start(bf16[16,48,256]{2,1,0:T(8,128)(2,1)} %get-tuple-element.62), calls=%async_computation | async-start | bytes 786432 | tf_op jit(solution)/shard_map/all_to_all | solution.py:640
  23.7 1.7 fusion
  26.6 4.6 %hidden_kernel.1 = (bf16[128,640]{1,0:T(8,128)(2,1)}, bf16[128,640]{1,0:T(8,128)(2,1)}, f32[128,640]{1,0:T(8,128)}, f32[128,640]{1,0:T(8,128)}) custom-call(bf16[640,1536]{1,0:T(8,128)(2,1)} %f0_ref.2, bf16[640,1536]{1,0:T(8,128)(2,1)} %collective-permute-done.f1_ref, bf16[1536,128]{1,0:T(8,128)(2,1)} %w1_ref), custom_call_target="tpu_custom_call" | custom-call | flops 4000000000 | bytes 4000000 | tf_op jit(solution)/shard_map/hidden_kernel/pallas_call | solution.py:196
  32.6 7.5 %all-to-all-done.parts_ref = bf16[16,48,256]{2,1,0:T(8,128)(2,1)S(1)} async-done(((bf16[16,48,256]{2,1,0:T(8,128)(2,1)}), bf16[16,48,256]{2,1,0:T(8,128)(2,1)S(1)}, u32[]{:S(2)}, u32[]{:S(2)}) %all-to-all-start) | async-done | bytes 393248 | tf_op jit(solution)/shard_map/all_to_all | solution.py:640
  40.9 1.9 %rows_kernel.1 = (bf16[16,48,256]{2,1,0:T(8,128)(2,1)}, f32[48,256]{1,0:T(8,128)}, f32[48,1]{1,0:T(8,128)}) custom-call(bf16[16,48,256]{2,1,0:T(8,128)(2,1)} %copy-done.16), custom_call_target="tpu_custom_call" | custom-call | flops 1000000000 | bytes 1000000 | tf_op jit(solution)/shard_map/rows_kernel/pallas_call | solution.py:196
  42.8 21.5 %all_to_all.30.got_ref = bf16[16,48,256]{2,1,0:T(8,128)(2,1)S(1)} all-to-all(bf16[16,48,256]{2,1,0:T(8,128)(2,1)} %get-tuple-element.73), channel_id=1, replica_groups=mesh['dp'=2,'proto'=16] {'proto'}, dimensions={0} | all-to-all | bytes 786432 | tf_op jit(solution)/shard_map/all_to_all | solution.py:662
  64.3 1.7 collective-permute-done.1.other_ref
  66.8 3.7 %kern_kernel.1 = (f32[256,2048]{1,0:T(8,128)}, f32[32,2,128]{2,1,0:T(2,128)}, bf16[1280,256]{1,0:T(8,128)(2,1)}) custom-call(s32[1]{0:T(128)} %bitcast.d_ref, bf16[16,48,256]{2,1,0:T(8,128)(2,1)} %copy-done.17, bf16[16,48,256]{2,1,0:T(8,128)(2,1)} %copy-done.21, bf16[256,2048]{1,0:T(8,128)(2,1)} %fusion.3.tpnb_ref), custom_call_target="tpu_custom_call" | custom-call | flops 3000000000 | bytes 3000000 | tf_op jit(solution)/shard_map/kern_kernel/pallas_call | solution.py:196
  70.5 2.9 %all-to-all-start.2 = ((f32[32,2,128]{2,1,0:T(2,128)}), f32[32,2,128]{2,1,0:T(2,128)S(1)}, u32[]{:S(2)}, u32[]{:S(2)}) async-start(f32[32,2,128]{2,1,0:T(2,128)} %get-tuple-element.75), calls=%async_computation.2 | async-start | bytes 65536 | tf_op jit(solution)/shard_map/all_to_all | solution.py:671
  73.4 7.1 %student_kernel.1 = (bf16[1280,2048]{1,0:T(8,128)(2,1)}, f32[640,256]{1,0:T(8,128)}, f32[640,256]{1,0:T(8,128)}, f32[1280,1]{1,0:T(8,128)}) custom-call(bf16[1280,256]{1,0:T(8,128)(2,1)} %get-tuple-element.78.z_ref, bf16[256,2048]{1,0:T(8,128)(2,1)} %fusion.1.pnb_ref), custom_call_target="tpu_custom_call" | custom-call | flops 5000000000 | bytes 10000000 | tf_op jit(solution)/shard_map/student_kernel/pallas_call | solution.py:324
  81.5 3.1 %second_kernel.1 = f32[32,2,640]{2,1,0:T(2,128)} custom-call(s32[1]{0:T(128)} %bitcast.d_ref, f32[32,2,128]{2,1,0:T(2,128)} %copy-done.20, f32[256,2048]{1,0:T(8,128)} %get-tuple-element.76.kern_ref, f32[1280,1]{1,0:T(8,128)} %get-tuple-element.80.esum_ref), custom_call_target="tpu_custom_call" | custom-call | flops 1000000000 | bytes 1000000 | tf_op jit(solution)/shard_map/second_kernel/pallas_call | solution.py:196
  84.6 5.7 %all-to-all-start.3 = ((f32[32,2,640]{2,1,0:T(2,128)}), f32[32,2,640]{2,1,0:T(2,128)}, u32[]{:S(2)}, u32[]{:S(2)}) async-start(f32[32,2,640]{2,1,0:T(2,128)} %second_kernel.1), calls=%async_computation.3 | async-start | bytes 327680 | tf_op jit(solution)/shard_map/all_to_all | solution.py:680
  91.1 7.9 %all-to-all-done.3.got_ref = f32[32,2,640]{2,1,0:T(2,128)} async-done(((f32[32,2,640]{2,1,0:T(2,128)}), f32[32,2,640]{2,1,0:T(2,128)}, u32[]{:S(2)}, u32[]{:S(2)}) %all-to-all-start.3) | async-done | bytes 163872 | tf_op jit(solution)/shard_map/all_to_all | solution.py:680
  99.0 3.7 %third_kernel.1 = (f32[640,1]{1,0:T(8,128)}, bf16[256,2048]{1,0:T(8,128)(2,1)}, f32[128,384]{1,0:T(8,128)}, f32[128,384]{1,0:T(8,128)}) custom-call(s32[1]{0:T(128)} %bitcast.d_ref, f32[32,2,640]{2,1,0:T(2,128)} %all-to-all-done.3.got_ref, f32[256,2048]{1,0:T(8,128)} %get-tuple-element.76.kern_ref, bf16[256,2048]{1,0:T(8,128)(2,1)} %fusion.1.pnb_ref), custom_call_target="tpu_custom_call" | custom-call | flops 2000000000 | bytes 2000000 | tf_op jit(solution)/shard_map/third_kernel/pallas_call | solution.py:196
  102.8 1.6 collective-permute-done.3.b1_ref
  105.1 2.0 %message_kernel.1 = bf16[16,56,256]{2,1,0:T(8,128)(2,1)} custom-call(bf16[640,256]{1,0:T(8,128)(2,1)} %add_convert_fusion.sums_ref, f32[128,384]{1,0:T(8,128)} %get-tuple-element.87.b0_ref, f32[128,384]{1,0:T(8,128)} %copy-done.22), custom_call_target="tpu_custom_call" | custom-call | flops 1000000000 | bytes 1000000 | tf_op jit(solution)/shard_map/message_kernel/pallas_call | solution.py:196
  107.2 3.6 %all-to-all-start.4 = ((bf16[16,56,256]{2,1,0:T(8,128)(2,1)}), bf16[16,56,256]{2,1,0:T(8,128)(2,1)S(1)}, u32[]{:S(2)}, u32[]{:S(2)}) async-start(bf16[16,56,256]{2,1,0:T(8,128)(2,1)} %message_kernel.1), calls=%async_computation.4 | async-start | bytes 917504 | tf_op jit(solution)/shard_map/all_to_all | solution.py:699
  111.4 2.5 %collective-permute-done.4 = f32[640,1]{1,0:T(8,128)S(1)} collective-permute-done((f32[640,1]{1,0:T(8,128)S(1)}, f32[640,1]{1,0:T(8,128)S(1)}, u32[]{:S(2)}, u32[]{:S(2)}) %collective-permute-start.4) | collective-permute-done | bytes 2592 | tf_op jit(solution)/shard_map/ppermute | solution.py:28
  114.1 5.7 %fusion.4.own_ref = f32[256,2048]{1,0:T(8,128)} fusion(bf16[1280,2048]{1,0:T(8,128)(2,1)} %get-tuple-element.95, bf16[1280,256]{1,0:T(8,128)(2,1)} %get-tuple-element.78.z_ref, f32[1280]{0:T(1024)S(1)} %maximum_reduce_fusion), kind=kOutput, calls=%fused_computation.9 | convolution fusion | flops 1343160320 | bytes 8000512 | tf_op jit(solution)/shard_map/dot_general | solution.py:23
  119.8 5.3 %all-to-all-done.4.got_ref = bf16[16,56,256]{2,1,0:T(8,128)(2,1)S(1)} async-done(((bf16[16,56,256]{2,1,0:T(8,128)(2,1)}), bf16[16,56,256]{2,1,0:T(8,128)(2,1)S(1)}, u32[]{:S(2)}, u32[]{:S(2)}) %all-to-all-start.4) | async-done | bytes 458784 | tf_op jit(solution)/shard_map/all_to_all | solution.py:699
  126.8 2.1 %bottleneck_kernel.1 = bf16[16,48,256]{2,1,0:T(8,128)(2,1)} custom-call(bf16[16,56,256]{2,1,0:T(8,128)(2,1)} %copy-done.15, f32[48,256]{1,0:T(8,128)} %get-tuple-element.97.zn_ref, f32[48,1]{1,0:T(8,128)} %get-tuple-element.98.zinv_ref, f32[40,1]{1,0:T(8,128)} %constant_dynamic-slice_fusion.2.view_ref, f32[40,1]{1,0:T(8,128)} %constant_dynamic-slice_fusion.1.scale_ref), custom_call_target="tpu_custom_call" | custom-call | flops 1000000000 | bytes 1000000 | tf_op jit(solution)/shard_map/bottleneck_kernel/pallas_call | solution.py:196
  128.9 4.4 %all-to-all-start.5 = ((bf16[16,48,256]{2,1,0:T(8,128)(2,1)}), bf16[16,48,256]{2,1,0:T(8,128)(2,1)}, u32[]{:S(2)}, u32[]{:S(2)}) async-start(bf16[16,48,256]{2,1,0:T(8,128)(2,1)} %bottleneck_kernel.1), calls=%async_computation.5 | async-start | bytes 786432 | tf_op jit(solution)/shard_map/all_to_all | solution.py:717
  133.3 1.5 copy-done.1
  134.9 2.0 %copy-done.11 = bf16[14336,128]{1,0:T(8,128)(2,1)S(1)} copy-done((bf16[14336,128]{1,0:T(8,128)(2,1)S(1)}, bf16[14336,128]{1,0:T(8,128)(2,1)}, u32[]{:S(2)}) %copy-start.11) | copy-done | bytes 3670040
  136.9 8.5 %slopes_kernel.1 = (f32[640,2048]{1,0:T(8,128)S(1)}, bf16[2048,256]{1,0:T(8,128)(2,1)S(1)}, bf16[96,2048]{1,0:T(8,128)(2,1)S(1)}) custom-call(s32[1]{0:T(128)} %bitcast.d_ref, s32[1]{0:T(128)} %bitcast.2.p_ref, bf16[640,1536]{1,0:T(8,128)(2,1)S(1)} %copy-done.1, bf16[16,896,128]{2,1,0:T(8,128)(2,1)S(1)} %bitcast.6, ...), custom_call_target="tpu_custom_call" | custom-call | flops 10000000000 | bytes 30000000 | tf_op jit(solution)/shard_map/slopes_kernel/pallas_call | solution.py:449
  145.4 2.3 %copy-done.3 = f32[640,2048]{1,0:T(8,128)} copy-done((f32[640,2048]{1,0:T(8,128)}, f32[640,2048]{1,0:T(8,128)S(1)}, u32[]{:S(2)}) %copy-start.3) | copy-done | bytes 5242904
  148.8 1.4 unsort_kernel.1.dz_ref.dz0_ref.left_ref
  150.3 2.5 %copy-done.4 = f32[640,2048]{1,0:T(8,128)S(1)} copy-done((f32[640,2048]{1,0:T(8,128)S(1)}, f32[640,2048]{1,0:T(8,128)}, u32[]{:S(2)}) %copy-start.4) | copy-done | bytes 5242904
  152.8 3.5 %features_kernel.1 = bf16[96,640]{1,0:T(8,128)(2,1)} custom-call(bf16[768,256]{1,0:T(8,128)(2,1)S(1)} %unsort_kernel.1.dz_ref.dz0_ref.left_ref, f32[640,2048]{1,0:T(8,128)S(1)} %copy-done.4, bf16[2048,256]{1,0:T(8,128)(2,1)S(1)} %get-tuple-element.108.w2_ref, bf16[96,2048]{1,0:T(8,128)(2,1)S(1)} %get-tuple-element.109.w1_ref), custom_call_target="tpu_custom_call" | custom-call | tf_op jit(solution)/shard_map/features_kernel/pallas_call | solution.py:502
  156.4 6.5 %protos_kernel.1 = f32[256,4096]{1,0:T(8,128)} custom-call(s32[1]{0:T(128)} %bitcast.d_ref, bf16[256,4096]{1,0:T(8,128)(2,1)S(1)} %copy-done, f32[256,2048]{1,0:T(8,128)S(1)} %copy-done.5, f32[256,2048]{1,0:T(8,128)} %collective-permute-done.7.other_ref, bf16[768,256]{1,0:T(8,128)(2,1)S(1)} %unsort_kernel.1.dz_ref.dz0_ref.left_ref, ...), custom_call_target="tpu_custom_call" | custom-call | tf_op jit(solution)/shard_map/protos_kernel/pallas_call | solution.py:572
  162.9 3.7 %weights_kernel.1 = (f32[1536,128]{1,0:T(8,128)}, f32[128,256]{1,0:T(8,128)}) custom-call(bf16[640,1536]{1,0:T(8,128)(2,1)S(1)} %copy-done.2, bf16[640,1536]{1,0:T(8,128)(2,1)} %collective-permute-done.f1_ref, bf16[768,256]{1,0:T(8,128)(2,1)S(1)} %unsort_kernel.1.dz_ref.dz0_ref.left_ref, bf16[768,256]{1,0:T(8,128)(2,1)S(1)} %collective-permute-done.6.dz1_ref.right_ref, ...), custom_call_target="tpu_custom_call" | custom-call | flops 1000000000 | bytes 1000000 | tf_op jit(solution)/shard_map/weights_kernel/pallas_call | solution.py:196
  (76 shorter events, 13.5 us)
Async XLA Ops:
  7.2 99.9 %all-gather.3.cloned.1.call-start = ((), (), s32[]{:S(2)}) async-start(), calls=%async_computation.6 | async-start | bytes 3899392 | tf_op jit(solution)/shard_map/all_gather | solution.py:625
  7.2 16.5 %collective-permute-start = (bf16[640,1536]{1,0:T(8,128)(2,1)}, bf16[640,1536]{1,0:T(8,128)(2,1)}, u32[]{:S(2)}, u32[]{:S(2)}) collective-permute-start(bf16[640,1536]{1,0:T(8,128)(2,1)} %f0_ref.2), channel_id=1, source_target_pairs={{0,16},{16,0},{1,17},{17,1},{2,18},{18,2},{3,19},{19,3},{4,20},{20... | collective-permute-start | bytes 5898248 | tf_op jit(solution)/shard_map/ppermute | solution.py:28
  10.2 13.5 %copy-start = (bf16[256,4096]{1,0:T(8,128)(2,1)S(1)}, bf16[256,4096]{1,0:T(8,128)(2,1)}, u32[]{:S(2)}) copy-start(bf16[256,4096]{1,0:T(8,128)(2,1)} %protos_ref.1) | copy-start | bytes 6291460
  15.8 24.4 %all-to-all-start = ((bf16[16,48,256]{2,1,0:T(8,128)(2,1)}), bf16[16,48,256]{2,1,0:T(8,128)(2,1)S(1)}, u32[]{:S(2)}, u32[]{:S(2)}) async-start(bf16[16,48,256]{2,1,0:T(8,128)(2,1)} %get-tuple-element.62), calls=%async_computation | async-start | bytes 786432 | tf_op jit(solution)/shard_map/all_to_all | solution.py:640
  26.6 4.7 %copy-start.13 = (bf16[256,4096]{1,0:T(8,128)(2,1)S(1)}, bf16[256,4096]{1,0:T(8,128)(2,1)}, u32[]{:S(2)}) copy-start(bf16[256,4096]{1,0:T(8,128)(2,1)} %param.19) | copy-start | bytes 6291460
  64.3 1.7 copy-start.17
  64.3 1.7 collective-permute-start.1
  70.5 10.4 %all-to-all-start.2 = ((f32[32,2,128]{2,1,0:T(2,128)}), f32[32,2,128]{2,1,0:T(2,128)S(1)}, u32[]{:S(2)}, u32[]{:S(2)}) async-start(f32[32,2,128]{2,1,0:T(2,128)} %get-tuple-element.75), calls=%async_computation.2 | async-start | bytes 65536 | tf_op jit(solution)/shard_map/all_to_all | solution.py:671
  80.5 9.8 %copy-start.14 = (f32[640,256]{1,0:T(8,128)S(1)}, f32[640,256]{1,0:T(8,128)}, u32[]{:S(2)}) copy-start(f32[640,256]{1,0:T(8,128)} %get-tuple-element.83) | copy-start | bytes 1966084
  84.6 5.7 %collective-permute-start.2 = (f32[640,256]{1,0:T(8,128)}, f32[640,256]{1,0:T(8,128)S(1)}, u32[]{:S(2)}, u32[]{:S(2)}) collective-permute-start(f32[640,256]{1,0:T(8,128)} %get-tuple-element.84), channel_id=1, source_target_pairs={{0,16},{16,0},{1,17},{17,1},{2,18},{18,2},{3,19},{19,3},{4,20},{20... | collective-permute-start | bytes 1966088 | tf_op jit(solution)/shard_map/ppermute | solution.py:28
  84.6 14.5 %all-to-all-start.3 = ((f32[32,2,640]{2,1,0:T(2,128)}), f32[32,2,640]{2,1,0:T(2,128)}, u32[]{:S(2)}, u32[]{:S(2)}) async-start(f32[32,2,640]{2,1,0:T(2,128)} %second_kernel.1), calls=%async_computation.3 | async-start | bytes 327680 | tf_op jit(solution)/shard_map/all_to_all | solution.py:680
  102.8 1.7 collective-permute-start.3
  105.1 5.7 %copy-start.18 = (f32[640,1]{1,0:T(8,128)S(1)}, f32[640,1]{1,0:T(8,128)}, u32[]{:S(2)}) copy-start(f32[640,1]{1,0:T(8,128)} %get-tuple-element.93) | copy-start | bytes 7684
  105.1 5.7 %copy-start.19 = (f32[640,1]{1,0:T(8,128)S(1)}, f32[640,1]{1,0:T(8,128)}, u32[]{:S(2)}) copy-start(f32[640,1]{1,0:T(8,128)} %get-tuple-element.94) | copy-start | bytes 7684
  107.1 26.2 %collective-permute-start.5 = (bf16[16,896,128]{2,1,0:T(8,128)(2,1)}, bf16[16,896,128]{2,1,0:T(8,128)(2,1)}, u32[]{:S(2)}, u32[]{:S(2)}) collective-permute-start(bf16[16,896,128]{2,1,0:T(8,128)(2,1)} %bitcast.5), channel_id=1, source_target_pairs={{0,16},{16,0},{1,17},{17,1},{2,18},{18,2},{3,19},{19,3},{4,20},{20... | collective-permute-start | bytes 11010056 | tf_op jit(solution)/shard_map/ppermute | solution.py:28
  107.2 17.8 %all-to-all-start.4 = ((bf16[16,56,256]{2,1,0:T(8,128)(2,1)}), bf16[16,56,256]{2,1,0:T(8,128)(2,1)S(1)}, u32[]{:S(2)}, u32[]{:S(2)}) async-start(bf16[16,56,256]{2,1,0:T(8,128)(2,1)} %message_kernel.1), calls=%async_computation.4 | async-start | bytes 917504 | tf_op jit(solution)/shard_map/all_to_all | solution.py:699
  110.9 3.1 %collective-permute-start.4 = (f32[640,1]{1,0:T(8,128)S(1)}, f32[640,1]{1,0:T(8,128)S(1)}, u32[]{:S(2)}, u32[]{:S(2)}) collective-permute-start(f32[640,1]{1,0:T(8,128)S(1)} %multiply_divide_fusion), channel_id=1, source_target_pairs={{0,16},{16,0},{1,17},{17,1},{2,18},{18,2},{3,19},{19,3},{4,20},{20... | collective-permute-start | bytes 7688 | tf_op jit(solution)/shard_map/ppermute | solution.py:28
  125.1 1.7 copy-start.15
  125.1 31.3 %collective-permute-start.7 = (f32[256,2048]{1,0:T(8,128)}, f32[256,2048]{1,0:T(8,128)}, u32[]{:S(2)}, u32[]{:S(2)}) collective-permute-start(f32[256,2048]{1,0:T(8,128)} %fusion.4.own_ref), channel_id=1, source_target_pairs={{0,16},{16,0},{1,17},{17,1},{2,18},{18,2},{3,19},{19,3},{4,20},{20... | collective-permute-start | bytes 6291464 | tf_op jit(solution)/shard_map/ppermute | solution.py:28
  125.1 31.3 %collective-permute-start.8 = (bf16[256,2048]{1,0:T(8,128)(2,1)}, bf16[256,2048]{1,0:T(8,128)(2,1)}, u32[]{:S(2)}, u32[]{:S(2)}) collective-permute-start(bf16[256,2048]{1,0:T(8,128)(2,1)} %get-tuple-element.117.lown_ref), channel_id=1, source_target_pairs={{0,16},{16,0},{1,17},{17,1},{2,18},{18,2},{3,19},{19,3},{4,20},{20... | collective-permute-start | bytes 3145736 | tf_op jit(solution)/shard_map/ppermute | solution.py:28
  128.9 18.8 %all-to-all-start.5 = ((bf16[16,48,256]{2,1,0:T(8,128)(2,1)}), bf16[16,48,256]{2,1,0:T(8,128)(2,1)}, u32[]{:S(2)}, u32[]{:S(2)}) async-start(bf16[16,48,256]{2,1,0:T(8,128)(2,1)} %bottleneck_kernel.1), calls=%async_computation.5 | async-start | bytes 786432 | tf_op jit(solution)/shard_map/all_to_all | solution.py:717
  134.9 2.0 %copy-start.11 = (bf16[14336,128]{1,0:T(8,128)(2,1)S(1)}, bf16[14336,128]{1,0:T(8,128)(2,1)}, u32[]{:S(2)}) copy-start(bf16[14336,128]{1,0:T(8,128)(2,1)} %all-gather.3.cloned.1.call-done) | copy-start | bytes 11010052
  145.4 2.3 %copy-start.3 = (f32[640,2048]{1,0:T(8,128)}, f32[640,2048]{1,0:T(8,128)S(1)}, u32[]{:S(2)}) copy-start(f32[640,2048]{1,0:T(8,128)S(1)} %get-tuple-element.107.slope_ref) | copy-start | bytes 15728644
  150.2 6.1 %collective-permute-start.6 = (bf16[768,256]{1,0:T(8,128)(2,1)S(1)}, bf16[768,256]{1,0:T(8,128)(2,1)S(1)}, u32[]{:S(2)}, u32[]{:S(2)}) collective-permute-start(bf16[768,256]{1,0:T(8,128)(2,1)S(1)} %unsort_kernel.1.dz_ref.dz0_ref.left_ref), channel_id=1, source_target_pairs={{0,16},{16,0},{1,17},{17,1},{2,18},{18,2},{3,19},{19,3},{4,20},{20... | collective-permute-start | bytes 1179656 | tf_op jit(solution)/shard_map/ppermute | solution.py:28
  150.3 2.5 %copy-start.4 = (f32[640,2048]{1,0:T(8,128)S(1)}, f32[640,2048]{1,0:T(8,128)}, u32[]{:S(2)}) copy-start(f32[640,2048]{1,0:T(8,128)} %copy-done.3) | copy-start | bytes 15728644
  152.8 3.6 %copy-start.5 = (f32[256,2048]{1,0:T(8,128)S(1)}, f32[256,2048]{1,0:T(8,128)}, u32[]{:S(2)}) copy-start(f32[256,2048]{1,0:T(8,128)} %fusion.4.own_ref) | copy-start | bytes 6291460
  156.3 6.5 %copy-start.2 = (bf16[640,1536]{1,0:T(8,128)(2,1)S(1)}, bf16[640,1536]{1,0:T(8,128)(2,1)}, u32[]{:S(2)}) copy-start(bf16[640,1536]{1,0:T(8,128)(2,1)} %f0_ref.2) | copy-start | bytes 5898244
  156.3 6.5 %copy-start.6 = (bf16[128,256]{1,0:T(8,128)(2,1)S(1)}, bf16[128,256]{1,0:T(8,128)(2,1)}, u32[]{:S(2)}) copy-start(bf16[128,256]{1,0:T(8,128)(2,1)} %w2_ref.1) | copy-start | bytes 196612
  156.3 6.5 %copy-start.7 = (f32[128,640]{1,0:T(8,128)S(1)}, f32[128,640]{1,0:T(8,128)}, u32[]{:S(2)}) copy-start(f32[128,640]{1,0:T(8,128)} %get-tuple-element.112.s0_ref) | copy-start | bytes 983044
  156.3 6.5 %copy-start.8 = (f32[128,640]{1,0:T(8,128)S(1)}, f32[128,640]{1,0:T(8,128)}, u32[]{:S(2)}) copy-start(f32[128,640]{1,0:T(8,128)} %get-tuple-element.113.s1_ref) | copy-start | bytes 983044
  156.3 6.6 %copy-start.9 = (bf16[128,640]{1,0:T(8,128)(2,1)S(1)}, bf16[128,640]{1,0:T(8,128)(2,1)}, u32[]{:S(2)}) copy-start(bf16[128,640]{1,0:T(8,128)(2,1)} %get-tuple-element.110.h0_ref) | copy-start | bytes 491524
  156.3 6.6 %copy-start.10 = (bf16[128,640]{1,0:T(8,128)(2,1)S(1)}, bf16[128,640]{1,0:T(8,128)(2,1)}, u32[]{:S(2)}) copy-start(bf16[128,640]{1,0:T(8,128)(2,1)} %get-tuple-element.111.h1_ref) | copy-start | bytes 491524
  (6 other events, 5.5 us)
Sparse Core Ops, SparseCore 0:
  10.7 83.2 all-gather.2

commit v5 on v4

--- a/solution.py
+++ b/solution.py
@@ -221,8 +221,8 @@
 
 def head_kernel(d_ref, *refs):
     sources, im_ref, view_ref = refs[:6], refs[6], refs[7]
-    parts_ref, back_ref, vs_ref = refs[8:11]
-    held, sems = refs[11:17], refs[17]
+    parts_ref, place_ref, vs_ref, pack_ref = refs[8:12]
+    held, sems = refs[12:18], refs[18]
     copies = [pltpu.make_async_copy(a, b, sems.at[k]) for k, (a, b) in enumerate(zip(sources, held))]
     for copy in copies:
         copy.start()
@@ -235,17 +235,22 @@
     down, along = grids((rows, rows))
     imc = to_col(im)
     same = im == imc
-    before = jnp.where(same & (along < down), 1.0, 0.0)
     after = jnp.where(same & (down < along), 1.0, 0.0)
-    col = (imc * per + jnp.sum(before, axis=1, keepdims=True)).astype(jnp.int32)
-    row = (im * per + jnp.sum(after, axis=0, keepdims=True)).astype(jnp.int32)
-    back_ref[...] = jnp.where(col == along, 1.0, 0.0).astype(BF16)
-    hit = row == down
+    row = im * per + jnp.sum(after, axis=0, keepdims=True)
+    place_ref[...] = row
+    hit = row.astype(jnp.int32) == down
     vs_ref[...] = jnp.sum(jnp.where(hit, view_ref[...].reshape(1, rows).astype(F32), 0.0), axis=1, keepdims=True)
     order = jnp.where(hit, 1.0, 0.0).astype(BF16)
 
     for copy in copies:
         copy.wait()
+
+    deep, hs = w1_ref.shape[0] // 2, w1_ref.shape[1]
+    half = hs // 2
+    pack_ref[:deep] = w1_ref[pl.ds(pl.multiple_of(d_ref[0] * deep, deep), deep)]
+    w2_half = w2_ref[pl.ds(pl.multiple_of(d_ref[0] * half, half), half)]
+    pack_ref[deep : deep + half] = w2_half[:, :hs]
+    pack_ref[deep + half :] = w2_half[:, hs:]
 
     def part(x, first, second):
         act = dot(x[...], first[...], ((1,), (0,)))
@@ -350,19 +355,18 @@
     own, other = to_row(esum_ref[:half]), to_row(esum_ref[half:])
     first = d_ref[0] == 0
     mass = to_row(mass)
-    mass = jnp.concatenate([mass, jnp.zeros((1, half - mass.shape[1]), F32)], axis=1)
     n = msg_ref.shape[0] // 2
     for k, row in enumerate((jnp.where(first, own, other), jnp.where(first, other, own))):
-        part = jnp.concatenate([mass, row], axis=0)
+        part = jnp.concatenate([mass, row], axis=1)
         msg_ref[k * n : (k + 1) * n] = jnp.broadcast_to(part[None], (n,) + part.shape)
 
 
 def third_kernel(d_ref, got_ref, kern_ref, pnb_ref, esum_ref, last_ref, mine_ref, yours_ref):
     teach = kern_ref.shape[0]
     got = jnp.sum(got_ref[...], axis=0)
-    esum_ref[...] = to_col(got[1:])
+    esum_ref[...] = to_col(got[:, teach:])
     kern = kern_ref[...]
-    scale, mass = row_mass(kern, to_col(got[:1, :teach]))
+    scale, mass = row_mass(kern, to_col(got[:, :teach]))
     last = (kern * scale).astype(BF16)
     last_ref[...] = last
     sums = dot(last, pnb_ref[...], ((1,), (1,)))
@@ -386,8 +390,9 @@
     out_ref[...] = jnp.concatenate([sums, both, tail.reshape(n, teach // n, bot)], axis=1).astype(BF16)
 
 
-def bottleneck_kernel(factor, got_ref, zn_ref, zinv_ref, view_ref, scale_ref, out_ref):
-    sr = view_ref.shape[0]
+def bottleneck_kernel(factor, p_ref, got_ref, zn_ref, zinv_ref, view_ref, scale_ref, out_ref):
+    sr = view_ref.shape[0] // out_ref.shape[0]
+    mine = pl.ds(pl.multiple_of(p_ref[0] * sr, sr), sr)
     tr = zn_ref.shape[0] - sr
     per = sr // (tr // 2)
     out = jnp.sum(got_ref[...].astype(F32), axis=0)
@@ -396,9 +401,9 @@
     sums = out[sr : sr + tr] * image
     zn, zinv = zn_ref[:sr], zinv_ref[:sr]
     znb = zn.astype(BF16).astype(F32)
-    view = view_ref[...].astype(jnp.int32)
+    view = view_ref[mine].astype(jnp.int32)
     which = lax.broadcasted_iota(jnp.int32, (sr, 1), 0)
-    dzn = scale_ref[...] * out[:sr]
+    dzn = scale_ref[mine] * out[:sr]
     own = []
     for t in range(tr):
         base = (t // 2) * per
@@ -464,132 +469,146 @@
             ),
         ),
         out_shape=(shape((rows, n * hs), F32), shape((n * hs, 2 * hs), BF16), shape((width, n * hs), BF16)),
-        compiler_params=params(20),
+        compiler_params=params(),
         cost_estimate=pl.CostEstimate(flops=10**10, bytes_accessed=3 * 10**7, transcendentals=0),
     )(d.reshape(1), p.reshape(1), features, own, other)
 
 
-def unsort_kernel(got_ref, back_ref, out_ref):
-    n, slot, bot = got_ref.shape
-    rows = back_ref.shape[0]
-    sr = rows // n
-    got = got_ref[...].astype(F32)
-    dz = got[:, :sr].reshape(rows, bot).astype(BF16)
-    out_ref[:rows] = dot(back_ref[...], dz, ((1,), (0,))).astype(BF16)
-    out_ref[rows:] = got[:, sr:].reshape(n * (slot - sr), bot).astype(BF16)
-
-
-def features_kernel(dz_ref, slope_ref, w2_ref, w1_ref, out_ref, acc_ref):
-    step = pl.program_id(0)
-
-    @pl.when(step == 0)
-    def _():
-        acc_ref[...] = jnp.zeros_like(acc_ref)
-
-    pre = dot(dz_ref[...], w2_ref[...], ((1,), (1,)))
-    dhid = (pre * slope_ref[...]).astype(BF16)
-    acc_ref[...] += dot(w1_ref[...], dhid, ((1,), (1,)))
-
-    @pl.when(step == pl.num_programs(0) - 1)
-    def _():
-        out_ref[...] = acc_ref[...].astype(BF16)
-
-
-def feature_grads(dz, slope, w2, w1_block):
+def fetch(pairs, sems):
+    copies = [pltpu.make_async_copy(x, y, sems.at[k]) for k, (x, y) in enumerate(pairs)]
+    for copy in copies:
+        copy.start()
+    return copies
+
+
+def put_back(got, place):
+    n, _, bot = got.shape
+    rows = place.shape[1]
+    _, along = grids((rows, rows))
+    back = jnp.where(to_col(place).astype(jnp.int32) == along, 1.0, 0.0).astype(BF16)
+    dz = got.astype(F32)[:, : rows // n].reshape(rows, bot).astype(BF16)
+    return dot(back, dz, ((1,), (0,))).astype(BF16)
+
+
+def features_kernel(step, *refs):
+    ins, (dz_ref, out_ref), held, sems = refs[:5], refs[5:7], refs[7:12], refs[12]
+    got, place, slope, w2, w1 = held
+    pieces = [pl.ds(k, step) for k in range(0, slope.shape[1], step)]
+    small = fetch([(ins[k], held[k]) for k in (0, 1, 4)], sems.at[pl.ds(0, 3)])
+    large = []
+    for k, piece in enumerate(pieces):
+        pairs = [(ins[2].at[:, piece], slope.at[:, piece]), (ins[3].at[piece], w2.at[piece])]
+        large.append(fetch(pairs, sems.at[pl.ds(3 + 2 * k, 2)]))
+    for copy in small:
+        copy.wait()
+    dz = put_back(got[...], place[...])
+    dz_ref[...] = dz
+    total = None
+    for piece, copies in zip(pieces, large):
+        for copy in copies:
+            copy.wait()
+        dhid = (dot(dz, w2[piece], ((1,), (1,))) * slope[:, piece]).astype(BF16)
+        part = dot(w1[:, piece], dhid, ((1,), (1,)))
+        total = part if total is None else total + part
+    out_ref[...] = total.astype(BF16)
+
+
+def feature_grads(got, place, slope, w2, w1):
+    args = (got, place, slope, w2, w1)
     rows, hidden = slope.shape
-    width, bot = w1_block.shape[0], w2.shape[1]
-    step = 2 * bot
+    bot, step = got.shape[2], 512
     return pl.pallas_call(
-        features_kernel,
+        functools.partial(features_kernel, step),
         name="features_kernel",
-        grid=(hidden // step,),
-        out_shape=shape((width, rows), BF16),
-        in_specs=[
-            pl.BlockSpec((rows, bot), lambda k: (0, 0)),
-            pl.BlockSpec((rows, step), lambda k: (0, k)),
-            pl.BlockSpec((step, bot), lambda k: (k, 0)),
-            pl.BlockSpec((width, step), lambda k: (0, k)),
-        ],
-        out_specs=pl.BlockSpec((width, rows), lambda k: (0, 0)),
-        scratch_shapes=[pltpu.VMEM((width, rows), F32)],
-        compiler_params=params(12),
-    )(dz, slope, w2, w1_block)
-
-
-def weights_kernel(f0_ref, f1_ref, dz0_ref, dz1_ref, h0_ref, h1_ref, s0_ref, s1_ref, w2_ref, g1_ref, g2_ref):
-    g1, g2 = [], []
-    rows = f0_ref.shape[0]
-    for f, z, h, s in ((f0_ref, dz0_ref, h0_ref, s0_ref), (f1_ref, dz1_ref, h1_ref, s1_ref)):
-        dz = z[:rows]
-        g2.append(dot(h[...], dz, ((1,), (0,))))
-        dhid = (dot(w2_ref[...], dz, ((1,), (1,))) * s[...]).astype(BF16)
-        g1.append(dot(dhid, f[...], ((1,), (0,))))
-    g1_ref[...] = (g1[0] + g1[1]).T
-    g2_ref[...] = g2[0] + g2[1]
-
-
-def protos_kernel(d_ref, protos_ref, own_ref, other_ref, left_ref, right_ref, lown_ref, lother_ref, out_ref, turned_ref):
-    half = pl.program_id(0) // (pl.num_programs(0) // 2)
-    mine = half == d_ref[0]
-
-    @pl.when(pl.program_id(0) == 0)
-    def _():
-        first = d_ref[0] == 0
-        a, b = left_ref[...].astype(F32), right_ref[...].astype(F32)
-        scaled = jnp.concatenate([jnp.where(first, a, b), jnp.where(first, b, a)], axis=0)
-        turned_ref[...] = scaled.T.astype(BF16)
-
-    def finish(dpn_ref, last_ref):
-        mat = protos_ref[...].astype(F32)
+        grid=(1,),
+        out_shape=(shape((rows, bot), BF16), shape((w1.shape[0], rows), BF16)),
+        in_specs=[pl.BlockSpec(memory_space=pl.ANY)] * len(args),
+        out_specs=(block((rows, bot)), block((w1.shape[0], rows))),
+        scratch_shapes=[pltpu.VMEM(x.shape, x.dtype) for x in args]
+        + [pltpu.SemaphoreType.DMA((3 + 2 * (hidden // step),))],
+        compiler_params=params(),
+    )(*args)
+
+
+def last_kernel(tile, d_ref, *refs):
+    ins, (gp_hbm, g1_hbm, g2_hbm) = refs[:16], refs[16:19]
+    held, (gp, g1, g2, sems, tile_sems, out_sems) = refs[19:35], refs[35:]
+    dz0, got0, got1, place1, protos, down, dother, lown, lother, f0, f1, h0, h1, s0, s1, w2 = held
+    cols = protos.shape[1] // 2
+    steps = cols // tile
+    rows = dz0.shape[0]
+    n, slot, bot = got0.shape
+    early = fetch([(ins[k], held[k]) for k in range(4)], sems)
+    tiles = []
+    for k in range(2 * steps):
+        own = k < steps
+        here = pl.multiple_of((d_ref[0] if own else 1 - d_ref[0]) * cols + (k % steps) * tile, tile)
+        there = pl.ds((k % steps) * tile, tile)
+        a, b = (5, 7) if own else (6, 8)
+        pairs = [
+            (ins[4].at[:, pl.ds(here, tile)], protos.at[:, pl.ds(here, tile)]),
+            (ins[a].at[:, there], held[a].at[:, there]),
+            (ins[b].at[:, there], held[b].at[:, there]),
+        ]
+        tiles.append((here, there, a, b, fetch(pairs, tile_sems.at[k])))
+    late = fetch([(ins[k], held[k]) for k in range(9, 16)], sems.at[pl.ds(4, 7)])
+    for copy in early:
+        copy.wait()
+    first = d_ref[0] == 0
+    right0 = got0[...].astype(F32)[:, rows // n :].reshape(-1, bot)
+    right1 = got1[...].astype(F32)[:, rows // n :].reshape(-1, bot)
+    right = jnp.concatenate([jnp.where(first, right0, right1), jnp.where(first, right1, right0)], axis=0)
+    right = right.T.astype(BF16)
+    dz1 = put_back(got1[...], place1[...])
+    outs = []
+    for k, (here, there, a, b, copies) in enumerate(tiles):
+        for copy in copies:
+            copy.wait()
+        mat = protos[:, pl.ds(here, tile)].astype(F32)
         inv = lax.rsqrt(jnp.sum(mat * mat, axis=0, keepdims=True) + 1e-06)
         pn = mat * inv
-        dpn = dpn_ref[...] - dot(turned_ref[...], last_ref[...], ((1,), (0,)))
-        out_ref[...] = inv * (dpn - pn * jnp.sum(pn * dpn, axis=0, keepdims=True))
-
-    @pl.when(mine)
-    def _():
-        finish(own_ref, lown_ref)
-
-    @pl.when(jnp.logical_not(mine))
-    def _():
-        finish(other_ref, lother_ref)
-
-
-def protos_grads(d, protos, own, other, mine, yours, lown, lother):
-    bot, wide = protos.shape
-    tile = 1024
-    steps = wide // tile
-    halfsteps = steps // 2
-    teach = lown.shape[0]
-    after = mine.shape[0] // (teach // 2) - 1
-
-    def place(i, d_ref, same):
-        at = d_ref[0] if same else 1 - d_ref[0]
-        return (0, jnp.clip(i - at * halfsteps, 0, halfsteps - 1))
-
-    own_map = lambda i, d_ref: place(i, d_ref, True)
-    other_map = lambda i, d_ref: place(i, d_ref, False)
+        dpn = held[a][:, there].astype(F32) - dot(right, held[b][:, there], ((1,), (0,)))
+        gp[:, pl.ds(here, tile)] = inv * (dpn - pn * jnp.sum(pn * dpn, axis=0, keepdims=True))
+        out = pltpu.make_async_copy(gp.at[:, pl.ds(here, tile)], gp_hbm.at[:, pl.ds(here, tile)], out_sems.at[k])
+        out.start()
+        outs.append(out)
+    for copy in late:
+        copy.wait()
+    sums1, sums2 = [], []
+    for f, dz, h, sl in ((f0, dz0[...], h0, s0), (f1, dz1, h1, s1)):
+        sums2.append(dot(h[...], dz, ((1,), (0,))))
+        dhid = (dot(w2[...], dz, ((1,), (1,))) * sl[...]).astype(BF16)
+        sums1.append(dot(dhid, f[...], ((1,), (0,))))
+    g1[...] = (sums1[0] + sums1[1]).T
+    g2[...] = sums2[0] + sums2[1]
+    for k, (x, y) in enumerate(((g1, g1_hbm), (g2, g2_hbm))):
+        out = pltpu.make_async_copy(x, y, out_sems.at[2 * steps + k])
+        out.start()
+        outs.append(out)
+    for out in outs:
+        out.wait()
+
+
+def last_grads(d, head_w1, *args):
+    tile = 512
+    protos, head_w2 = args[4], args[15]
+    tiles = protos.shape[1] // tile
+    outs = (shape(protos.shape, F32), shape(head_w1.shape, F32), shape(head_w2.shape, F32))
+    anywhere = pl.BlockSpec(memory_space=pl.ANY)
     return pl.pallas_call(
-        protos_kernel,
-        name="protos_kernel",
-        grid_spec=pltpu.PrefetchScalarGridSpec(
-            num_scalar_prefetch=1,
-            grid=(steps,),
-            in_specs=[
-                pl.BlockSpec((bot, tile), lambda i, d_ref: (0, i)),
-                pl.BlockSpec((bot, tile), own_map),
-                pl.BlockSpec((bot, tile), other_map),
-                pl.BlockSpec((teach // 2, bot), lambda i, d_ref: (after, 0)),
-                pl.BlockSpec((teach // 2, bot), lambda i, d_ref: (after, 0)),
-                pl.BlockSpec((teach, tile), own_map),
-                pl.BlockSpec((teach, tile), other_map),
-            ],
-            out_specs=pl.BlockSpec((bot, tile), lambda i, d_ref: (0, i)),
-            scratch_shapes=[pltpu.VMEM((bot, teach), BF16)],
-        ),
-        out_shape=jax.ShapeDtypeStruct((bot, wide), F32),
-        compiler_params=params(16),
-    )(d.reshape(1), protos, own, other, mine, yours, lown, lother)
+        functools.partial(last_kernel, tile),
+        name="last_kernel",
+        out_shape=outs,
+        in_specs=[pl.BlockSpec(memory_space=pltpu.SMEM)] + [anywhere] * len(args),
+        out_specs=(anywhere,) * 3,
+        scratch_shapes=[pltpu.VMEM(x.shape, x.dtype) for x in args + outs]
+        + [
+            pltpu.SemaphoreType.DMA((11,)),
+            pltpu.SemaphoreType.DMA((tiles, 3)),
+            pltpu.SemaphoreType.DMA((tiles + 2,)),
+        ],
+        compiler_params=params(),
+    )(d.reshape(1), *args)
 
 
 def tied(*values):
@@ -617,26 +636,26 @@
     everyone = nd * n
     factor = 10.0 / (9 * teach * nd)
 
-    w2_half = lax.dynamic_slice_in_dim(head_w2, d * (hs // 2), hs // 2, 0)
-    weights = jnp.concatenate(
-        [lax.dynamic_slice_in_dim(head_w1, d * (wide // 2), wide // 2, 0), w2_half[:, :hs], w2_half[:, hs:]], axis=0
-    )
-    weights, head_w1_late = tied(weights, head_w1)
-    weights = lax.all_gather(weights, "proto")
     feat_other = swap(features, "dp", 1)
-    heads = (features, head_w1_late, head_w2, teacher_features, teacher_w1, teacher_w2)
-    parts, back, view = pl.pallas_call(
+    heads = (features, head_w1, head_w2, teacher_features, teacher_w1, teacher_w2)
+    parts, place, view, weights = pl.pallas_call(
         head_kernel,
         grid=(1,),
-        out_shape=(shape((n, sr + tr, bot), BF16), shape((rows, rows), BF16), shape((rows, 1), F32)),
+        out_shape=(
+            shape((n, sr + tr, bot), BF16),
+            shape((1, rows), F32),
+            shape((rows, 1), F32),
+            shape((wide // 2 + hs, hs), BF16),
+        ),
         in_specs=[pl.BlockSpec(memory_space=pltpu.SMEM)]
         + [pl.BlockSpec(memory_space=pl.ANY)] * 6
         + [block((rows,))] * 2,
-        out_specs=(block((n, sr + tr, bot)), block((rows, rows)), block((rows, 1))),
+        out_specs=(block((n, sr + tr, bot)), block((1, rows)), block((rows, 1)), block((wide // 2 + hs, hs))),
         scratch_shapes=[pltpu.VMEM(x.shape, x.dtype) for x in heads] + [pltpu.SemaphoreType.DMA((6,))],
         compiler_params=params(),
         name="head_kernel",
     )(d.reshape(1), *heads, crop_image, crop_view)
+    weights = lax.all_gather(weights, "proto")
     parts_got = lax.all_to_all(parts, "proto", 0, 0)
     w1_late, protos_late, tprotos_late, feat_late, feat_other_late, _ = tied(
         head_w1, protos, teacher_protos, features, feat_other, parts
@@ -673,7 +692,7 @@
     exb, sums, sums_other, esum = student_sums(student, pnb)
     msg = call(
         second_kernel,
-        shape((everyone, 2, rows), F32),
+        shape((everyone, 1, nd * teach + rows), F32),
         [d],
         msg_got, kern, esum,
     )
@@ -698,38 +717,33 @@
     msg = call(message_kernel, shape((n, sr + 2 * tr, bot), BF16), [], sums, mine, yours)
     msg_got = lax.all_to_all(msg, "proto", 0, 0)
 
-    esum, view_late, weights, last, _ = tied(esum, view, weights, last, msg)
+    esum, view_late, last, weights, place, _ = tied(esum, view, last, weights, place, msg)
     weights_other, last_other = swap(weights, "dp", 1), swap(last, "dp", 1)
+    place_other = swap(place, "dp", 1)
     crop_scale = jnp.where(view_late == 2, 2.0, 1.0) * factor / esum
     scale_other = swap(crop_scale, "dp", 1)
-    my_view = lax.dynamic_slice_in_dim(view_late, p * sr, sr, 0)
-    my_scale = lax.dynamic_slice_in_dim(crop_scale, p * sr, sr, 0)
     left = (student.astype(F32) * jnp.concatenate([crop_scale, scale_other], axis=0)).astype(BF16)
-    dpn = dot(left, exb, ((0,), (0,)))
+    dpn = dot(left, exb, ((0,), (0,))).astype(BF16)
     msg_got, dpn = tied(msg_got, dpn)
     dpn_other = swap(dpn, "dp", 1)
     dz = call(
         functools.partial(bottleneck_kernel, factor),
         shape((n, sr + tr, bot), BF16),
-        [],
-        msg_got, zn, zinv, my_view, my_scale,
+        [p],
+        msg_got, zn, zinv, view_late, crop_scale,
     )
     got = lax.all_to_all(dz, "proto", 0, 0)
     weights, feat_late, _ = tied(weights, features, dz)
-    slope, w2_all, w1_block = slopes_of(d, p, feat_late, weights, weights_other, wide // n)
-    got, slope, w2_all, w1_block = tied(got, slope, w2_all, w1_block)
-
-    dz = call(unsort_kernel, shape((rows + teach, bot), BF16), [], got, back, mib=8)
-    dz_other = swap(dz, "dp", 1)
-    grad_features = feature_grads(dz, slope, w2_all, w1_block).T
-    grad_w1, grad_w2 = call(
-        weights_kernel,
-        (shape(head_w1.shape, F32), shape(head_w2.shape, F32)),
-        [],
-        features, feat_other, dz, dz_other, h0, h1, s0, s1, head_w2,
-        mib=16,
-    )
-    grad_protos = protos_grads(d, protos, dpn, dpn_other, dz, dz_other, last, last_other)
+    slopes = slopes_of(d, p, feat_late, weights, weights_other, wide // n)
+    got, slopes = tied(got, slopes)
+
+    got_other = swap(got, "dp", 1)
+    dz, grad_features = feature_grads(got, place, *slopes)
+    grad_protos, grad_w1, grad_w2 = last_grads(
+        d, head_w1, dz, got, got_other, place_other, protos, dpn, dpn_other, last, last_other,
+        features, feat_other, h0, h1, s0, s1, head_w2,
+    )
+    grad_features = grad_features.T
     return (grad_features, grad_w1, grad_w2, grad_protos)
 
 

time: 175 us -> 168 us (0.960)
  local copies, waits for them, and re-layouts: 15.4 us -> 5.04 us
  starting transfers between devices: 26.2 us -> 29.1 us
  waiting for transfers between devices: 27 us -> 29 us
    unnamed x46 -> x40, local copies, waits for them, and re-layouts: 12.3 us -> 4.8 us
    pallas_call x9 -> x7, Pallas kernels: 26.3 us -> 21.1 us  [call(): pl.pallas_call(kernel, grid=(1,), out_shape=outs, in_specs=[pl.BlockSpec(...]
    pallas_call x2, Pallas kernels: 9.95 us -> 13.3 us  [the longest x1 8.55 us: last_grads(): pl.pallas_call(functools.partial(last_kernel, tile), name='last_kernel',...]
    pallas_call x1, Pallas kernels: 8.46 us -> 11.4 us  [slopes_of(): pl.pallas_call(slopes_kernel, name='slopes_kernel', grid_spec=pltpu.Prefe...]
    all_to_all x2, starting transfers between devices: 8.62 us -> 11 us  [paired_body(): msg_got = lax.all_to_all(msg, ALL, 0, 0)]
    dynamic_slice x3 -> x0, local copies, waits for them, and re-layouts: 2.15 us -> none  [the longest x1 0.94 us: paired_body(): lax.dynamic_slice_in_dim(head_w1, d * (wide // 2), wide // 2, 0)]
    all_to_all x1, waiting for transfers between devices: 5.25 us -> 7.26 us  [paired_body(): msg_got = lax.all_to_all(msg, 'proto', 0, 0)]
    ppermute x9 -> x10, waiting for transfers between devices: 5.91 us -> 5.03 us  [swap(): return lax.ppermute(value, axis, [(i, i ^ step) for i in range(count)])]
  transfers between devices with their start and end apart: 15 -> 16, of which waited for: 7 -> 8; matrix products, arithmetic and copies ran while one was open for 8% -> 6% of each run, Pallas kernels for 27% -> 30%
where the time goes in v5:
time: 168 us; the launch traced here: 167 us
  Pallas kernels  58.5 us (35%)
  starting transfers between devices  29.1 us (17%)
  waiting for transfers between devices  29 us (17%)
  blocking collectives  21.9 us (13%)
  between operations  14.3 us (9%)
  local copies, waits for them, and re-layouts  5.04 us (3%)
  other arithmetic  5.03 us (3%)
  matrix products  4.34 us (3%)
    all_to_all x1, blocking collectives, paired_body(): got = lax.all_to_all(got, 'proto', 0, 0)  21.9 us
    pallas_call x7, Pallas kernels, call(): pl.pallas_call(kernel, grid=(1,), out_shape=outs, in_specs=[pl.BlockSpec(...  21.1 us
    pallas_call x1, Pallas kernels, slopes_of(): pl.pallas_call(slopes_kernel, name='slopes_kernel', grid_spec=pltpu.Prefe...  11.4 us
    all_to_all x2, starting transfers between devices, paired_body(): msg_got = lax.all_to_all(msg, ALL, 0, 0)  11 us
    pallas_call x1, Pallas kernels, last_grads(): pl.pallas_call(functools.partial(last_kernel, tile), name='last_kernel',...  8.55 us
    all_to_all x2, waiting for transfers between devices, paired_body(): msg_got = lax.all_to_all(msg, ALL, 0, 0)  8.21 us
    all_to_all x1, waiting for transfers between devices, paired_body(): parts_got = lax.all_to_all(parts, 'proto', 0, 0)  8.03 us
    all_to_all x1, starting transfers between devices, paired_body(): parts_got = lax.all_to_all(parts, 'proto', 0, 0)  7.91 us
  transfers between devices with their start and end apart: 16, of which 8 were waited for; matrix products, arithmetic and copies ran while one was open for 6% of the time, Pallas kernels for 30%

profile of v5, /device:TPU:0, one launch (start us, length us, event | category | flops | bytes accessed | tf_op | source)
XLA Modules:
  0.0 167.2 jit_solution(7769883936811563444)
XLA Ops:
  7.7 5.6 %head_kernel.1 = (bf16[16,48,256]{2,1,0:T(8,128)(2,1)}, f32[1,640]{1,0:T(1,128)}, f32[640,1]{1,0:T(8,128)}, bf16[896,128]{1,0:T(8,128)(2,1)}) custom-call(s32[1]{0:T(128)} %bitcast.1.d_ref, bf16[640,1536]{1,0:T(8,128)(2,1)} %refs_9_.1, bf16[1536,128]{1,0:T(8,128)(2,1)} %w1_ref, bf16[128,256]{1,0:T(8,128)(2,1)} %refs_15_.1, bf16[128,1536]{1,0:T(8,128)(2,1)} %refs_3_.1, ...), custom_call_target="tpu_custom_call" | custom-call | tf_op jit(solution)/shard_map/head_kernel/pallas_call | solution.py:641
  13.4 7.9 %all-to-all-start = ((bf16[16,48,256]{2,1,0:T(8,128)(2,1)}), bf16[16,48,256]{2,1,0:T(8,128)(2,1)S(1)}, u32[]{:S(2)}, u32[]{:S(2)}) async-start(bf16[16,48,256]{2,1,0:T(8,128)(2,1)} %get-tuple-element.64), calls=%async_computation | async-start | bytes 786432 | tf_op jit(solution)/shard_map/all_to_all | solution.py:659
  21.3 1.7 %fusion = (f32[2048]{0:T(1024)S(1)}, f32[2048]{0:T(1024)S(1)}) fusion(bf16[256,4096]{1,0:T(8,128)(2,1)S(1)} %copy-done, s32[]{:T(128)S(6)} %select_n.8, bf16[256,4096]{1,0:T(8,128)(2,1)} %param.19), kind=kLoop, calls=%fused_computation.5 | loop fusion | flops 3141632 | bytes 2113540 | tf_op jit(solution)/shard_map/reduce_sum | solution.py:48
  23.0 1.2 fusion.1.pnb_ref
  24.2 4.7 %hidden_kernel.1 = (bf16[128,640]{1,0:T(8,128)(2,1)}, bf16[128,640]{1,0:T(8,128)(2,1)}, f32[128,640]{1,0:T(8,128)}, f32[128,640]{1,0:T(8,128)}) custom-call(bf16[640,1536]{1,0:T(8,128)(2,1)} %refs_9_.1, bf16[640,1536]{1,0:T(8,128)(2,1)} %collective-permute-done.f1_ref.refs_10_, bf16[1536,128]{1,0:T(8,128)(2,1)} %w1_ref), custom_call_target="tpu_custom_call" | custom-call | flops 4000000000 | bytes 4000000 | tf_op jit(solution)/shard_map/hidden_kernel/pallas_call | solution.py:196
  28.9 1.2 fusion.3.tpnb_ref
  30.1 8.0 %all-to-all-done.parts_ref = bf16[16,48,256]{2,1,0:T(8,128)(2,1)S(1)} async-done(((bf16[16,48,256]{2,1,0:T(8,128)(2,1)}), bf16[16,48,256]{2,1,0:T(8,128)(2,1)S(1)}, u32[]{:S(2)}, u32[]{:S(2)}) %all-to-all-start) | async-done | bytes 393248 | tf_op jit(solution)/shard_map/all_to_all | solution.py:659
  38.1 0.7 copy-done.9
  38.9 1.9 %rows_kernel.1 = (bf16[16,48,256]{2,1,0:T(8,128)(2,1)}, f32[48,256]{1,0:T(8,128)}, f32[48,1]{1,0:T(8,128)}) custom-call(bf16[16,48,256]{2,1,0:T(8,128)(2,1)} %copy-done.9), custom_call_target="tpu_custom_call" | custom-call | flops 1000000000 | bytes 1000000 | tf_op jit(solution)/shard_map/rows_kernel/pallas_call | solution.py:196
  40.8 21.9 %all_to_all.30.got_ref = bf16[16,48,256]{2,1,0:T(8,128)(2,1)S(1)} all-to-all(bf16[16,48,256]{2,1,0:T(8,128)(2,1)} %get-tuple-element.75), channel_id=1, replica_groups=mesh['dp'=2,'proto'=16] {'proto'}, dimensions={0} | all-to-all | bytes 786432 | tf_op jit(solution)/shard_map/all_to_all | solution.py:681
  62.6 1.7 %collective-permute-done.1.other_ref = bf16[16,48,256]{2,1,0:T(8,128)(2,1)S(1)} collective-permute-done((bf16[16,48,256]{2,1,0:T(8,128)(2,1)S(1)}, bf16[16,48,256]{2,1,0:T(8,128)(2,1)S(1)}, u32[]{:S(2)}, u32[]{:S(2)}) %collective-permute-start.1) | collective-permute-done | bytes 393248 | tf_op jit(solution)/shard_map/ppermute | solution.py:28
  64.4 0.7 copy-done.18
  65.1 3.6 %kern_kernel.1 = (f32[256,2048]{1,0:T(8,128)}, f32[32,2,128]{2,1,0:T(2,128)}, bf16[1280,256]{1,0:T(8,128)(2,1)}) custom-call(s32[1]{0:T(128)} %bitcast.1.d_ref, bf16[16,48,256]{2,1,0:T(8,128)(2,1)} %copy-done.10, bf16[16,48,256]{2,1,0:T(8,128)(2,1)} %copy-done.18, bf16[256,2048]{1,0:T(8,128)(2,1)} %fusion.3.tpnb_ref), custom_call_target="tpu_custom_call" | custom-call | flops 3000000000 | bytes 3000000 | tf_op jit(solution)/shard_map/kern_kernel/pallas_call | solution.py:196
  68.7 5.6 %all-to-all-start.2 = ((f32[32,2,128]{2,1,0:T(2,128)}), f32[32,2,128]{2,1,0:T(2,128)S(1)}, u32[]{:S(2)}, u32[]{:S(2)}) async-start(f32[32,2,128]{2,1,0:T(2,128)} %get-tuple-element.77), calls=%async_computation.2 | async-start | bytes 65536 | tf_op jit(solution)/shard_map/all_to_all | solution.py:690
  74.3 7.0 %student_kernel.1 = (bf16[1280,2048]{1,0:T(8,128)(2,1)}, f32[640,256]{1,0:T(8,128)}, f32[640,256]{1,0:T(8,128)}, f32[1280,1]{1,0:T(8,128)}) custom-call(bf16[1280,256]{1,0:T(8,128)(2,1)} %get-tuple-element.80.z_ref, bf16[256,2048]{1,0:T(8,128)(2,1)} %fusion.1.pnb_ref), custom_call_target="tpu_custom_call" | custom-call | flops 5000000000 | bytes 10000000 | tf_op jit(solution)/shard_map/student_kernel/pallas_call | solution.py:329
  82.5 3.0 %second_kernel.1 = f32[32,1,896]{2,1,0:T(1,128)} custom-call(s32[1]{0:T(128)} %bitcast.1.d_ref, f32[32,2,128]{2,1,0:T(2,128)} %copy-done.14, f32[256,2048]{1,0:T(8,128)} %get-tuple-element.78.kern_ref, f32[1280,1]{1,0:T(8,128)} %get-tuple-element.82.esum_ref), custom_call_target="tpu_custom_call" | custom-call | flops 1000000000 | bytes 1000000 | tf_op jit(solution)/shard_map/second_kernel/pallas_call | solution.py:196
  85.5 5.4 %all-to-all-start.3 = ((f32[32,1,896]{2,1,0:T(1,128)}), f32[32,1,896]{2,1,0:T(1,128)S(1)}, u32[]{:S(2)}, u32[]{:S(2)}) async-start(f32[32,1,896]{2,1,0:T(1,128)} %second_kernel.1), calls=%async_computation.3 | async-start | bytes 229376 | tf_op jit(solution)/shard_map/all_to_all | solution.py:699
  91.0 0.8 add_convert_fusion.sums_ref
  91.8 7.6 %all-to-all-done.3.got_ref = f32[32,1,896]{2,1,0:T(1,128)S(1)} async-done(((f32[32,1,896]{2,1,0:T(1,128)}), f32[32,1,896]{2,1,0:T(1,128)S(1)}, u32[]{:S(2)}, u32[]{:S(2)}) %all-to-all-start.3) | async-done | bytes 114720 | tf_op jit(solution)/shard_map/all_to_all | solution.py:699
  100.0 3.7 %third_kernel.1 = (f32[640,1]{1,0:T(8,128)}, bf16[256,2048]{1,0:T(8,128)(2,1)}, f32[128,384]{1,0:T(8,128)}, f32[128,384]{1,0:T(8,128)}) custom-call(s32[1]{0:T(128)} %bitcast.1.d_ref, f32[32,1,896]{2,1,0:T(1,128)} %copy-done.13, f32[256,2048]{1,0:T(8,128)} %get-tuple-element.78.kern_ref, bf16[256,2048]{1,0:T(8,128)(2,1)} %fusion.1.pnb_ref), custom_call_target="tpu_custom_call" | custom-call | flops 2000000000 | bytes 2000000 | tf_op jit(solution)/shard_map/third_kernel/pallas_call | solution.py:196
  103.7 1.6 collective-permute-done.3.b1_ref
  105.4 0.7 copy-done.19
  106.0 2.1 %message_kernel.1 = bf16[16,56,256]{2,1,0:T(8,128)(2,1)} custom-call(bf16[640,256]{1,0:T(8,128)(2,1)} %add_convert_fusion.sums_ref, f32[128,384]{1,0:T(8,128)} %get-tuple-element.89.b0_ref, f32[128,384]{1,0:T(8,128)} %copy-done.19), custom_call_target="tpu_custom_call" | custom-call | flops 1000000000 | bytes 1000000 | tf_op jit(solution)/shard_map/message_kernel/pallas_call | solution.py:196
  108.2 4.2 %all-to-all-start.4 = ((bf16[16,56,256]{2,1,0:T(8,128)(2,1)}), bf16[16,56,256]{2,1,0:T(8,128)(2,1)}, u32[]{:S(2)}, u32[]{:S(2)}) async-start(bf16[16,56,256]{2,1,0:T(8,128)(2,1)} %message_kernel.1), calls=%async_computation.4 | async-start | bytes 917504 | tf_op jit(solution)/shard_map/all_to_all | solution.py:718
  113.3 1.6 collective-permute-done.4
  115.2 4.3 %convolution_convert_fusion.refs_5_ = bf16[256,2048]{1,0:T(8,128)(2,1)S(1)} fusion(bf16[1280,2048]{1,0:T(8,128)(2,1)} %get-tuple-element.98, bf16[1280,256]{1,0:T(8,128)(2,1)} %get-tuple-element.80.z_ref, f32[1280]{0:T(1024)S(1)} %maximum_reduce_fusion), kind=kOutput, calls=%fused_computation.4 | convolution fusion | flops 1343684608 | bytes 6951936 | tf_op jit(solution)/shard_map/dot_general | solution.py:23
  119.5 7.3 %all-to-all-done.4.got_ref = bf16[16,56,256]{2,1,0:T(8,128)(2,1)} async-done(((bf16[16,56,256]{2,1,0:T(8,128)(2,1)}), bf16[16,56,256]{2,1,0:T(8,128)(2,1)}, u32[]{:S(2)}, u32[]{:S(2)}) %all-to-all-start.4) | async-done | bytes 458784 | tf_op jit(solution)/shard_map/all_to_all | solution.py:718
  126.8 2.2 %bottleneck_kernel.1 = bf16[16,48,256]{2,1,0:T(8,128)(2,1)} custom-call(s32[1]{0:T(128)} %bitcast.p_ref, bf16[16,56,256]{2,1,0:T(8,128)(2,1)} %all-to-all-done.4.got_ref, f32[48,256]{1,0:T(8,128)} %get-tuple-element.100.zn_ref, f32[48,1]{1,0:T(8,128)} %get-tuple-element.101.zinv_ref, f32[640,1]{1,0:T(8,128)} %get-tuple-element.96.view_ref, f32[640,1]{1,0:T(8,128)} %copy-done.3), custom_call_target="tpu_custom_call" | custom-call | flops 1000000000 | bytes 1000000 | tf_op jit(solution)/shard_map/bottleneck_kernel/pallas_call | solution.py:196
  129.0 4.1 %all-to-all-start.5 = ((bf16[16,48,256]{2,1,0:T(8,128)(2,1)}), bf16[16,48,256]{2,1,0:T(8,128)(2,1)S(1)}, u32[]{:S(2)}, u32[]{:S(2)}) async-start(bf16[16,48,256]{2,1,0:T(8,128)(2,1)} %bottleneck_kernel.1), calls=%async_computation.5 | async-start | bytes 786432 | tf_op jit(solution)/shard_map/all_to_all | solution.py:735
  133.2 11.4 %slopes_kernel.1 = (f32[640,2048]{1,0:T(8,128)}, bf16[2048,256]{1,0:T(8,128)(2,1)}, bf16[96,2048]{1,0:T(8,128)(2,1)}) custom-call(s32[1]{0:T(128)} %bitcast.1.d_ref, s32[1]{0:T(128)} %bitcast.p_ref, bf16[640,1536]{1,0:T(8,128)(2,1)} %refs_9_.1, bf16[16,896,128]{2,1,0:T(8,128)(2,1)} %bitcast.6, bf16[16,896,128]{2,1,0:T(8,128)(2,1)} %collective-permute-done.5.other_ref), custom_call_target="tpu_custom_call" | custom-call | flops 10000000000 | bytes 30000000 | tf_op jit(solution)/shard_map/slopes_kernel/pallas_call | solution.py:454
  145.9 4.7 %features_kernel.1 = (bf16[640,256]{1,0:T(8,128)(2,1)}, bf16[96,640]{1,0:T(8,128)(2,1)}) custom-call(bf16[16,48,256]{2,1,0:T(8,128)(2,1)} %copy-done.1, f32[1,640]{1,0:T(1,128)} %get-tuple-element.109.refs_1_, f32[640,2048]{1,0:T(8,128)} %get-tuple-element.110.refs_2_, bf16[2048,256]{1,0:T(8,128)(2,1)} %get-tuple-element.111.refs_3_, ...), custom_call_target="tpu_custom_call" | custom-call | tf_op jit(solution)/shard_map/features_kernel/pallas_call | solution.py:520
  151.8 8.6 %last_kernel.1 = (f32[256,4096]{1,0:T(8,128)}, f32[1536,128]{1,0:T(8,128)}, f32[128,256]{1,0:T(8,128)}) custom-call(s32[1]{0:T(128)} %bitcast.1.d_ref, bf16[640,256]{1,0:T(8,128)(2,1)} %get-tuple-element.114.refs_0_, bf16[16,48,256]{2,1,0:T(8,128)(2,1)} %copy-done.1, bf16[16,48,256]{2,1,0:T(8,128)(2,1)} %copy-done.8, f32[1,640]{1,0:T(1,128)} %copy-done.16, ...), custom_call_target="tpu_custom_call" | custom-call | tf_op jit(solution)/shard_map/last_kernel/pallas_call | solution.py:598
  (65 shorter events, 6.0 us)
Async XLA Ops:
  7.2 100.9 %all-gather.3.cloned.1.call-start = ((), (), s32[]{:S(2)}) async-start(), calls=%async_computation.6 | async-start | bytes 3899392 | tf_op jit(solution)/shard_map/all_gather | solution.py:658
  7.2 14.1 %collective-permute-start = (bf16[640,1536]{1,0:T(8,128)(2,1)}, bf16[640,1536]{1,0:T(8,128)(2,1)}, u32[]{:S(2)}, u32[]{:S(2)}) collective-permute-start(bf16[640,1536]{1,0:T(8,128)(2,1)} %refs_9_.1), channel_id=1, source_target_pairs={{0,16},{16,0},{1,17},{17,1},{2,18},{18,2},{3,19},{19,3},{4,20},{20... | collective-permute-start | bytes 5898248 | tf_op jit(solution)/shard_map/ppermute | solution.py:28
  7.7 13.6 %copy-start = (bf16[256,4096]{1,0:T(8,128)(2,1)S(1)}, bf16[256,4096]{1,0:T(8,128)(2,1)}, u32[]{:S(2)}) copy-start(bf16[256,4096]{1,0:T(8,128)(2,1)} %refs_4_.3) | copy-start | bytes 6291460
  13.4 24.8 %all-to-all-start = ((bf16[16,48,256]{2,1,0:T(8,128)(2,1)}), bf16[16,48,256]{2,1,0:T(8,128)(2,1)S(1)}, u32[]{:S(2)}, u32[]{:S(2)}) async-start(bf16[16,48,256]{2,1,0:T(8,128)(2,1)} %get-tuple-element.64), calls=%async_computation | async-start | bytes 786432 | tf_op jit(solution)/shard_map/all_to_all | solution.py:659
  24.2 4.7 %copy-start.2 = (bf16[256,4096]{1,0:T(8,128)(2,1)S(1)}, bf16[256,4096]{1,0:T(8,128)(2,1)}, u32[]{:S(2)}) copy-start(bf16[256,4096]{1,0:T(8,128)(2,1)} %param.19) | copy-start | bytes 6291460
  38.1 0.7 copy-start.9
  62.6 1.7 %copy-start.10 = (bf16[16,48,256]{2,1,0:T(8,128)(2,1)}, bf16[16,48,256]{2,1,0:T(8,128)(2,1)S(1)}, u32[]{:S(2)}) copy-start(bf16[16,48,256]{2,1,0:T(8,128)(2,1)S(1)} %all_to_all.30.got_ref) | copy-start | bytes 1179652
  62.6 1.7 %collective-permute-start.1 = (bf16[16,48,256]{2,1,0:T(8,128)(2,1)S(1)}, bf16[16,48,256]{2,1,0:T(8,128)(2,1)S(1)}, u32[]{:S(2)}, u32[]{:S(2)}) collective-permute-start(bf16[16,48,256]{2,1,0:T(8,128)(2,1)S(1)} %all_to_all.30.got_ref), channel_id=1, source_target_pairs={{0,16},{16,0},{1,17},{17,1},{2,18},{18,2},{3,19},{19,3},{4,20},{20... | collective-permute-start | bytes 1179656 | tf_op jit(solution)/shard_map/ppermute | solution.py:28
  64.4 0.8 copy-start.18
  68.7 13.2 %all-to-all-start.2 = ((f32[32,2,128]{2,1,0:T(2,128)}), f32[32,2,128]{2,1,0:T(2,128)S(1)}, u32[]{:S(2)}, u32[]{:S(2)}) async-start(f32[32,2,128]{2,1,0:T(2,128)} %get-tuple-element.77), calls=%async_computation.2 | async-start | bytes 65536 | tf_op jit(solution)/shard_map/all_to_all | solution.py:690
  81.3 4.3 %copy-start.17 = (f32[640,256]{1,0:T(8,128)S(1)}, f32[640,256]{1,0:T(8,128)}, u32[]{:S(2)}) copy-start(f32[640,256]{1,0:T(8,128)} %get-tuple-element.86) | copy-start | bytes 1966084
  81.3 9.7 %copy-start.7 = (f32[640,256]{1,0:T(8,128)S(1)}, f32[640,256]{1,0:T(8,128)}, u32[]{:S(2)}) copy-start(f32[640,256]{1,0:T(8,128)} %get-tuple-element.85) | copy-start | bytes 1966084
  85.5 5.4 %collective-permute-start.2 = (f32[640,256]{1,0:T(8,128)S(1)}, f32[640,256]{1,0:T(8,128)S(1)}, u32[]{:S(2)}, u32[]{:S(2)}) collective-permute-start(f32[640,256]{1,0:T(8,128)S(1)} %copy-done.17), channel_id=1, source_target_pairs={{0,16},{16,0},{1,17},{17,1},{2,18},{18,2},{3,19},{19,3},{4,20},{20... | collective-permute-start | bytes 1966088 | tf_op jit(solution)/shard_map/ppermute | solution.py:28
  85.5 13.9 %all-to-all-start.3 = ((f32[32,1,896]{2,1,0:T(1,128)}), f32[32,1,896]{2,1,0:T(1,128)S(1)}, u32[]{:S(2)}, u32[]{:S(2)}) async-start(f32[32,1,896]{2,1,0:T(1,128)} %second_kernel.1), calls=%async_computation.3 | async-start | bytes 229376 | tf_op jit(solution)/shard_map/all_to_all | solution.py:699
  103.7 1.7 collective-permute-start.3
  106.0 6.4 %copy-start.11 = (f32[640,1]{1,0:T(8,128)S(1)}, f32[640,1]{1,0:T(8,128)}, u32[]{:S(2)}) copy-start(f32[640,1]{1,0:T(8,128)} %get-tuple-element.96.view_ref) | copy-start | bytes 7684
  106.0 6.5 %copy-start.12 = (f32[640,1]{1,0:T(8,128)S(1)}, f32[640,1]{1,0:T(8,128)}, u32[]{:S(2)}) copy-start(f32[640,1]{1,0:T(8,128)} %get-tuple-element.97) | copy-start | bytes 7684
  106.0 7.1 %copy-start.4 = (bf16[256,2048]{1,0:T(8,128)(2,1)S(1)}, bf16[256,2048]{1,0:T(8,128)(2,1)}, u32[]{:S(2)}) copy-start(bf16[256,2048]{1,0:T(8,128)(2,1)} %get-tuple-element.116.refs_7_) | copy-start | bytes 3145732
  108.1 25.1 %collective-permute-start.5 = (bf16[16,896,128]{2,1,0:T(8,128)(2,1)}, bf16[16,896,128]{2,1,0:T(8,128)(2,1)}, u32[]{:S(2)}, u32[]{:S(2)}) collective-permute-start(bf16[16,896,128]{2,1,0:T(8,128)(2,1)} %bitcast.5), channel_id=1, source_target_pairs={{0,16},{16,0},{1,17},{17,1},{2,18},{18,2},{3,19},{19,3},{4,20},{20... | collective-permute-start | bytes 11010056 | tf_op jit(solution)/shard_map/ppermute | solution.py:28
  108.2 18.5 %all-to-all-start.4 = ((bf16[16,56,256]{2,1,0:T(8,128)(2,1)}), bf16[16,56,256]{2,1,0:T(8,128)(2,1)}, u32[]{:S(2)}, u32[]{:S(2)}) async-start(bf16[16,56,256]{2,1,0:T(8,128)(2,1)} %message_kernel.1), calls=%async_computation.4 | async-start | bytes 917504 | tf_op jit(solution)/shard_map/all_to_all | solution.py:718
  112.6 6.9 %copy-start.3 = (f32[640,1]{1,0:T(8,128)}, f32[640,1]{1,0:T(8,128)S(1)}, u32[]{:S(2)}) copy-start(f32[640,1]{1,0:T(8,128)S(1)} %multiply_divide_fusion.scale_ref) | copy-start | bytes 7684
  112.6 2.4 %collective-permute-start.4 = (f32[640,1]{1,0:T(8,128)S(1)}, f32[640,1]{1,0:T(8,128)S(1)}, u32[]{:S(2)}, u32[]{:S(2)}) collective-permute-start(f32[640,1]{1,0:T(8,128)S(1)} %multiply_divide_fusion.scale_ref), channel_id=1, source_target_pairs={{0,16},{16,0},{1,17},{17,1},{2,18},{18,2},{3,19},{19,3},{4,20},{20... | collective-permute-start | bytes 7688 | tf_op jit(solution)/shard_map/ppermute | solution.py:28
  113.1 37.5 %collective-permute-start.9 = (bf16[256,2048]{1,0:T(8,128)(2,1)S(1)}, bf16[256,2048]{1,0:T(8,128)(2,1)S(1)}, u32[]{:S(2)}, u32[]{:S(2)}) collective-permute-start(bf16[256,2048]{1,0:T(8,128)(2,1)S(1)} %copy-done.4), channel_id=1, source_target_pairs={{0,16},{16,0},{1,17},{17,1},{2,18},{18,2},{3,19},{19,3},{4,20},{20... | collective-permute-start | bytes 3145736 | tf_op jit(solution)/shard_map/ppermute | solution.py:28
  119.5 13.6 %copy-start.6 = (bf16[256,2048]{1,0:T(8,128)(2,1)}, bf16[256,2048]{1,0:T(8,128)(2,1)S(1)}, u32[]{:S(2)}) copy-start(bf16[256,2048]{1,0:T(8,128)(2,1)S(1)} %convolution_convert_fusion.refs_5_) | copy-start | bytes 3145732
  129.0 16.1 %all-to-all-start.5 = ((bf16[16,48,256]{2,1,0:T(8,128)(2,1)}), bf16[16,48,256]{2,1,0:T(8,128)(2,1)S(1)}, u32[]{:S(2)}, u32[]{:S(2)}) async-start(bf16[16,48,256]{2,1,0:T(8,128)(2,1)} %bottleneck_kernel.1), calls=%async_computation.5 | async-start | bytes 786432 | tf_op jit(solution)/shard_map/all_to_all | solution.py:735
  133.1 12.1 %copy-start.15 = (f32[1,640]{1,0:T(1,128)S(1)}, f32[1,640]{1,0:T(1,128)}, u32[]{:S(2)}) copy-start(f32[1,640]{1,0:T(1,128)} %get-tuple-element.109.refs_1_) | copy-start | bytes 7684
  133.2 17.5 %collective-permute-start.8 = (bf16[256,2048]{1,0:T(8,128)(2,1)S(1)}, bf16[256,2048]{1,0:T(8,128)(2,1)}, u32[]{:S(2)}, u32[]{:S(2)}) collective-permute-start(bf16[256,2048]{1,0:T(8,128)(2,1)S(1)} %convolution_convert_fusion.refs_5_), channel_id=1, source_target_pairs={{0,16},{16,0},{1,17},{17,1},{2,18},{18,2},{3,19},{19,3},{4,20},{20... | collective-permute-start | bytes 3145736 | tf_op jit(solution)/shard_map/ppermute | solution.py:28
  145.1 0.7 copy-start.1
  145.1 5.5 %collective-permute-start.6 = (bf16[16,48,256]{2,1,0:T(8,128)(2,1)S(1)}, bf16[16,48,256]{2,1,0:T(8,128)(2,1)S(1)}, u32[]{:S(2)}, u32[]{:S(2)}) collective-permute-start(bf16[16,48,256]{2,1,0:T(8,128)(2,1)S(1)} %all-to-all-done.5.refs_0_.refs_1_), channel_id=1, source_target_pairs={{0,16},{16,0},{1,17},{17,1},{2,18},{18,2},{3,19},{19,3},{4,20},{20... | collective-permute-start | bytes 1179656 | tf_op jit(solution)/shard_map/ppermute | solution.py:28
  145.2 5.4 %collective-permute-start.7 = (f32[1,640]{1,0:T(1,128)S(1)}, f32[1,640]{1,0:T(1,128)S(1)}, u32[]{:S(2)}, u32[]{:S(2)}) collective-permute-start(f32[1,640]{1,0:T(1,128)S(1)} %copy-done.15), channel_id=1, source_target_pairs={{0,16},{16,0},{1,17},{17,1},{2,18},{18,2},{3,19},{19,3},{4,20},{20... | collective-permute-start | bytes 7688 | tf_op jit(solution)/shard_map/ppermute | solution.py:28
  150.7 1.0 copy-start.5
  150.7 1.1 copy-start.8
  (4 other events, 2.5 us)
Sparse Core Ops, SparseCore 0:
  13.5 82.9 all-gather.2

commit v6 on v5

--- a/solution.py
+++ b/solution.py
@@ -9,6 +9,7 @@
 
 ITERS = 3
 ALL = ("dp", "proto")
+NEAR = 4
 F32 = jnp.float32
 BF16 = jnp.bfloat16
 
@@ -434,12 +435,14 @@
     act = dot(f_ref[:, :deep], a, ((1,), (0,))) + dot(f_ref[:, deep:], b, ((1,), (0,)))
     phi = 0.5 * (1.0 + lax.erf(act * 0.7071067811865476))
     slope_ref[...] = phi + act * jnp.exp(-0.5 * act * act) * 0.3989422804014327
-    width = w1_ref.shape[0]
+    groups, width = w1_ref.shape[0], w1_ref.shape[1]
     blocks = deep // width
-    at = pl.multiple_of(lax.rem(p_ref[0], blocks) * width, width)
-    mine = (p_ref[0] // blocks) == d_ref[0]
-    rows = jnp.where(mine, own_ref[:, pl.ds(at, width)], other_ref[:, pl.ds(at, width)])
-    w1_ref[...] = jnp.concatenate([rows[0], rows[1]], axis=1)
+    for k in range(groups):
+        chip = p_ref[0] ^ (k * NEAR)
+        at = pl.multiple_of(lax.rem(chip, blocks) * width, width)
+        mine = (chip // blocks) == d_ref[0]
+        rows = jnp.where(mine, own_ref[:, pl.ds(at, width)], other_ref[:, pl.ds(at, width)])
+        w1_ref[k] = jnp.concatenate([rows[0], rows[1]], axis=1)
     half = hs // 2
     for k in range(2):
         for part, x in ((0, low), (1, high)):
@@ -447,7 +450,7 @@
             w2_ref[k * hs + part * half : k * hs + (part + 1) * half] = tail
 
 
-def slopes_of(d, p, features, own, other, width):
+def slopes_of(d, p, features, own, other, width, groups):
     n, tall, hs = own.shape
     rows = features.shape[0]
     whole = lambda k, d, p: (0, 0)
@@ -465,12 +468,12 @@
             out_specs=(
                 pl.BlockSpec((rows, 2 * hs), lambda k, d, p: (0, k)),
                 pl.BlockSpec((2 * hs, 2 * hs), lambda k, d, p: (k, 0)),
-                pl.BlockSpec((width, 2 * hs), lambda k, d, p: (0, k)),
+                pl.BlockSpec((groups, width, 2 * hs), lambda k, d, p: (0, 0, k)),
             ),
         ),
-        out_shape=(shape((rows, n * hs), F32), shape((n * hs, 2 * hs), BF16), shape((width, n * hs), BF16)),
+        out_shape=(shape((rows, n * hs), F32), shape((n * hs, 2 * hs), BF16), shape((groups, width, n * hs), BF16)),
         compiler_params=params(),
-        cost_estimate=pl.CostEstimate(flops=10**10, bytes_accessed=3 * 10**7, transcendentals=0),
+        cost_estimate=pl.CostEstimate(flops=4 * 10**9, bytes_accessed=3 * 10**7, transcendentals=0),
     )(d.reshape(1), p.reshape(1), features, own, other)
 
 
@@ -491,8 +494,9 @@
 
 
 def features_kernel(step, *refs):
-    ins, (dz_ref, out_ref), held, sems = refs[:5], refs[5:7], refs[7:12], refs[12]
+    ins, (dz_ref, own_ref, far_ref), held, sems = refs[:5], refs[5:8], refs[8:13], refs[13]
     got, place, slope, w2, w1 = held
+    groups, width = w1.shape[:2]
     pieces = [pl.ds(k, step) for k in range(0, slope.shape[1], step)]
     small = fetch([(ins[k], held[k]) for k in (0, 1, 4)], sems.at[pl.ds(0, 3)])
     large = []
@@ -508,22 +512,26 @@
         for copy in copies:
             copy.wait()
         dhid = (dot(dz, w2[piece], ((1,), (1,))) * slope[:, piece]).astype(BF16)
-        part = dot(w1[:, piece], dhid, ((1,), (1,)))
+        part = dot(w1[:, :, piece].reshape(groups * width, step), dhid, ((1,), (1,)))
         total = part if total is None else total + part
-    out_ref[...] = total.astype(BF16)
+    own_ref[...] = total[:width]
+    for k in range(1, groups):
+        far_ref[k - 1] = total[k * width : (k + 1) * width].astype(BF16)
 
 
 def feature_grads(got, place, slope, w2, w1):
     args = (got, place, slope, w2, w1)
     rows, hidden = slope.shape
-    bot, step = got.shape[2], 512
+    bot, step = got.shape[2], 256
+    groups, width = w1.shape[:2]
+    outs = (shape((rows, bot), BF16), shape((width, rows), F32), shape((groups - 1, width, rows), BF16))
     return pl.pallas_call(
         functools.partial(features_kernel, step),
         name="features_kernel",
         grid=(1,),
-        out_shape=(shape((rows, bot), BF16), shape((w1.shape[0], rows), BF16)),
+        out_shape=outs,
         in_specs=[pl.BlockSpec(memory_space=pl.ANY)] * len(args),
-        out_specs=(block((rows, bot)), block((w1.shape[0], rows))),
+        out_specs=tuple(block(x.shape) for x in outs),
         scratch_shapes=[pltpu.VMEM(x.shape, x.dtype) for x in args]
         + [pltpu.SemaphoreType.DMA((3 + 2 * (hidden // step),))],
         compiler_params=params(),
@@ -655,7 +663,7 @@
         compiler_params=params(),
         name="head_kernel",
     )(d.reshape(1), *heads, crop_image, crop_view)
-    weights = lax.all_gather(weights, "proto")
+    weights = [weights] + [swap(weights, "proto", k) for k in range(1, NEAR)]
     parts_got = lax.all_to_all(parts, "proto", 0, 0)
     w1_late, protos_late, tprotos_late, feat_late, feat_other_late, _ = tied(
         head_w1, protos, teacher_protos, features, feat_other, parts
@@ -670,7 +678,8 @@
     cols = protos.shape[1] // nd
     pnb = unit_cols(lax.dynamic_slice_in_dim(protos_late, d * cols, cols, 1))[0].astype(BF16)
     tpnb = unit_cols(lax.dynamic_slice_in_dim(tprotos_late, d * cols, cols, 1))[0].astype(BF16)
-    parts_got, h0, h1, s0, s1, pnb, tpnb = tied(parts_got, h0, h1, s0, s1, pnb, tpnb)
+    weights = jnp.stack(weights)
+    parts_got, h0, h1, s0, s1, pnb, tpnb, weights = tied(parts_got, h0, h1, s0, s1, pnb, tpnb, weights)
 
     got, zn, zinv = call(
         rows_kernel,
@@ -734,23 +743,25 @@
     )
     got = lax.all_to_all(dz, "proto", 0, 0)
     weights, feat_late, _ = tied(weights, features, dz)
-    slopes = slopes_of(d, p, feat_late, weights, weights_other, wide // n)
+    slopes = slopes_of(d, p, feat_late, weights, weights_other, wide // n, n // NEAR)
     got, slopes = tied(got, slopes)
 
     got_other = swap(got, "dp", 1)
-    dz, grad_features = feature_grads(got, place, *slopes)
+    dz, grad_features, far = feature_grads(got, place, *slopes)
+    far = [swap(far[k - 1], "proto", k * NEAR) for k in range(1, n // NEAR)]
     grad_protos, grad_w1, grad_w2 = last_grads(
         d, head_w1, dz, got, got_other, place_other, protos, dpn, dpn_other, last, last_other,
         features, feat_other, h0, h1, s0, s1, head_w2,
     )
-    grad_features = grad_features.T
+    grad_protos, *far = tied(grad_protos, *far)
+    grad_features = (grad_features + sum(x.astype(F32) for x in far)).astype(BF16).T
     return (grad_features, grad_w1, grad_w2, grad_protos)
 
 
 def body(features, teacher_features, *rest):
     n = lax.axis_size("proto")
     slot = (features.shape[0] // n, teacher_features.shape[0] // n)
-    paired = lax.axis_size("dp") == 2 and n % 2 == 0 and slot[0] % 8 == 0 and slot[1] % 8 == 0
+    paired = lax.axis_size("dp") == 2 and n == 4 * NEAR and slot[0] % 8 == 0 and slot[1] % 8 == 0
     paired = paired and features.shape[0] % teacher_features.shape[0] == 0
     return (paired_body if paired else general_body)(features, teacher_features, *rest)
 

time: 168 us -> 156 us (0.929)
  between operations: 14.3 us -> 0.95 us
  Pallas kernels: 58.5 us -> 50.2 us
  starting transfers between devices: 29.1 us -> 34.3 us
  other arithmetic: 5.03 us -> 7.89 us
  waiting for transfers between devices: 29 us -> 31.3 us
  blocking collectives: 21.9 us -> 20.1 us
    ppermute x10 -> x16, starting transfers between devices: 1.88 us -> 10.6 us  [swap(): return lax.ppermute(value, axis, [(i, i ^ step) for i in range(count)])]
    all_to_all x1, waiting for transfers between devices: 8.03 us -> 0.01 us  [paired_body(): parts_got = lax.all_to_all(parts, 'proto', 0, 0)]
    pallas_call x1, Pallas kernels: 11.4 us -> 4.48 us  [slopes_of(): pl.pallas_call(slopes_kernel, name='slopes_kernel', grid_spec=pltpu.Prefe...]
    all_to_all x1, waiting for transfers between devices: 0.49 us -> 7.31 us  [paired_body(): got = lax.all_to_all(dz, 'proto', 0, 0)]
    ppermute x10 -> x16, waiting for transfers between devices: 5.03 us -> 8.87 us  [swap(): return lax.ppermute(value, axis, [(i, i ^ step) for i in range(count)])]
    all_to_all x2, starting transfers between devices: 11 us -> 8.37 us  [paired_body(): msg_got = lax.all_to_all(msg, ALL, 0, 0)]
    another operation x0 -> x1, other arithmetic: none -> 2 us  [paired_body(): weights = jnp.stack(weights)]
    all_to_all x1, blocking collectives: 21.9 us -> 20.1 us  [paired_body(): got = lax.all_to_all(got, 'proto', 0, 0)]
  transfers between devices with their start and end apart: 16 -> 21, of which waited for: 8 -> 8; matrix products, arithmetic and copies ran while one was open for 6% -> 8% of each run, Pallas kernels for 30% -> 23%
where the time goes in v6:
time: 156 us; the launch traced here: 155 us
  Pallas kernels  50.2 us (32%)
  starting transfers between devices  34.3 us (22%)
  waiting for transfers between devices  31.3 us (20%)
  blocking collectives  20.1 us (13%)
  other arithmetic  7.89 us (5%)
  local copies, waits for them, and re-layouts  5.75 us (4%)
  matrix products  4.34 us (3%)
    pallas_call x7, Pallas kernels, call(): pl.pallas_call(kernel, grid=(1,), out_shape=outs, in_specs=[pl.BlockSpec(...  20.9 us
    all_to_all x1, blocking collectives, paired_body(): got = lax.all_to_all(got, 'proto', 0, 0)  20.1 us
    ppermute x16, starting transfers between devices, swap(): return lax.ppermute(value, axis, [(i, i ^ step) for i in range(count)])  10.6 us
    ppermute x16, waiting for transfers between devices, swap(): return lax.ppermute(value, axis, [(i, i ^ step) for i in range(count)])  8.87 us
    pallas_call x1, Pallas kernels, last_grads(): pl.pallas_call(functools.partial(last_kernel, tile), name='last_kernel',...  8.59 us
    all_to_all x2, starting transfers between devices, paired_body(): msg_got = lax.all_to_all(msg, ALL, 0, 0)  8.37 us
    all_to_all x1, waiting for transfers between devices, paired_body(): msg_got = lax.all_to_all(msg, 'proto', 0, 0)  7.99 us
    all_to_all x1, waiting for transfers between devices, paired_body(): got = lax.all_to_all(dz, 'proto', 0, 0)  7.31 us
  transfers between devices with their start and end apart: 21, of which 8 were waited for; matrix products, arithmetic and copies ran while one was open for 8% of the time, Pallas kernels for 23%

profile of v6, /device:TPU:0, one launch (start us, length us, event | category | flops | bytes accessed | tf_op | source)
XLA Modules:
  0.0 154.8 jit_solution(10635103203712132244)
XLA Ops:
  1.2 5.4 %head_kernel.1 = (bf16[16,48,256]{2,1,0:T(8,128)(2,1)}, f32[1,640]{1,0:T(1,128)}, f32[640,1]{1,0:T(8,128)}, bf16[896,128]{1,0:T(8,128)(2,1)}) custom-call(s32[1]{0:T(128)} %bitcast.1.d_ref, bf16[640,1536]{1,0:T(8,128)(2,1)} %refs_9_.1, bf16[1536,128]{1,0:T(8,128)(2,1)} %w1_ref, bf16[128,256]{1,0:T(8,128)(2,1)} %refs_15_.1, bf16[128,1536]{1,0:T(8,128)(2,1)} %refs_3_.1, ...), custom_call_target="tpu_custom_call" | custom-call | tf_op jit(solution)/shard_map/head_kernel/pallas_call | solution.py:649
  6.6 3.5 %collective-permute-start.3 = (bf16[896,128]{1,0:T(8,128)(2,1)}, bf16[896,128]{1,0:T(8,128)(2,1)S(1)}, u32[]{:S(2)}, u32[]{:S(2)}) collective-permute-start(bf16[896,128]{1,0:T(8,128)(2,1)} %get-tuple-element.80), channel_id=1, source_target_pairs={{0,3},{1,2},{2,1},{3,0},{4,7},{5,6},{6,5},{7,4},{8,11},{9,10},{10,... | collective-permute-start | bytes 688136 | tf_op jit(solution)/shard_map/ppermute | solution.py:29
  10.8 7.3 %all-to-all-start = ((bf16[16,48,256]{2,1,0:T(8,128)(2,1)}), bf16[16,48,256]{2,1,0:T(8,128)(2,1)S(1)}, u32[]{:S(2)}, u32[]{:S(2)}) async-start(bf16[16,48,256]{2,1,0:T(8,128)(2,1)} %get-tuple-element.70), calls=%async_computation | async-start | bytes 786432 | tf_op jit(solution)/shard_map/all_to_all | solution.py:667
  18.1 4.6 %collective-permute-done.2 = bf16[896,128]{1,0:T(8,128)(2,1)S(1)} collective-permute-done((bf16[896,128]{1,0:T(8,128)(2,1)}, bf16[896,128]{1,0:T(8,128)(2,1)S(1)}, u32[]{:S(2)}, u32[]{:S(2)}) %collective-permute-start.2) | collective-permute-done | bytes 229408 | tf_op jit(solution)/shard_map/ppermute | solution.py:29
  22.8 2.0 %pad_maximum_fusion.own_ref = bf16[4,896,128]{2,1,0:T(8,128)(2,1)} fusion(bf16[1,896,128]{2,1,0:T(8,128)(2,1)S(1)} %bitcast.16, bf16[1,896,128]{2,1,0:T(8,128)(2,1)S(1)} %bitcast.17, bf16[1,896,128]{2,1,0:T(8,128)(2,1)S(1)} %bitcast.18, bf16[1,896,128]{2,1,0:T(8,128)(2,1)} %bitcast.15), kind=kLoop, calls=%fused_computation.10 | loop fusion | flops 1376256 | bytes 1835008 | tf_op jit(solution)/shard_map/stack | solution.py:681
  24.8 1.7 %fusion = (f32[2048]{0:T(1024)S(1)}, f32[2048]{0:T(1024)S(1)}) fusion(bf16[256,4096]{1,0:T(8,128)(2,1)S(1)} %copy-done, s32[]{:T(128)S(6)} %select_n.8, bf16[256,4096]{1,0:T(8,128)(2,1)} %param.19), kind=kLoop, calls=%fused_computation.5 | loop fusion | flops 3141632 | bytes 2113540 | tf_op jit(solution)/shard_map/reduce_sum | solution.py:49
  26.5 1.4 fusion.3.tpnb_ref
  27.8 4.4 %hidden_kernel.1 = (bf16[128,640]{1,0:T(8,128)(2,1)}, bf16[128,640]{1,0:T(8,128)(2,1)}, f32[128,640]{1,0:T(8,128)}, f32[128,640]{1,0:T(8,128)}) custom-call(bf16[640,1536]{1,0:T(8,128)(2,1)} %refs_9_.1, bf16[640,1536]{1,0:T(8,128)(2,1)} %collective-permute-done.f1_ref.refs_10_, bf16[1536,128]{1,0:T(8,128)(2,1)} %w1_ref), custom_call_target="tpu_custom_call" | custom-call | flops 4000000000 | bytes 4000000 | tf_op jit(solution)/shard_map/hidden_kernel/pallas_call | solution.py:197
  32.3 1.2 fusion.1.pnb_ref
  34.2 1.9 %rows_kernel.1 = (bf16[16,48,256]{2,1,0:T(8,128)(2,1)}, f32[48,256]{1,0:T(8,128)}, f32[48,1]{1,0:T(8,128)}) custom-call(bf16[16,48,256]{2,1,0:T(8,128)(2,1)} %copy-done.9), custom_call_target="tpu_custom_call" | custom-call | flops 1000000000 | bytes 1000000 | tf_op jit(solution)/shard_map/rows_kernel/pallas_call | solution.py:197
  36.1 20.1 %all_to_all.30.got_ref = bf16[16,48,256]{2,1,0:T(8,128)(2,1)S(1)} all-to-all(bf16[16,48,256]{2,1,0:T(8,128)(2,1)} %get-tuple-element.82), channel_id=1, replica_groups=mesh['dp'=2,'proto'=16] {'proto'}, dimensions={0} | all-to-all | bytes 786432 | tf_op jit(solution)/shard_map/all_to_all | solution.py:690
  56.2 1.7 %collective-permute-done.4.other_ref = bf16[16,48,256]{2,1,0:T(8,128)(2,1)S(1)} collective-permute-done((bf16[16,48,256]{2,1,0:T(8,128)(2,1)S(1)}, bf16[16,48,256]{2,1,0:T(8,128)(2,1)S(1)}, u32[]{:S(2)}, u32[]{:S(2)}) %collective-permute-start.4) | collective-permute-done | bytes 393248 | tf_op jit(solution)/shard_map/ppermute | solution.py:29
  58.7 3.6 %kern_kernel.1 = (f32[256,2048]{1,0:T(8,128)}, f32[32,2,128]{2,1,0:T(2,128)}, bf16[1280,256]{1,0:T(8,128)(2,1)}) custom-call(s32[1]{0:T(128)} %bitcast.1.d_ref, bf16[16,48,256]{2,1,0:T(8,128)(2,1)} %copy-done.10, bf16[16,48,256]{2,1,0:T(8,128)(2,1)} %copy-done.19, bf16[256,2048]{1,0:T(8,128)(2,1)} %fusion.3.tpnb_ref), custom_call_target="tpu_custom_call" | custom-call | flops 3000000000 | bytes 3000000 | tf_op jit(solution)/shard_map/kern_kernel/pallas_call | solution.py:197
  62.3 2.6 %all-to-all-start.2 = ((f32[32,2,128]{2,1,0:T(2,128)}), f32[32,2,128]{2,1,0:T(2,128)S(1)}, u32[]{:S(2)}, u32[]{:S(2)}) async-start(f32[32,2,128]{2,1,0:T(2,128)} %get-tuple-element.84), calls=%async_computation.2 | async-start | bytes 65536 | tf_op jit(solution)/shard_map/all_to_all | solution.py:699
  64.9 7.0 %student_kernel.1 = (bf16[1280,2048]{1,0:T(8,128)(2,1)}, f32[640,256]{1,0:T(8,128)}, f32[640,256]{1,0:T(8,128)}, f32[1280,1]{1,0:T(8,128)}) custom-call(bf16[1280,256]{1,0:T(8,128)(2,1)} %get-tuple-element.87.z_ref, bf16[256,2048]{1,0:T(8,128)(2,1)} %fusion.1.pnb_ref), custom_call_target="tpu_custom_call" | custom-call | flops 5000000000 | bytes 10000000 | tf_op jit(solution)/shard_map/student_kernel/pallas_call | solution.py:330
  72.7 3.0 %second_kernel.1 = f32[32,1,896]{2,1,0:T(1,128)} custom-call(s32[1]{0:T(128)} %bitcast.1.d_ref, f32[32,2,128]{2,1,0:T(2,128)} %copy-done.15, f32[256,2048]{1,0:T(8,128)} %get-tuple-element.85.kern_ref, f32[1280,1]{1,0:T(8,128)} %get-tuple-element.89.esum_ref), custom_call_target="tpu_custom_call" | custom-call | flops 1000000000 | bytes 1000000 | tf_op jit(solution)/shard_map/second_kernel/pallas_call | solution.py:197
  75.8 5.7 %all-to-all-start.3 = ((f32[32,1,896]{2,1,0:T(1,128)}), f32[32,1,896]{2,1,0:T(1,128)S(1)}, u32[]{:S(2)}, u32[]{:S(2)}) async-start(f32[32,1,896]{2,1,0:T(1,128)} %second_kernel.1), calls=%async_computation.3 | async-start | bytes 229376 | tf_op jit(solution)/shard_map/all_to_all | solution.py:708
  82.4 7.0 %all-to-all-done.3.got_ref = f32[32,1,896]{2,1,0:T(1,128)S(1)} async-done(((f32[32,1,896]{2,1,0:T(1,128)}), f32[32,1,896]{2,1,0:T(1,128)S(1)}, u32[]{:S(2)}, u32[]{:S(2)}) %all-to-all-start.3) | async-done | bytes 114720 | tf_op jit(solution)/shard_map/all_to_all | solution.py:708
  90.0 3.7 %third_kernel.1 = (f32[640,1]{1,0:T(8,128)}, bf16[256,2048]{1,0:T(8,128)(2,1)}, f32[128,384]{1,0:T(8,128)}, f32[128,384]{1,0:T(8,128)}) custom-call(s32[1]{0:T(128)} %bitcast.1.d_ref, f32[32,1,896]{2,1,0:T(1,128)} %copy-done.14, f32[256,2048]{1,0:T(8,128)} %get-tuple-element.85.kern_ref, bf16[256,2048]{1,0:T(8,128)(2,1)} %fusion.1.pnb_ref), custom_call_target="tpu_custom_call" | custom-call | flops 2000000000 | bytes 2000000 | tf_op jit(solution)/shard_map/third_kernel/pallas_call | solution.py:197
  93.7 1.6 %collective-permute-done.6.b1_ref = f32[128,384]{1,0:T(8,128)S(1)} collective-permute-done((f32[128,384]{1,0:T(8,128)}, f32[128,384]{1,0:T(8,128)S(1)}, u32[]{:S(2)}, u32[]{:S(2)}) %collective-permute-start.6) | collective-permute-done | bytes 196640 | tf_op jit(solution)/shard_map/ppermute | solution.py:29
  96.1 2.1 %message_kernel.1 = bf16[16,56,256]{2,1,0:T(8,128)(2,1)} custom-call(bf16[640,256]{1,0:T(8,128)(2,1)} %add_convert_fusion.sums_ref, f32[128,384]{1,0:T(8,128)} %get-tuple-element.96.b0_ref, f32[128,384]{1,0:T(8,128)} %copy-done.20), custom_call_target="tpu_custom_call" | custom-call | flops 1000000000 | bytes 1000000 | tf_op jit(solution)/shard_map/message_kernel/pallas_call | solution.py:197
  98.1 4.2 %all-to-all-start.4 = ((bf16[16,56,256]{2,1,0:T(8,128)(2,1)}), bf16[16,56,256]{2,1,0:T(8,128)(2,1)}, u32[]{:S(2)}, u32[]{:S(2)}) async-start(bf16[16,56,256]{2,1,0:T(8,128)(2,1)} %message_kernel.1), calls=%async_computation.4 | async-start | bytes 917504 | tf_op jit(solution)/shard_map/all_to_all | solution.py:727
  104.3 4.3 %convolution_convert_fusion.refs_5_ = bf16[256,2048]{1,0:T(8,128)(2,1)S(1)} fusion(bf16[1280,2048]{1,0:T(8,128)(2,1)} %get-tuple-element.105, bf16[1280,256]{1,0:T(8,128)(2,1)} %get-tuple-element.87.z_ref, f32[1280]{0:T(1024)S(1)} %maximum_reduce_fusion), kind=kOutput, calls=%fused_computation.4 | convolution fusion | flops 1343684608 | bytes 6951936 | tf_op jit(solution)/shard_map/dot_general | solution.py:24
  108.7 8.0 %all-to-all-done.4.got_ref = bf16[16,56,256]{2,1,0:T(8,128)(2,1)} async-done(((bf16[16,56,256]{2,1,0:T(8,128)(2,1)}), bf16[16,56,256]{2,1,0:T(8,128)(2,1)}, u32[]{:S(2)}, u32[]{:S(2)}) %all-to-all-start.4) | async-done | bytes 458784 | tf_op jit(solution)/shard_map/all_to_all | solution.py:727
  116.7 2.2 %bottleneck_kernel.1 = bf16[16,48,256]{2,1,0:T(8,128)(2,1)} custom-call(s32[1]{0:T(128)} %bitcast.p_ref, bf16[16,56,256]{2,1,0:T(8,128)(2,1)} %all-to-all-done.4.got_ref, f32[48,256]{1,0:T(8,128)} %get-tuple-element.107.zn_ref, f32[48,1]{1,0:T(8,128)} %get-tuple-element.108.zinv_ref, f32[640,1]{1,0:T(8,128)} %get-tuple-element.103.view_ref, f32[640,1]{1,0:T(8,128)} %copy-done.3), custom_call_target="tpu_custom_call" | custom-call | flops 1000000000 | bytes 1000000 | tf_op jit(solution)/shard_map/bottleneck_kernel/pallas_call | solution.py:197
  118.9 3.9 %all-to-all-start.5 = ((bf16[16,48,256]{2,1,0:T(8,128)(2,1)}), bf16[16,48,256]{2,1,0:T(8,128)(2,1)S(1)}, u32[]{:S(2)}, u32[]{:S(2)}) async-start(bf16[16,48,256]{2,1,0:T(8,128)(2,1)} %bottleneck_kernel.1), calls=%async_computation.5 | async-start | bytes 786432 | tf_op jit(solution)/shard_map/all_to_all | solution.py:744
  122.9 4.5 %slopes_kernel.1 = (f32[640,512]{1,0:T(8,128)}, bf16[512,256]{1,0:T(8,128)(2,1)}, bf16[4,96,512]{2,1,0:T(8,128)(2,1)}) custom-call(s32[1]{0:T(128)} %bitcast.1.d_ref, s32[1]{0:T(128)} %bitcast.p_ref, bf16[640,1536]{1,0:T(8,128)(2,1)} %refs_9_.1, bf16[4,896,128]{2,1,0:T(8,128)(2,1)} %pad_maximum_fusion.own_ref, ...), custom_call_target="tpu_custom_call" | custom-call | flops 4000000000 | bytes 30000000 | tf_op jit(solution)/shard_map/slopes_kernel/pallas_call | solution.py:457
  127.4 7.3 %all-to-all-done.5.refs_0_.refs_1_ = bf16[16,48,256]{2,1,0:T(8,128)(2,1)S(1)} async-done(((bf16[16,48,256]{2,1,0:T(8,128)(2,1)}), bf16[16,48,256]{2,1,0:T(8,128)(2,1)S(1)}, u32[]{:S(2)}, u32[]{:S(2)}) %all-to-all-start.5) | async-done | bytes 393248 | tf_op jit(solution)/shard_map/all_to_all | solution.py:744
  135.4 3.7 %features_kernel.1 = (bf16[640,256]{1,0:T(8,128)(2,1)}, f32[96,640]{1,0:T(8,128)}, bf16[3,96,640]{2,1,0:T(8,128)(2,1)}) custom-call(bf16[16,48,256]{2,1,0:T(8,128)(2,1)} %copy-done.1, f32[1,640]{1,0:T(1,128)} %get-tuple-element.116.refs_1_, f32[640,512]{1,0:T(8,128)} %get-tuple-element.117.refs_2_, bf16[512,256]{1,0:T(8,128)(2,1)} %get-tuple-element.118.refs_3_, ...), custom_call_target="tpu_custom_call" | custom-call | tf_op jit(solution)/shard_map/features_kernel/pallas_call | solution.py:528
  140.2 1.8 %collective-permute-start.15 = (bf16[96,640]{1,0:T(8,128)(2,1)S(1)}, bf16[96,640]{1,0:T(8,128)(2,1)S(1)}, u32[]{:S(2)}, u32[]{:S(2)}) collective-permute-start(bf16[96,640]{1,0:T(8,128)(2,1)S(1)} %get-tuple-element.136), channel_id=1, source_target_pairs={{0,12},{1,13},{2,14},{3,15},{4,8},{5,9},{6,10},{7,11},{8,4},{9,5},... | collective-permute-start | bytes 368648 | tf_op jit(solution)/shard_map/ppermute | solution.py:29
  142.9 1.8 %collective-permute-start.13 = (bf16[96,640]{1,0:T(8,128)(2,1)S(1)}, bf16[96,640]{1,0:T(8,128)(2,1)S(1)}, u32[]{:S(2)}, u32[]{:S(2)}) collective-permute-start(bf16[96,640]{1,0:T(8,128)(2,1)S(1)} %get-tuple-element.138), channel_id=1, source_target_pairs={{0,4},{1,5},{2,6},{3,7},{4,0},{5,1},{6,2},{7,3},{8,12},{9,13},{10,... | collective-permute-start | bytes 368648 | tf_op jit(solution)/shard_map/ppermute | solution.py:29
  145.5 8.6 %last_kernel.1 = (f32[256,4096]{1,0:T(8,128)}, f32[1536,128]{1,0:T(8,128)}, f32[128,256]{1,0:T(8,128)}) custom-call(s32[1]{0:T(128)} %bitcast.1.d_ref, bf16[640,256]{1,0:T(8,128)(2,1)} %get-tuple-element.121.refs_0_, bf16[16,48,256]{2,1,0:T(8,128)(2,1)} %copy-done.1, bf16[16,48,256]{2,1,0:T(8,128)(2,1)} %copy-done.8, f32[1,640]{1,0:T(1,128)} %copy-done.17, ...), custom_call_target="tpu_custom_call" | custom-call | tf_op jit(solution)/shard_map/last_kernel/pallas_call | solution.py:606
  (79 shorter events, 11.8 us)
Async XLA Ops:
  0.6 24.1 %collective-permute-start = (bf16[640,1536]{1,0:T(8,128)(2,1)}, bf16[640,1536]{1,0:T(8,128)(2,1)}, u32[]{:S(2)}, u32[]{:S(2)}) collective-permute-start(bf16[640,1536]{1,0:T(8,128)(2,1)} %refs_9_.1), channel_id=1, source_target_pairs={{0,16},{16,0},{1,17},{17,1},{2,18},{18,2},{3,19},{19,3},{4,20},{20... | collective-permute-start | bytes 5898248 | tf_op jit(solution)/shard_map/ppermute | solution.py:29
  6.6 18.2 %copy-start = (bf16[256,4096]{1,0:T(8,128)(2,1)S(1)}, bf16[256,4096]{1,0:T(8,128)(2,1)}, u32[]{:S(2)}) copy-start(bf16[256,4096]{1,0:T(8,128)(2,1)} %refs_4_.3) | copy-start | bytes 6291460
  6.6 11.5 %collective-permute-start.3 = (bf16[896,128]{1,0:T(8,128)(2,1)}, bf16[896,128]{1,0:T(8,128)(2,1)S(1)}, u32[]{:S(2)}, u32[]{:S(2)}) collective-permute-start(bf16[896,128]{1,0:T(8,128)(2,1)} %get-tuple-element.80), channel_id=1, source_target_pairs={{0,3},{1,2},{2,1},{3,0},{4,7},{5,6},{6,5},{7,4},{8,11},{9,10},{10,... | collective-permute-start | bytes 688136 | tf_op jit(solution)/shard_map/ppermute | solution.py:29
  10.2 12.6 %collective-permute-start.2 = (bf16[896,128]{1,0:T(8,128)(2,1)}, bf16[896,128]{1,0:T(8,128)(2,1)S(1)}, u32[]{:S(2)}, u32[]{:S(2)}) collective-permute-start(bf16[896,128]{1,0:T(8,128)(2,1)} %get-tuple-element.80), channel_id=1, source_target_pairs={{0,2},{1,3},{2,0},{3,1},{4,6},{5,7},{6,4},{7,5},{8,10},{9,11},{10,... | collective-permute-start | bytes 688136 | tf_op jit(solution)/shard_map/ppermute | solution.py:29
  10.7 12.1 %collective-permute-start.1 = (bf16[896,128]{1,0:T(8,128)(2,1)}, bf16[896,128]{1,0:T(8,128)(2,1)S(1)}, u32[]{:S(2)}, u32[]{:S(2)}) collective-permute-start(bf16[896,128]{1,0:T(8,128)(2,1)} %get-tuple-element.80), channel_id=1, source_target_pairs={{0,1},{1,0},{2,3},{3,2},{4,5},{5,4},{6,7},{7,6},{8,9},{9,8},{10,11... | collective-permute-start | bytes 688136 | tf_op jit(solution)/shard_map/ppermute | solution.py:29
  10.8 22.7 %all-to-all-start = ((bf16[16,48,256]{2,1,0:T(8,128)(2,1)}), bf16[16,48,256]{2,1,0:T(8,128)(2,1)S(1)}, u32[]{:S(2)}, u32[]{:S(2)}) async-start(bf16[16,48,256]{2,1,0:T(8,128)(2,1)} %get-tuple-element.70), calls=%async_computation | async-start | bytes 786432 | tf_op jit(solution)/shard_map/all_to_all | solution.py:667
  18.1 8.4 %copy-start.2 = (bf16[256,4096]{1,0:T(8,128)(2,1)S(1)}, bf16[256,4096]{1,0:T(8,128)(2,1)}, u32[]{:S(2)}) copy-start(bf16[256,4096]{1,0:T(8,128)(2,1)} %param.19) | copy-start | bytes 6291460
  56.2 1.7 %collective-permute-start.4 = (bf16[16,48,256]{2,1,0:T(8,128)(2,1)S(1)}, bf16[16,48,256]{2,1,0:T(8,128)(2,1)S(1)}, u32[]{:S(2)}, u32[]{:S(2)}) collective-permute-start(bf16[16,48,256]{2,1,0:T(8,128)(2,1)S(1)} %all_to_all.30.got_ref), channel_id=1, source_target_pairs={{0,16},{16,0},{1,17},{17,1},{2,18},{18,2},{3,19},{19,3},{4,20},{20... | collective-permute-start | bytes 1179656 | tf_op jit(solution)/shard_map/ppermute | solution.py:29
  62.3 9.8 %all-to-all-start.2 = ((f32[32,2,128]{2,1,0:T(2,128)}), f32[32,2,128]{2,1,0:T(2,128)S(1)}, u32[]{:S(2)}, u32[]{:S(2)}) async-start(f32[32,2,128]{2,1,0:T(2,128)} %get-tuple-element.84), calls=%async_computation.2 | async-start | bytes 65536 | tf_op jit(solution)/shard_map/all_to_all | solution.py:699
  71.9 3.8 %copy-start.18 = (f32[640,256]{1,0:T(8,128)S(1)}, f32[640,256]{1,0:T(8,128)}, u32[]{:S(2)}) copy-start(f32[640,256]{1,0:T(8,128)} %get-tuple-element.93) | copy-start | bytes 1966084
  71.9 9.7 %copy-start.7 = (f32[640,256]{1,0:T(8,128)S(1)}, f32[640,256]{1,0:T(8,128)}, u32[]{:S(2)}) copy-start(f32[640,256]{1,0:T(8,128)} %get-tuple-element.92) | copy-start | bytes 1966084
  75.7 5.9 %collective-permute-start.5 = (f32[640,256]{1,0:T(8,128)S(1)}, f32[640,256]{1,0:T(8,128)S(1)}, u32[]{:S(2)}, u32[]{:S(2)}) collective-permute-start(f32[640,256]{1,0:T(8,128)S(1)} %copy-done.18), channel_id=1, source_target_pairs={{0,16},{16,0},{1,17},{17,1},{2,18},{18,2},{3,19},{19,3},{4,20},{20... | collective-permute-start | bytes 1966088 | tf_op jit(solution)/shard_map/ppermute | solution.py:29
  75.8 13.6 %all-to-all-start.3 = ((f32[32,1,896]{2,1,0:T(1,128)}), f32[32,1,896]{2,1,0:T(1,128)S(1)}, u32[]{:S(2)}, u32[]{:S(2)}) async-start(f32[32,1,896]{2,1,0:T(1,128)} %second_kernel.1), calls=%async_computation.3 | async-start | bytes 229376 | tf_op jit(solution)/shard_map/all_to_all | solution.py:708
  93.7 1.7 %collective-permute-start.6 = (f32[128,384]{1,0:T(8,128)}, f32[128,384]{1,0:T(8,128)S(1)}, u32[]{:S(2)}, u32[]{:S(2)}) collective-permute-start(f32[128,384]{1,0:T(8,128)} %get-tuple-element.97), channel_id=1, source_target_pairs={{0,16},{16,0},{1,17},{17,1},{2,18},{18,2},{3,19},{19,3},{4,20},{20... | collective-permute-start | bytes 589832 | tf_op jit(solution)/shard_map/ppermute | solution.py:29
  96.1 6.3 %copy-start.11 = (f32[640,1]{1,0:T(8,128)S(1)}, f32[640,1]{1,0:T(8,128)}, u32[]{:S(2)}) copy-start(f32[640,1]{1,0:T(8,128)} %get-tuple-element.103.view_ref) | copy-start | bytes 7684
  96.1 6.3 %copy-start.12 = (f32[640,1]{1,0:T(8,128)S(1)}, f32[640,1]{1,0:T(8,128)}, u32[]{:S(2)}) copy-start(f32[640,1]{1,0:T(8,128)} %get-tuple-element.104) | copy-start | bytes 7684
  96.1 7.1 %copy-start.4 = (bf16[256,2048]{1,0:T(8,128)(2,1)S(1)}, bf16[256,2048]{1,0:T(8,128)(2,1)}, u32[]{:S(2)}) copy-start(bf16[256,2048]{1,0:T(8,128)(2,1)} %get-tuple-element.123.refs_7_) | copy-start | bytes 3145732
  98.1 18.6 %all-to-all-start.4 = ((bf16[16,56,256]{2,1,0:T(8,128)(2,1)}), bf16[16,56,256]{2,1,0:T(8,128)(2,1)}, u32[]{:S(2)}, u32[]{:S(2)}) async-start(bf16[16,56,256]{2,1,0:T(8,128)(2,1)} %message_kernel.1), calls=%async_computation.4 | async-start | bytes 917504 | tf_op jit(solution)/shard_map/all_to_all | solution.py:727
  102.4 6.2 %copy-start.3 = (f32[640,1]{1,0:T(8,128)}, f32[640,1]{1,0:T(8,128)S(1)}, u32[]{:S(2)}) copy-start(f32[640,1]{1,0:T(8,128)S(1)} %multiply_divide_fusion.scale_ref) | copy-start | bytes 7684
  102.5 1.7 %collective-permute-start.7 = (f32[640,1]{1,0:T(8,128)S(1)}, f32[640,1]{1,0:T(8,128)S(1)}, u32[]{:S(2)}, u32[]{:S(2)}) collective-permute-start(f32[640,1]{1,0:T(8,128)S(1)} %multiply_divide_fusion.scale_ref), channel_id=1, source_target_pairs={{0,16},{16,0},{1,17},{17,1},{2,18},{18,2},{3,19},{19,3},{4,20},{20... | collective-permute-start | bytes 7688 | tf_op jit(solution)/shard_map/ppermute | solution.py:29
  102.8 20.1 %collective-permute-start.8 = (bf16[4,896,128]{2,1,0:T(8,128)(2,1)}, bf16[4,896,128]{2,1,0:T(8,128)(2,1)}, u32[]{:S(2)}, u32[]{:S(2)}) collective-permute-start(bf16[4,896,128]{2,1,0:T(8,128)(2,1)} %pad_maximum_fusion.own_ref), channel_id=1, source_target_pairs={{0,16},{16,0},{1,17},{17,1},{2,18},{18,2},{3,19},{19,3},{4,20},{20... | collective-permute-start | bytes 2752520 | tf_op jit(solution)/shard_map/ppermute | solution.py:29
  103.2 39.7 %collective-permute-start.12 = (bf16[256,2048]{1,0:T(8,128)(2,1)S(1)}, bf16[256,2048]{1,0:T(8,128)(2,1)S(1)}, u32[]{:S(2)}, u32[]{:S(2)}) collective-permute-start(bf16[256,2048]{1,0:T(8,128)(2,1)S(1)} %copy-done.4), channel_id=1, source_target_pairs={{0,16},{16,0},{1,17},{17,1},{2,18},{18,2},{3,19},{19,3},{4,20},{20... | collective-permute-start | bytes 3145736 | tf_op jit(solution)/shard_map/ppermute | solution.py:29
  108.7 14.1 %copy-start.6 = (bf16[256,2048]{1,0:T(8,128)(2,1)}, bf16[256,2048]{1,0:T(8,128)(2,1)S(1)}, u32[]{:S(2)}) copy-start(bf16[256,2048]{1,0:T(8,128)(2,1)S(1)} %convolution_convert_fusion.refs_5_) | copy-start | bytes 3145732
  118.9 15.8 %all-to-all-start.5 = ((bf16[16,48,256]{2,1,0:T(8,128)(2,1)}), bf16[16,48,256]{2,1,0:T(8,128)(2,1)S(1)}, u32[]{:S(2)}, u32[]{:S(2)}) async-start(bf16[16,48,256]{2,1,0:T(8,128)(2,1)} %bottleneck_kernel.1), calls=%async_computation.5 | async-start | bytes 786432 | tf_op jit(solution)/shard_map/all_to_all | solution.py:744
  122.8 11.9 %copy-start.16 = (f32[1,640]{1,0:T(1,128)S(1)}, f32[1,640]{1,0:T(1,128)}, u32[]{:S(2)}) copy-start(f32[1,640]{1,0:T(1,128)} %get-tuple-element.116.refs_1_) | copy-start | bytes 7684
  122.8 21.9 %collective-permute-start.11 = (bf16[256,2048]{1,0:T(8,128)(2,1)S(1)}, bf16[256,2048]{1,0:T(8,128)(2,1)}, u32[]{:S(2)}, u32[]{:S(2)}) collective-permute-start(bf16[256,2048]{1,0:T(8,128)(2,1)S(1)} %convolution_convert_fusion.refs_5_), channel_id=1, source_target_pairs={{0,16},{16,0},{1,17},{17,1},{2,18},{18,2},{3,19},{19,3},{4,20},{20... | collective-permute-start | bytes 3145736 | tf_op jit(solution)/shard_map/ppermute | solution.py:29
  134.7 10.0 %collective-permute-start.9 = (bf16[16,48,256]{2,1,0:T(8,128)(2,1)S(1)}, bf16[16,48,256]{2,1,0:T(8,128)(2,1)S(1)}, u32[]{:S(2)}, u32[]{:S(2)}) collective-permute-start(bf16[16,48,256]{2,1,0:T(8,128)(2,1)S(1)} %all-to-all-done.5.refs_0_.refs_1_), channel_id=1, source_target_pairs={{0,16},{16,0},{1,17},{17,1},{2,18},{18,2},{3,19},{19,3},{4,20},{20... | collective-permute-start | bytes 1179656 | tf_op jit(solution)/shard_map/ppermute | solution.py:29
  134.7 7.3 %collective-permute-start.10 = (f32[1,640]{1,0:T(1,128)S(1)}, f32[1,640]{1,0:T(1,128)S(1)}, u32[]{:S(2)}, u32[]{:S(2)}) collective-permute-start(f32[1,640]{1,0:T(1,128)S(1)} %copy-done.16), channel_id=1, source_target_pairs={{0,16},{16,0},{1,17},{17,1},{2,18},{18,2},{3,19},{19,3},{4,20},{20... | collective-permute-start | bytes 7688 | tf_op jit(solution)/shard_map/ppermute | solution.py:29
  140.2 13.8 %collective-permute-start.15 = (bf16[96,640]{1,0:T(8,128)(2,1)S(1)}, bf16[96,640]{1,0:T(8,128)(2,1)S(1)}, u32[]{:S(2)}, u32[]{:S(2)}) collective-permute-start(bf16[96,640]{1,0:T(8,128)(2,1)S(1)} %get-tuple-element.136), channel_id=1, source_target_pairs={{0,12},{1,13},{2,14},{3,15},{4,8},{5,9},{6,10},{7,11},{8,4},{9,5},... | collective-permute-start | bytes 368648 | tf_op jit(solution)/shard_map/ppermute | solution.py:29
  142.0 12.0 %collective-permute-start.14 = (bf16[96,640]{1,0:T(8,128)(2,1)S(1)}, bf16[96,640]{1,0:T(8,128)(2,1)S(1)}, u32[]{:S(2)}, u32[]{:S(2)}) collective-permute-start(bf16[96,640]{1,0:T(8,128)(2,1)S(1)} %get-tuple-element.137), channel_id=1, source_target_pairs={{0,8},{1,9},{2,10},{3,11},{4,12},{5,13},{6,14},{7,15},{8,0},{9,1},... | collective-permute-start | bytes 368648 | tf_op jit(solution)/shard_map/ppermute | solution.py:29
  142.9 11.2 %collective-permute-start.13 = (bf16[96,640]{1,0:T(8,128)(2,1)S(1)}, bf16[96,640]{1,0:T(8,128)(2,1)S(1)}, u32[]{:S(2)}, u32[]{:S(2)}) collective-permute-start(bf16[96,640]{1,0:T(8,128)(2,1)S(1)} %get-tuple-element.138), channel_id=1, source_target_pairs={{0,4},{1,5},{2,6},{3,7},{4,0},{5,1},{6,2},{7,3},{8,12},{9,13},{10,... | collective-permute-start | bytes 368648 | tf_op jit(solution)/shard_map/ppermute | solution.py:29
  145.5 8.6 %copy-start.13 = (f32[96,640]{1,0:T(8,128)S(1)}, f32[96,640]{1,0:T(8,128)}, u32[]{:S(2)}) copy-start(f32[96,640]{1,0:T(8,128)} %get-tuple-element.120) | copy-start | bytes 737284
  (10 other events, 11.2 us)

commit v7 on v6

--- a/solution.py
+++ b/solution.py
@@ -494,7 +494,8 @@
 
 
 def features_kernel(step, *refs):
-    ins, (dz_ref, own_ref, far_ref), held, sems = refs[:5], refs[5:8], refs[8:13], refs[13]
+    ins, held, sems = refs[:5], refs[-6:-1], refs[-1]
+    dz_ref, own_ref, *far_refs = refs[5:-6]
     got, place, slope, w2, w1 = held
     groups, width = w1.shape[:2]
     pieces = [pl.ds(k, step) for k in range(0, slope.shape[1], step)]
@@ -515,8 +516,8 @@
         part = dot(w1[:, :, piece].reshape(groups * width, step), dhid, ((1,), (1,)))
         total = part if total is None else total + part
     own_ref[...] = total[:width]
-    for k in range(1, groups):
-        far_ref[k - 1] = total[k * width : (k + 1) * width].astype(BF16)
+    for k, far_ref in enumerate(far_refs, 1):
+        far_ref[...] = total[k * width : (k + 1) * width].astype(BF16)
 
 
 def feature_grads(got, place, slope, w2, w1):
@@ -524,7 +525,7 @@
     rows, hidden = slope.shape
     bot, step = got.shape[2], 256
     groups, width = w1.shape[:2]
-    outs = (shape((rows, bot), BF16), shape((width, rows), F32), shape((groups - 1, width, rows), BF16))
+    outs = (shape((rows, bot), BF16), shape((width, rows), F32)) + (shape((width, rows), BF16),) * (groups - 1)
     return pl.pallas_call(
         functools.partial(features_kernel, step),
         name="features_kernel",
@@ -665,9 +666,21 @@
     )(d.reshape(1), *heads, crop_image, crop_view)
     weights = [weights] + [swap(weights, "proto", k) for k in range(1, NEAR)]
     parts_got = lax.all_to_all(parts, "proto", 0, 0)
-    w1_late, protos_late, tprotos_late, feat_late, feat_other_late, _ = tied(
-        head_w1, protos, teacher_protos, features, feat_other, parts
-    )
+    protos_late, tprotos_late, _ = tied(protos, teacher_protos, parts)
+    cols = protos.shape[1] // nd
+    pnb = unit_cols(lax.dynamic_slice_in_dim(protos_late, d * cols, cols, 1))[0].astype(BF16)
+    tpnb = unit_cols(lax.dynamic_slice_in_dim(tprotos_late, d * cols, cols, 1))[0].astype(BF16)
+    parts_got, pnb, tpnb = tied(parts_got, pnb, tpnb)
+
+    got, zn, zinv = call(
+        rows_kernel,
+        (shape((n, sr + tr, bot), BF16), shape((sr + tr, bot), F32), shape((sr + tr, 1), F32)),
+        [],
+        parts_got,
+    )
+    sent = got
+    got = lax.all_to_all(got, "proto", 0, 0)
+    w1_late, feat_late, feat_other_late, weights, _ = tied(head_w1, features, feat_other, weights, sent)
     h0, h1, s0, s1 = call(
         hidden_kernel,
         (shape((hs, rows), BF16),) * 2 + (shape((hs, rows), F32),) * 2,
@@ -675,19 +688,8 @@
         feat_late, feat_other_late, w1_late,
         us=4,
     )
-    cols = protos.shape[1] // nd
-    pnb = unit_cols(lax.dynamic_slice_in_dim(protos_late, d * cols, cols, 1))[0].astype(BF16)
-    tpnb = unit_cols(lax.dynamic_slice_in_dim(tprotos_late, d * cols, cols, 1))[0].astype(BF16)
     weights = jnp.stack(weights)
-    parts_got, h0, h1, s0, s1, pnb, tpnb, weights = tied(parts_got, h0, h1, s0, s1, pnb, tpnb, weights)
-
-    got, zn, zinv = call(
-        rows_kernel,
-        (shape((n, sr + tr, bot), BF16), shape((sr + tr, bot), F32), shape((sr + tr, 1), F32)),
-        [],
-        parts_got,
-    )
-    got = lax.all_to_all(got, "proto", 0, 0)
+    got, h0, h1, s0, s1, weights = tied(got, h0, h1, s0, s1, weights)
     got_other = swap(got, "dp", 1)
     kern, msg, student = call(
         kern_kernel,
@@ -747,8 +749,8 @@
     got, slopes = tied(got, slopes)
 
     got_other = swap(got, "dp", 1)
-    dz, grad_features, far = feature_grads(got, place, *slopes)
-    far = [swap(far[k - 1], "proto", k * NEAR) for k in range(1, n // NEAR)]
+    dz, grad_features, *far = feature_grads(got, place, *slopes)
+    far = [swap(x, "proto", k * NEAR) for k, x in enumerate(far, 1)]
     grad_protos, grad_w1, grad_w2 = last_grads(
         d, head_w1, dz, got, got_other, place_other, protos, dpn, dpn_other, last, last_other,
         features, feat_other, h0, h1, s0, s1, head_w2,

time: 156 us -> 147 us (0.942)
  blocking collectives: 20.1 us -> 0 us
  waiting for transfers between devices: 31.3 us -> 40.7 us
  starting transfers between devices: 34.3 us -> 38 us
    all_to_all x1 -> x0, blocking collectives: 20.1 us -> none  [paired_body(): got = lax.all_to_all(got, 'proto', 0, 0)]
    all_to_all x1, waiting for transfers between devices: 0.01 us -> 7.8 us  [paired_body(): parts_got = lax.all_to_all(parts, 'proto', 0, 0)]
    all_to_all x0 -> x1, waiting for transfers between devices: none -> 6.26 us  [paired_body(): got = lax.all_to_all(got, 'proto', 0, 0)]
    ppermute x16, waiting for transfers between devices: 8.87 us -> 4.21 us  [swap(): return lax.ppermute(value, axis, [(i, i ^ step) for i in range(count)])]
    all_to_all x0 -> x1, starting transfers between devices: none -> 3.62 us  [paired_body(): got = lax.all_to_all(got, 'proto', 0, 0)]
    unnamed x42 -> x44, local copies, waits for them, and re-layouts: 4.45 us -> 4.54 us
  transfers between devices with their start and end apart: 21 -> 22, of which waited for: 8 -> 9; matrix products, arithmetic and copies ran while one was open for 8% -> 7% of each run, Pallas kernels for 23% -> 26%
where the time goes in v7:
time: 147 us; the launch traced here: 146 us
  Pallas kernels  50.3 us (34%)
  waiting for transfers between devices  40.7 us (28%)
  starting transfers between devices  38 us (26%)
  other arithmetic  7.04 us (5%)
  local copies, waits for them, and re-layouts  4.78 us (3%)
  matrix products  4.34 us (3%)
    pallas_call x7, Pallas kernels, call(): pl.pallas_call(kernel, grid=(1,), out_shape=outs, in_specs=[pl.BlockSpec(...  20.9 us
    ppermute x16, starting transfers between devices, swap(): return lax.ppermute(value, axis, [(i, i ^ step) for i in range(count)])  10.6 us
    pallas_call x1, Pallas kernels, last_grads(): pl.pallas_call(functools.partial(last_kernel, tile), name='last_kernel',...  8.59 us
    all_to_all x2, starting transfers between devices, paired_body(): msg_got = lax.all_to_all(msg, ALL, 0, 0)  8.36 us
    all_to_all x1, waiting for transfers between devices, paired_body(): msg_got = lax.all_to_all(msg, 'proto', 0, 0)  7.99 us
    all_to_all x1, waiting for transfers between devices, paired_body(): parts_got = lax.all_to_all(parts, 'proto', 0, 0)  7.8 us
    all_to_all x1, waiting for transfers between devices, paired_body(): got = lax.all_to_all(dz, 'proto', 0, 0)  7.3 us
    all_to_all x1, starting transfers between devices, paired_body(): parts_got = lax.all_to_all(parts, 'proto', 0, 0)  7.28 us
  transfers between devices with their start and end apart: 22, of which 9 were waited for; matrix products, arithmetic and copies ran while one was open for 7% of the time, Pallas kernels for 26%

profile of v7, /device:TPU:0, one launch (start us, length us, event | category | flops | bytes accessed | tf_op | source)
XLA Modules:
  0.0 146.1 jit_solution(13052358338158863785)
XLA Ops:
  1.2 5.5 %head_kernel.1 = (bf16[16,48,256]{2,1,0:T(8,128)(2,1)}, f32[1,640]{1,0:T(1,128)}, f32[640,1]{1,0:T(8,128)}, bf16[896,128]{1,0:T(8,128)(2,1)}) custom-call(s32[1]{0:T(128)} %bitcast.1.d_ref, bf16[640,1536]{1,0:T(8,128)(2,1)} %refs_9_.1, bf16[1536,128]{1,0:T(8,128)(2,1)} %w1_ref, bf16[128,256]{1,0:T(8,128)(2,1)} %refs_15_.1, bf16[128,1536]{1,0:T(8,128)(2,1)} %refs_3_.1, ...), custom_call_target="tpu_custom_call" | custom-call | tf_op jit(solution)/shard_map/head_kernel/pallas_call | solution.py:650
  6.7 3.6 %collective-permute-start.3 = (bf16[896,128]{1,0:T(8,128)(2,1)}, bf16[896,128]{1,0:T(8,128)(2,1)S(1)}, u32[]{:S(2)}, u32[]{:S(2)}) collective-permute-start(bf16[896,128]{1,0:T(8,128)(2,1)} %get-tuple-element.90), channel_id=1, source_target_pairs={{0,3},{1,2},{2,1},{3,0},{4,7},{5,6},{6,5},{7,4},{8,11},{9,10},{10,... | collective-permute-start | bytes 688136 | tf_op jit(solution)/shard_map/ppermute | solution.py:29
  10.9 7.3 %all-to-all-start = ((bf16[16,48,256]{2,1,0:T(8,128)(2,1)}), bf16[16,48,256]{2,1,0:T(8,128)(2,1)S(1)}, u32[]{:S(2)}, u32[]{:S(2)}) async-start(bf16[16,48,256]{2,1,0:T(8,128)(2,1)} %get-tuple-element.77), calls=%async_computation | async-start | bytes 786432 | tf_op jit(solution)/shard_map/all_to_all | solution.py:668
  18.2 1.8 %fusion = (f32[2048]{0:T(1024)S(1)}, f32[2048]{0:T(1024)S(1)}) fusion(bf16[256,4096]{1,0:T(8,128)(2,1)S(1)} %copy-done, s32[]{:T(128)S(6)} %select_n.8, bf16[256,4096]{1,0:T(8,128)(2,1)} %param.19), kind=kLoop, calls=%fused_computation.5 | loop fusion | flops 3141632 | bytes 2113540 | tf_op jit(solution)/shard_map/reduce_sum | solution.py:49
  20.1 1.3 fusion.3.tpnb_ref
  21.5 1.2 fusion.1.pnb_ref
  22.7 7.8 %all-to-all-done.parts_ref = bf16[16,48,256]{2,1,0:T(8,128)(2,1)S(1)} async-done(((bf16[16,48,256]{2,1,0:T(8,128)(2,1)}), bf16[16,48,256]{2,1,0:T(8,128)(2,1)S(1)}, u32[]{:S(2)}, u32[]{:S(2)}) %all-to-all-start) | async-done | bytes 393248 | tf_op jit(solution)/shard_map/all_to_all | solution.py:668
  31.2 1.9 %rows_kernel.1 = (bf16[16,48,256]{2,1,0:T(8,128)(2,1)}, f32[48,256]{1,0:T(8,128)}, f32[48,1]{1,0:T(8,128)}) custom-call(bf16[16,48,256]{2,1,0:T(8,128)(2,1)} %copy-done.10), custom_call_target="tpu_custom_call" | custom-call | flops 1000000000 | bytes 1000000 | tf_op jit(solution)/shard_map/rows_kernel/pallas_call | solution.py:197
  33.1 3.6 %all-to-all-start.1 = ((bf16[16,48,256]{2,1,0:T(8,128)(2,1)}), bf16[16,48,256]{2,1,0:T(8,128)(2,1)S(1)}, u32[]{:S(2)}, u32[]{:S(2)}) async-start(bf16[16,48,256]{2,1,0:T(8,128)(2,1)} %get-tuple-element.81), calls=%async_computation.1 | async-start | bytes 786432 | tf_op jit(solution)/shard_map/all_to_all | solution.py:682
  37.9 4.4 %hidden_kernel.1 = (bf16[128,640]{1,0:T(8,128)(2,1)}, bf16[128,640]{1,0:T(8,128)(2,1)}, f32[128,640]{1,0:T(8,128)}, f32[128,640]{1,0:T(8,128)}) custom-call(bf16[640,1536]{1,0:T(8,128)(2,1)} %refs_9_.1, bf16[640,1536]{1,0:T(8,128)(2,1)} %collective-permute-done.f1_ref.refs_10_, bf16[1536,128]{1,0:T(8,128)(2,1)} %w1_ref), custom_call_target="tpu_custom_call" | custom-call | flops 4000000000 | bytes 4000000 | tf_op jit(solution)/shard_map/hidden_kernel/pallas_call | solution.py:197
  42.3 6.3 %all-to-all-done.1.got_ref = bf16[16,48,256]{2,1,0:T(8,128)(2,1)S(1)} async-done(((bf16[16,48,256]{2,1,0:T(8,128)(2,1)}), bf16[16,48,256]{2,1,0:T(8,128)(2,1)S(1)}, u32[]{:S(2)}, u32[]{:S(2)}) %all-to-all-start.1) | async-done | bytes 393248 | tf_op jit(solution)/shard_map/all_to_all | solution.py:682
  48.6 1.7 %collective-permute-done.4.other_ref = bf16[16,48,256]{2,1,0:T(8,128)(2,1)S(1)} collective-permute-done((bf16[16,48,256]{2,1,0:T(8,128)(2,1)S(1)}, bf16[16,48,256]{2,1,0:T(8,128)(2,1)S(1)}, u32[]{:S(2)}, u32[]{:S(2)}) %collective-permute-start.4) | collective-permute-done | bytes 393248 | tf_op jit(solution)/shard_map/ppermute | solution.py:29
  51.1 3.6 %kern_kernel.1 = (f32[256,2048]{1,0:T(8,128)}, f32[32,2,128]{2,1,0:T(2,128)}, bf16[1280,256]{1,0:T(8,128)(2,1)}) custom-call(s32[1]{0:T(128)} %bitcast.1.d_ref, bf16[16,48,256]{2,1,0:T(8,128)(2,1)} %copy-done.9, bf16[16,48,256]{2,1,0:T(8,128)(2,1)} %copy-done.20, bf16[256,2048]{1,0:T(8,128)(2,1)} %fusion.3.tpnb_ref), custom_call_target="tpu_custom_call" | custom-call | flops 3000000000 | bytes 3000000 | tf_op jit(solution)/shard_map/kern_kernel/pallas_call | solution.py:197
  54.6 2.6 %all-to-all-start.2 = ((f32[32,2,128]{2,1,0:T(2,128)}), f32[32,2,128]{2,1,0:T(2,128)S(1)}, u32[]{:S(2)}, u32[]{:S(2)}) async-start(f32[32,2,128]{2,1,0:T(2,128)} %get-tuple-element.96), calls=%async_computation.2 | async-start | bytes 65536 | tf_op jit(solution)/shard_map/all_to_all | solution.py:701
  57.2 7.1 %student_kernel.1 = (bf16[1280,2048]{1,0:T(8,128)(2,1)}, f32[640,256]{1,0:T(8,128)}, f32[640,256]{1,0:T(8,128)}, f32[1280,1]{1,0:T(8,128)}) custom-call(bf16[1280,256]{1,0:T(8,128)(2,1)} %get-tuple-element.99.z_ref, bf16[256,2048]{1,0:T(8,128)(2,1)} %fusion.1.pnb_ref), custom_call_target="tpu_custom_call" | custom-call | flops 5000000000 | bytes 10000000 | tf_op jit(solution)/shard_map/student_kernel/pallas_call | solution.py:330
  65.1 3.0 %second_kernel.1 = f32[32,1,896]{2,1,0:T(1,128)} custom-call(s32[1]{0:T(128)} %bitcast.1.d_ref, f32[32,2,128]{2,1,0:T(2,128)} %copy-done.16, f32[256,2048]{1,0:T(8,128)} %get-tuple-element.97.kern_ref, f32[1280,1]{1,0:T(8,128)} %get-tuple-element.101.esum_ref), custom_call_target="tpu_custom_call" | custom-call | flops 1000000000 | bytes 1000000 | tf_op jit(solution)/shard_map/second_kernel/pallas_call | solution.py:197
  68.2 5.7 %all-to-all-start.3 = ((f32[32,1,896]{2,1,0:T(1,128)}), f32[32,1,896]{2,1,0:T(1,128)S(1)}, u32[]{:S(2)}, u32[]{:S(2)}) async-start(f32[32,1,896]{2,1,0:T(1,128)} %second_kernel.1), calls=%async_computation.3 | async-start | bytes 229376 | tf_op jit(solution)/shard_map/all_to_all | solution.py:710
  74.8 7.0 %all-to-all-done.3.got_ref = f32[32,1,896]{2,1,0:T(1,128)S(1)} async-done(((f32[32,1,896]{2,1,0:T(1,128)}), f32[32,1,896]{2,1,0:T(1,128)S(1)}, u32[]{:S(2)}, u32[]{:S(2)}) %all-to-all-start.3) | async-done | bytes 114720 | tf_op jit(solution)/shard_map/all_to_all | solution.py:710
  82.4 3.7 %third_kernel.1 = (f32[640,1]{1,0:T(8,128)}, bf16[256,2048]{1,0:T(8,128)(2,1)}, f32[128,384]{1,0:T(8,128)}, f32[128,384]{1,0:T(8,128)}) custom-call(s32[1]{0:T(128)} %bitcast.1.d_ref, f32[32,1,896]{2,1,0:T(1,128)} %copy-done.15, f32[256,2048]{1,0:T(8,128)} %get-tuple-element.97.kern_ref, bf16[256,2048]{1,0:T(8,128)(2,1)} %fusion.1.pnb_ref), custom_call_target="tpu_custom_call" | custom-call | flops 2000000000 | bytes 2000000 | tf_op jit(solution)/shard_map/third_kernel/pallas_call | solution.py:197
  86.1 1.6 %collective-permute-done.6.b1_ref = f32[128,384]{1,0:T(8,128)S(1)} collective-permute-done((f32[128,384]{1,0:T(8,128)}, f32[128,384]{1,0:T(8,128)S(1)}, u32[]{:S(2)}, u32[]{:S(2)}) %collective-permute-start.6) | collective-permute-done | bytes 196640 | tf_op jit(solution)/shard_map/ppermute | solution.py:29
  88.4 2.1 %message_kernel.1 = bf16[16,56,256]{2,1,0:T(8,128)(2,1)} custom-call(bf16[640,256]{1,0:T(8,128)(2,1)} %add_convert_fusion.sums_ref, f32[128,384]{1,0:T(8,128)} %get-tuple-element.108.b0_ref, f32[128,384]{1,0:T(8,128)} %copy-done.21), custom_call_target="tpu_custom_call" | custom-call | flops 1000000000 | bytes 1000000 | tf_op jit(solution)/shard_map/message_kernel/pallas_call | solution.py:197
  90.5 4.2 %all-to-all-start.4 = ((bf16[16,56,256]{2,1,0:T(8,128)(2,1)}), bf16[16,56,256]{2,1,0:T(8,128)(2,1)}, u32[]{:S(2)}, u32[]{:S(2)}) async-start(bf16[16,56,256]{2,1,0:T(8,128)(2,1)} %message_kernel.1), calls=%async_computation.4 | async-start | bytes 917504 | tf_op jit(solution)/shard_map/all_to_all | solution.py:729
  96.7 4.3 %convolution_convert_fusion.refs_5_ = bf16[256,2048]{1,0:T(8,128)(2,1)S(1)} fusion(bf16[1280,2048]{1,0:T(8,128)(2,1)} %get-tuple-element.117, bf16[1280,256]{1,0:T(8,128)(2,1)} %get-tuple-element.99.z_ref, f32[1280]{0:T(1024)S(1)} %maximum_reduce_fusion), kind=kOutput, calls=%fused_computation.4 | convolution fusion | flops 1343684608 | bytes 6951936 | tf_op jit(solution)/shard_map/dot_general | solution.py:24
  101.0 8.0 %all-to-all-done.4.got_ref = bf16[16,56,256]{2,1,0:T(8,128)(2,1)} async-done(((bf16[16,56,256]{2,1,0:T(8,128)(2,1)}), bf16[16,56,256]{2,1,0:T(8,128)(2,1)}, u32[]{:S(2)}, u32[]{:S(2)}) %all-to-all-start.4) | async-done | bytes 458784 | tf_op jit(solution)/shard_map/all_to_all | solution.py:729
  109.0 2.2 %bottleneck_kernel.1 = bf16[16,48,256]{2,1,0:T(8,128)(2,1)} custom-call(s32[1]{0:T(128)} %bitcast.p_ref, bf16[16,56,256]{2,1,0:T(8,128)(2,1)} %all-to-all-done.4.got_ref, f32[48,256]{1,0:T(8,128)} %get-tuple-element.119.zn_ref, f32[48,1]{1,0:T(8,128)} %get-tuple-element.120.zinv_ref, f32[640,1]{1,0:T(8,128)} %get-tuple-element.115.view_ref, f32[640,1]{1,0:T(8,128)} %copy-done.3), custom_call_target="tpu_custom_call" | custom-call | flops 1000000000 | bytes 1000000 | tf_op jit(solution)/shard_map/bottleneck_kernel/pallas_call | solution.py:197
  111.3 3.9 %all-to-all-start.5 = ((bf16[16,48,256]{2,1,0:T(8,128)(2,1)}), bf16[16,48,256]{2,1,0:T(8,128)(2,1)S(1)}, u32[]{:S(2)}, u32[]{:S(2)}) async-start(bf16[16,48,256]{2,1,0:T(8,128)(2,1)} %bottleneck_kernel.1), calls=%async_computation.5 | async-start | bytes 786432 | tf_op jit(solution)/shard_map/all_to_all | solution.py:746
  115.2 4.5 %slopes_kernel.1 = (f32[640,512]{1,0:T(8,128)}, bf16[512,256]{1,0:T(8,128)(2,1)}, bf16[4,96,512]{2,1,0:T(8,128)(2,1)}) custom-call(s32[1]{0:T(128)} %bitcast.1.d_ref, s32[1]{0:T(128)} %bitcast.p_ref, bf16[640,1536]{1,0:T(8,128)(2,1)} %refs_9_.1, bf16[4,896,128]{2,1,0:T(8,128)(2,1)} %pad_maximum_fusion.own_ref, ...), custom_call_target="tpu_custom_call" | custom-call | flops 4000000000 | bytes 30000000 | tf_op jit(solution)/shard_map/slopes_kernel/pallas_call | solution.py:457
  119.7 7.3 %all-to-all-done.5.refs_0_.refs_1_ = bf16[16,48,256]{2,1,0:T(8,128)(2,1)S(1)} async-done(((bf16[16,48,256]{2,1,0:T(8,128)(2,1)}), bf16[16,48,256]{2,1,0:T(8,128)(2,1)S(1)}, u32[]{:S(2)}, u32[]{:S(2)}) %all-to-all-start.5) | async-done | bytes 393248 | tf_op jit(solution)/shard_map/all_to_all | solution.py:746
  127.8 3.7 %features_kernel.1 = (bf16[640,256]{1,0:T(8,128)(2,1)}, f32[96,640]{1,0:T(8,128)}, bf16[96,640]{1,0:T(8,128)(2,1)}, bf16[96,640]{1,0:T(8,128)(2,1)}, bf16[96,640]{1,0:T(8,128)(2,1)}) custom-call(bf16[16,48,256]{2,1,0:T(8,128)(2,1)} %copy-done.1, f32[1,640]{1,0:T(1,128)} %get-tuple-element.128.refs_1_, f32[640,512]{1,0:T(8,128)} %get-tuple-element.129.refs_2_, ...), custom_call_target="tpu_custom_call" | custom-call | tf_op jit(solution)/shard_map/features_kernel/pallas_call | solution.py:529
  132.7 1.2 collective-permute-start.14
  133.9 2.1 %collective-permute-start.15 = (bf16[96,640]{1,0:T(8,128)(2,1)}, bf16[96,640]{1,0:T(8,128)(2,1)S(1)}, u32[]{:S(2)}, u32[]{:S(2)}) collective-permute-start(bf16[96,640]{1,0:T(8,128)(2,1)} %get-tuple-element.143), channel_id=1, source_target_pairs={{0,12},{1,13},{2,14},{3,15},{4,8},{5,9},{6,10},{7,11},{8,4},{9,5},... | collective-permute-start | bytes 368648 | tf_op jit(solution)/shard_map/ppermute | solution.py:29
  136.8 8.6 %last_kernel.1 = (f32[256,4096]{1,0:T(8,128)}, f32[1536,128]{1,0:T(8,128)}, f32[128,256]{1,0:T(8,128)}) custom-call(s32[1]{0:T(128)} %bitcast.1.d_ref, bf16[640,256]{1,0:T(8,128)(2,1)} %get-tuple-element.133.refs_0_, bf16[16,48,256]{2,1,0:T(8,128)(2,1)} %copy-done.1, bf16[16,48,256]{2,1,0:T(8,128)(2,1)} %copy-done.8, f32[1,640]{1,0:T(1,128)} %copy-done.18, ...), custom_call_target="tpu_custom_call" | custom-call | tf_op jit(solution)/shard_map/last_kernel/pallas_call | solution.py:607
  (81 shorter events, 12.2 us)
Async XLA Ops:
  0.6 17.6 %copy-start = (bf16[256,4096]{1,0:T(8,128)(2,1)S(1)}, bf16[256,4096]{1,0:T(8,128)(2,1)}, u32[]{:S(2)}) copy-start(bf16[256,4096]{1,0:T(8,128)(2,1)} %refs_4_.3) | copy-start | bytes 6291460
  0.6 36.1 %collective-permute-start = (bf16[640,1536]{1,0:T(8,128)(2,1)}, bf16[640,1536]{1,0:T(8,128)(2,1)}, u32[]{:S(2)}, u32[]{:S(2)}) collective-permute-start(bf16[640,1536]{1,0:T(8,128)(2,1)} %refs_9_.1), channel_id=1, source_target_pairs={{0,16},{16,0},{1,17},{17,1},{2,18},{18,2},{3,19},{19,3},{4,20},{20... | collective-permute-start | bytes 5898248 | tf_op jit(solution)/shard_map/ppermute | solution.py:29
  6.7 30.0 %collective-permute-start.3 = (bf16[896,128]{1,0:T(8,128)(2,1)}, bf16[896,128]{1,0:T(8,128)(2,1)S(1)}, u32[]{:S(2)}, u32[]{:S(2)}) collective-permute-start(bf16[896,128]{1,0:T(8,128)(2,1)} %get-tuple-element.90), channel_id=1, source_target_pairs={{0,3},{1,2},{2,1},{3,0},{4,7},{5,6},{6,5},{7,4},{8,11},{9,10},{10,... | collective-permute-start | bytes 688136 | tf_op jit(solution)/shard_map/ppermute | solution.py:29
  10.3 26.5 %collective-permute-start.2 = (bf16[896,128]{1,0:T(8,128)(2,1)}, bf16[896,128]{1,0:T(8,128)(2,1)S(1)}, u32[]{:S(2)}, u32[]{:S(2)}) collective-permute-start(bf16[896,128]{1,0:T(8,128)(2,1)} %get-tuple-element.90), channel_id=1, source_target_pairs={{0,2},{1,3},{2,0},{3,1},{4,6},{5,7},{6,4},{7,5},{8,10},{9,11},{10,... | collective-permute-start | bytes 688136 | tf_op jit(solution)/shard_map/ppermute | solution.py:29
  10.8 26.0 %collective-permute-start.1 = (bf16[896,128]{1,0:T(8,128)(2,1)}, bf16[896,128]{1,0:T(8,128)(2,1)S(1)}, u32[]{:S(2)}, u32[]{:S(2)}) collective-permute-start(bf16[896,128]{1,0:T(8,128)(2,1)} %get-tuple-element.90), channel_id=1, source_target_pairs={{0,1},{1,0},{2,3},{3,2},{4,5},{5,4},{6,7},{7,6},{8,9},{9,8},{10,11... | collective-permute-start | bytes 688136 | tf_op jit(solution)/shard_map/ppermute | solution.py:29
  10.9 19.6 %all-to-all-start = ((bf16[16,48,256]{2,1,0:T(8,128)(2,1)}), bf16[16,48,256]{2,1,0:T(8,128)(2,1)S(1)}, u32[]{:S(2)}, u32[]{:S(2)}) async-start(bf16[16,48,256]{2,1,0:T(8,128)(2,1)} %get-tuple-element.77), calls=%async_computation | async-start | bytes 786432 | tf_op jit(solution)/shard_map/all_to_all | solution.py:668
  22.7 14.1 %copy-start.14 = (bf16[896,128]{1,0:T(8,128)(2,1)S(1)}, bf16[896,128]{1,0:T(8,128)(2,1)}, u32[]{:S(2)}) copy-start(bf16[896,128]{1,0:T(8,128)(2,1)} %get-tuple-element.90) | copy-start | bytes 688132
  33.1 15.4 %all-to-all-start.1 = ((bf16[16,48,256]{2,1,0:T(8,128)(2,1)}), bf16[16,48,256]{2,1,0:T(8,128)(2,1)S(1)}, u32[]{:S(2)}, u32[]{:S(2)}) async-start(bf16[16,48,256]{2,1,0:T(8,128)(2,1)} %get-tuple-element.81), calls=%async_computation.1 | async-start | bytes 786432 | tf_op jit(solution)/shard_map/all_to_all | solution.py:682
  48.6 1.7 %collective-permute-start.4 = (bf16[16,48,256]{2,1,0:T(8,128)(2,1)S(1)}, bf16[16,48,256]{2,1,0:T(8,128)(2,1)S(1)}, u32[]{:S(2)}, u32[]{:S(2)}) collective-permute-start(bf16[16,48,256]{2,1,0:T(8,128)(2,1)S(1)} %all-to-all-done.1.got_ref), channel_id=1, source_target_pairs={{0,16},{16,0},{1,17},{17,1},{2,18},{18,2},{3,19},{19,3},{4,20},{20... | collective-permute-start | bytes 1179656 | tf_op jit(solution)/shard_map/ppermute | solution.py:29
  54.6 9.8 %all-to-all-start.2 = ((f32[32,2,128]{2,1,0:T(2,128)}), f32[32,2,128]{2,1,0:T(2,128)S(1)}, u32[]{:S(2)}, u32[]{:S(2)}) async-start(f32[32,2,128]{2,1,0:T(2,128)} %get-tuple-element.96), calls=%async_computation.2 | async-start | bytes 65536 | tf_op jit(solution)/shard_map/all_to_all | solution.py:701
  64.3 9.7 %copy-start.7 = (f32[640,256]{1,0:T(8,128)S(1)}, f32[640,256]{1,0:T(8,128)}, u32[]{:S(2)}) copy-start(f32[640,256]{1,0:T(8,128)} %get-tuple-element.104) | copy-start | bytes 1966084
  68.1 5.9 %collective-permute-start.5 = (f32[640,256]{1,0:T(8,128)S(1)}, f32[640,256]{1,0:T(8,128)S(1)}, u32[]{:S(2)}, u32[]{:S(2)}) collective-permute-start(f32[640,256]{1,0:T(8,128)S(1)} %copy-done.19), channel_id=1, source_target_pairs={{0,16},{16,0},{1,17},{17,1},{2,18},{18,2},{3,19},{19,3},{4,20},{20... | collective-permute-start | bytes 1966088 | tf_op jit(solution)/shard_map/ppermute | solution.py:29
  68.2 13.6 %all-to-all-start.3 = ((f32[32,1,896]{2,1,0:T(1,128)}), f32[32,1,896]{2,1,0:T(1,128)S(1)}, u32[]{:S(2)}, u32[]{:S(2)}) async-start(f32[32,1,896]{2,1,0:T(1,128)} %second_kernel.1), calls=%async_computation.3 | async-start | bytes 229376 | tf_op jit(solution)/shard_map/all_to_all | solution.py:710
  86.1 1.7 %collective-permute-start.6 = (f32[128,384]{1,0:T(8,128)}, f32[128,384]{1,0:T(8,128)S(1)}, u32[]{:S(2)}, u32[]{:S(2)}) collective-permute-start(f32[128,384]{1,0:T(8,128)} %get-tuple-element.109), channel_id=1, source_target_pairs={{0,16},{16,0},{1,17},{17,1},{2,18},{18,2},{3,19},{19,3},{4,20},{20... | collective-permute-start | bytes 589832 | tf_op jit(solution)/shard_map/ppermute | solution.py:29
  88.4 6.3 %copy-start.11 = (f32[640,1]{1,0:T(8,128)S(1)}, f32[640,1]{1,0:T(8,128)}, u32[]{:S(2)}) copy-start(f32[640,1]{1,0:T(8,128)} %get-tuple-element.115.view_ref) | copy-start | bytes 7684
  88.4 6.3 %copy-start.12 = (f32[640,1]{1,0:T(8,128)S(1)}, f32[640,1]{1,0:T(8,128)}, u32[]{:S(2)}) copy-start(f32[640,1]{1,0:T(8,128)} %get-tuple-element.116) | copy-start | bytes 7684
  88.4 7.1 %copy-start.4 = (bf16[256,2048]{1,0:T(8,128)(2,1)S(1)}, bf16[256,2048]{1,0:T(8,128)(2,1)}, u32[]{:S(2)}) copy-start(bf16[256,2048]{1,0:T(8,128)(2,1)} %get-tuple-element.135.refs_7_) | copy-start | bytes 3145732
  90.5 18.5 %all-to-all-start.4 = ((bf16[16,56,256]{2,1,0:T(8,128)(2,1)}), bf16[16,56,256]{2,1,0:T(8,128)(2,1)}, u32[]{:S(2)}, u32[]{:S(2)}) async-start(bf16[16,56,256]{2,1,0:T(8,128)(2,1)} %message_kernel.1), calls=%async_computation.4 | async-start | bytes 917504 | tf_op jit(solution)/shard_map/all_to_all | solution.py:729
  94.8 6.2 %copy-start.3 = (f32[640,1]{1,0:T(8,128)}, f32[640,1]{1,0:T(8,128)S(1)}, u32[]{:S(2)}) copy-start(f32[640,1]{1,0:T(8,128)S(1)} %multiply_divide_fusion.scale_ref) | copy-start | bytes 7684
  94.8 1.7 %collective-permute-start.7 = (f32[640,1]{1,0:T(8,128)S(1)}, f32[640,1]{1,0:T(8,128)S(1)}, u32[]{:S(2)}, u32[]{:S(2)}) collective-permute-start(f32[640,1]{1,0:T(8,128)S(1)} %multiply_divide_fusion.scale_ref), channel_id=1, source_target_pairs={{0,16},{16,0},{1,17},{17,1},{2,18},{18,2},{3,19},{19,3},{4,20},{20... | collective-permute-start | bytes 7688 | tf_op jit(solution)/shard_map/ppermute | solution.py:29
  95.1 20.1 %collective-permute-start.8 = (bf16[4,896,128]{2,1,0:T(8,128)(2,1)}, bf16[4,896,128]{2,1,0:T(8,128)(2,1)}, u32[]{:S(2)}, u32[]{:S(2)}) collective-permute-start(bf16[4,896,128]{2,1,0:T(8,128)(2,1)} %pad_maximum_fusion.own_ref), channel_id=1, source_target_pairs={{0,16},{16,0},{1,17},{17,1},{2,18},{18,2},{3,19},{19,3},{4,20},{20... | collective-permute-start | bytes 2752520 | tf_op jit(solution)/shard_map/ppermute | solution.py:29
  95.5 38.4 %collective-permute-start.12 = (bf16[256,2048]{1,0:T(8,128)(2,1)S(1)}, bf16[256,2048]{1,0:T(8,128)(2,1)S(1)}, u32[]{:S(2)}, u32[]{:S(2)}) collective-permute-start(bf16[256,2048]{1,0:T(8,128)(2,1)S(1)} %copy-done.4), channel_id=1, source_target_pairs={{0,16},{16,0},{1,17},{17,1},{2,18},{18,2},{3,19},{19,3},{4,20},{20... | collective-permute-start | bytes 3145736 | tf_op jit(solution)/shard_map/ppermute | solution.py:29
  101.0 14.1 %copy-start.6 = (bf16[256,2048]{1,0:T(8,128)(2,1)}, bf16[256,2048]{1,0:T(8,128)(2,1)S(1)}, u32[]{:S(2)}) copy-start(bf16[256,2048]{1,0:T(8,128)(2,1)S(1)} %convolution_convert_fusion.refs_5_) | copy-start | bytes 3145732
  111.3 15.8 %all-to-all-start.5 = ((bf16[16,48,256]{2,1,0:T(8,128)(2,1)}), bf16[16,48,256]{2,1,0:T(8,128)(2,1)S(1)}, u32[]{:S(2)}, u32[]{:S(2)}) async-start(bf16[16,48,256]{2,1,0:T(8,128)(2,1)} %bottleneck_kernel.1), calls=%async_computation.5 | async-start | bytes 786432 | tf_op jit(solution)/shard_map/all_to_all | solution.py:746
  115.1 11.9 %copy-start.17 = (f32[1,640]{1,0:T(1,128)S(1)}, f32[1,640]{1,0:T(1,128)}, u32[]{:S(2)}) copy-start(f32[1,640]{1,0:T(1,128)} %get-tuple-element.128.refs_1_) | copy-start | bytes 7684
  115.1 20.9 %collective-permute-start.11 = (bf16[256,2048]{1,0:T(8,128)(2,1)S(1)}, bf16[256,2048]{1,0:T(8,128)(2,1)}, u32[]{:S(2)}, u32[]{:S(2)}) collective-permute-start(bf16[256,2048]{1,0:T(8,128)(2,1)S(1)} %convolution_convert_fusion.refs_5_), channel_id=1, source_target_pairs={{0,16},{16,0},{1,17},{17,1},{2,18},{18,2},{3,19},{19,3},{4,20},{20... | collective-permute-start | bytes 3145736 | tf_op jit(solution)/shard_map/ppermute | solution.py:29
  127.0 9.0 %collective-permute-start.9 = (bf16[16,48,256]{2,1,0:T(8,128)(2,1)S(1)}, bf16[16,48,256]{2,1,0:T(8,128)(2,1)S(1)}, u32[]{:S(2)}, u32[]{:S(2)}) collective-permute-start(bf16[16,48,256]{2,1,0:T(8,128)(2,1)S(1)} %all-to-all-done.5.refs_0_.refs_1_), channel_id=1, source_target_pairs={{0,16},{16,0},{1,17},{17,1},{2,18},{18,2},{3,19},{19,3},{4,20},{20... | collective-permute-start | bytes 1179656 | tf_op jit(solution)/shard_map/ppermute | solution.py:29
  127.0 5.7 %collective-permute-start.10 = (f32[1,640]{1,0:T(1,128)S(1)}, f32[1,640]{1,0:T(1,128)S(1)}, u32[]{:S(2)}, u32[]{:S(2)}) collective-permute-start(f32[1,640]{1,0:T(1,128)S(1)} %copy-done.17), channel_id=1, source_target_pairs={{0,16},{16,0},{1,17},{17,1},{2,18},{18,2},{3,19},{19,3},{4,20},{20... | collective-permute-start | bytes 7688 | tf_op jit(solution)/shard_map/ppermute | solution.py:29
  131.5 13.8 %collective-permute-start.13 = (bf16[96,640]{1,0:T(8,128)(2,1)}, bf16[96,640]{1,0:T(8,128)(2,1)S(1)}, u32[]{:S(2)}, u32[]{:S(2)}) collective-permute-start(bf16[96,640]{1,0:T(8,128)(2,1)} %get-tuple-element.141), channel_id=1, source_target_pairs={{0,4},{1,5},{2,6},{3,7},{4,0},{5,1},{6,2},{7,3},{8,12},{9,13},{10,... | collective-permute-start | bytes 368648 | tf_op jit(solution)/shard_map/ppermute | solution.py:29
  132.7 12.7 %collective-permute-start.14 = (bf16[96,640]{1,0:T(8,128)(2,1)}, bf16[96,640]{1,0:T(8,128)(2,1)S(1)}, u32[]{:S(2)}, u32[]{:S(2)}) collective-permute-start(bf16[96,640]{1,0:T(8,128)(2,1)} %get-tuple-element.142), channel_id=1, source_target_pairs={{0,8},{1,9},{2,10},{3,11},{4,12},{5,13},{6,14},{7,15},{8,0},{9,1},... | collective-permute-start | bytes 368648 | tf_op jit(solution)/shard_map/ppermute | solution.py:29
  133.9 11.5 %collective-permute-start.15 = (bf16[96,640]{1,0:T(8,128)(2,1)}, bf16[96,640]{1,0:T(8,128)(2,1)S(1)}, u32[]{:S(2)}, u32[]{:S(2)}) collective-permute-start(bf16[96,640]{1,0:T(8,128)(2,1)} %get-tuple-element.143), channel_id=1, source_target_pairs={{0,12},{1,13},{2,14},{3,15},{4,8},{5,9},{6,10},{7,11},{8,4},{9,5},... | collective-permute-start | bytes 368648 | tf_op jit(solution)/shard_map/ppermute | solution.py:29
  136.8 8.6 %copy-start.13 = (f32[96,640]{1,0:T(8,128)S(1)}, f32[96,640]{1,0:T(8,128)}, u32[]{:S(2)}) copy-start(f32[96,640]{1,0:T(8,128)} %get-tuple-element.132) | copy-start | bytes 737284
  (12 other events, 17.8 us)

commit v8 on v7

--- a/solution.py
+++ b/solution.py
@@ -176,7 +176,7 @@
     return (grad_features, grad_w1, grad_w2, grad_protos)
 
 
-def params(mib=56):
+def params(mib=50):
     return pltpu.CompilerParams(vmem_limit_bytes=mib * 1024 * 1024)
 
 
@@ -192,7 +192,7 @@
     return pl.BlockSpec(dims, lambda i: (0,) * len(dims))
 
 
-def call(kernel, outs, scalars, *args, us=1, mib=56):
+def call(kernel, outs, scalars, *args, us=1, mib=50):
     smem = [jnp.asarray(s, jnp.int32).reshape(1) for s in scalars]
     return pl.pallas_call(
         kernel,
@@ -264,12 +264,11 @@
     parts_ref[...] = jnp.concatenate([z, t], axis=1).astype(BF16)
 
 
-def rows_kernel(parts_ref, out_ref, zn_ref, zinv_ref):
+def rows_kernel(parts_ref, out_ref, zn_ref):
     z = jnp.sum(parts_ref[...].astype(F32), axis=0)
     inv = lax.rsqrt(jnp.sum(z * z, axis=1, keepdims=True) + 1e-06)
     zn = z * inv
-    zn_ref[...] = zn
-    zinv_ref[...] = inv
+    zn_ref[...] = jnp.concatenate([zn, jnp.broadcast_to(inv, (zn.shape[0], 128))], axis=1)
     out_ref[...] = jnp.broadcast_to(zn[None], out_ref.shape).astype(BF16)
 
 
@@ -391,7 +390,7 @@
     out_ref[...] = jnp.concatenate([sums, both, tail.reshape(n, teach // n, bot)], axis=1).astype(BF16)
 
 
-def bottleneck_kernel(factor, p_ref, got_ref, zn_ref, zinv_ref, view_ref, scale_ref, out_ref):
+def bottleneck_kernel(factor, p_ref, got_ref, zn_ref, view_ref, scale_ref, out_ref):
     sr = view_ref.shape[0] // out_ref.shape[0]
     mine = pl.ds(pl.multiple_of(p_ref[0] * sr, sr), sr)
     tr = zn_ref.shape[0] - sr
@@ -400,7 +399,8 @@
     tail = out[sr + tr :]
     image = factor / (tail[:, :1] + tail[:, 128:129])
     sums = out[sr : sr + tr] * image
-    zn, zinv = zn_ref[:sr], zinv_ref[:sr]
+    bot = got_ref.shape[2]
+    zn, zinv = zn_ref[:sr, :bot], zn_ref[:sr, bot : bot + 1]
     znb = zn.astype(BF16).astype(F32)
     view = view_ref[mine].astype(jnp.int32)
     which = lax.broadcasted_iota(jnp.int32, (sr, 1), 0)
@@ -661,7 +661,7 @@
         + [block((rows,))] * 2,
         out_specs=(block((n, sr + tr, bot)), block((1, rows)), block((rows, 1)), block((wide // 2 + hs, hs))),
         scratch_shapes=[pltpu.VMEM(x.shape, x.dtype) for x in heads] + [pltpu.SemaphoreType.DMA((6,))],
-        compiler_params=params(),
+        compiler_params=params(62),
         name="head_kernel",
     )(d.reshape(1), *heads, crop_image, crop_view)
     weights = [weights] + [swap(weights, "proto", k) for k in range(1, NEAR)]
@@ -672,11 +672,12 @@
     tpnb = unit_cols(lax.dynamic_slice_in_dim(tprotos_late, d * cols, cols, 1))[0].astype(BF16)
     parts_got, pnb, tpnb = tied(parts_got, pnb, tpnb)
 
-    got, zn, zinv = call(
+    got, zn = call(
         rows_kernel,
-        (shape((n, sr + tr, bot), BF16), shape((sr + tr, bot), F32), shape((sr + tr, 1), F32)),
+        (shape((n, sr + tr, bot), BF16), shape((sr + tr, bot + 128), F32)),
         [],
         parts_got,
+        mib=40,
     )
     sent = got
     got = lax.all_to_all(got, "proto", 0, 0)
@@ -690,6 +691,7 @@
     )
     weights = jnp.stack(weights)
     got, h0, h1, s0, s1, weights = tied(got, h0, h1, s0, s1, weights)
+    weights_other = swap(weights, "dp", 1)
     got_other = swap(got, "dp", 1)
     kern, msg, student = call(
         kern_kernel,
@@ -706,6 +708,7 @@
         shape((everyone, 1, nd * teach + rows), F32),
         [d],
         msg_got, kern, esum,
+        mib=56,
     )
     msg_got = lax.all_to_all(msg, ALL, 0, 0)
     sums, sums_other, _ = tied(sums, sums_other, msg)
@@ -729,19 +732,18 @@
     msg_got = lax.all_to_all(msg, "proto", 0, 0)
 
     esum, view_late, last, weights, place, _ = tied(esum, view, last, weights, place, msg)
-    weights_other, last_other = swap(weights, "dp", 1), swap(last, "dp", 1)
     place_other = swap(place, "dp", 1)
     crop_scale = jnp.where(view_late == 2, 2.0, 1.0) * factor / esum
     scale_other = swap(crop_scale, "dp", 1)
     left = (student.astype(F32) * jnp.concatenate([crop_scale, scale_other], axis=0)).astype(BF16)
     dpn = dot(left, exb, ((0,), (0,))).astype(BF16)
     msg_got, dpn = tied(msg_got, dpn)
-    dpn_other = swap(dpn, "dp", 1)
+    dpn_other, last_other = swap(dpn, "dp", 1), swap(last, "dp", 1)
     dz = call(
         functools.partial(bottleneck_kernel, factor),
         shape((n, sr + tr, bot), BF16),
         [p],
-        msg_got, zn, zinv, view_late, crop_scale,
+        msg_got, zn, view_late, crop_scale,
     )
     got = lax.all_to_all(dz, "proto", 0, 0)
     weights, feat_late, _ = tied(weights, features, dz)

time: 147 us -> 140 us (0.952)
  Pallas kernels: 50.3 us -> 37.6 us
  local copies, waits for them, and re-layouts: 4.78 us -> 13.3 us
  waiting for transfers between devices: 40.7 us -> 37.2 us
    unnamed x44 -> x54, local copies, waits for them, and re-layouts: 4.54 us -> 13.1 us
    pallas_call x7, Pallas kernels: 20.9 us -> 13 us  [call(): pl.pallas_call(kernel, grid=(1,), out_shape=outs, in_specs=[pl.BlockSpec(...]
    all_to_all x1, waiting for transfers between devices: 6.26 us -> 2.89 us  [paired_body(): got = lax.all_to_all(got, 'proto', 0, 0)]
    pallas_call x1, Pallas kernels: 7.05 us -> 5.18 us  [student_sums(): pl.pallas_call(student_kernel, name='student_kernel', grid=(4,), out_shap...]
  transfers between devices with their start and end apart: 22 -> 22, of which waited for: 9 -> 9; matrix products, arithmetic and copies ran while one was open for 7% -> 8% of each run, Pallas kernels for 26% -> 21%
where the time goes in v8:
time: 140 us; the launch traced here: 139 us
  starting transfers between devices  38 us (27%)
  Pallas kernels  37.6 us (27%)
  waiting for transfers between devices  37.2 us (27%)
  local copies, waits for them, and re-layouts  13.3 us (10%)
  other arithmetic  7.93 us (6%)
  matrix products  4.36 us (3%)
    unnamed x54, local copies, waits for them, and re-layouts  13.1 us
    pallas_call x7, Pallas kernels, call(): pl.pallas_call(kernel, grid=(1,), out_shape=outs, in_specs=[pl.BlockSpec(...  13 us
    ppermute x16, starting transfers between devices, swap(): return lax.ppermute(value, axis, [(i, i ^ step) for i in range(count)])  10.6 us
    all_to_all x2, starting transfers between devices, paired_body(): msg_got = lax.all_to_all(msg, ALL, 0, 0)  8.75 us
    all_to_all x1, waiting for transfers between devices, paired_body(): parts_got = lax.all_to_all(parts, 'proto', 0, 0)  8.34 us
    all_to_all x1, waiting for transfers between devices, paired_body(): msg_got = lax.all_to_all(msg, 'proto', 0, 0)  7.94 us
    pallas_call x1, Pallas kernels, last_grads(): pl.pallas_call(functools.partial(last_kernel, tile), name='last_kernel',...  7.67 us
    all_to_all x1, starting transfers between devices, paired_body(): parts_got = lax.all_to_all(parts, 'proto', 0, 0)  7.32 us
  transfers between devices with their start and end apart: 22, of which 9 were waited for; matrix products, arithmetic and copies ran while one was open for 8% of the time, Pallas kernels for 21%

profile of v8, /device:TPU:0, one launch (start us, length us, event | category | flops | bytes accessed | tf_op | source)
XLA Modules:
  0.0 139.4 jit_solution(14878442199056143440)
XLA Ops:
  1.2 5.4 %head_kernel.1 = (bf16[16,48,256]{2,1,0:T(8,128)(2,1)}, f32[1,640]{1,0:T(1,128)}, f32[640,1]{1,0:T(8,128)}, bf16[896,128]{1,0:T(8,128)(2,1)}) custom-call(s32[1]{0:T(128)} %bitcast.1.d_ref, bf16[640,1536]{1,0:T(8,128)(2,1)} %refs_9_.1, bf16[1536,128]{1,0:T(8,128)(2,1)} %w1_ref, bf16[128,256]{1,0:T(8,128)(2,1)} %refs_15_.1, bf16[128,1536]{1,0:T(8,128)(2,1)} %refs_3_.1, ...), custom_call_target="tpu_custom_call" | custom-call | tf_op jit(solution)/shard_map/head_kernel/pallas_call | solution.py:650
  6.6 2.6 %collective-permute-start.1 = (bf16[896,128]{1,0:T(8,128)(2,1)}, bf16[896,128]{1,0:T(8,128)(2,1)}, u32[]{:S(2)}, u32[]{:S(2)}) collective-permute-start(bf16[896,128]{1,0:T(8,128)(2,1)} %get-tuple-element.89), channel_id=1, source_target_pairs={{0,1},{1,0},{2,3},{3,2},{4,5},{5,4},{6,7},{7,6},{8,9},{9,8},{10,11... | collective-permute-start | bytes 688136 | tf_op jit(solution)/shard_map/ppermute | solution.py:29
  9.2 1.5 %collective-permute-start.2 = (bf16[896,128]{1,0:T(8,128)(2,1)}, bf16[896,128]{1,0:T(8,128)(2,1)}, u32[]{:S(2)}, u32[]{:S(2)}) collective-permute-start(bf16[896,128]{1,0:T(8,128)(2,1)} %get-tuple-element.89), channel_id=1, source_target_pairs={{0,2},{1,3},{2,0},{3,1},{4,6},{5,7},{6,4},{7,5},{8,10},{9,11},{10,... | collective-permute-start | bytes 688136 | tf_op jit(solution)/shard_map/ppermute | solution.py:29
  10.7 7.3 %all-to-all-start = ((bf16[16,48,256]{2,1,0:T(8,128)(2,1)}), bf16[16,48,256]{2,1,0:T(8,128)(2,1)S(1)}, u32[]{:S(2)}, u32[]{:S(2)}) async-start(bf16[16,48,256]{2,1,0:T(8,128)(2,1)} %get-tuple-element.76), calls=%async_computation | async-start | bytes 786432 | tf_op jit(solution)/shard_map/all_to_all | solution.py:668
  18.1 2.1 %fusion = (f32[2048]{0:T(1024)S(1)}, f32[2048]{0:T(1024)S(1)}) fusion(bf16[256,4096]{1,0:T(8,128)(2,1)} %refs_4_.3, s32[]{:T(128)S(6)} %select_n.8, bf16[256,4096]{1,0:T(8,128)(2,1)} %param.19), kind=kLoop, calls=%fused_computation.5 | loop fusion | flops 3141632 | bytes 2113540 | tf_op jit(solution)/shard_map/reduce_sum | solution.py:49
  20.9 1.2 fusion.3.tpnb_ref
  22.2 8.3 %all-to-all-done.parts_ref = bf16[16,48,256]{2,1,0:T(8,128)(2,1)S(1)} async-done(((bf16[16,48,256]{2,1,0:T(8,128)(2,1)}), bf16[16,48,256]{2,1,0:T(8,128)(2,1)S(1)}, u32[]{:S(2)}, u32[]{:S(2)}) %all-to-all-start) | async-done | bytes 393248 | tf_op jit(solution)/shard_map/all_to_all | solution.py:668
  32.0 3.7 %all-to-all-start.1 = ((bf16[16,48,256]{2,1,0:T(8,128)(2,1)}), bf16[16,48,256]{2,1,0:T(8,128)(2,1)S(1)}, u32[]{:S(2)}, u32[]{:S(2)}) async-start(bf16[16,48,256]{2,1,0:T(8,128)(2,1)} %copy-done.4), calls=%async_computation.1 | async-start | bytes 786432 | tf_op jit(solution)/shard_map/all_to_all | solution.py:683
  35.8 2.3 %pad_maximum_fusion.own_ref = bf16[4,896,128]{2,1,0:T(8,128)(2,1)} fusion(bf16[1,896,128]{2,1,0:T(8,128)(2,1)} %bitcast.5, bf16[1,896,128]{2,1,0:T(8,128)(2,1)} %bitcast.4, bf16[1,896,128]{2,1,0:T(8,128)(2,1)} %bitcast.3, bf16[1,896,128]{2,1,0:T(8,128)(2,1)} %bitcast.9), kind=kLoop, calls=%fused_computation.10 | loop fusion | flops 1376256 | bytes 1835008 | tf_op jit(solution)/shard_map/stack | solution.py:692
  39.1 2.9 %hidden_kernel.1 = (bf16[128,640]{1,0:T(8,128)(2,1)S(1)}, bf16[128,640]{1,0:T(8,128)(2,1)S(1)}, f32[128,640]{1,0:T(8,128)S(1)}, f32[128,640]{1,0:T(8,128)S(1)}) custom-call(bf16[640,1536]{1,0:T(8,128)(2,1)S(1)} %copy-done, bf16[640,1536]{1,0:T(8,128)(2,1)} %collective-permute-done.f1_ref.refs_10_, bf16[1536,128]{1,0:T(8,128)(2,1)S(1)} %copy-done.5), custom_call_target="tpu_custom_call" | custom-call | flops 4000000000 | bytes 4000000 | tf_op jit(solution)/shard_map/hidden_kernel/pallas_call | solution.py:197
  44.8 2.9 %all-to-all-done.1.got_ref = bf16[16,48,256]{2,1,0:T(8,128)(2,1)S(1)} async-done(((bf16[16,48,256]{2,1,0:T(8,128)(2,1)}), bf16[16,48,256]{2,1,0:T(8,128)(2,1)S(1)}, u32[]{:S(2)}, u32[]{:S(2)}) %all-to-all-start.1) | async-done | bytes 393248 | tf_op jit(solution)/shard_map/all_to_all | solution.py:683
  47.7 1.7 %collective-permute-done.4.other_ref = bf16[16,48,256]{2,1,0:T(8,128)(2,1)S(1)} collective-permute-done((bf16[16,48,256]{2,1,0:T(8,128)(2,1)S(1)}, bf16[16,48,256]{2,1,0:T(8,128)(2,1)S(1)}, u32[]{:S(2)}, u32[]{:S(2)}) %collective-permute-start.4) | collective-permute-done | bytes 393248 | tf_op jit(solution)/shard_map/ppermute | solution.py:29
  49.4 1.2 copy-done.1
  50.7 1.9 %kern_kernel.1 = (f32[256,2048]{1,0:T(8,128)}, f32[32,2,128]{2,1,0:T(2,128)}, bf16[1280,256]{1,0:T(8,128)(2,1)S(1)}) custom-call(s32[1]{0:T(128)} %bitcast.1.d_ref, bf16[16,48,256]{2,1,0:T(8,128)(2,1)S(1)} %all-to-all-done.1.got_ref, bf16[16,48,256]{2,1,0:T(8,128)(2,1)S(1)} %collective-permute-done.4.other_ref, bf16[256,2048]{1,0:T(8,128)(2,1)S(1)} %copy-done.1), custom_call_target="tpu_custom_call" | custom-call | flops 3000000000 | bytes 3000000 | tf_op jit(solution)/shard_map/kern_kernel/pallas_call | solution.py:197
  53.4 3.0 %all-to-all-start.2 = ((f32[32,2,128]{2,1,0:T(2,128)}), f32[32,2,128]{2,1,0:T(2,128)S(1)}, u32[]{:S(2)}, u32[]{:S(2)}) async-start(f32[32,2,128]{2,1,0:T(2,128)} %get-tuple-element.95), calls=%async_computation.2 | async-start | bytes 65536 | tf_op jit(solution)/shard_map/all_to_all | solution.py:703
  57.5 5.2 %student_kernel.1 = (bf16[1280,2048]{1,0:T(8,128)(2,1)}, f32[640,256]{1,0:T(8,128)S(1)}, f32[640,256]{1,0:T(8,128)S(1)}, f32[1280,1]{1,0:T(8,128)S(1)}) custom-call(bf16[1280,256]{1,0:T(8,128)(2,1)S(1)} %copy-done.21, bf16[256,2048]{1,0:T(8,128)(2,1)S(1)} %fusion.1.pnb_ref), custom_call_target="tpu_custom_call" | custom-call | flops 5000000000 | bytes 10000000 | tf_op jit(solution)/shard_map/student_kernel/pallas_call | solution.py:329
  64.3 3.0 %second_kernel.1 = f32[32,1,896]{2,1,0:T(1,128)} custom-call(s32[1]{0:T(128)} %bitcast.1.d_ref, f32[32,2,128]{2,1,0:T(2,128)} %copy-done.26, f32[256,2048]{1,0:T(8,128)} %get-tuple-element.96.kern_ref, f32[1280,1]{1,0:T(8,128)} %copy-done.19), custom_call_target="tpu_custom_call" | custom-call | flops 1000000000 | bytes 1000000 | tf_op jit(solution)/shard_map/second_kernel/pallas_call | solution.py:197
  67.5 5.7 %all-to-all-start.3 = ((f32[32,1,896]{2,1,0:T(1,128)}), f32[32,1,896]{2,1,0:T(1,128)S(1)}, u32[]{:S(2)}, u32[]{:S(2)}) async-start(f32[32,1,896]{2,1,0:T(1,128)} %second_kernel.1), calls=%async_computation.3 | async-start | bytes 229376 | tf_op jit(solution)/shard_map/all_to_all | solution.py:713
  74.4 6.6 %all-to-all-done.3.got_ref = f32[32,1,896]{2,1,0:T(1,128)S(1)} async-done(((f32[32,1,896]{2,1,0:T(1,128)}), f32[32,1,896]{2,1,0:T(1,128)S(1)}, u32[]{:S(2)}, u32[]{:S(2)}) %all-to-all-start.3) | async-done | bytes 114720 | tf_op jit(solution)/shard_map/all_to_all | solution.py:713
  81.0 3.2 %third_kernel.1 = (f32[640,1]{1,0:T(8,128)S(1)}, bf16[256,2048]{1,0:T(8,128)(2,1)}, f32[128,384]{1,0:T(8,128)S(1)}, f32[128,384]{1,0:T(8,128)S(1)}) custom-call(s32[1]{0:T(128)} %bitcast.1.d_ref, f32[32,1,896]{2,1,0:T(1,128)S(1)} %all-to-all-done.3.got_ref, f32[256,2048]{1,0:T(8,128)} %get-tuple-element.96.kern_ref, bf16[256,2048]{1,0:T(8,128)(2,1)S(1)} %fusion.1.pnb_ref), custom_call_target="tpu_custom_call" | custom-call | flops 2000000000 | bytes 2000000 | tf_op jit(solution)/shard_map/third_kernel/pallas_call | solution.py:197
  84.2 1.4 %collective-permute-done.6.b1_ref = f32[128,384]{1,0:T(8,128)S(1)} collective-permute-done((f32[128,384]{1,0:T(8,128)S(1)}, f32[128,384]{1,0:T(8,128)S(1)}, u32[]{:S(2)}, u32[]{:S(2)}) %collective-permute-start.6) | collective-permute-done | bytes 196640 | tf_op jit(solution)/shard_map/ppermute | solution.py:29
  86.5 3.6 %all-to-all-start.4 = ((bf16[16,56,256]{2,1,0:T(8,128)(2,1)}), bf16[16,56,256]{2,1,0:T(8,128)(2,1)S(1)}, u32[]{:S(2)}, u32[]{:S(2)}) async-start(bf16[16,56,256]{2,1,0:T(8,128)(2,1)} %message_kernel.1), calls=%async_computation.4 | async-start | bytes 917504 | tf_op jit(solution)/shard_map/all_to_all | solution.py:732
  92.0 4.4 %convolution_convert_fusion.refs_5_ = bf16[256,2048]{1,0:T(8,128)(2,1)S(1)} fusion(bf16[1280,2048]{1,0:T(8,128)(2,1)} %get-tuple-element.116, bf16[1280,256]{1,0:T(8,128)(2,1)} %copy-done.20, f32[1280]{0:T(1024)S(1)} %maximum_reduce_fusion), kind=kOutput, calls=%fused_computation.4 | convolution fusion | flops 1343684608 | bytes 6951936 | tf_op jit(solution)/shard_map/dot_general | solution.py:24
  96.4 7.9 %all-to-all-done.4.got_ref = bf16[16,56,256]{2,1,0:T(8,128)(2,1)S(1)} async-done(((bf16[16,56,256]{2,1,0:T(8,128)(2,1)}), bf16[16,56,256]{2,1,0:T(8,128)(2,1)S(1)}, u32[]{:S(2)}, u32[]{:S(2)}) %all-to-all-start.4) | async-done | bytes 458784 | tf_op jit(solution)/shard_map/all_to_all | solution.py:732
  105.3 4.0 %all-to-all-start.5 = ((bf16[16,48,256]{2,1,0:T(8,128)(2,1)}), bf16[16,48,256]{2,1,0:T(8,128)(2,1)S(1)}, u32[]{:S(2)}, u32[]{:S(2)}) async-start(bf16[16,48,256]{2,1,0:T(8,128)(2,1)} %bottleneck_kernel.1), calls=%async_computation.5 | async-start | bytes 786432 | tf_op jit(solution)/shard_map/all_to_all | solution.py:748
  109.4 1.2 copy-done.3
  110.6 3.5 %slopes_kernel.1 = (f32[640,512]{1,0:T(8,128)S(1)}, bf16[512,256]{1,0:T(8,128)(2,1)S(1)}, bf16[4,96,512]{2,1,0:T(8,128)(2,1)S(1)}) custom-call(s32[1]{0:T(128)} %bitcast.1.d_ref, s32[1]{0:T(128)} %bitcast.p_ref, bf16[640,1536]{1,0:T(8,128)(2,1)} %refs_9_.1, bf16[4,896,128]{2,1,0:T(8,128)(2,1)S(1)} %copy-done.3, ...), custom_call_target="tpu_custom_call" | custom-call | flops 4000000000 | bytes 30000000 | tf_op jit(solution)/shard_map/slopes_kernel/pallas_call | solution.py:457
  114.8 6.4 %all-to-all-done.5.refs_0_.refs_1_ = bf16[16,48,256]{2,1,0:T(8,128)(2,1)S(1)} async-done(((bf16[16,48,256]{2,1,0:T(8,128)(2,1)}), bf16[16,48,256]{2,1,0:T(8,128)(2,1)S(1)}, u32[]{:S(2)}, u32[]{:S(2)}) %all-to-all-start.5) | async-done | bytes 393248 | tf_op jit(solution)/shard_map/all_to_all | solution.py:748
  122.7 2.8 %features_kernel.1 = (bf16[640,256]{1,0:T(8,128)(2,1)S(1)}, f32[96,640]{1,0:T(8,128)S(1)}, bf16[96,640]{1,0:T(8,128)(2,1)S(1)}, bf16[96,640]{1,0:T(8,128)(2,1)S(1)}, bf16[96,640]{1,0:T(8,128)(2,1)S(1)}) custom-call(bf16[16,48,256]{2,1,0:T(8,128)(2,1)S(1)} %all-to-all-done.5.refs_0_.refs_1_, f32[1,640]{1,0:T(1,128)S(1)} %copy-done.18, ...), custom_call_target="tpu_custom_call" | custom-call | tf_op jit(solution)/shard_map/features_kernel/pallas_call | solution.py:529
  126.6 1.2 collective-permute-start.14
  127.8 2.1 %collective-permute-start.15 = (bf16[96,640]{1,0:T(8,128)(2,1)S(1)}, bf16[96,640]{1,0:T(8,128)(2,1)S(1)}, u32[]{:S(2)}, u32[]{:S(2)}) collective-permute-start(bf16[96,640]{1,0:T(8,128)(2,1)S(1)} %get-tuple-element.141), channel_id=1, source_target_pairs={{0,12},{1,13},{2,14},{3,15},{4,8},{5,9},{6,10},{7,11},{8,4},{9,5},... | collective-permute-start | bytes 368648 | tf_op jit(solution)/shard_map/ppermute | solution.py:29
  130.0 7.7 %last_kernel.1 = (f32[256,4096]{1,0:T(8,128)}, f32[1536,128]{1,0:T(8,128)}, f32[128,256]{1,0:T(8,128)}) custom-call(s32[1]{0:T(128)} %bitcast.1.d_ref, bf16[640,256]{1,0:T(8,128)(2,1)S(1)} %get-tuple-element.131.refs_0_, bf16[16,48,256]{2,1,0:T(8,128)(2,1)S(1)} %all-to-all-done.5.refs_0_.refs_1_, bf16[16,48,256]{2,1,0:T(8,128)(2,1)S(1)} %collective-permute-done.9.refs_2_, ...), custom_call_target="tpu_custom_call" | custom-call | tf_op jit(solution)/shard_map/last_kernel/pallas_call | solution.py:607
  (91 shorter events, 20.2 us)
Async XLA Ops:
  0.6 35.2 %collective-permute-start = (bf16[640,1536]{1,0:T(8,128)(2,1)}, bf16[640,1536]{1,0:T(8,128)(2,1)}, u32[]{:S(2)}, u32[]{:S(2)}) collective-permute-start(bf16[640,1536]{1,0:T(8,128)(2,1)} %refs_9_.1), channel_id=1, source_target_pairs={{0,16},{16,0},{1,17},{17,1},{2,18},{18,2},{3,19},{19,3},{4,20},{20... | collective-permute-start | bytes 5898248 | tf_op jit(solution)/shard_map/ppermute | solution.py:29
  6.6 29.2 %collective-permute-start.1 = (bf16[896,128]{1,0:T(8,128)(2,1)}, bf16[896,128]{1,0:T(8,128)(2,1)}, u32[]{:S(2)}, u32[]{:S(2)}) collective-permute-start(bf16[896,128]{1,0:T(8,128)(2,1)} %get-tuple-element.89), channel_id=1, source_target_pairs={{0,1},{1,0},{2,3},{3,2},{4,5},{5,4},{6,7},{7,6},{8,9},{9,8},{10,11... | collective-permute-start | bytes 688136 | tf_op jit(solution)/shard_map/ppermute | solution.py:29
  9.2 26.6 %collective-permute-start.2 = (bf16[896,128]{1,0:T(8,128)(2,1)}, bf16[896,128]{1,0:T(8,128)(2,1)}, u32[]{:S(2)}, u32[]{:S(2)}) collective-permute-start(bf16[896,128]{1,0:T(8,128)(2,1)} %get-tuple-element.89), channel_id=1, source_target_pairs={{0,2},{1,3},{2,0},{3,1},{4,6},{5,7},{6,4},{7,5},{8,10},{9,11},{10,... | collective-permute-start | bytes 688136 | tf_op jit(solution)/shard_map/ppermute | solution.py:29
  10.7 25.1 %collective-permute-start.3 = (bf16[896,128]{1,0:T(8,128)(2,1)}, bf16[896,128]{1,0:T(8,128)(2,1)}, u32[]{:S(2)}, u32[]{:S(2)}) collective-permute-start(bf16[896,128]{1,0:T(8,128)(2,1)} %get-tuple-element.89), channel_id=1, source_target_pairs={{0,3},{1,2},{2,1},{3,0},{4,7},{5,6},{6,5},{7,4},{8,11},{9,10},{10,... | collective-permute-start | bytes 688136 | tf_op jit(solution)/shard_map/ppermute | solution.py:29
  10.7 19.8 %all-to-all-start = ((bf16[16,48,256]{2,1,0:T(8,128)(2,1)}), bf16[16,48,256]{2,1,0:T(8,128)(2,1)S(1)}, u32[]{:S(2)}, u32[]{:S(2)}) async-start(bf16[16,48,256]{2,1,0:T(8,128)(2,1)} %get-tuple-element.76), calls=%async_computation | async-start | bytes 786432 | tf_op jit(solution)/shard_map/all_to_all | solution.py:668
  32.0 6.1 %copy-start = (bf16[640,1536]{1,0:T(8,128)(2,1)S(1)}, bf16[640,1536]{1,0:T(8,128)(2,1)}, u32[]{:S(2)}) copy-start(bf16[640,1536]{1,0:T(8,128)(2,1)} %refs_9_.1) | copy-start | bytes 5898244
  32.0 15.7 %all-to-all-start.1 = ((bf16[16,48,256]{2,1,0:T(8,128)(2,1)}), bf16[16,48,256]{2,1,0:T(8,128)(2,1)S(1)}, u32[]{:S(2)}, u32[]{:S(2)}) async-start(bf16[16,48,256]{2,1,0:T(8,128)(2,1)} %copy-done.4), calls=%async_computation.1 | async-start | bytes 786432 | tf_op jit(solution)/shard_map/all_to_all | solution.py:683
  47.7 1.7 %collective-permute-start.4 = (bf16[16,48,256]{2,1,0:T(8,128)(2,1)S(1)}, bf16[16,48,256]{2,1,0:T(8,128)(2,1)S(1)}, u32[]{:S(2)}, u32[]{:S(2)}) collective-permute-start(bf16[16,48,256]{2,1,0:T(8,128)(2,1)S(1)} %all-to-all-done.1.got_ref), channel_id=1, source_target_pairs={{0,16},{16,0},{1,17},{17,1},{2,18},{18,2},{3,19},{19,3},{4,20},{20... | collective-permute-start | bytes 1179656 | tf_op jit(solution)/shard_map/ppermute | solution.py:29
  53.4 10.2 %all-to-all-start.2 = ((f32[32,2,128]{2,1,0:T(2,128)}), f32[32,2,128]{2,1,0:T(2,128)S(1)}, u32[]{:S(2)}, u32[]{:S(2)}) async-start(f32[32,2,128]{2,1,0:T(2,128)} %get-tuple-element.95), calls=%async_computation.2 | async-start | bytes 65536 | tf_op jit(solution)/shard_map/all_to_all | solution.py:703
  67.3 6.0 %collective-permute-start.5 = (f32[640,256]{1,0:T(8,128)S(1)}, f32[640,256]{1,0:T(8,128)}, u32[]{:S(2)}, u32[]{:S(2)}) collective-permute-start(f32[640,256]{1,0:T(8,128)S(1)} %get-tuple-element.104), channel_id=1, source_target_pairs={{0,16},{16,0},{1,17},{17,1},{2,18},{18,2},{3,19},{19,3},{4,20},{20... | collective-permute-start | bytes 1966088 | tf_op jit(solution)/shard_map/ppermute | solution.py:29
  67.5 13.6 %all-to-all-start.3 = ((f32[32,1,896]{2,1,0:T(1,128)}), f32[32,1,896]{2,1,0:T(1,128)S(1)}, u32[]{:S(2)}, u32[]{:S(2)}) async-start(f32[32,1,896]{2,1,0:T(1,128)} %second_kernel.1), calls=%async_computation.3 | async-start | bytes 229376 | tf_op jit(solution)/shard_map/all_to_all | solution.py:713
  84.2 1.4 %collective-permute-start.6 = (f32[128,384]{1,0:T(8,128)S(1)}, f32[128,384]{1,0:T(8,128)S(1)}, u32[]{:S(2)}, u32[]{:S(2)}) collective-permute-start(f32[128,384]{1,0:T(8,128)S(1)} %get-tuple-element.108), channel_id=1, source_target_pairs={{0,16},{16,0},{1,17},{17,1},{2,18},{18,2},{3,19},{19,3},{4,20},{20... | collective-permute-start | bytes 589832 | tf_op jit(solution)/shard_map/ppermute | solution.py:29
  85.7 4.4 %copy-start.10 = (f32[640,1]{1,0:T(8,128)S(1)}, f32[640,1]{1,0:T(8,128)}, u32[]{:S(2)}) copy-start(f32[640,1]{1,0:T(8,128)} %get-tuple-element.114.view_ref) | copy-start | bytes 7684
  85.7 4.7 %copy-start.2 = (bf16[4,896,128]{2,1,0:T(8,128)(2,1)S(1)}, bf16[4,896,128]{2,1,0:T(8,128)(2,1)}, u32[]{:S(2)}) copy-start(bf16[4,896,128]{2,1,0:T(8,128)(2,1)} %pad_maximum_fusion.own_ref) | copy-start | bytes 2752516
  86.5 17.8 %all-to-all-start.4 = ((bf16[16,56,256]{2,1,0:T(8,128)(2,1)}), bf16[16,56,256]{2,1,0:T(8,128)(2,1)S(1)}, u32[]{:S(2)}, u32[]{:S(2)}) async-start(bf16[16,56,256]{2,1,0:T(8,128)(2,1)} %message_kernel.1), calls=%async_computation.4 | async-start | bytes 917504 | tf_op jit(solution)/shard_map/all_to_all | solution.py:732
  90.1 1.7 %collective-permute-start.7 = (f32[640,1]{1,0:T(8,128)S(1)}, f32[640,1]{1,0:T(8,128)S(1)}, u32[]{:S(2)}, u32[]{:S(2)}) collective-permute-start(f32[640,1]{1,0:T(8,128)S(1)} %multiply_divide_fusion.scale_ref), channel_id=1, source_target_pairs={{0,16},{16,0},{1,17},{17,1},{2,18},{18,2},{3,19},{19,3},{4,20},{20... | collective-permute-start | bytes 7688 | tf_op jit(solution)/shard_map/ppermute | solution.py:29
  90.3 19.1 %collective-permute-start.8 = (bf16[4,896,128]{2,1,0:T(8,128)(2,1)S(1)}, bf16[4,896,128]{2,1,0:T(8,128)(2,1)}, u32[]{:S(2)}, u32[]{:S(2)}) collective-permute-start(bf16[4,896,128]{2,1,0:T(8,128)(2,1)S(1)} %copy-done.2), channel_id=1, source_target_pairs={{0,16},{16,0},{1,17},{17,1},{2,18},{18,2},{3,19},{19,3},{4,20},{20... | collective-permute-start | bytes 2752520 | tf_op jit(solution)/shard_map/ppermute | solution.py:29
  90.8 37.0 %collective-permute-start.12 = (bf16[256,2048]{1,0:T(8,128)(2,1)}, bf16[256,2048]{1,0:T(8,128)(2,1)}, u32[]{:S(2)}, u32[]{:S(2)}) collective-permute-start(bf16[256,2048]{1,0:T(8,128)(2,1)} %get-tuple-element.133.refs_7_), channel_id=1, source_target_pairs={{0,16},{16,0},{1,17},{17,1},{2,18},{18,2},{3,19},{19,3},{4,20},{20... | collective-permute-start | bytes 3145736 | tf_op jit(solution)/shard_map/ppermute | solution.py:29
  92.0 12.3 %copy-start.23 = (f32[48,384]{1,0:T(8,128)S(1)}, f32[48,384]{1,0:T(8,128)}, u32[]{:S(2)}) copy-start(f32[48,384]{1,0:T(8,128)} %copy-done.22) | copy-start | bytes 221188
  105.3 15.9 %copy-start.18 = (f32[1,640]{1,0:T(1,128)S(1)}, f32[1,640]{1,0:T(1,128)}, u32[]{:S(2)}) copy-start(f32[1,640]{1,0:T(1,128)} %get-tuple-element.126.refs_1_) | copy-start | bytes 7684
  105.3 15.9 %all-to-all-start.5 = ((bf16[16,48,256]{2,1,0:T(8,128)(2,1)}), bf16[16,48,256]{2,1,0:T(8,128)(2,1)S(1)}, u32[]{:S(2)}, u32[]{:S(2)}) async-start(bf16[16,48,256]{2,1,0:T(8,128)(2,1)} %bottleneck_kernel.1), calls=%async_computation.5 | async-start | bytes 786432 | tf_op jit(solution)/shard_map/all_to_all | solution.py:748
  109.3 20.6 %collective-permute-start.11 = (bf16[256,2048]{1,0:T(8,128)(2,1)S(1)}, bf16[256,2048]{1,0:T(8,128)(2,1)}, u32[]{:S(2)}, u32[]{:S(2)}) collective-permute-start(bf16[256,2048]{1,0:T(8,128)(2,1)S(1)} %convolution_convert_fusion.refs_5_), channel_id=1, source_target_pairs={{0,16},{16,0},{1,17},{17,1},{2,18},{18,2},{3,19},{19,3},{4,20},{20... | collective-permute-start | bytes 3145736 | tf_op jit(solution)/shard_map/ppermute | solution.py:29
  114.8 15.1 %copy-start.7 = (f32[128,640]{1,0:T(8,128)S(1)}, f32[128,640]{1,0:T(8,128)}, u32[]{:S(2)}) copy-start(f32[128,640]{1,0:T(8,128)} %copy-done.6) | copy-start | bytes 983044
  114.8 15.1 %copy-start.11 = (bf16[128,256]{1,0:T(8,128)(2,1)S(1)}, bf16[128,256]{1,0:T(8,128)(2,1)}, u32[]{:S(2)}) copy-start(bf16[128,256]{1,0:T(8,128)(2,1)} %refs_15_.1) | copy-start | bytes 196612
  121.2 8.7 %copy-start.9 = (f32[128,640]{1,0:T(8,128)S(1)}, f32[128,640]{1,0:T(8,128)}, u32[]{:S(2)}) copy-start(f32[128,640]{1,0:T(8,128)} %copy-done.8) | copy-start | bytes 983044
  121.2 8.7 %collective-permute-start.9 = (bf16[16,48,256]{2,1,0:T(8,128)(2,1)S(1)}, bf16[16,48,256]{2,1,0:T(8,128)(2,1)S(1)}, u32[]{:S(2)}, u32[]{:S(2)}) collective-permute-start(bf16[16,48,256]{2,1,0:T(8,128)(2,1)S(1)} %all-to-all-done.5.refs_0_.refs_1_), channel_id=1, source_target_pairs={{0,16},{16,0},{1,17},{17,1},{2,18},{18,2},{3,19},{19,3},{4,20},{20... | collective-permute-start | bytes 1179656 | tf_op jit(solution)/shard_map/ppermute | solution.py:29
  121.2 5.4 %collective-permute-start.10 = (f32[1,640]{1,0:T(1,128)S(1)}, f32[1,640]{1,0:T(1,128)S(1)}, u32[]{:S(2)}, u32[]{:S(2)}) collective-permute-start(f32[1,640]{1,0:T(1,128)S(1)} %copy-done.18), channel_id=1, source_target_pairs={{0,16},{16,0},{1,17},{17,1},{2,18},{18,2},{3,19},{19,3},{4,20},{20... | collective-permute-start | bytes 7688 | tf_op jit(solution)/shard_map/ppermute | solution.py:29
  122.7 7.3 %copy-start.15 = (bf16[128,640]{1,0:T(8,128)(2,1)S(1)}, bf16[128,640]{1,0:T(8,128)(2,1)}, u32[]{:S(2)}) copy-start(bf16[128,640]{1,0:T(8,128)(2,1)} %copy-done.14) | copy-start | bytes 491524
  122.7 7.3 %copy-start.17 = (bf16[128,640]{1,0:T(8,128)(2,1)S(1)}, bf16[128,640]{1,0:T(8,128)(2,1)}, u32[]{:S(2)}) copy-start(bf16[128,640]{1,0:T(8,128)(2,1)} %copy-done.16) | copy-start | bytes 491524
  125.5 12.2 %collective-permute-start.13 = (bf16[96,640]{1,0:T(8,128)(2,1)S(1)}, bf16[96,640]{1,0:T(8,128)(2,1)S(1)}, u32[]{:S(2)}, u32[]{:S(2)}) collective-permute-start(bf16[96,640]{1,0:T(8,128)(2,1)S(1)} %get-tuple-element.139), channel_id=1, source_target_pairs={{0,4},{1,5},{2,6},{3,7},{4,0},{5,1},{6,2},{7,3},{8,12},{9,13},{10,... | collective-permute-start | bytes 368648 | tf_op jit(solution)/shard_map/ppermute | solution.py:29
  126.6 12.0 %collective-permute-start.14 = (bf16[96,640]{1,0:T(8,128)(2,1)S(1)}, bf16[96,640]{1,0:T(8,128)(2,1)S(1)}, u32[]{:S(2)}, u32[]{:S(2)}) collective-permute-start(bf16[96,640]{1,0:T(8,128)(2,1)S(1)} %get-tuple-element.140), channel_id=1, source_target_pairs={{0,8},{1,9},{2,10},{3,11},{4,12},{5,13},{6,14},{7,15},{8,0},{9,1},... | collective-permute-start | bytes 368648 | tf_op jit(solution)/shard_map/ppermute | solution.py:29
  127.8 10.8 %collective-permute-start.15 = (bf16[96,640]{1,0:T(8,128)(2,1)S(1)}, bf16[96,640]{1,0:T(8,128)(2,1)S(1)}, u32[]{:S(2)}, u32[]{:S(2)}) collective-permute-start(bf16[96,640]{1,0:T(8,128)(2,1)S(1)} %get-tuple-element.141), channel_id=1, source_target_pairs={{0,12},{1,13},{2,14},{3,15},{4,8},{5,9},{6,10},{7,11},{8,4},{9,5},... | collective-permute-start | bytes 368648 | tf_op jit(solution)/shard_map/ppermute | solution.py:29
  (17 other events, 17.7 us)

commit v9 on v8

--- a/solution.py
+++ b/solution.py
@@ -664,7 +664,6 @@
         compiler_params=params(62),
         name="head_kernel",
     )(d.reshape(1), *heads, crop_image, crop_view)
-    weights = [weights] + [swap(weights, "proto", k) for k in range(1, NEAR)]
     parts_got = lax.all_to_all(parts, "proto", 0, 0)
     protos_late, tprotos_late, _ = tied(protos, teacher_protos, parts)
     cols = protos.shape[1] // nd
@@ -681,7 +680,7 @@
     )
     sent = got
     got = lax.all_to_all(got, "proto", 0, 0)
-    w1_late, feat_late, feat_other_late, weights, _ = tied(head_w1, features, feat_other, weights, sent)
+    w1_late, feat_late, feat_other_late, _ = tied(head_w1, features, feat_other, sent)
     h0, h1, s0, s1 = call(
         hidden_kernel,
         (shape((hs, rows), BF16),) * 2 + (shape((hs, rows), F32),) * 2,
@@ -689,9 +688,7 @@
         feat_late, feat_other_late, w1_late,
         us=4,
     )
-    weights = jnp.stack(weights)
-    got, h0, h1, s0, s1, weights = tied(got, h0, h1, s0, s1, weights)
-    weights_other = swap(weights, "dp", 1)
+    got, h0, h1, s0, s1 = tied(got, h0, h1, s0, s1)
     got_other = swap(got, "dp", 1)
     kern, msg, student = call(
         kern_kernel,
@@ -701,7 +698,8 @@
         us=3,
     )
     msg_got = lax.all_to_all(msg, ALL, 0, 0)
-    student, _ = tied(student, msg)
+    student, weights, _ = tied(student, weights, msg)
+    weights = [weights] + [swap(weights, "proto", k) for k in range(1, NEAR)]
     exb, sums, sums_other, esum = student_sums(student, pnb)
     msg = call(
         second_kernel,
@@ -711,10 +709,12 @@
         mib=56,
     )
     msg_got = lax.all_to_all(msg, ALL, 0, 0)
-    sums, sums_other, _ = tied(sums, sums_other, msg)
+    sums, sums_other, *weights, _ = tied(sums, sums_other, *weights, msg)
+    weights = jnp.stack(weights)
     sums_other = swap(sums_other, "dp", 1)
     sums = (sums + sums_other).astype(BF16)
-    msg_got, sums = tied(msg_got, sums)
+    msg_got, sums, weights = tied(msg_got, sums, weights)
+    weights_other = swap(weights, "dp", 1)
     esum, last, mine, yours = call(
         third_kernel,
         (

time: 140 us -> 138 us (0.986)
  local copies, waits for them, and re-layouts: 13.3 us -> 10.4 us
  waiting for transfers between devices: 37.2 us -> 39.9 us
    unnamed x54, local copies, waits for them, and re-layouts: 13.1 us -> 10.2 us
    all_to_all x1, waiting for transfers between devices: 2.89 us -> 5.27 us  [paired_body(): got = lax.all_to_all(got, 'proto', 0, 0)]
    all_to_all x2, waiting for transfers between devices: 6.68 us -> 5 us  [paired_body(): msg_got = lax.all_to_all(msg, ALL, 0, 0)]
  transfers between devices with their start and end apart: 22 -> 22, of which waited for: 9 -> 11; matrix products, arithmetic and copies ran while one was open for 8% -> 8% of each run, Pallas kernels for 21% -> 23%
where the time goes in v9:
time: 138 us; the launch traced here: 137 us
  waiting for transfers between devices  39.9 us (29%)
  Pallas kernels  37.7 us (27%)
  starting transfers between devices  37 us (27%)
  local copies, waits for them, and re-layouts  10.4 us (8%)
  other arithmetic  7.14 us (5%)
  matrix products  4.34 us (3%)
    pallas_call x7, Pallas kernels, call(): pl.pallas_call(kernel, grid=(1,), out_shape=outs, in_specs=[pl.BlockSpec(...  13 us
    unnamed x54, local copies, waits for them, and re-layouts  10.2 us
    ppermute x16, starting transfers between devices, swap(): return lax.ppermute(value, axis, [(i, i ^ step) for i in range(count)])  9.87 us
    all_to_all x1, waiting for transfers between devices, paired_body(): parts_got = lax.all_to_all(parts, 'proto', 0, 0)  9.55 us
    all_to_all x1, starting transfers between devices, paired_body(): parts_got = lax.all_to_all(parts, 'proto', 0, 0)  8.03 us
    all_to_all x1, waiting for transfers between devices, paired_body(): msg_got = lax.all_to_all(msg, 'proto', 0, 0)  7.97 us
    all_to_all x2, starting transfers between devices, paired_body(): msg_got = lax.all_to_all(msg, ALL, 0, 0)  7.81 us
    pallas_call x1, Pallas kernels, last_grads(): pl.pallas_call(functools.partial(last_kernel, tile), name='last_kernel',...  7.7 us
  transfers between devices with their start and end apart: 22, of which 11 were waited for; matrix products, arithmetic and copies ran while one was open for 8% of the time, Pallas kernels for 23%

profile of v9, /device:TPU:0, one launch (start us, length us, event | category | flops | bytes accessed | tf_op | source)
XLA Modules:
  0.0 137.5 jit_solution(2929590005400885791)
XLA Ops:
  1.2 5.4 %head_kernel.1 = (bf16[16,48,256]{2,1,0:T(8,128)(2,1)}, f32[1,640]{1,0:T(1,128)}, f32[640,1]{1,0:T(8,128)}, bf16[896,128]{1,0:T(8,128)(2,1)}) custom-call(s32[1]{0:T(128)} %bitcast.1.d_ref, bf16[640,1536]{1,0:T(8,128)(2,1)} %refs_9_.1, bf16[1536,128]{1,0:T(8,128)(2,1)} %w1_ref, bf16[128,256]{1,0:T(8,128)(2,1)} %refs_15_.1, bf16[128,1536]{1,0:T(8,128)(2,1)} %refs_3_.1, ...), custom_call_target="tpu_custom_call" | custom-call | tf_op jit(solution)/shard_map/head_kernel/pallas_call | solution.py:650
  6.6 8.0 %all-to-all-start = ((bf16[16,48,256]{2,1,0:T(8,128)(2,1)}), bf16[16,48,256]{2,1,0:T(8,128)(2,1)S(1)}, u32[]{:S(2)}, u32[]{:S(2)}) async-start(bf16[16,48,256]{2,1,0:T(8,128)(2,1)} %get-tuple-element.77), calls=%async_computation | async-start | bytes 786432 | tf_op jit(solution)/shard_map/all_to_all | solution.py:667
  14.7 2.1 %fusion = (f32[2048]{0:T(1024)S(1)}, f32[2048]{0:T(1024)S(1)}) fusion(bf16[256,4096]{1,0:T(8,128)(2,1)} %refs_4_.3, s32[]{:T(128)S(6)} %select_n.8, bf16[256,4096]{1,0:T(8,128)(2,1)} %param.19), kind=kLoop, calls=%fused_computation.5 | loop fusion | flops 3141632 | bytes 2113540 | tf_op jit(solution)/shard_map/reduce_sum | solution.py:49
  16.8 1.2 fusion.3.tpnb_ref
  18.3 9.6 %all-to-all-done.parts_ref = bf16[16,48,256]{2,1,0:T(8,128)(2,1)S(1)} async-done(((bf16[16,48,256]{2,1,0:T(8,128)(2,1)}), bf16[16,48,256]{2,1,0:T(8,128)(2,1)S(1)}, u32[]{:S(2)}, u32[]{:S(2)}) %all-to-all-start) | async-done | bytes 393248 | tf_op jit(solution)/shard_map/all_to_all | solution.py:667
  28.7 3.7 %all-to-all-start.1 = ((bf16[16,48,256]{2,1,0:T(8,128)(2,1)}), bf16[16,48,256]{2,1,0:T(8,128)(2,1)S(1)}, u32[]{:S(2)}, u32[]{:S(2)}) async-start(bf16[16,48,256]{2,1,0:T(8,128)(2,1)} %copy-done.4), calls=%async_computation.1 | async-start | bytes 786432 | tf_op jit(solution)/shard_map/all_to_all | solution.py:682
  33.5 2.9 %hidden_kernel.1 = (bf16[128,640]{1,0:T(8,128)(2,1)S(1)}, bf16[128,640]{1,0:T(8,128)(2,1)S(1)}, f32[128,640]{1,0:T(8,128)S(1)}, f32[128,640]{1,0:T(8,128)S(1)}) custom-call(bf16[640,1536]{1,0:T(8,128)(2,1)S(1)} %copy-done, bf16[640,1536]{1,0:T(8,128)(2,1)} %collective-permute-done.f1_ref.refs_10_, bf16[1536,128]{1,0:T(8,128)(2,1)S(1)} %copy-done.5), custom_call_target="tpu_custom_call" | custom-call | flops 4000000000 | bytes 4000000 | tf_op jit(solution)/shard_map/hidden_kernel/pallas_call | solution.py:197
  39.2 5.3 %all-to-all-done.1.got_ref = bf16[16,48,256]{2,1,0:T(8,128)(2,1)S(1)} async-done(((bf16[16,48,256]{2,1,0:T(8,128)(2,1)}), bf16[16,48,256]{2,1,0:T(8,128)(2,1)S(1)}, u32[]{:S(2)}, u32[]{:S(2)}) %all-to-all-start.1) | async-done | bytes 393248 | tf_op jit(solution)/shard_map/all_to_all | solution.py:682
  44.5 1.7 %collective-permute-done.1.other_ref = bf16[16,48,256]{2,1,0:T(8,128)(2,1)S(1)} collective-permute-done((bf16[16,48,256]{2,1,0:T(8,128)(2,1)S(1)}, bf16[16,48,256]{2,1,0:T(8,128)(2,1)S(1)}, u32[]{:S(2)}, u32[]{:S(2)}) %collective-permute-start.1) | collective-permute-done | bytes 393248 | tf_op jit(solution)/shard_map/ppermute | solution.py:29
  46.2 1.2 copy-done.1
  47.4 1.9 %kern_kernel.1 = (f32[256,2048]{1,0:T(8,128)}, f32[32,2,128]{2,1,0:T(2,128)}, bf16[1280,256]{1,0:T(8,128)(2,1)S(1)}) custom-call(s32[1]{0:T(128)} %bitcast.1.d_ref, bf16[16,48,256]{2,1,0:T(8,128)(2,1)S(1)} %all-to-all-done.1.got_ref, bf16[16,48,256]{2,1,0:T(8,128)(2,1)S(1)} %collective-permute-done.1.other_ref, bf16[256,2048]{1,0:T(8,128)(2,1)S(1)} %copy-done.1), custom_call_target="tpu_custom_call" | custom-call | flops 3000000000 | bytes 3000000 | tf_op jit(solution)/shard_map/kern_kernel/pallas_call | solution.py:197
  49.3 2.6 %all-to-all-start.2 = ((f32[32,2,128]{2,1,0:T(2,128)}), f32[32,2,128]{2,1,0:T(2,128)S(1)}, u32[]{:S(2)}, u32[]{:S(2)}) async-start(f32[32,2,128]{2,1,0:T(2,128)} %get-tuple-element.91), calls=%async_computation.2 | async-start | bytes 65536 | tf_op jit(solution)/shard_map/all_to_all | solution.py:700
  52.0 2.7 %collective-permute-start.4 = (bf16[896,128]{1,0:T(8,128)(2,1)S(1)}, bf16[896,128]{1,0:T(8,128)(2,1)S(1)}, u32[]{:S(2)}, u32[]{:S(2)}) collective-permute-start(bf16[896,128]{1,0:T(8,128)(2,1)S(1)} %copy-done.23), channel_id=1, source_target_pairs={{0,3},{1,2},{2,1},{3,0},{4,7},{5,6},{6,5},{7,4},{8,11},{9,10},{10,... | collective-permute-start | bytes 688136 | tf_op jit(solution)/shard_map/ppermute | solution.py:29
  55.5 5.3 %student_kernel.1 = (bf16[1280,2048]{1,0:T(8,128)(2,1)}, f32[640,256]{1,0:T(8,128)S(1)}, f32[640,256]{1,0:T(8,128)}, f32[1280,1]{1,0:T(8,128)S(1)}) custom-call(bf16[1280,256]{1,0:T(8,128)(2,1)S(1)} %get-tuple-element.95.z_ref, bf16[256,2048]{1,0:T(8,128)(2,1)S(1)} %fusion.1.pnb_ref), custom_call_target="tpu_custom_call" | custom-call | flops 5000000000 | bytes 10000000 | tf_op jit(solution)/shard_map/student_kernel/pallas_call | solution.py:329
  62.3 3.0 %second_kernel.1 = f32[32,1,896]{2,1,0:T(1,128)} custom-call(s32[1]{0:T(128)} %bitcast.1.d_ref, f32[32,2,128]{2,1,0:T(2,128)} %copy-done.26, f32[256,2048]{1,0:T(8,128)} %get-tuple-element.92.kern_ref, f32[1280,1]{1,0:T(8,128)} %copy-done.19), custom_call_target="tpu_custom_call" | custom-call | flops 1000000000 | bytes 1000000 | tf_op jit(solution)/shard_map/second_kernel/pallas_call | solution.py:197
  66.2 5.2 %all-to-all-start.3 = ((f32[32,1,896]{2,1,0:T(1,128)}), f32[32,1,896]{2,1,0:T(1,128)S(1)}, u32[]{:S(2)}, u32[]{:S(2)}) async-start(f32[32,1,896]{2,1,0:T(1,128)} %second_kernel.1), calls=%async_computation.3 | async-start | bytes 229376 | tf_op jit(solution)/shard_map/all_to_all | solution.py:711
  71.4 1.3 pad_maximum_fusion.own_ref
  72.7 1.5 %add_convert_fusion.sums_ref = bf16[640,256]{1,0:T(8,128)(2,1)S(1)} fusion(f32[640,256]{1,0:T(8,128)S(1)} %get-tuple-element.101, f32[640,256]{1,0:T(8,128)} %collective-permute-done.5), kind=kLoop, calls=%fused_computation.12 | loop fusion | flops 327680 | bytes 1638400 | tf_op jit(solution)/shard_map/convert_element_type | solution.py:715
  74.2 5.0 %all-to-all-done.3.got_ref = f32[32,1,896]{2,1,0:T(1,128)S(1)} async-done(((f32[32,1,896]{2,1,0:T(1,128)}), f32[32,1,896]{2,1,0:T(1,128)S(1)}, u32[]{:S(2)}, u32[]{:S(2)}) %all-to-all-start.3) | async-done | bytes 114720 | tf_op jit(solution)/shard_map/all_to_all | solution.py:711
  79.2 3.2 %third_kernel.1 = (f32[640,1]{1,0:T(8,128)S(1)}, bf16[256,2048]{1,0:T(8,128)(2,1)}, f32[128,384]{1,0:T(8,128)S(1)}, f32[128,384]{1,0:T(8,128)S(1)}) custom-call(s32[1]{0:T(128)} %bitcast.1.d_ref, f32[32,1,896]{2,1,0:T(1,128)S(1)} %all-to-all-done.3.got_ref, f32[256,2048]{1,0:T(8,128)} %get-tuple-element.92.kern_ref, bf16[256,2048]{1,0:T(8,128)(2,1)S(1)} %fusion.1.pnb_ref), custom_call_target="tpu_custom_call" | custom-call | flops 2000000000 | bytes 2000000 | tf_op jit(solution)/shard_map/third_kernel/pallas_call | solution.py:197
  82.3 1.4 %collective-permute-done.6.b1_ref = f32[128,384]{1,0:T(8,128)S(1)} collective-permute-done((f32[128,384]{1,0:T(8,128)S(1)}, f32[128,384]{1,0:T(8,128)S(1)}, u32[]{:S(2)}, u32[]{:S(2)}) %collective-permute-start.6) | collective-permute-done | bytes 196640 | tf_op jit(solution)/shard_map/ppermute | solution.py:29
  84.6 3.6 %all-to-all-start.4 = ((bf16[16,56,256]{2,1,0:T(8,128)(2,1)}), bf16[16,56,256]{2,1,0:T(8,128)(2,1)S(1)}, u32[]{:S(2)}, u32[]{:S(2)}) async-start(bf16[16,56,256]{2,1,0:T(8,128)(2,1)} %message_kernel.1), calls=%async_computation.4 | async-start | bytes 917504 | tf_op jit(solution)/shard_map/all_to_all | solution.py:732
  90.1 4.3 %convolution_convert_fusion.refs_5_ = bf16[256,2048]{1,0:T(8,128)(2,1)S(1)} fusion(bf16[1280,2048]{1,0:T(8,128)(2,1)} %get-tuple-element.118, bf16[1280,256]{1,0:T(8,128)(2,1)} %copy-done.20, f32[1280]{0:T(1024)S(1)} %maximum_reduce_fusion), kind=kOutput, calls=%fused_computation.4 | convolution fusion | flops 1343684608 | bytes 6951936 | tf_op jit(solution)/shard_map/dot_general | solution.py:24
  94.5 8.0 %all-to-all-done.4.got_ref = bf16[16,56,256]{2,1,0:T(8,128)(2,1)S(1)} async-done(((bf16[16,56,256]{2,1,0:T(8,128)(2,1)}), bf16[16,56,256]{2,1,0:T(8,128)(2,1)S(1)}, u32[]{:S(2)}, u32[]{:S(2)}) %all-to-all-start.4) | async-done | bytes 458784 | tf_op jit(solution)/shard_map/all_to_all | solution.py:732
  103.4 4.0 %all-to-all-start.5 = ((bf16[16,48,256]{2,1,0:T(8,128)(2,1)}), bf16[16,48,256]{2,1,0:T(8,128)(2,1)S(1)}, u32[]{:S(2)}, u32[]{:S(2)}) async-start(bf16[16,48,256]{2,1,0:T(8,128)(2,1)} %bottleneck_kernel.1), calls=%async_computation.5 | async-start | bytes 786432 | tf_op jit(solution)/shard_map/all_to_all | solution.py:748
  107.5 1.2 copy-done.3
  108.7 3.5 %slopes_kernel.1 = (f32[640,512]{1,0:T(8,128)S(1)}, bf16[512,256]{1,0:T(8,128)(2,1)S(1)}, bf16[4,96,512]{2,1,0:T(8,128)(2,1)S(1)}) custom-call(s32[1]{0:T(128)} %bitcast.1.d_ref, s32[1]{0:T(128)} %bitcast.p_ref, bf16[640,1536]{1,0:T(8,128)(2,1)} %refs_9_.1, bf16[4,896,128]{2,1,0:T(8,128)(2,1)S(1)} %copy-done.3, ...), custom_call_target="tpu_custom_call" | custom-call | flops 4000000000 | bytes 30000000 | tf_op jit(solution)/shard_map/slopes_kernel/pallas_call | solution.py:457
  112.9 6.4 %all-to-all-done.5.refs_0_.refs_1_ = bf16[16,48,256]{2,1,0:T(8,128)(2,1)S(1)} async-done(((bf16[16,48,256]{2,1,0:T(8,128)(2,1)}), bf16[16,48,256]{2,1,0:T(8,128)(2,1)S(1)}, u32[]{:S(2)}, u32[]{:S(2)}) %all-to-all-start.5) | async-done | bytes 393248 | tf_op jit(solution)/shard_map/all_to_all | solution.py:748
  120.8 2.8 %features_kernel.1 = (bf16[640,256]{1,0:T(8,128)(2,1)S(1)}, f32[96,640]{1,0:T(8,128)S(1)}, bf16[96,640]{1,0:T(8,128)(2,1)S(1)}, bf16[96,640]{1,0:T(8,128)(2,1)S(1)}, bf16[96,640]{1,0:T(8,128)(2,1)S(1)}) custom-call(bf16[16,48,256]{2,1,0:T(8,128)(2,1)S(1)} %all-to-all-done.5.refs_0_.refs_1_, f32[1,640]{1,0:T(1,128)S(1)} %copy-done.18, ...), custom_call_target="tpu_custom_call" | custom-call | tf_op jit(solution)/shard_map/features_kernel/pallas_call | solution.py:529
  124.7 1.2 collective-permute-start.14
  125.9 2.1 %collective-permute-start.15 = (bf16[96,640]{1,0:T(8,128)(2,1)S(1)}, bf16[96,640]{1,0:T(8,128)(2,1)S(1)}, u32[]{:S(2)}, u32[]{:S(2)}) collective-permute-start(bf16[96,640]{1,0:T(8,128)(2,1)S(1)} %get-tuple-element.143), channel_id=1, source_target_pairs={{0,12},{1,13},{2,14},{3,15},{4,8},{5,9},{6,10},{7,11},{8,4},{9,5},... | collective-permute-start | bytes 368648 | tf_op jit(solution)/shard_map/ppermute | solution.py:29
  128.1 7.7 %last_kernel.1 = (f32[256,4096]{1,0:T(8,128)}, f32[1536,128]{1,0:T(8,128)}, f32[128,256]{1,0:T(8,128)}) custom-call(s32[1]{0:T(128)} %bitcast.1.d_ref, bf16[640,256]{1,0:T(8,128)(2,1)S(1)} %get-tuple-element.133.refs_0_, bf16[16,48,256]{2,1,0:T(8,128)(2,1)S(1)} %all-to-all-done.5.refs_0_.refs_1_, bf16[16,48,256]{2,1,0:T(8,128)(2,1)S(1)} %collective-permute-done.9.refs_2_, ...), custom_call_target="tpu_custom_call" | custom-call | tf_op jit(solution)/shard_map/last_kernel/pallas_call | solution.py:607
  (91 shorter events, 17.4 us)
Async XLA Ops:
  0.6 31.8 %collective-permute-start = (bf16[640,1536]{1,0:T(8,128)(2,1)}, bf16[640,1536]{1,0:T(8,128)(2,1)}, u32[]{:S(2)}, u32[]{:S(2)}) collective-permute-start(bf16[640,1536]{1,0:T(8,128)(2,1)} %refs_9_.1), channel_id=1, source_target_pairs={{0,16},{16,0},{1,17},{17,1},{2,18},{18,2},{3,19},{19,3},{4,20},{20... | collective-permute-start | bytes 5898248 | tf_op jit(solution)/shard_map/ppermute | solution.py:29
  6.6 10.2 %copy-start.22 = (bf16[256,4096]{1,0:T(8,128)(2,1)S(1)}, bf16[256,4096]{1,0:T(8,128)(2,1)}, u32[]{:S(2)}) copy-start(bf16[256,4096]{1,0:T(8,128)(2,1)} %param.19) | copy-start | bytes 6291460
  6.6 21.2 %all-to-all-start = ((bf16[16,48,256]{2,1,0:T(8,128)(2,1)}), bf16[16,48,256]{2,1,0:T(8,128)(2,1)S(1)}, u32[]{:S(2)}, u32[]{:S(2)}) async-start(bf16[16,48,256]{2,1,0:T(8,128)(2,1)} %get-tuple-element.77), calls=%async_computation | async-start | bytes 786432 | tf_op jit(solution)/shard_map/all_to_all | solution.py:667
  18.3 14.2 %copy-start = (bf16[640,1536]{1,0:T(8,128)(2,1)S(1)}, bf16[640,1536]{1,0:T(8,128)(2,1)}, u32[]{:S(2)}) copy-start(bf16[640,1536]{1,0:T(8,128)(2,1)} %refs_9_.1) | copy-start | bytes 5898244
  28.7 15.7 %all-to-all-start.1 = ((bf16[16,48,256]{2,1,0:T(8,128)(2,1)}), bf16[16,48,256]{2,1,0:T(8,128)(2,1)S(1)}, u32[]{:S(2)}, u32[]{:S(2)}) async-start(bf16[16,48,256]{2,1,0:T(8,128)(2,1)} %copy-done.4), calls=%async_computation.1 | async-start | bytes 786432 | tf_op jit(solution)/shard_map/all_to_all | solution.py:682
  44.5 1.7 %collective-permute-start.1 = (bf16[16,48,256]{2,1,0:T(8,128)(2,1)S(1)}, bf16[16,48,256]{2,1,0:T(8,128)(2,1)S(1)}, u32[]{:S(2)}, u32[]{:S(2)}) collective-permute-start(bf16[16,48,256]{2,1,0:T(8,128)(2,1)S(1)} %all-to-all-done.1.got_ref), channel_id=1, source_target_pairs={{0,16},{16,0},{1,17},{17,1},{2,18},{18,2},{3,19},{19,3},{4,20},{20... | collective-permute-start | bytes 1179656 | tf_op jit(solution)/shard_map/ppermute | solution.py:29
  49.3 11.4 %copy-start.20 = (bf16[1280,256]{1,0:T(8,128)(2,1)}, bf16[1280,256]{1,0:T(8,128)(2,1)S(1)}, u32[]{:S(2)}) copy-start(bf16[1280,256]{1,0:T(8,128)(2,1)S(1)} %get-tuple-element.95.z_ref) | copy-start | bytes 1966084
  49.3 12.3 %all-to-all-start.2 = ((f32[32,2,128]{2,1,0:T(2,128)}), f32[32,2,128]{2,1,0:T(2,128)S(1)}, u32[]{:S(2)}, u32[]{:S(2)}) async-start(f32[32,2,128]{2,1,0:T(2,128)} %get-tuple-element.91), calls=%async_computation.2 | async-start | bytes 65536 | tf_op jit(solution)/shard_map/all_to_all | solution.py:700
  52.0 13.4 %collective-permute-start.4 = (bf16[896,128]{1,0:T(8,128)(2,1)S(1)}, bf16[896,128]{1,0:T(8,128)(2,1)S(1)}, u32[]{:S(2)}, u32[]{:S(2)}) collective-permute-start(bf16[896,128]{1,0:T(8,128)(2,1)S(1)} %copy-done.23), channel_id=1, source_target_pairs={{0,3},{1,2},{2,1},{3,0},{4,7},{5,6},{6,5},{7,4},{8,11},{9,10},{10,... | collective-permute-start | bytes 688136 | tf_op jit(solution)/shard_map/ppermute | solution.py:29
  54.7 11.3 %collective-permute-start.3 = (bf16[896,128]{1,0:T(8,128)(2,1)S(1)}, bf16[896,128]{1,0:T(8,128)(2,1)}, u32[]{:S(2)}, u32[]{:S(2)}) collective-permute-start(bf16[896,128]{1,0:T(8,128)(2,1)S(1)} %copy-done.23), channel_id=1, source_target_pairs={{0,2},{1,3},{2,0},{3,1},{4,6},{5,7},{6,4},{7,5},{8,10},{9,11},{10,... | collective-permute-start | bytes 688136 | tf_op jit(solution)/shard_map/ppermute | solution.py:29
  55.3 10.9 %collective-permute-start.2 = (bf16[896,128]{1,0:T(8,128)(2,1)S(1)}, bf16[896,128]{1,0:T(8,128)(2,1)}, u32[]{:S(2)}, u32[]{:S(2)}) collective-permute-start(bf16[896,128]{1,0:T(8,128)(2,1)S(1)} %copy-done.23), channel_id=1, source_target_pairs={{0,1},{1,0},{2,3},{3,2},{4,5},{5,4},{6,7},{7,6},{8,9},{9,8},{10,11... | collective-permute-start | bytes 688136 | tf_op jit(solution)/shard_map/ppermute | solution.py:29
  61.7 9.7 %copy-start.24 = (bf16[896,128]{1,0:T(8,128)(2,1)S(1)}, bf16[896,128]{1,0:T(8,128)(2,1)}, u32[]{:S(2)}) copy-start(bf16[896,128]{1,0:T(8,128)(2,1)} %get-tuple-element.103) | copy-start | bytes 688132
  66.2 6.5 %collective-permute-start.5 = (f32[640,256]{1,0:T(8,128)}, f32[640,256]{1,0:T(8,128)}, u32[]{:S(2)}, u32[]{:S(2)}) collective-permute-start(f32[640,256]{1,0:T(8,128)} %get-tuple-element.102), channel_id=1, source_target_pairs={{0,16},{16,0},{1,17},{17,1},{2,18},{18,2},{3,19},{19,3},{4,20},{20... | collective-permute-start | bytes 1966088 | tf_op jit(solution)/shard_map/ppermute | solution.py:29
  66.2 13.0 %all-to-all-start.3 = ((f32[32,1,896]{2,1,0:T(1,128)}), f32[32,1,896]{2,1,0:T(1,128)S(1)}, u32[]{:S(2)}, u32[]{:S(2)}) async-start(f32[32,1,896]{2,1,0:T(1,128)} %second_kernel.1), calls=%async_computation.3 | async-start | bytes 229376 | tf_op jit(solution)/shard_map/all_to_all | solution.py:711
  72.7 15.8 %copy-start.2 = (bf16[4,896,128]{2,1,0:T(8,128)(2,1)}, bf16[4,896,128]{2,1,0:T(8,128)(2,1)S(1)}, u32[]{:S(2)}) copy-start(bf16[4,896,128]{2,1,0:T(8,128)(2,1)S(1)} %pad_maximum_fusion.own_ref) | copy-start | bytes 2752516
  82.3 1.4 %collective-permute-start.6 = (f32[128,384]{1,0:T(8,128)S(1)}, f32[128,384]{1,0:T(8,128)S(1)}, u32[]{:S(2)}, u32[]{:S(2)}) collective-permute-start(f32[128,384]{1,0:T(8,128)S(1)} %get-tuple-element.110), channel_id=1, source_target_pairs={{0,16},{16,0},{1,17},{17,1},{2,18},{18,2},{3,19},{19,3},{4,20},{20... | collective-permute-start | bytes 589832 | tf_op jit(solution)/shard_map/ppermute | solution.py:29
  84.6 17.8 %all-to-all-start.4 = ((bf16[16,56,256]{2,1,0:T(8,128)(2,1)}), bf16[16,56,256]{2,1,0:T(8,128)(2,1)S(1)}, u32[]{:S(2)}, u32[]{:S(2)}) async-start(bf16[16,56,256]{2,1,0:T(8,128)(2,1)} %message_kernel.1), calls=%async_computation.4 | async-start | bytes 917504 | tf_op jit(solution)/shard_map/all_to_all | solution.py:732
  88.2 1.7 %collective-permute-start.7 = (f32[640,1]{1,0:T(8,128)S(1)}, f32[640,1]{1,0:T(8,128)S(1)}, u32[]{:S(2)}, u32[]{:S(2)}) collective-permute-start(f32[640,1]{1,0:T(8,128)S(1)} %multiply_divide_fusion.scale_ref), channel_id=1, source_target_pairs={{0,16},{16,0},{1,17},{17,1},{2,18},{18,2},{3,19},{19,3},{4,20},{20... | collective-permute-start | bytes 7688 | tf_op jit(solution)/shard_map/ppermute | solution.py:29
  88.5 19.1 %collective-permute-start.8 = (bf16[4,896,128]{2,1,0:T(8,128)(2,1)S(1)}, bf16[4,896,128]{2,1,0:T(8,128)(2,1)}, u32[]{:S(2)}, u32[]{:S(2)}) collective-permute-start(bf16[4,896,128]{2,1,0:T(8,128)(2,1)S(1)} %pad_maximum_fusion.own_ref), channel_id=1, source_target_pairs={{0,16},{16,0},{1,17},{17,1},{2,18},{18,2},{3,19},{19,3},{4,20},{20... | collective-permute-start | bytes 2752520 | tf_op jit(solution)/shard_map/ppermute | solution.py:29
  88.9 37.0 %collective-permute-start.12 = (bf16[256,2048]{1,0:T(8,128)(2,1)}, bf16[256,2048]{1,0:T(8,128)(2,1)}, u32[]{:S(2)}, u32[]{:S(2)}) collective-permute-start(bf16[256,2048]{1,0:T(8,128)(2,1)} %get-tuple-element.135.refs_7_), channel_id=1, source_target_pairs={{0,16},{16,0},{1,17},{17,1},{2,18},{18,2},{3,19},{19,3},{4,20},{20... | collective-permute-start | bytes 3145736 | tf_op jit(solution)/shard_map/ppermute | solution.py:29
  103.4 15.9 %copy-start.18 = (f32[1,640]{1,0:T(1,128)S(1)}, f32[1,640]{1,0:T(1,128)}, u32[]{:S(2)}) copy-start(f32[1,640]{1,0:T(1,128)} %get-tuple-element.128.refs_1_) | copy-start | bytes 7684
  103.4 15.9 %all-to-all-start.5 = ((bf16[16,48,256]{2,1,0:T(8,128)(2,1)}), bf16[16,48,256]{2,1,0:T(8,128)(2,1)S(1)}, u32[]{:S(2)}, u32[]{:S(2)}) async-start(bf16[16,48,256]{2,1,0:T(8,128)(2,1)} %bottleneck_kernel.1), calls=%async_computation.5 | async-start | bytes 786432 | tf_op jit(solution)/shard_map/all_to_all | solution.py:748
  107.4 20.6 %collective-permute-start.11 = (bf16[256,2048]{1,0:T(8,128)(2,1)S(1)}, bf16[256,2048]{1,0:T(8,128)(2,1)}, u32[]{:S(2)}, u32[]{:S(2)}) collective-permute-start(bf16[256,2048]{1,0:T(8,128)(2,1)S(1)} %convolution_convert_fusion.refs_5_), channel_id=1, source_target_pairs={{0,16},{16,0},{1,17},{17,1},{2,18},{18,2},{3,19},{19,3},{4,20},{20... | collective-permute-start | bytes 3145736 | tf_op jit(solution)/shard_map/ppermute | solution.py:29
  112.9 15.1 %copy-start.7 = (f32[128,640]{1,0:T(8,128)S(1)}, f32[128,640]{1,0:T(8,128)}, u32[]{:S(2)}) copy-start(f32[128,640]{1,0:T(8,128)} %copy-done.6) | copy-start | bytes 983044
  112.9 15.1 %copy-start.11 = (bf16[128,256]{1,0:T(8,128)(2,1)S(1)}, bf16[128,256]{1,0:T(8,128)(2,1)}, u32[]{:S(2)}) copy-start(bf16[128,256]{1,0:T(8,128)(2,1)} %refs_15_.1) | copy-start | bytes 196612
  119.3 8.7 %copy-start.9 = (f32[128,640]{1,0:T(8,128)S(1)}, f32[128,640]{1,0:T(8,128)}, u32[]{:S(2)}) copy-start(f32[128,640]{1,0:T(8,128)} %copy-done.8) | copy-start | bytes 983044
  119.3 8.7 %collective-permute-start.9 = (bf16[16,48,256]{2,1,0:T(8,128)(2,1)S(1)}, bf16[16,48,256]{2,1,0:T(8,128)(2,1)S(1)}, u32[]{:S(2)}, u32[]{:S(2)}) collective-permute-start(bf16[16,48,256]{2,1,0:T(8,128)(2,1)S(1)} %all-to-all-done.5.refs_0_.refs_1_), channel_id=1, source_target_pairs={{0,16},{16,0},{1,17},{17,1},{2,18},{18,2},{3,19},{19,3},{4,20},{20... | collective-permute-start | bytes 1179656 | tf_op jit(solution)/shard_map/ppermute | solution.py:29
  119.3 5.4 %collective-permute-start.10 = (f32[1,640]{1,0:T(1,128)S(1)}, f32[1,640]{1,0:T(1,128)S(1)}, u32[]{:S(2)}, u32[]{:S(2)}) collective-permute-start(f32[1,640]{1,0:T(1,128)S(1)} %copy-done.18), channel_id=1, source_target_pairs={{0,16},{16,0},{1,17},{17,1},{2,18},{18,2},{3,19},{19,3},{4,20},{20... | collective-permute-start | bytes 7688 | tf_op jit(solution)/shard_map/ppermute | solution.py:29
  120.8 7.3 %copy-start.17 = (bf16[128,640]{1,0:T(8,128)(2,1)S(1)}, bf16[128,640]{1,0:T(8,128)(2,1)}, u32[]{:S(2)}) copy-start(bf16[128,640]{1,0:T(8,128)(2,1)} %copy-done.16) | copy-start | bytes 491524
  123.6 12.2 %collective-permute-start.13 = (bf16[96,640]{1,0:T(8,128)(2,1)S(1)}, bf16[96,640]{1,0:T(8,128)(2,1)S(1)}, u32[]{:S(2)}, u32[]{:S(2)}) collective-permute-start(bf16[96,640]{1,0:T(8,128)(2,1)S(1)} %get-tuple-element.141), channel_id=1, source_target_pairs={{0,4},{1,5},{2,6},{3,7},{4,0},{5,1},{6,2},{7,3},{8,12},{9,13},{10,... | collective-permute-start | bytes 368648 | tf_op jit(solution)/shard_map/ppermute | solution.py:29
  124.7 12.0 %collective-permute-start.14 = (bf16[96,640]{1,0:T(8,128)(2,1)S(1)}, bf16[96,640]{1,0:T(8,128)(2,1)S(1)}, u32[]{:S(2)}, u32[]{:S(2)}) collective-permute-start(bf16[96,640]{1,0:T(8,128)(2,1)S(1)} %get-tuple-element.142), channel_id=1, source_target_pairs={{0,8},{1,9},{2,10},{3,11},{4,12},{5,13},{6,14},{7,15},{8,0},{9,1},... | collective-permute-start | bytes 368648 | tf_op jit(solution)/shard_map/ppermute | solution.py:29
  125.9 10.8 %collective-permute-start.15 = (bf16[96,640]{1,0:T(8,128)(2,1)S(1)}, bf16[96,640]{1,0:T(8,128)(2,1)S(1)}, u32[]{:S(2)}, u32[]{:S(2)}) collective-permute-start(bf16[96,640]{1,0:T(8,128)(2,1)S(1)} %get-tuple-element.143), channel_id=1, source_target_pairs={{0,12},{1,13},{2,14},{3,15},{4,8},{5,9},{6,10},{7,11},{8,4},{9,5},... | collective-permute-start | bytes 368648 | tf_op jit(solution)/shard_map/ppermute | solution.py:29
  (17 other events, 35.8 us)

commit v10 on v9

--- a/solution.py
+++ b/solution.py
@@ -176,7 +176,7 @@
     return (grad_features, grad_w1, grad_w2, grad_protos)
 
 
-def params(mib=50):
+def params(mib=51):
     return pltpu.CompilerParams(vmem_limit_bytes=mib * 1024 * 1024)
 
 
@@ -192,7 +192,7 @@
     return pl.BlockSpec(dims, lambda i: (0,) * len(dims))
 
 
-def call(kernel, outs, scalars, *args, us=1, mib=50):
+def call(kernel, outs, scalars, *args, us=1, mib=51):
     smem = [jnp.asarray(s, jnp.int32).reshape(1) for s in scalars]
     return pl.pallas_call(
         kernel,
@@ -645,7 +645,6 @@
     everyone = nd * n
     factor = 10.0 / (9 * teach * nd)
 
-    feat_other = swap(features, "dp", 1)
     heads = (features, head_w1, head_w2, teacher_features, teacher_w1, teacher_w2)
     parts, place, view, weights = pl.pallas_call(
         head_kernel,
@@ -665,7 +664,8 @@
         name="head_kernel",
     )(d.reshape(1), *heads, crop_image, crop_view)
     parts_got = lax.all_to_all(parts, "proto", 0, 0)
-    protos_late, tprotos_late, _ = tied(protos, teacher_protos, parts)
+    protos_late, tprotos_late, feat_late, _ = tied(protos, teacher_protos, features, parts)
+    feat_other = swap(feat_late, "dp", 1)
     cols = protos.shape[1] // nd
     pnb = unit_cols(lax.dynamic_slice_in_dim(protos_late, d * cols, cols, 1))[0].astype(BF16)
     tpnb = unit_cols(lax.dynamic_slice_in_dim(tprotos_late, d * cols, cols, 1))[0].astype(BF16)

time: 138 us -> 138 us (level)
  local copies, waits for them, and re-layouts: 10.4 us -> 5.87 us
  Pallas kernels: 37.7 us -> 40.9 us
  waiting for transfers between devices: 39.9 us -> 38.4 us
    unnamed x54 -> x50, local copies, waits for them, and re-layouts: 10.2 us -> 5.63 us
    ppermute x16, waiting for transfers between devices: 5.74 us -> 4.13 us  [swap(): return lax.ppermute(value, axis, [(i, i ^ step) for i in range(count)])]
  transfers between devices with their start and end apart: 22 -> 22, of which waited for: 11 -> 9; matrix products, arithmetic and copies ran while one was open for 8% -> 9% of each run, Pallas kernels for 23% -> 22%
where the time goes in v10:
time: 138 us; the launch traced here: 137 us
  Pallas kernels  40.9 us (30%)
  waiting for transfers between devices  38.4 us (28%)
  starting transfers between devices  37.5 us (27%)
  other arithmetic  7.55 us (5%)
  local copies, waits for them, and re-layouts  5.87 us (4%)
  matrix products  5.34 us (4%)
    pallas_call x7, Pallas kernels, call(): pl.pallas_call(kernel, grid=(1,), out_shape=outs, in_specs=[pl.BlockSpec(...  13.7 us
    ppermute x16, starting transfers between devices, swap(): return lax.ppermute(value, axis, [(i, i ^ step) for i in range(count)])  10 us
    all_to_all x1, waiting for transfers between devices, paired_body(): parts_got = lax.all_to_all(parts, 'proto', 0, 0)  9.35 us
    pallas_call x1, Pallas kernels, last_grads(): pl.pallas_call(functools.partial(last_kernel, tile), name='last_kernel',...  8.45 us
    all_to_all x2, starting transfers between devices, paired_body(): msg_got = lax.all_to_all(msg, ALL, 0, 0)  8.45 us
    all_to_all x1, starting transfers between devices, paired_body(): parts_got = lax.all_to_all(parts, 'proto', 0, 0)  8.02 us
    all_to_all x1, waiting for transfers between devices, paired_body(): got = lax.all_to_all(dz, 'proto', 0, 0)  7.52 us
    all_to_all x1, waiting for transfers between devices, paired_body(): msg_got = lax.all_to_all(msg, 'proto', 0, 0)  6.97 us
  transfers between devices with their start and end apart: 22, of which 9 were waited for; matrix products, arithmetic and copies ran while one was open for 9% of the time, Pallas kernels for 22%

profile of v10, /device:TPU:0, one launch (start us, length us, event | category | flops | bytes accessed | tf_op | source)
XLA Modules:
  0.0 136.6 jit_solution(5151848737895003995)
XLA Ops:
  0.6 5.5 %head_kernel.1 = (bf16[16,48,256]{2,1,0:T(8,128)(2,1)}, f32[1,640]{1,0:T(1,128)}, f32[640,1]{1,0:T(8,128)}, bf16[896,128]{1,0:T(8,128)(2,1)}) custom-call(s32[1]{0:T(128)} %bitcast.1.d_ref, bf16[640,1536]{1,0:T(8,128)(2,1)} %refs_9_.1, bf16[1536,128]{1,0:T(8,128)(2,1)} %w1_ref, bf16[128,256]{1,0:T(8,128)(2,1)} %refs_15_.1, bf16[128,1536]{1,0:T(8,128)(2,1)} %refs_3_.1, ...), custom_call_target="tpu_custom_call" | custom-call | tf_op jit(solution)/shard_map/head_kernel/pallas_call | solution.py:649
  6.6 8.0 %all-to-all-start = ((bf16[16,48,256]{2,1,0:T(8,128)(2,1)}), bf16[16,48,256]{2,1,0:T(8,128)(2,1)S(1)}, u32[]{:S(2)}, u32[]{:S(2)}) async-start(bf16[16,48,256]{2,1,0:T(8,128)(2,1)} %get-tuple-element.78), calls=%async_computation | async-start | bytes 786432 | tf_op jit(solution)/shard_map/all_to_all | solution.py:666
  14.7 2.1 %fusion = (f32[2048]{0:T(1024)S(1)}, f32[2048]{0:T(1024)S(1)}) fusion(bf16[256,4096]{1,0:T(8,128)(2,1)} %refs_4_.3, s32[]{:T(128)S(6)} %select_n.8, bf16[256,4096]{1,0:T(8,128)(2,1)} %param.19), kind=kLoop, calls=%fused_computation.5 | loop fusion | flops 3141632 | bytes 2113540 | tf_op jit(solution)/shard_map/reduce_sum | solution.py:49
  17.1 1.3 fusion.1.pnb_ref
  18.4 9.3 %all-to-all-done.parts_ref = bf16[16,48,256]{2,1,0:T(8,128)(2,1)S(1)} async-done(((bf16[16,48,256]{2,1,0:T(8,128)(2,1)}), bf16[16,48,256]{2,1,0:T(8,128)(2,1)S(1)}, u32[]{:S(2)}, u32[]{:S(2)}) %all-to-all-start) | async-done | bytes 393248 | tf_op jit(solution)/shard_map/all_to_all | solution.py:666
  29.3 3.6 %all-to-all-start.1 = ((bf16[16,48,256]{2,1,0:T(8,128)(2,1)}), bf16[16,48,256]{2,1,0:T(8,128)(2,1)S(1)}, u32[]{:S(2)}, u32[]{:S(2)}) async-start(bf16[16,48,256]{2,1,0:T(8,128)(2,1)} %get-tuple-element.82), calls=%async_computation.1 | async-start | bytes 786432 | tf_op jit(solution)/shard_map/all_to_all | solution.py:682
  32.9 3.5 %hidden_kernel.1 = (bf16[128,640]{1,0:T(8,128)(2,1)S(1)}, bf16[128,640]{1,0:T(8,128)(2,1)S(1)}, f32[128,640]{1,0:T(8,128)S(1)}, f32[128,640]{1,0:T(8,128)S(1)}) custom-call(bf16[640,1536]{1,0:T(8,128)(2,1)} %refs_9_.1, bf16[640,1536]{1,0:T(8,128)(2,1)} %collective-permute-done.f1_ref.refs_10_, bf16[1536,128]{1,0:T(8,128)(2,1)S(1)} %copy-done.2), custom_call_target="tpu_custom_call" | custom-call | flops 4000000000 | bytes 4000000 | tf_op jit(solution)/shard_map/hidden_kernel/pallas_call | solution.py:197
  39.3 5.7 %all-to-all-done.1.got_ref = bf16[16,48,256]{2,1,0:T(8,128)(2,1)S(1)} async-done(((bf16[16,48,256]{2,1,0:T(8,128)(2,1)}), bf16[16,48,256]{2,1,0:T(8,128)(2,1)S(1)}, u32[]{:S(2)}, u32[]{:S(2)}) %all-to-all-start.1) | async-done | bytes 393248 | tf_op jit(solution)/shard_map/all_to_all | solution.py:682
  45.0 1.7 %collective-permute-done.1.other_ref = bf16[16,48,256]{2,1,0:T(8,128)(2,1)S(1)} collective-permute-done((bf16[16,48,256]{2,1,0:T(8,128)(2,1)S(1)}, bf16[16,48,256]{2,1,0:T(8,128)(2,1)S(1)}, u32[]{:S(2)}, u32[]{:S(2)}) %collective-permute-start.1) | collective-permute-done | bytes 393248 | tf_op jit(solution)/shard_map/ppermute | solution.py:29
  46.7 1.9 %kern_kernel.1 = (f32[256,2048]{1,0:T(8,128)}, f32[32,2,128]{2,1,0:T(2,128)}, bf16[1280,256]{1,0:T(8,128)(2,1)S(1)}) custom-call(s32[1]{0:T(128)} %bitcast.1.d_ref, bf16[16,48,256]{2,1,0:T(8,128)(2,1)S(1)} %all-to-all-done.1.got_ref, bf16[16,48,256]{2,1,0:T(8,128)(2,1)S(1)} %collective-permute-done.1.other_ref, bf16[256,2048]{1,0:T(8,128)(2,1)S(1)} %fusion.3.tpnb_ref), custom_call_target="tpu_custom_call" | custom-call | flops 3000000000 | bytes 3000000 | tf_op jit(solution)/shard_map/kern_kernel/pallas_call | solution.py:197
  48.6 2.6 %all-to-all-start.2 = ((f32[32,2,128]{2,1,0:T(2,128)}), f32[32,2,128]{2,1,0:T(2,128)S(1)}, u32[]{:S(2)}, u32[]{:S(2)}) async-start(f32[32,2,128]{2,1,0:T(2,128)} %get-tuple-element.93), calls=%async_computation.2 | async-start | bytes 65536 | tf_op jit(solution)/shard_map/all_to_all | solution.py:700
  51.2 2.7 %collective-permute-start.4 = (bf16[896,128]{1,0:T(8,128)(2,1)S(1)}, bf16[896,128]{1,0:T(8,128)(2,1)S(1)}, u32[]{:S(2)}, u32[]{:S(2)}) collective-permute-start(bf16[896,128]{1,0:T(8,128)(2,1)S(1)} %copy-done.21), channel_id=1, source_target_pairs={{0,3},{1,2},{2,1},{3,0},{4,7},{5,6},{6,5},{7,4},{8,11},{9,10},{10,... | collective-permute-start | bytes 688136 | tf_op jit(solution)/shard_map/ppermute | solution.py:29
  54.8 6.5 %student_kernel.1 = (bf16[1280,2048]{1,0:T(8,128)(2,1)}, f32[640,256]{1,0:T(8,128)S(1)}, f32[640,256]{1,0:T(8,128)}, f32[1280,1]{1,0:T(8,128)S(1)}) custom-call(bf16[1280,256]{1,0:T(8,128)(2,1)S(1)} %get-tuple-element.97.z_ref, bf16[256,2048]{1,0:T(8,128)(2,1)} %fusion.1.pnb_ref), custom_call_target="tpu_custom_call" | custom-call | flops 5000000000 | bytes 10000000 | tf_op jit(solution)/shard_map/student_kernel/pallas_call | solution.py:329
  62.8 3.0 %second_kernel.1 = f32[32,1,896]{2,1,0:T(1,128)} custom-call(s32[1]{0:T(128)} %bitcast.1.d_ref, f32[32,2,128]{2,1,0:T(2,128)} %copy-done.24, f32[256,2048]{1,0:T(8,128)} %get-tuple-element.94.kern_ref, f32[1280,1]{1,0:T(8,128)} %copy-done.15), custom_call_target="tpu_custom_call" | custom-call | flops 1000000000 | bytes 1000000 | tf_op jit(solution)/shard_map/second_kernel/pallas_call | solution.py:197
  66.5 5.8 %all-to-all-start.3 = ((f32[32,1,896]{2,1,0:T(1,128)}), f32[32,1,896]{2,1,0:T(1,128)S(1)}, u32[]{:S(2)}, u32[]{:S(2)}) async-start(f32[32,1,896]{2,1,0:T(1,128)} %second_kernel.1), calls=%async_computation.3 | async-start | bytes 229376 | tf_op jit(solution)/shard_map/all_to_all | solution.py:711
  72.4 1.2 pad_maximum_fusion.own_ref
  73.5 1.9 %add_convert_fusion.sums_ref = bf16[640,256]{1,0:T(8,128)(2,1)} fusion(f32[640,256]{1,0:T(8,128)S(1)} %get-tuple-element.103, f32[640,256]{1,0:T(8,128)} %collective-permute-done.5), kind=kLoop, calls=%fused_computation.12 | loop fusion | flops 327680 | bytes 1638400 | tf_op jit(solution)/shard_map/convert_element_type | solution.py:715
  75.4 4.7 %all-to-all-done.3.got_ref = f32[32,1,896]{2,1,0:T(1,128)S(1)} async-done(((f32[32,1,896]{2,1,0:T(1,128)}), f32[32,1,896]{2,1,0:T(1,128)S(1)}, u32[]{:S(2)}, u32[]{:S(2)}) %all-to-all-start.3) | async-done | bytes 114720 | tf_op jit(solution)/shard_map/all_to_all | solution.py:711
  80.2 2.5 %third_kernel.1 = (f32[640,1]{1,0:T(8,128)S(1)}, bf16[256,2048]{1,0:T(8,128)(2,1)S(1)}, f32[128,384]{1,0:T(8,128)S(1)}, f32[128,384]{1,0:T(8,128)S(1)}) custom-call(s32[1]{0:T(128)} %bitcast.1.d_ref, f32[32,1,896]{2,1,0:T(1,128)S(1)} %all-to-all-done.3.got_ref, f32[256,2048]{1,0:T(8,128)} %get-tuple-element.94.kern_ref, bf16[256,2048]{1,0:T(8,128)(2,1)S(1)} %copy-done), custom_call_target="tpu_custom_call" | custom-call | flops 2000000000 | bytes 2000000 | tf_op jit(solution)/shard_map/third_kernel/pallas_call | solution.py:197
  82.8 1.4 %collective-permute-done.6.b1_ref = f32[128,384]{1,0:T(8,128)S(1)} collective-permute-done((f32[128,384]{1,0:T(8,128)S(1)}, f32[128,384]{1,0:T(8,128)S(1)}, u32[]{:S(2)}, u32[]{:S(2)}) %collective-permute-start.6) | collective-permute-done | bytes 196640 | tf_op jit(solution)/shard_map/ppermute | solution.py:29
  85.0 3.6 %all-to-all-start.4 = ((bf16[16,56,256]{2,1,0:T(8,128)(2,1)}), bf16[16,56,256]{2,1,0:T(8,128)(2,1)S(1)}, u32[]{:S(2)}, u32[]{:S(2)}) async-start(bf16[16,56,256]{2,1,0:T(8,128)(2,1)} %message_kernel.1), calls=%async_computation.4 | async-start | bytes 917504 | tf_op jit(solution)/shard_map/all_to_all | solution.py:732
  90.6 5.3 %convolution_convert_fusion.refs_5_ = bf16[256,2048]{1,0:T(8,128)(2,1)} fusion(bf16[1280,2048]{1,0:T(8,128)(2,1)} %get-tuple-element.120, bf16[1280,256]{1,0:T(8,128)(2,1)} %copy-done.16, f32[1280]{0:T(1024)S(1)} %maximum_reduce_fusion), kind=kOutput, calls=%fused_computation.4 | convolution fusion | flops 1343684608 | bytes 6951936 | tf_op jit(solution)/shard_map/dot_general | solution.py:24
  95.9 7.0 %all-to-all-done.4.got_ref = bf16[16,56,256]{2,1,0:T(8,128)(2,1)S(1)} async-done(((bf16[16,56,256]{2,1,0:T(8,128)(2,1)}), bf16[16,56,256]{2,1,0:T(8,128)(2,1)S(1)}, u32[]{:S(2)}, u32[]{:S(2)}) %all-to-all-start.4) | async-done | bytes 458784 | tf_op jit(solution)/shard_map/all_to_all | solution.py:732
  102.9 1.0 bottleneck_kernel.1
  103.9 3.9 %all-to-all-start.5 = ((bf16[16,48,256]{2,1,0:T(8,128)(2,1)}), bf16[16,48,256]{2,1,0:T(8,128)(2,1)S(1)}, u32[]{:S(2)}, u32[]{:S(2)}) async-start(bf16[16,48,256]{2,1,0:T(8,128)(2,1)} %bottleneck_kernel.1), calls=%async_computation.5 | async-start | bytes 786432 | tf_op jit(solution)/shard_map/all_to_all | solution.py:748
  107.8 4.3 %slopes_kernel.1 = (f32[640,512]{1,0:T(8,128)}, bf16[512,256]{1,0:T(8,128)(2,1)S(1)}, bf16[4,96,512]{2,1,0:T(8,128)(2,1)S(1)}) custom-call(s32[1]{0:T(128)} %bitcast.1.d_ref, s32[1]{0:T(128)} %bitcast.p_ref, bf16[640,1536]{1,0:T(8,128)(2,1)} %refs_9_.1, bf16[4,896,128]{2,1,0:T(8,128)(2,1)S(1)} %pad_maximum_fusion.own_ref, ...), custom_call_target="tpu_custom_call" | custom-call | flops 4000000000 | bytes 30000000 | tf_op jit(solution)/shard_map/slopes_kernel/pallas_call | solution.py:457
  112.1 7.5 %all-to-all-done.5.refs_0_.refs_1_ = bf16[16,48,256]{2,1,0:T(8,128)(2,1)S(1)} async-done(((bf16[16,48,256]{2,1,0:T(8,128)(2,1)}), bf16[16,48,256]{2,1,0:T(8,128)(2,1)S(1)}, u32[]{:S(2)}, u32[]{:S(2)}) %all-to-all-start.5) | async-done | bytes 393248 | tf_op jit(solution)/shard_map/all_to_all | solution.py:748
  120.1 2.6 %features_kernel.1 = (bf16[640,256]{1,0:T(8,128)(2,1)S(1)}, f32[96,640]{1,0:T(8,128)S(1)}, bf16[96,640]{1,0:T(8,128)(2,1)S(1)}, bf16[96,640]{1,0:T(8,128)(2,1)S(1)}, bf16[96,640]{1,0:T(8,128)(2,1)S(1)}) custom-call(bf16[16,48,256]{2,1,0:T(8,128)(2,1)S(1)} %all-to-all-done.5.refs_0_.refs_1_, f32[1,640]{1,0:T(1,128)S(1)} %copy-done.14, ...), custom_call_target="tpu_custom_call" | custom-call | tf_op jit(solution)/shard_map/features_kernel/pallas_call | solution.py:529
  122.8 1.2 collective-permute-start.13
  123.9 1.2 collective-permute-start.14
  125.1 2.1 %collective-permute-start.15 = (bf16[96,640]{1,0:T(8,128)(2,1)S(1)}, bf16[96,640]{1,0:T(8,128)(2,1)S(1)}, u32[]{:S(2)}, u32[]{:S(2)}) collective-permute-start(bf16[96,640]{1,0:T(8,128)(2,1)S(1)} %get-tuple-element.145), channel_id=1, source_target_pairs={{0,12},{1,13},{2,14},{3,15},{4,8},{5,9},{6,10},{7,11},{8,4},{9,5},... | collective-permute-start | bytes 368648 | tf_op jit(solution)/shard_map/ppermute | solution.py:29
  127.3 8.4 %last_kernel.1 = (f32[256,4096]{1,0:T(8,128)}, f32[1536,128]{1,0:T(8,128)}, f32[128,256]{1,0:T(8,128)}) custom-call(s32[1]{0:T(128)} %bitcast.1.d_ref, bf16[640,256]{1,0:T(8,128)(2,1)S(1)} %get-tuple-element.135.refs_0_, bf16[16,48,256]{2,1,0:T(8,128)(2,1)S(1)} %all-to-all-done.5.refs_0_.refs_1_, bf16[16,48,256]{2,1,0:T(8,128)(2,1)S(1)} %collective-permute-done.9.refs_2_, ...), custom_call_target="tpu_custom_call" | custom-call | tf_op jit(solution)/shard_map/last_kernel/pallas_call | solution.py:607
  (87 shorter events, 12.4 us)
Async XLA Ops:
  6.1 26.8 %collective-permute-start = (bf16[640,1536]{1,0:T(8,128)(2,1)}, bf16[640,1536]{1,0:T(8,128)(2,1)}, u32[]{:S(2)}, u32[]{:S(2)}) collective-permute-start(bf16[640,1536]{1,0:T(8,128)(2,1)} %refs_9_.1), channel_id=1, source_target_pairs={{0,16},{16,0},{1,17},{17,1},{2,18},{18,2},{3,19},{19,3},{4,20},{20... | collective-permute-start | bytes 5898248 | tf_op jit(solution)/shard_map/ppermute | solution.py:29
  6.6 21.1 %all-to-all-start = ((bf16[16,48,256]{2,1,0:T(8,128)(2,1)}), bf16[16,48,256]{2,1,0:T(8,128)(2,1)S(1)}, u32[]{:S(2)}, u32[]{:S(2)}) async-start(bf16[16,48,256]{2,1,0:T(8,128)(2,1)} %get-tuple-element.78), calls=%async_computation | async-start | bytes 786432 | tf_op jit(solution)/shard_map/all_to_all | solution.py:666
  18.4 14.5 %copy-start.2 = (bf16[1536,128]{1,0:T(8,128)(2,1)S(1)}, bf16[1536,128]{1,0:T(8,128)(2,1)}, u32[]{:S(2)}) copy-start(bf16[1536,128]{1,0:T(8,128)(2,1)} %w1_ref) | copy-start | bytes 1179652
  29.3 15.7 %all-to-all-start.1 = ((bf16[16,48,256]{2,1,0:T(8,128)(2,1)}), bf16[16,48,256]{2,1,0:T(8,128)(2,1)S(1)}, u32[]{:S(2)}, u32[]{:S(2)}) async-start(bf16[16,48,256]{2,1,0:T(8,128)(2,1)} %get-tuple-element.82), calls=%async_computation.1 | async-start | bytes 786432 | tf_op jit(solution)/shard_map/all_to_all | solution.py:682
  45.0 1.7 %collective-permute-start.1 = (bf16[16,48,256]{2,1,0:T(8,128)(2,1)S(1)}, bf16[16,48,256]{2,1,0:T(8,128)(2,1)S(1)}, u32[]{:S(2)}, u32[]{:S(2)}) collective-permute-start(bf16[16,48,256]{2,1,0:T(8,128)(2,1)S(1)} %all-to-all-done.1.got_ref), channel_id=1, source_target_pairs={{0,16},{16,0},{1,17},{17,1},{2,18},{18,2},{3,19},{19,3},{4,20},{20... | collective-permute-start | bytes 1179656 | tf_op jit(solution)/shard_map/ppermute | solution.py:29
  48.6 12.7 %copy-start.16 = (bf16[1280,256]{1,0:T(8,128)(2,1)}, bf16[1280,256]{1,0:T(8,128)(2,1)S(1)}, u32[]{:S(2)}) copy-start(bf16[1280,256]{1,0:T(8,128)(2,1)S(1)} %get-tuple-element.97.z_ref) | copy-start | bytes 1966084
  48.6 13.5 %all-to-all-start.2 = ((f32[32,2,128]{2,1,0:T(2,128)}), f32[32,2,128]{2,1,0:T(2,128)S(1)}, u32[]{:S(2)}, u32[]{:S(2)}) async-start(f32[32,2,128]{2,1,0:T(2,128)} %get-tuple-element.93), calls=%async_computation.2 | async-start | bytes 65536 | tf_op jit(solution)/shard_map/all_to_all | solution.py:700
  51.2 14.5 %collective-permute-start.4 = (bf16[896,128]{1,0:T(8,128)(2,1)S(1)}, bf16[896,128]{1,0:T(8,128)(2,1)S(1)}, u32[]{:S(2)}, u32[]{:S(2)}) collective-permute-start(bf16[896,128]{1,0:T(8,128)(2,1)S(1)} %copy-done.21), channel_id=1, source_target_pairs={{0,3},{1,2},{2,1},{3,0},{4,7},{5,6},{6,5},{7,4},{8,11},{9,10},{10,... | collective-permute-start | bytes 688136 | tf_op jit(solution)/shard_map/ppermute | solution.py:29
  54.0 11.8 %collective-permute-start.3 = (bf16[896,128]{1,0:T(8,128)(2,1)S(1)}, bf16[896,128]{1,0:T(8,128)(2,1)S(1)}, u32[]{:S(2)}, u32[]{:S(2)}) collective-permute-start(bf16[896,128]{1,0:T(8,128)(2,1)S(1)} %copy-done.21), channel_id=1, source_target_pairs={{0,2},{1,3},{2,0},{3,1},{4,6},{5,7},{6,4},{7,5},{8,10},{9,11},{10,... | collective-permute-start | bytes 688136 | tf_op jit(solution)/shard_map/ppermute | solution.py:29
  54.5 11.3 %collective-permute-start.2 = (bf16[896,128]{1,0:T(8,128)(2,1)S(1)}, bf16[896,128]{1,0:T(8,128)(2,1)S(1)}, u32[]{:S(2)}, u32[]{:S(2)}) collective-permute-start(bf16[896,128]{1,0:T(8,128)(2,1)S(1)} %copy-done.21), channel_id=1, source_target_pairs={{0,1},{1,0},{2,3},{3,2},{4,5},{5,4},{6,7},{7,6},{8,9},{9,8},{10,11... | collective-permute-start | bytes 688136 | tf_op jit(solution)/shard_map/ppermute | solution.py:29
  65.8 14.4 %copy-start = (bf16[256,2048]{1,0:T(8,128)(2,1)S(1)}, bf16[256,2048]{1,0:T(8,128)(2,1)}, u32[]{:S(2)}) copy-start(bf16[256,2048]{1,0:T(8,128)(2,1)} %fusion.1.pnb_ref) | copy-start | bytes 3145732
  65.8 7.7 %collective-permute-start.5 = (f32[640,256]{1,0:T(8,128)}, f32[640,256]{1,0:T(8,128)}, u32[]{:S(2)}, u32[]{:S(2)}) collective-permute-start(f32[640,256]{1,0:T(8,128)} %get-tuple-element.104), channel_id=1, source_target_pairs={{0,16},{16,0},{1,17},{17,1},{2,18},{18,2},{3,19},{19,3},{4,20},{20... | collective-permute-start | bytes 1966088 | tf_op jit(solution)/shard_map/ppermute | solution.py:29
  66.5 13.6 %all-to-all-start.3 = ((f32[32,1,896]{2,1,0:T(1,128)}), f32[32,1,896]{2,1,0:T(1,128)S(1)}, u32[]{:S(2)}, u32[]{:S(2)}) async-start(f32[32,1,896]{2,1,0:T(1,128)} %second_kernel.1), calls=%async_computation.3 | async-start | bytes 229376 | tf_op jit(solution)/shard_map/all_to_all | solution.py:711
  82.7 1.5 %collective-permute-start.6 = (f32[128,384]{1,0:T(8,128)S(1)}, f32[128,384]{1,0:T(8,128)S(1)}, u32[]{:S(2)}, u32[]{:S(2)}) collective-permute-start(f32[128,384]{1,0:T(8,128)S(1)} %get-tuple-element.112), channel_id=1, source_target_pairs={{0,16},{16,0},{1,17},{17,1},{2,18},{18,2},{3,19},{19,3},{4,20},{20... | collective-permute-start | bytes 589832 | tf_op jit(solution)/shard_map/ppermute | solution.py:29
  85.0 17.8 %all-to-all-start.4 = ((bf16[16,56,256]{2,1,0:T(8,128)(2,1)}), bf16[16,56,256]{2,1,0:T(8,128)(2,1)S(1)}, u32[]{:S(2)}, u32[]{:S(2)}) async-start(bf16[16,56,256]{2,1,0:T(8,128)(2,1)} %message_kernel.1), calls=%async_computation.4 | async-start | bytes 917504 | tf_op jit(solution)/shard_map/all_to_all | solution.py:732
  88.7 1.7 %collective-permute-start.7 = (f32[640,1]{1,0:T(8,128)S(1)}, f32[640,1]{1,0:T(8,128)S(1)}, u32[]{:S(2)}, u32[]{:S(2)}) collective-permute-start(f32[640,1]{1,0:T(8,128)S(1)} %multiply_divide_fusion.scale_ref), channel_id=1, source_target_pairs={{0,16},{16,0},{1,17},{17,1},{2,18},{18,2},{3,19},{19,3},{4,20},{20... | collective-permute-start | bytes 7688 | tf_op jit(solution)/shard_map/ppermute | solution.py:29
  88.9 18.9 %collective-permute-start.8 = (bf16[4,896,128]{2,1,0:T(8,128)(2,1)S(1)}, bf16[4,896,128]{2,1,0:T(8,128)(2,1)}, u32[]{:S(2)}, u32[]{:S(2)}) collective-permute-start(bf16[4,896,128]{2,1,0:T(8,128)(2,1)S(1)} %pad_maximum_fusion.own_ref), channel_id=1, source_target_pairs={{0,16},{16,0},{1,17},{17,1},{2,18},{18,2},{3,19},{19,3},{4,20},{20... | collective-permute-start | bytes 2752520 | tf_op jit(solution)/shard_map/ppermute | solution.py:29
  89.4 35.8 %collective-permute-start.12 = (bf16[256,2048]{1,0:T(8,128)(2,1)S(1)}, bf16[256,2048]{1,0:T(8,128)(2,1)}, u32[]{:S(2)}, u32[]{:S(2)}) collective-permute-start(bf16[256,2048]{1,0:T(8,128)(2,1)S(1)} %get-tuple-element.137.refs_7_), channel_id=1, source_target_pairs={{0,16},{16,0},{1,17},{17,1},{2,18},{18,2},{3,19},{19,3},{4,20},{20... | collective-permute-start | bytes 3145736 | tf_op jit(solution)/shard_map/ppermute | solution.py:29
  90.6 12.3 %copy-start.18 = (f32[48,384]{1,0:T(8,128)S(1)}, f32[48,384]{1,0:T(8,128)}, u32[]{:S(2)}) copy-start(f32[48,384]{1,0:T(8,128)} %copy-done.17) | copy-start | bytes 221188
  103.9 15.8 %all-to-all-start.5 = ((bf16[16,48,256]{2,1,0:T(8,128)(2,1)}), bf16[16,48,256]{2,1,0:T(8,128)(2,1)S(1)}, u32[]{:S(2)}, u32[]{:S(2)}) async-start(bf16[16,48,256]{2,1,0:T(8,128)(2,1)} %bottleneck_kernel.1), calls=%async_computation.5 | async-start | bytes 786432 | tf_op jit(solution)/shard_map/all_to_all | solution.py:748
  107.7 11.9 %copy-start.14 = (f32[1,640]{1,0:T(1,128)S(1)}, f32[1,640]{1,0:T(1,128)}, u32[]{:S(2)}) copy-start(f32[1,640]{1,0:T(1,128)} %get-tuple-element.130.refs_1_) | copy-start | bytes 7684
  107.7 19.5 %collective-permute-start.11 = (bf16[256,2048]{1,0:T(8,128)(2,1)}, bf16[256,2048]{1,0:T(8,128)(2,1)}, u32[]{:S(2)}, u32[]{:S(2)}) collective-permute-start(bf16[256,2048]{1,0:T(8,128)(2,1)} %convolution_convert_fusion.refs_5_), channel_id=1, source_target_pairs={{0,16},{16,0},{1,17},{17,1},{2,18},{18,2},{3,19},{19,3},{4,20},{20... | collective-permute-start | bytes 3145736 | tf_op jit(solution)/shard_map/ppermute | solution.py:29
  112.1 15.2 %copy-start.4 = (f32[128,640]{1,0:T(8,128)S(1)}, f32[128,640]{1,0:T(8,128)}, u32[]{:S(2)}) copy-start(f32[128,640]{1,0:T(8,128)} %copy-done.3) | copy-start | bytes 983044
  112.1 15.2 %copy-start.6 = (f32[128,640]{1,0:T(8,128)S(1)}, f32[128,640]{1,0:T(8,128)}, u32[]{:S(2)}) copy-start(f32[128,640]{1,0:T(8,128)} %copy-done.5) | copy-start | bytes 983044
  112.1 15.2 %copy-start.9 = (bf16[128,256]{1,0:T(8,128)(2,1)S(1)}, bf16[128,256]{1,0:T(8,128)(2,1)}, u32[]{:S(2)}) copy-start(bf16[128,256]{1,0:T(8,128)(2,1)} %refs_15_.1) | copy-start | bytes 196612
  112.1 15.2 %copy-start.11 = (bf16[128,640]{1,0:T(8,128)(2,1)S(1)}, bf16[128,640]{1,0:T(8,128)(2,1)}, u32[]{:S(2)}) copy-start(bf16[128,640]{1,0:T(8,128)(2,1)} %copy-done.10) | copy-start | bytes 491524
  112.1 15.2 %copy-start.13 = (bf16[128,640]{1,0:T(8,128)(2,1)S(1)}, bf16[128,640]{1,0:T(8,128)(2,1)}, u32[]{:S(2)}) copy-start(bf16[128,640]{1,0:T(8,128)(2,1)} %copy-done.12) | copy-start | bytes 491524
  119.6 7.6 %collective-permute-start.9 = (bf16[16,48,256]{2,1,0:T(8,128)(2,1)S(1)}, bf16[16,48,256]{2,1,0:T(8,128)(2,1)S(1)}, u32[]{:S(2)}, u32[]{:S(2)}) collective-permute-start(bf16[16,48,256]{2,1,0:T(8,128)(2,1)S(1)} %all-to-all-done.5.refs_0_.refs_1_), channel_id=1, source_target_pairs={{0,16},{16,0},{1,17},{17,1},{2,18},{18,2},{3,19},{19,3},{4,20},{20... | collective-permute-start | bytes 1179656 | tf_op jit(solution)/shard_map/ppermute | solution.py:29
  119.6 4.3 %collective-permute-start.10 = (f32[1,640]{1,0:T(1,128)S(1)}, f32[1,640]{1,0:T(1,128)S(1)}, u32[]{:S(2)}, u32[]{:S(2)}) collective-permute-start(f32[1,640]{1,0:T(1,128)S(1)} %copy-done.14), channel_id=1, source_target_pairs={{0,16},{16,0},{1,17},{17,1},{2,18},{18,2},{3,19},{19,3},{4,20},{20... | collective-permute-start | bytes 7688 | tf_op jit(solution)/shard_map/ppermute | solution.py:29
  122.8 13.0 %collective-permute-start.13 = (bf16[96,640]{1,0:T(8,128)(2,1)S(1)}, bf16[96,640]{1,0:T(8,128)(2,1)S(1)}, u32[]{:S(2)}, u32[]{:S(2)}) collective-permute-start(bf16[96,640]{1,0:T(8,128)(2,1)S(1)} %get-tuple-element.143), channel_id=1, source_target_pairs={{0,4},{1,5},{2,6},{3,7},{4,0},{5,1},{6,2},{7,3},{8,12},{9,13},{10,... | collective-permute-start | bytes 368648 | tf_op jit(solution)/shard_map/ppermute | solution.py:29
  123.9 12.0 %collective-permute-start.14 = (bf16[96,640]{1,0:T(8,128)(2,1)S(1)}, bf16[96,640]{1,0:T(8,128)(2,1)S(1)}, u32[]{:S(2)}, u32[]{:S(2)}) collective-permute-start(bf16[96,640]{1,0:T(8,128)(2,1)S(1)} %get-tuple-element.144), channel_id=1, source_target_pairs={{0,8},{1,9},{2,10},{3,11},{4,12},{5,13},{6,14},{7,15},{8,0},{9,1},... | collective-permute-start | bytes 368648 | tf_op jit(solution)/shard_map/ppermute | solution.py:29
  125.1 10.8 %collective-permute-start.15 = (bf16[96,640]{1,0:T(8,128)(2,1)S(1)}, bf16[96,640]{1,0:T(8,128)(2,1)S(1)}, u32[]{:S(2)}, u32[]{:S(2)}) collective-permute-start(bf16[96,640]{1,0:T(8,128)(2,1)S(1)} %get-tuple-element.145), channel_id=1, source_target_pairs={{0,12},{1,13},{2,14},{3,15},{4,8},{5,9},{6,10},{7,11},{8,4},{9,5},... | collective-permute-start | bytes 368648 | tf_op jit(solution)/shard_map/ppermute | solution.py:29
  (15 other events, 46.8 us)
